TPU v7x, 32 devices: a whole 2x2x4 slice. The times are simulated.
32 devices in a mesh: seq: 4 (over y, x), fsdp: 8 (over z, core).
Axes of the slice: x: 2, y: 2, z: 4, core: 2. Of those that a mesh axis runs over, the one named last changes fastest.
Arguments:
- tokens: bfloat16 [16, 1024, 2048], P('fsdp', 'seq'), may hold values from -6 to 6
- cotangent: bfloat16 [16, 1024, 2048], P('fsdp', 'seq'), may hold values from -6 to 6
- lengths: int32 [16], P('fsdp'), may hold values from 256 to 1024, as said below
- attn_gain: float32 [2048], replicated, may hold values from 0.25 to 1.75
- query_weight: bfloat16 [2048, 2048], P('fsdp'), may hold values from -0.125 to 0.125
- key_weight: bfloat16 [2048, 512], P('fsdp'), may hold values from -0.125 to 0.125
- value_weight: bfloat16 [2048, 512], P('fsdp'), may hold values from -0.125 to 0.125
- query_gain: float32 [64], replicated, may hold values from 0.25 to 1.75
- key_gain: float32 [64], replicated, may hold values from 0.25 to 1.75
- out_weight: bfloat16 [2048, 2048], P('fsdp'), may hold values from -0.375 to 0.375
- ffn_gain: float32 [2048], replicated, may hold values from 0.25 to 1.75
- gate_weight: bfloat16 [8192, 2048], P('fsdp'), may hold values from -0.125 to 0.125
- up_weight: bfloat16 [8192, 2048], P('fsdp'), may hold values from -0.125 to 0.125
- down_weight: bfloat16 [8192, 2048], P('fsdp'), may hold values from -0.0625 to 0.0625
Outputs:
- output: bfloat16 [16, 1024, 2048], P('fsdp', 'seq')
- grad_tokens: bfloat16 [16, 1024, 2048], P('fsdp', 'seq')
- grad_attn_gain: float32 [2048], P('fsdp')
- grad_query_weight: float32 [2048, 2048], P('fsdp')
- grad_key_weight: float32 [2048, 512], P('fsdp')
- grad_value_weight: float32 [2048, 512], P('fsdp')
- grad_query_gain: float32 [64], P('fsdp')
- grad_key_gain: float32 [64], P('fsdp')
- grad_out_weight: float32 [2048, 2048], P('fsdp')
- grad_ffn_gain: float32 [2048], P('fsdp')
- grad_gate_weight: float32 [8192, 2048], P('fsdp')
- grad_up_weight: float32 [8192, 2048], P('fsdp')
- grad_down_weight: float32 [8192, 2048], P('fsdp')
Inputs may be any that keep to these rules, and one draw needn't show every extreme that they name: `lengths`: of the 2 slots of each index of fsdp, one, which one drawn from the seed, holds 1024 valid tokens.
All inputs are finite; a program needn't handle non-finite values.
Results may differ from a plain program's by a relative error of at most 0.02.
Values may be sent and summed in bfloat16 or wider, within the bound.
A program may use at most 768 MiB of HBM per device.

v0:
```python
import jax
import jax.numpy as jnp
from jax import lax
from jax.sharding import PartitionSpec as P

EPSILON = 1e-05
ROPE_BASE = 1000000.0
NEGATIVE = -1e30
TRANSPOSED = (((1,), (1,)), ((), ()))
LEADING = (((0,), (0,)), ((), ()))


def normed(values, gain_vec):
    return (
        values * lax.rsqrt(jnp.mean(values * values, axis=-1, keepdims=True) + EPSILON) * gain_vec
    )


def rotate(values):
    length = values.shape[1]
    head_width = values.shape[-1]
    half_width = head_width // 2
    places = jnp.arange(length, dtype=jnp.float32)
    freqs = ROPE_BASE ** (-(jnp.arange(half_width, dtype=jnp.float32) * 2.0) / head_width)
    angles = places[:, None] * freqs[None, :]
    shaped = (1, length) + (1,) * (values.ndim - 3) + (half_width,)
    cosine = jnp.cos(angles).reshape(shaped)
    sine = jnp.sin(angles).reshape(shaped)
    front = values[..., :half_width]
    behind = values[..., half_width:]
    return jnp.concatenate(
        [front * cosine - behind * sine, behind * cosine + front * sine], axis=-1
    )


def prepare(raw_heads, gain_vec):
    return rotate(normed(raw_heads, gain_vec))


def allowed_block(first_row, block_rows, length, lengths):
    query_pos = first_row + jnp.arange(block_rows, dtype=jnp.int32)
    key_pos = jnp.arange(length, dtype=jnp.int32)
    causal = key_pos[None, :] <= query_pos[:, None]
    valid = key_pos[None, :] < lengths[:, None]
    return (causal[None] & valid[:, None, :])[:, None, None]


def attend(queries, keys, values, lengths):
    slot_count, length, heads_kv, group_size, head_width = queries.shape
    block_rows = min(512, length)
    factor = head_width ** (-0.5)

    def one_block(block_index):
        first_row = block_index * block_rows
        query_part = lax.dynamic_slice_in_dim(queries, first_row, block_rows, 1)
        allowed = allowed_block(first_row, block_rows, length, lengths)
        scores = jnp.einsum(
            "bqhgd,bkhd->bhgqk", query_part, keys, preferred_element_type=jnp.float32
        )
        logits = jnp.where(allowed, scores * factor, NEGATIVE)
        highest = jnp.max(logits, axis=-1, keepdims=True)
        shifted = jnp.exp(logits - highest)
        row_total = jnp.sum(shifted, axis=-1, keepdims=True)
        probs = (shifted / row_total).astype(jnp.bfloat16)
        mixed_part = jnp.einsum(
            "bhgqk,bkhd->bqhgd", probs, values, preferred_element_type=jnp.float32
        )
        return (mixed_part.astype(jnp.bfloat16), (highest + jnp.log(row_total))[..., 0])

    results, log_sums = lax.map(one_block, jnp.arange(length // block_rows))
    results = jnp.moveaxis(results, 0, 1).reshape(
        slot_count, length, heads_kv * group_size * head_width
    )
    log_sums = jnp.moveaxis(log_sums, 0, 3).reshape(slot_count, heads_kv, group_size, length)
    return (results, log_sums)


def attend_back(queries, keys, values, grad_attended, log_sums, lengths):
    slot_count, length, heads_kv, group_size, head_width = queries.shape
    block_rows = min(512, length)
    factor = head_width ** (-0.5)

    def block_step(carry, block_index):
        grad_keys, grad_values = carry
        first_row = block_index * block_rows
        query_part = lax.dynamic_slice_in_dim(queries, first_row, block_rows, 1)
        grad_part = lax.dynamic_slice_in_dim(grad_attended, first_row, block_rows, 1)
        lse_part = lax.dynamic_slice_in_dim(log_sums, first_row, block_rows, 3)
        allowed = allowed_block(first_row, block_rows, length, lengths)
        scores = jnp.einsum(
            "bqhgd,bkhd->bhgqk", query_part, keys, preferred_element_type=jnp.float32
        )
        logits = jnp.where(allowed, scores * factor, NEGATIVE)
        probs = jnp.exp(logits - lse_part[..., None])
        grad_probs = jnp.einsum(
            "bqhgd,bkhd->bhgqk", grad_part, values, preferred_element_type=jnp.float32
        )
        inner = jnp.sum(probs * grad_probs, axis=-1, keepdims=True)
        grad_scores = (probs * (grad_probs - inner) * factor).astype(jnp.bfloat16)
        grad_query_part = jnp.einsum(
            "bhgqk,bkhd->bqhgd", grad_scores, keys, preferred_element_type=jnp.float32
        )
        grad_keys = grad_keys + jnp.einsum(
            "bhgqk,bqhgd->bkhd", grad_scores, query_part, preferred_element_type=jnp.float32
        )
        grad_values = grad_values + jnp.einsum(
            "bhgqk,bqhgd->bkhd",
            probs.astype(jnp.bfloat16),
            grad_part,
            preferred_element_type=jnp.float32,
        )
        return ((grad_keys, grad_values), grad_query_part)

    empty_kv = jnp.zeros((slot_count, length, heads_kv, head_width), jnp.float32)
    (grad_keys, grad_values), grad_queries = lax.scan(
        block_step, (empty_kv, empty_kv), jnp.arange(length // block_rows)
    )
    grad_queries = jnp.moveaxis(grad_queries, 0, 1).reshape(
        slot_count, length, heads_kv * group_size, head_width
    )
    return (grad_queries, grad_keys, grad_values)


def swiglu_back(gate_vals, up_vals, grad_mids):
    sigmoid_gate = jax.nn.sigmoid(gate_vals)
    active = gate_vals * sigmoid_gate
    mids = (active * up_vals).astype(jnp.bfloat16)
    gate_cot = (
        grad_mids * up_vals * sigmoid_gate * (1.0 + gate_vals * (1.0 - sigmoid_gate))
    ).astype(jnp.bfloat16)
    up_cot = (grad_mids * active).astype(jnp.bfloat16)
    return (gate_cot, up_cot, mids)


def on_device(
    tokens,
    cotangent,
    lengths,
    attn_gain,
    query_weight,
    key_weight,
    value_weight,
    query_gain,
    key_gain,
    out_weight,
    ffn_gain,
    gate_weight,
    up_weight,
    down_weight,
):
    slot_count, seq_rows, model_width = tokens.shape
    seq_count = lax.axis_size("seq")
    seq_place = lax.axis_index("seq")
    head_width = query_gain.shape[0]
    query_width = query_weight.shape[1]
    kv_width = key_weight.shape[1]
    token_rows = slot_count * seq_rows
    slot_len = seq_rows * seq_count
    heads_q = query_width // seq_count // head_width
    heads_kv = kv_width // seq_count // head_width
    group_size = heads_q // heads_kv
    places = seq_place * seq_rows + jnp.arange(seq_rows, dtype=jnp.int32)
    live_mask = (places[None, :] < lengths[:, None]).astype(jnp.float32).reshape(token_rows, 1)
    inputs = tokens.astype(jnp.float32).reshape(token_rows, model_width)
    normal_in = normed(inputs, attn_gain).astype(jnp.bfloat16)
    pieces = (
        lax.all_gather(query_weight, "fsdp", axis=0, tiled=True),
        lax.all_gather(key_weight, "fsdp", axis=0, tiled=True),
        lax.all_gather(value_weight, "fsdp", axis=0, tiled=True),
    )
    columns = normal_in
    q_rows = (
        jnp.dot(columns, pieces[0], preferred_element_type=jnp.float32)
        .astype(jnp.bfloat16)
        .reshape(slot_count, seq_rows, query_width)
    )
    k_rows = (
        jnp.dot(columns, pieces[1], preferred_element_type=jnp.float32)
        .astype(jnp.bfloat16)
        .reshape(slot_count, seq_rows, kv_width)
    )
    v_rows = (
        jnp.dot(columns, pieces[2], preferred_element_type=jnp.float32)
        .astype(jnp.bfloat16)
        .reshape(slot_count, seq_rows, kv_width)
    )
    head_side = (
        lax.all_to_all(q_rows, "seq", split_axis=2, concat_axis=1, tiled=True),
        lax.all_to_all(k_rows, "seq", split_axis=2, concat_axis=1, tiled=True),
        lax.all_to_all(v_rows, "seq", split_axis=2, concat_axis=1, tiled=True),
    )
    queries = prepare(
        head_side[0].astype(jnp.float32).reshape(slot_count, slot_len, heads_q, head_width),
        query_gain,
    )
    queries = queries.astype(jnp.bfloat16).reshape(
        slot_count, slot_len, heads_kv, group_size, head_width
    )
    keys = prepare(
        head_side[1].astype(jnp.float32).reshape(slot_count, slot_len, heads_kv, head_width),
        key_gain,
    ).astype(jnp.bfloat16)
    values = head_side[2].reshape(slot_count, slot_len, heads_kv, head_width)
    attended, log_sums = attend(queries, keys, values, lengths)
    mixed = lax.all_to_all(attended, "seq", split_axis=1, concat_axis=2, tiled=True)
    mixed_rows = mixed.reshape(token_rows, query_width)
    columns = mixed_rows
    attn_proj = jnp.dot(
        columns,
        lax.all_gather(out_weight, "fsdp", axis=0, tiled=True),
        preferred_element_type=jnp.float32,
    )
    hidden_res = inputs + attn_proj
    normal_mid = normed(hidden_res, ffn_gain).astype(jnp.bfloat16)
    pieces = (
        lax.all_gather(gate_weight, "fsdp", axis=0, tiled=True),
        lax.all_gather(up_weight, "fsdp", axis=0, tiled=True),
        lax.all_gather(down_weight, "fsdp", axis=0, tiled=True),
    )
    gate_vals = lax.dot_general(
        normal_mid, pieces[0], TRANSPOSED, preferred_element_type=jnp.float32
    )
    up_vals = lax.dot_general(normal_mid, pieces[1], TRANSPOSED, preferred_element_type=jnp.float32)
    mids = (jax.nn.silu(gate_vals) * up_vals).astype(jnp.bfloat16)
    ffn_out = jnp.dot(mids, pieces[2], preferred_element_type=jnp.float32)
    output = (live_mask * (hidden_res + ffn_out)).astype(jnp.bfloat16).reshape(tokens.shape)
    out_cot = cotangent.astype(jnp.float32).reshape(token_rows, model_width) * live_mask
    out_low = out_cot.astype(jnp.bfloat16)
    pieces = (
        lax.all_gather(gate_weight, "fsdp", axis=0, tiled=True),
        lax.all_gather(up_weight, "fsdp", axis=0, tiled=True),
        lax.all_gather(down_weight, "fsdp", axis=0, tiled=True),
    )
    gate_vals = lax.dot_general(
        normal_mid, pieces[0], TRANSPOSED, preferred_element_type=jnp.float32
    )
    up_vals = lax.dot_general(normal_mid, pieces[1], TRANSPOSED, preferred_element_type=jnp.float32)
    grad_mids = lax.dot_general(out_low, pieces[2], TRANSPOSED, preferred_element_type=jnp.float32)
    gate_cot, up_cot, mids = swiglu_back(gate_vals, up_vals, grad_mids)
    mid_cot = jnp.dot(gate_cot, pieces[0], preferred_element_type=jnp.float32) + jnp.dot(
        up_cot, pieces[1], preferred_element_type=jnp.float32
    )
    mid_cot, gate_store, up_store, mids_store = (mid_cot, gate_cot, up_cot, mids)
    ffn_sums = lax.psum_scatter(
        jnp.concatenate(
            [
                lax.dot_general(
                    gate_store, normal_mid, LEADING, preferred_element_type=jnp.float32
                ),
                lax.dot_general(up_store, normal_mid, LEADING, preferred_element_type=jnp.float32),
                lax.dot_general(mids_store, out_low, LEADING, preferred_element_type=jnp.float32),
            ],
            axis=1,
        ).astype(jnp.bfloat16),
        "fsdp",
        scatter_dimension=0,
        tiled=True,
    ).astype(jnp.float32)
    grad_gate = ffn_sums[:, :model_width]
    grad_up = ffn_sums[:, model_width : 2 * model_width]
    grad_down = ffn_sums[:, 2 * model_width :]
    unused_mid, pull_mid = jax.vjp(normed, hidden_res, ffn_gain)
    res_norm_cot, grad_ffn_gain = pull_mid(mid_cot)
    res_cot = out_cot + res_norm_cot
    res_low = res_cot.astype(jnp.bfloat16)
    full_query, full_key, full_value, full_out = (
        lax.all_gather(query_weight, "fsdp", axis=0, tiled=True),
        lax.all_gather(key_weight, "fsdp", axis=0, tiled=True),
        lax.all_gather(value_weight, "fsdp", axis=0, tiled=True),
        lax.all_gather(out_weight, "fsdp", axis=0, tiled=True),
    )
    attended_cot = lax.dot_general(
        res_low, full_out, TRANSPOSED, preferred_element_type=jnp.float32
    )
    attended_cot = attended_cot.astype(jnp.bfloat16).reshape(slot_count, seq_rows, query_width)
    q_again = (
        jnp.dot(normal_in, full_query, preferred_element_type=jnp.float32)
        .astype(jnp.bfloat16)
        .reshape(slot_count, seq_rows, query_width)
    )
    k_again = (
        jnp.dot(normal_in, full_key, preferred_element_type=jnp.float32)
        .astype(jnp.bfloat16)
        .reshape(slot_count, seq_rows, kv_width)
    )
    v_again = (
        jnp.dot(normal_in, full_value, preferred_element_type=jnp.float32)
        .astype(jnp.bfloat16)
        .reshape(slot_count, seq_rows, kv_width)
    )
    back_side = (
        lax.all_to_all(q_again, "seq", split_axis=2, concat_axis=1, tiled=True),
        lax.all_to_all(k_again, "seq", split_axis=2, concat_axis=1, tiled=True),
        lax.all_to_all(v_again, "seq", split_axis=2, concat_axis=1, tiled=True),
        lax.all_to_all(attended_cot, "seq", split_axis=2, concat_axis=1, tiled=True),
    )
    q_float = back_side[0].astype(jnp.float32).reshape(slot_count, slot_len, heads_q, head_width)
    k_float = back_side[1].astype(jnp.float32).reshape(slot_count, slot_len, heads_kv, head_width)
    q_prep, pull_query = jax.vjp(prepare, q_float, query_gain)
    k_prep, pull_key = jax.vjp(prepare, k_float, key_gain)
    queries_back = q_prep.astype(jnp.bfloat16).reshape(
        slot_count, slot_len, heads_kv, group_size, head_width
    )
    keys_back = k_prep.astype(jnp.bfloat16)
    values_back = back_side[2].reshape(slot_count, slot_len, heads_kv, head_width)
    grad_heads = back_side[3].reshape(slot_count, slot_len, heads_kv, group_size, head_width)
    query_cot, key_cot, value_cot = attend_back(
        queries_back, keys_back, values_back, grad_heads, log_sums, lengths
    )
    q_raw_cot, grad_query_gain = pull_query(query_cot)
    k_raw_cot, grad_key_gain = pull_key(key_cot)
    token_side = (
        lax.all_to_all(
            q_raw_cot.astype(jnp.bfloat16).reshape(slot_count, slot_len, heads_q * head_width),
            "seq",
            split_axis=1,
            concat_axis=2,
            tiled=True,
        ),
        lax.all_to_all(
            k_raw_cot.astype(jnp.bfloat16).reshape(slot_count, slot_len, heads_kv * head_width),
            "seq",
            split_axis=1,
            concat_axis=2,
            tiled=True,
        ),
        lax.all_to_all(
            value_cot.astype(jnp.bfloat16).reshape(slot_count, slot_len, heads_kv * head_width),
            "seq",
            split_axis=1,
            concat_axis=2,
            tiled=True,
        ),
    )
    query_grad_rows = token_side[0].reshape(token_rows, query_width)
    key_grad_rows = token_side[1].reshape(token_rows, kv_width)
    value_grad_rows = token_side[2].reshape(token_rows, kv_width)
    in_cot = (
        lax.dot_general(query_grad_rows, full_query, TRANSPOSED, preferred_element_type=jnp.float32)
        + lax.dot_general(key_grad_rows, full_key, TRANSPOSED, preferred_element_type=jnp.float32)
        + lax.dot_general(
            value_grad_rows, full_value, TRANSPOSED, preferred_element_type=jnp.float32
        )
    )
    unused_in, pull_in = jax.vjp(normed, inputs, attn_gain)
    in_norm_cot, grad_attn_gain = pull_in(in_cot)
    grad_tokens = (res_cot + in_norm_cot).astype(jnp.bfloat16).reshape(tokens.shape)
    grad_proj = jnp.concatenate([query_grad_rows, key_grad_rows, value_grad_rows], axis=1)
    attn_sums = lax.psum_scatter(
        jnp.concatenate(
            [
                lax.dot_general(normal_in, grad_proj, LEADING, preferred_element_type=jnp.float32),
                lax.dot_general(mixed_rows, res_low, LEADING, preferred_element_type=jnp.float32),
            ],
            axis=1,
        ).astype(jnp.bfloat16),
        "fsdp",
        scatter_dimension=0,
        tiled=True,
    ).astype(jnp.float32)
    grad_query = attn_sums[:, :query_width]
    grad_key = attn_sums[:, query_width : query_width + kv_width]
    grad_value = attn_sums[:, query_width + kv_width : query_width + 2 * kv_width]
    grad_out = attn_sums[:, query_width + 2 * kv_width :]
    gain_parts = (
        lax.psum_scatter(grad_attn_gain, "fsdp", scatter_dimension=0, tiled=True),
        lax.psum_scatter(grad_ffn_gain, "fsdp", scatter_dimension=0, tiled=True),
        lax.psum_scatter(grad_query_gain, "fsdp", scatter_dimension=0, tiled=True),
        lax.psum_scatter(grad_key_gain, "fsdp", scatter_dimension=0, tiled=True),
    )
    summed = (
        lax.psum(grad_query.astype(jnp.bfloat16), "seq").astype(jnp.float32),
        lax.psum(grad_key.astype(jnp.bfloat16), "seq").astype(jnp.float32),
        lax.psum(grad_value.astype(jnp.bfloat16), "seq").astype(jnp.float32),
        lax.psum(grad_out.astype(jnp.bfloat16), "seq").astype(jnp.float32),
        lax.psum(grad_gate.astype(jnp.bfloat16), "seq").astype(jnp.float32),
        lax.psum(grad_up.astype(jnp.bfloat16), "seq").astype(jnp.float32),
        lax.psum(grad_down.astype(jnp.bfloat16), "seq").astype(jnp.float32),
        lax.psum(gain_parts[0].astype(jnp.bfloat16), "seq").astype(jnp.float32),
        lax.psum(gain_parts[1].astype(jnp.bfloat16), "seq").astype(jnp.float32),
        lax.psum(gain_parts[2].astype(jnp.bfloat16), "seq").astype(jnp.float32),
        lax.psum(gain_parts[3].astype(jnp.bfloat16), "seq").astype(jnp.float32),
    )
    return (
        output,
        grad_tokens,
        summed[7],
        summed[0],
        summed[1],
        summed[2],
        summed[9],
        summed[10],
        summed[3],
        summed[8],
        summed[4],
        summed[5],
        summed[6],
    )


def solution(mesh):
    return jax.shard_map(
        on_device,
        mesh=mesh,
        in_specs=(
            P("fsdp", "seq", None),
            P("fsdp", "seq", None),
            P("fsdp"),
            P(),
            P("fsdp", None),
            P("fsdp", None),
            P("fsdp", None),
            P(),
            P(),
            P("fsdp", None),
            P(),
            P("fsdp", None),
            P("fsdp", None),
            P("fsdp", None),
        ),
        out_specs=(
            P("fsdp", "seq", None),
            P("fsdp", "seq", None),
            P("fsdp"),
            P("fsdp", None),
            P("fsdp", None),
            P("fsdp", None),
            P("fsdp"),
            P("fsdp"),
            P("fsdp", None),
            P("fsdp"),
            P("fsdp", None),
            P("fsdp", None),
            P("fsdp", None),
        ),
        check_vma=False,
    )
```

profile of v0, /device:TPU:6, one launch (start us, length us, event | category | flops | bytes accessed | tf_op | source)
XLA Modules:
  0.0 3203.1 jit_solution(4966029347424838511)
XLA Ops:
  15.6 24.3 all-gather.12.cloned.1.call-done
  48.7 21.5 all-gather.10.cloned.1.call-done
  78.3 75.1 %all-gather.8.cloned.1.call-done = bf16[2048,2048]{1,0:T(8,128)(2,1)} async-done(((bf16[256,2048]{1,0:T(8,128)(2,1)}), bf16[2048,2048]{1,0:T(8,128)(2,1)}) %all-gather.8.cloned.1.call-update) | async-done | bytes 8388624 | tf_op jit(solution)/shard_map/all_gather | solution.py:167
  153.4 8.5 convolution_convert_fusion.6
  165.7 5.4 all-to-all-start
  174.5 20.8 all-to-all-done
  200.6 5.9 reshape.418
  212.2 97.9 %while.27 = (s32[]{:T(128)}, bf16[2,2,512,2,4,64]{2,5,4,3,1,0:T(8,128)(2,1)}, f32[2,2,2,4,512]{4,3,2,1,0:T(4,128)S(1)}, s32[2]{0:T(128)S(1)}, s32[2]{0:T(128)S(1...) while((s32[]{:T(128)}, ...), condition=%wide.region_6.7_spmd, body=%wide.region_3.6_spmd.sunk | while | flops 2250238464 | bytes 126099720 | solution.py:70
  214.6 13.7 bitcast_reduce_fusion.2
  228.3 15.4 fusion.142
  243.7 17.8 fusion.143
  265.1 13.9 bitcast_reduce_fusion.2
  279.0 15.4 fusion.142
  294.5 14.4 fusion.143
  310.2 7.7 copy.117
  317.8 8.7 reshape.430
  326.5 5.6 all-to-all-start.3
  336.1 19.0 all-to-all-done.3
  361.7 7.8 multiply_reduce_fusion.4
  371.9 152.2 %all-gather.18.cloned.1.call-done = bf16[8192,2048]{1,0:T(8,128)(2,1)} async-done(((bf16[1024,2048]{1,0:T(8,128)(2,1)}), bf16[8192,2048]{1,0:T(8,128)(2,1)}) %all-gather.18.cloned.1.call-update) | async-done | bytes 33554448 | tf_op jit(solution)/shard_map/all_gather | solution.py:217
  524.1 28.1 fusion.90
  552.1 260.2 %all-gather.16.cloned.1.call-done = bf16[8192,2048]{1,0:T(8,128)(2,1)} async-done(((bf16[1024,2048]{1,0:T(8,128)(2,1)}), bf16[8192,2048]{1,0:T(8,128)(2,1)}) %all-gather.16.cloned.1.call-update) | async-done | bytes 33554448 | tf_op jit(solution)/shard_map/all_gather | solution.py:216
  812.4 28.6 fusion.89
  841.0 259.8 %all-gather.20.cloned.1.call-done = bf16[8192,2048]{1,0:T(8,128)(2,1)} async-done(((bf16[1024,2048]{1,0:T(8,128)(2,1)}), bf16[8192,2048]{1,0:T(8,128)(2,1)}) %all-gather.20.cloned.1.call-update) | async-done | bytes 33554448 | tf_op jit(solution)/shard_map/all_gather | solution.py:218
  1100.8 38.6 %multiply_convert_fusion = (bf16[512,8192]{1,0:T(8,128)(2,1)}, bf16[512,8192]{1,0:T(8,128)(2,1)}, bf16[512,8192]{1,0:T(8,128)(2,1)}) fusion(f32[512,8192]{1,0:T(8,128)} %fusion.89, f32[512,8192]{1,0:T(8,128)} %fusion.90, bf16[512,2048]{1,0:T(8,128)(2,1)} %fusion.63, bf16[8192,2048]{1,0:T(8,128)(2,1)} %all-gather.20.cloned.1.call-done), kind=kOutput, calls=%fused_computation.72 | convolution fusion | flops 17242783744 | bytes 94371840 | tf_op jit(solution)/shard_map/dot_general | solution.py:238
  1139.4 23.9 fusion.91
  1163.4 25.6 multiply_reduce_fusion
  1190.3 9.7 convolution_convert_fusion.5
  1208.2 24.0 all-to-all-done.4
  1242.8 366.0 %while.28 = (s32[]{:T(128)}, f32[2,1024,2,64]{1,3,2,0:T(8,128)}, f32[2,1024,2,64]{1,3,2,0:T(8,128)}, f32[2,2,512,2,4,64]{2,5,4,3,1,0:T(8,128)}, s32[2]{0:T(128)S...) while((s32[]{:T(128)}, f32[2,1024,2,64]{1,3,2,0:T(8,128)}, ...), condition=%wide.region_11.12_spmd.clone, body=%wide.region_9.11_spmd.clone.sunk | while | flops 5589455360 | bytes 392929536 | solution.py:115
  1245.2 13.2 fusion.153
  1258.4 16.2 fusion.155
  1274.7 14.5 fusion.152
  1289.1 67.0 %fusion.154 = f32[2,1024,2,64]{1,3,2,0:T(8,128)} fusion(f32[2,2,512,4,1024]{4,2,3,1,0:T(8,128)} %fusion.152, f32[2,2,512,4,1024]{4,2,3,1,0:T(8,128)} %fusion.153, f32[2,2,4,512]{3,2,1,0:T(4,128)S(1)} %constant_dynamic-slice_fusion.2, pred[2,512,1024]{2,1,0:T(8,128)(4,1)} %copy-done.10, f32[2,1024,2,64]{1,3,2,0:T(8,128)} %get-tuple-element.480, ...), kind=kOutput, calls=%fused_computation.41.clone.1 | convolution fusion | flops 1166550016 | bytes 139526144 | tf_op jit(solution)/shard_map/while/body/eval_jaxpr/bhgqk,bqhgd->bkhd/dot_general | solution.py:103
  1356.2 68.2 %bitcast_dynamic-update-slice_fusion.5 = f32[2,2,512,2,4,64]{2,5,4,3,1,0:T(8,128)} fusion(f32[2,2,512,2,4,64]{2,5,4,3,1,0:T(8,128)} %get-tuple-element.482, s32[]{:T(128)S(6)} %copy.154, f32[2,2,512,4,1024]{4,2,3,1,0:T(8,128)} %fusion.152, f32[2,2,512,4,1024]{4,2,3,1,0:T(8,128)} %fusion.153, f32[2,2,4,512]{3,2,1,0:T(4,128)S(1)} %constant_dynamic-slice_fusion.2, ...), kind=kOutput, calls=%fused_computation.36.clone.1 | convolution fusion | flops 1166025728 | bytes 139001856 | tf_op jit(solution)/shard_map/while/body/eval_jaxpr/bhgqk,bkhd->bqhgd/dot_general | solution.py:100
  1426.5 13.2 fusion.153
  1439.7 16.5 fusion.155
  1456.3 14.5 fusion.152
  1470.7 69.5 %fusion.154 = f32[2,1024,2,64]{1,3,2,0:T(8,128)} fusion(f32[2,2,512,4,1024]{4,2,3,1,0:T(8,128)} %fusion.152, f32[2,2,512,4,1024]{4,2,3,1,0:T(8,128)} %fusion.153, f32[2,2,4,512]{3,2,1,0:T(4,128)S(1)} %constant_dynamic-slice_fusion.2, pred[2,512,1024]{2,1,0:T(8,128)(4,1)} %copy-done.10, f32[2,1024,2,64]{1,3,2,0:T(8,128)} %get-tuple-element.480, ...), kind=kOutput, calls=%fused_computation.41.clone.1 | convolution fusion | flops 1166550016 | bytes 139526144 | tf_op jit(solution)/shard_map/while/body/eval_jaxpr/bhgqk,bqhgd->bkhd/dot_general | solution.py:103
  1540.2 68.2 %bitcast_dynamic-update-slice_fusion.5 = f32[2,2,512,2,4,64]{2,5,4,3,1,0:T(8,128)} fusion(f32[2,2,512,2,4,64]{2,5,4,3,1,0:T(8,128)} %get-tuple-element.482, s32[]{:T(128)S(6)} %copy.154, f32[2,2,512,4,1024]{4,2,3,1,0:T(8,128)} %fusion.152, f32[2,2,512,4,1024]{4,2,3,1,0:T(8,128)} %fusion.153, f32[2,2,4,512]{3,2,1,0:T(4,128)S(1)} %constant_dynamic-slice_fusion.2, ...), kind=kOutput, calls=%fused_computation.36.clone.1 | convolution fusion | flops 1166025728 | bytes 139001856 | tf_op jit(solution)/shard_map/while/body/eval_jaxpr/bhgqk,bkhd->bqhgd/dot_general | solution.py:100
  1608.8 7.5 copy.96
  1616.3 6.6 reshape.409
  1646.1 5.5 fusion.60
  1651.6 6.2 copy.97
  1662.1 10.7 convolution_convert_fusion.4
  1675.7 8.0 all-to-all-done.5
  1686.3 8.5 convolution_convert_fusion.3
  1694.8 16.3 pad_maximum_fusion.1
  1712.7 25.8 convolution_convert_fusion.1
  1738.5 25.2 convolution_convert_fusion.2
  1763.8 25.3 convolution_convert_fusion
  1789.1 69.2 %pad_maximum_fusion = bf16[8192,6144]{0,1:T(8,128)(2,1)} fusion(bf16[8192,2048]{0,1:T(8,128)(2,1)} %convolution_convert_fusion, bf16[8192,2048]{0,1:T(8,128)(2,1)} %convolution_convert_fusion.1, bf16[8192,2048]{0,1:T(8,128)(2,1)} %convolution_convert_fusion.2), kind=kLoop, calls=%fused_computation.67 | loop fusion | flops 301989888 | bytes 201326592 | tf_op jit(solution)/shard_map/concatenate | solution.py:245
  1858.4 59.1 %reduce-scatter.3.cloned.1.call-done = bf16[256,5120]{1,0:T(8,128)(2,1)} async-done(((bf16[2048,5120]{1,0:T(8,128)(2,1)}), bf16[256,5120]{1,0:T(8,128)(2,1)}) %reduce-scatter.3.cloned.1.call-update) | async-done | bytes 2621456 | tf_op jit(solution)/shard_map/reduce_scatter | solution.py:349
  1922.4 950.8 %reduce-scatter.5.cloned.1.call-done = bf16[1024,6144]{0,1:T(8,128)(2,1)} async-done(((bf16[8192,6144]{0,1:T(8,128)(2,1)}), bf16[1024,6144]{0,1:T(8,128)(2,1)}) %reduce-scatter.5.cloned.1.call-update) | async-done | bytes 12582928 | tf_op jit(solution)/shard_map/reduce_scatter | solution.py:244
  2873.2 9.1 fusion.86
  2884.9 26.3 multiply_convert_fusion.3
  2912.9 7.1 fusion.92
  2924.2 26.1 all-reduce.8
  2950.6 8.3 all-reduce.9
  2961.0 6.1 fusion.62
  2967.1 199.5 %all-reduce.13.cloned.1.call-done = (bf16[1024,2048]{0,1:T(8,128)(2,1)}, bf16[1024,2048]{0,1:T(8,128)(2,1)}, bf16[1024,2048]{0,1:T(8,128)(2,1)}, bf16[256,2048]{...) async-done(((bf16[1024,2048]{0,1:T(8,128)(2,1)}, bf16[1024,2048]{0,1:T(8,128)(2,1)}, bf16[1024,2048]{0,1:T(8,128)(2,1)}, ...) | async-done | bytes 15204368 | tf_op jit(solution)/shard_map/psum | solution.py:376
  3174.7 7.1 copy.107
  3181.8 7.1 copy.108
  3189.0 7.1 copy.109
  (298 shorter events, 141.7 us)
Async XLA Ops:
  7.2 32.8 %all-gather.12.cloned.1.call-start = ((), (), s32[]{:S(2)}) async-start(), calls=%async_computation.12 | async-start | bytes 2359296 | tf_op jit(solution)/shard_map/all_gather | solution.py:169
  7.9 62.2 %all-gather.10.cloned.1.call-start = ((), (), s32[]{:S(2)}) async-start(), calls=%async_computation.11 | async-start | bytes 2359296 | tf_op jit(solution)/shard_map/all_gather | solution.py:168
  8.7 144.7 %all-gather.8.cloned.1.call-start = ((), (), s32[]{:S(2)}) async-start(), calls=%async_computation.10 | async-start | bytes 9437184 | tf_op jit(solution)/shard_map/all_gather | solution.py:167
  9.4 352.3 %all-gather.14.cloned.1.call-start = ((), (), s32[]{:S(2)}) async-start(), calls=%async_computation.13 | async-start | bytes 9437184 | tf_op jit(solution)/shard_map/all_gather | solution.py:210
  10.0 514.1 %all-gather.18.cloned.1.call-start = ((), (), s32[]{:S(2)}) async-start(), calls=%async_computation.15 | async-start | bytes 37748736 | tf_op jit(solution)/shard_map/all_gather | solution.py:217
  10.6 801.8 %all-gather.16.cloned.1.call-start = ((), (), s32[]{:S(2)}) async-start(), calls=%async_computation.14 | async-start | bytes 37748736 | tf_op jit(solution)/shard_map/all_gather | solution.py:216
  11.2 1089.6 %all-gather.20.cloned.1.call-start = ((), (), s32[]{:S(2)}) async-start(), calls=%async_computation.16 | async-start | bytes 37748736 | tf_op jit(solution)/shard_map/all_gather | solution.py:218
  15.6 54.6 %copy-start.33 = (bf16[512,2048]{1,0:T(8,128)(2,1)S(1)}, bf16[512,2048]{1,0:T(8,128)(2,1)}, u32[]{:S(2)}) copy-start(bf16[512,2048]{1,0:T(8,128)(2,1)} %fusion.66) | copy-start | bytes 6291460
  44.5 29.6 all-to-all-start.2
  74.1 91.6 %all-to-all-start.1 = ((bf16[2,256,512]{1,0,2:T(2,128)(2,1)}), bf16[2,256,512]{1,0,2:T(2,128)(2,1)S(1)}, u32[]{:S(2)}, u32[]{:S(2)}) async-start(bf16[2,256,512]{1,0,2:T(2,128)(2,1)} %copy.86), calls=%async_computation.1 | async-start | bytes 1048576 | tf_op jit(solution)/shard_map/all_to_all | solution.py:189
  165.7 29.6 all-to-all-start
  171.8 39.5 %copy-start.23 = (f32[1024,32]{0,1:T(8,128)}, f32[1024,32]{0,1:T(8,128)S(1)}, u32[]{:S(2)}) copy-start(f32[1024,32]{0,1:T(8,128)S(1)} %get-tuple-element.302) | copy-start | bytes 393220
  171.8 39.5 %copy-start.25 = (f32[1024,32]{0,1:T(8,128)}, f32[1024,32]{0,1:T(8,128)S(1)}, u32[]{:S(2)}) copy-start(f32[1024,32]{0,1:T(8,128)S(1)} %get-tuple-element.303) | copy-start | bytes 393220
  173.5 27.1 copy-start.8
  228.3 15.4 copy-start.29
  279.0 15.4 copy-start.29
  310.2 16.3 copy-start.1
  310.2 16.3 copy-start.3
  310.2 16.3 copy-start.11
  310.2 16.3 copy-start.51
  326.5 28.5 all-to-all-start.3
  356.4 5.3 copy-start.6
  361.7 9.8 copy-start.55
  371.9 440.5 %copy-start.27 = (bf16[512,2048]{1,0:T(8,128)(2,1)}, bf16[512,2048]{1,0:T(8,128)(2,1)S(1)}, u32[]{:S(2)}) copy-start(bf16[512,2048]{1,0:T(8,128)(2,1)S(1)} %multiply_convert_fusion.4) | copy-start | bytes 6291460
  1139.4 24.0 copy-start.15
  1139.4 24.0 copy-start.56
  1139.4 24.0 copy-start.63
  1163.3 25.6 copy-start.67
  1163.4 25.6 copy-start.18
  1163.4 25.6 copy-start.60
  1190.3 9.8 copy-start.13
  1200.1 8.1 copy-start.52
  1204.0 28.2 all-to-all-start.4
  1233.6 9.2 copy-start.2
  1233.6 9.2 copy-start.4
  1233.6 9.2 copy-start.12
  1233.6 9.2 copy-start.54
  1245.2 13.2 copy-start.10
  1426.5 13.2 copy-start.10
  1616.3 6.7 copy-start.24
  1616.3 6.7 copy-start.26
  1623.0 4.7 copy-start.9
  1623.0 4.7 copy-start.46
  1627.5 7.4 copy-start.39
  1627.5 7.4 copy-start.70
  1630.0 11.2 all-to-all-start.6
  1634.9 4.7 copy-start.41
  1634.9 5.9 copy-start.44
  1641.2 16.6 all-to-all-start.7
  1657.8 25.9 all-to-all-start.5
  1662.0 255.5 %reduce-scatter.3.cloned.1.call-start = ((), (), s32[]{:S(2)}) async-start(), calls=%async_computation.17 | async-start | bytes 23592960 | tf_op jit(solution)/shard_map/reduce_scatter | solution.py:349
  1686.3 8.5 copy-start.31
  1711.2 1162.1 %reduce-scatter.5.cloned.1.call-start = ((), (), s32[]{:S(2)}) async-start(), calls=%async_computation.18 | async-start | bytes 113246208 | tf_op jit(solution)/shard_map/reduce_scatter | solution.py:244
  1738.5 25.2 copy-start.35
  1858.3 1308.3 %all-reduce.13.cloned.1.call-start = ((), (), s32[]{:S(2)}) async-start(), calls=%async_computation.19 | async-start | bytes 30408704 | tf_op jit(solution)/shard_map/psum | solution.py:376
  2884.9 26.3 copy-start.20
  2884.9 26.3 copy-start.36
  2912.8 7.1 copy-start.7
  2912.8 7.1 copy-start.22
  2912.8 7.2 copy-start.37
  2912.8 7.2 copy-start.50
  2912.9 7.2 copy-start.58
  2920.1 41.0 %copy-start.65 = (f32[1,2,2,128]{3,1,2,0:T(2,128)S(1)}, f32[1,2,2,128]{3,1,2,0:T(2,128)}, u32[]{:S(2)}) copy-start(f32[1,2,2,128]{3,1,2,0:T(2,128)} %copy-done.64) | copy-start | bytes 6148
  3166.7 6.5 copy-start.40
  (33 other events, 62.1 us)
Sparse Core Ops, SparseCore 0:
  9.6 30.2 all-gather.11
  41.5 28.5 all-gather.9
  71.8 81.5 all-gather.7
  154.8 80.5 all-gather.13
  236.9 287.1 all-gather.17
  525.5 286.7 all-gather.15
  814.0 286.7 all-gather.19
  1711.3 206.1 reduce-scatter.2
  1919.8 953.3 reduce-scatter.4
  2882.5 284.1 all-reduce.12
where the time goes:
time: 3210 us; the launch traced here: 3200 us
  waiting for transfers between devices  2080 us (65%)
  matrix products  732 us (23%)
  other arithmetic  166 us (5%)
  local copies, waits for them, and re-layouts  133 us (4%)
  starting transfers between devices  38.2 us (1%)
  blocking collectives  34.4 us (1%)
    reduce_scatter x1, waiting for transfers between devices, on_device(): lax.psum_scatter(jnp.concatenate([lax.dot_general(gate_store, normal_mid,...  951 us
    all_gather x1, waiting for transfers between devices, on_device(): lax.all_gather(gate_weight, 'fsdp', axis=0, tiled=True)  260 us
    all_gather x1, waiting for transfers between devices, on_device(): lax.all_gather(down_weight, 'fsdp', axis=0, tiled=True)  260 us
    psum x1, waiting for transfers between devices, on_device(): lax.psum(grad_gate.astype(jnp.bfloat16), 'seq').astype(jnp.float32)  200 us
    all_gather x1, waiting for transfers between devices, on_device(): lax.all_gather(up_weight, 'fsdp', axis=0, tiled=True)  152 us
    dot_general x2, matrix products, block_step(): jnp.einsum('bhgqk,bqhgd->bkhd', grad_scores, query_part, preferred_elemen...  136 us
    dot_general x2, matrix products, block_step(): jnp.einsum('bhgqk,bkhd->bqhgd', grad_scores, keys, preferred_element_type...  136 us
    all_gather x1, waiting for transfers between devices, on_device(): lax.all_gather(query_weight, 'fsdp', axis=0, tiled=True)  75.1 us
  transfers between devices with their start and end apart: 18, of which 14 were waited for; matrix products, arithmetic and copies ran while one was open for 14% of the time, Pallas kernels for 0%

commit v1 on v0

v1 whole, which is shorter than its diff:
```python
import functools

import jax
import jax.numpy as jnp
import numpy as np
from jax import lax
from jax.experimental import pallas as pl
from jax.experimental.pallas import tpu as pltpu
from jax.sharding import PartitionSpec as P

EPSILON = 1e-05
ROPE_BASE = 1000000.0
NEGATIVE = -1e30
F32 = jnp.float32
BF16 = jnp.bfloat16
NN = (((1,), (0,)), ((), ()))
NT = (((1,), (1,)), ((), ()))
TN = (((0,), (0,)), ((), ()))
SMEM = pl.BlockSpec(memory_space=pltpu.SMEM)
VMEM = pl.BlockSpec(memory_space=pltpu.VMEM)
VMEM_LIMIT = 58 << 20
HEAD = 64
BLOCK = 256
CHUNKS = 2


def dot(a, b, dims=NN):
    return lax.dot_general(a, b, dims, preferred_element_type=F32)


def partner(v):
    lane = lax.broadcasted_iota(jnp.int32, v.shape, 1)
    return jnp.where(lane % HEAD < HEAD // 2, pltpu.roll(v, 96, 1), pltpu.roll(v, 32, 1))


def head_mean(v, ones):
    high = v.astype(BF16)
    rest = (v - high.astype(F32)).astype(BF16)
    return dot(high, ones) + dot(rest, ones)


def prepare_heads(sizes, place, qkv_ref, qg_ref, kg_ref, cos_ref, sin_ref, ones, q_s, k_s, v_s):
    hq, hkv, _ = sizes
    seqs, rows_in, _ = qkv_ref.shape
    for c in range(seqs):
        j = jnp.bitwise_xor(place, c)
        rows = slice(c * rows_in, (c + 1) * rows_in)
        cos = cos_ref[rows, :]
        sin = sin_ref[rows, :]
        for p in range((hq + hkv) // 2):
            is_query = p < hq // 2
            x = qkv_ref[j, :, p * 128 : (p + 1) * 128].astype(F32)
            gain = qg_ref[...] * HEAD**-0.5 if is_query else kg_ref[...]
            y = x * lax.rsqrt(head_mean(x * x, ones) + EPSILON) * gain
            y = (y * cos + partner(y) * sin).astype(BF16)
            for t in range(2):
                part = y[:, t * HEAD : (t + 1) * HEAD]
                if is_query:
                    q_s[2 * p + t, rows, :] = part
                else:
                    k_s[2 * p - hq + t, rows, :] = part
        for t in range(hkv):
            start = (hq + hkv + t) * HEAD
            v_s[t, rows, :] = qkv_ref[j, :, start : start + HEAD]


def allowed_keys(block, first, keys, length):
    bound = jnp.minimum(first + lax.broadcasted_iota(jnp.int32, (block, 1), 0), length - 1)
    return lax.broadcasted_iota(jnp.int32, (block, keys), 1) <= bound


def attend_kernel(
    sizes, place_ref, len_ref, qkv_ref, qg_ref, kg_ref, cos_ref, sin_ref, ones_ref,
    out_ref, lse_ref, q_s, k_s, v_s, o_s,
):
    hq, hkv, group = sizes
    seqs, rows_in, _ = qkv_ref.shape
    place = place_ref[0]
    prepare_heads(
        sizes, place, qkv_ref, qg_ref, kg_ref, cos_ref, sin_ref, ones_ref[...], q_s, k_s, v_s
    )
    for i in range(seqs * rows_in // BLOCK):
        keys = (i + 1) * BLOCK
        rows = slice(i * BLOCK, (i + 1) * BLOCK)
        keep = allowed_keys(BLOCK, i * BLOCK, keys, len_ref[0])

        def one_head(h, _):
            kv = h // group
            scores = dot(q_s[h, rows, :], k_s[kv, :keys, :], NT)
            scores = jnp.where(keep, scores, NEGATIVE)
            highest = jnp.max(scores, axis=1, keepdims=True)
            shifted = jnp.exp(scores - highest)
            total = jnp.sum(shifted, axis=1, keepdims=True)
            mixed = dot(shifted.astype(BF16), v_s[kv, :keys, :]) / total
            o_s[h, rows, :] = mixed.astype(BF16)
            lse_ref[h, rows, :] = highest + jnp.log(total)
            return 0

        lax.fori_loop(0, hq, one_head, 0)
    for c in range(seqs):
        j = jnp.bitwise_xor(place, c)
        rows = slice(c * rows_in, (c + 1) * rows_in)
        for p in range(hq // 2):
            out_ref[j, :, p * 128 : (p + 1) * 128] = jnp.concatenate(
                [o_s[2 * p, rows, :], o_s[2 * p + 1, rows, :]], axis=1
            )


def attend_back_kernel(
    sizes, place_ref, len_ref, qkv_ref, cot_ref, lse_ref, qg_ref, kg_ref, cos_ref, sin_ref,
    ones_ref, dqkv_ref, dgain_ref, q_s, k_s, v_s, cot_s, dq_s, dk_s, dv_s,
):
    hq, hkv, group = sizes
    seqs, rows_in, _ = qkv_ref.shape
    place = place_ref[0]
    ones = ones_ref[...]
    prepare_heads(sizes, place, qkv_ref, qg_ref, kg_ref, cos_ref, sin_ref, ones, q_s, k_s, v_s)
    for c in range(seqs):
        j = jnp.bitwise_xor(place, c)
        for h in range(hq):
            cot_s[h, c * rows_in : (c + 1) * rows_in, :] = cot_ref[
                j, :, h * HEAD : (h + 1) * HEAD
            ]
    dk_s[...] = jnp.zeros_like(dk_s)
    dv_s[...] = jnp.zeros_like(dv_s)
    for i in range(seqs * rows_in // BLOCK):
        keys = (i + 1) * BLOCK
        rows = slice(i * BLOCK, (i + 1) * BLOCK)
        keep = allowed_keys(BLOCK, i * BLOCK, keys, len_ref[0])

        def one_head(h, _):
            kv = h // group
            q = q_s[h, rows, :]
            cot = cot_s[h, rows, :]
            k = k_s[kv, :keys, :]
            scores = jnp.where(keep, dot(q, k, NT), NEGATIVE)
            probs = jnp.exp(scores - lse_ref[h, rows, :])
            prob_cot = dot(cot, v_s[kv, :keys, :], NT)
            inner = jnp.sum(probs * prob_cot, axis=1, keepdims=True)
            score_cot = (probs * (prob_cot - inner)).astype(BF16)
            dq_s[h, rows, :] = dot(score_cot, k) * HEAD**-0.5
            dk_s[kv, :keys, :] += dot(score_cot, q, TN)
            dv_s[kv, :keys, :] += dot(probs.astype(BF16), cot, TN)
            return 0

        lax.fori_loop(0, hq, one_head, 0)
    gain_sums = [jnp.zeros((1, 128), F32), jnp.zeros((1, 128), F32)]
    for c in range(seqs):
        j = jnp.bitwise_xor(place, c)
        rows = slice(c * rows_in, (c + 1) * rows_in)
        cos = cos_ref[rows, :]
        sin = sin_ref[rows, :]
        for p in range((hq + hkv) // 2):
            is_query = p < hq // 2
            x = qkv_ref[j, :, p * 128 : (p + 1) * 128].astype(F32)
            gain = qg_ref[...] if is_query else kg_ref[...]
            source, first = (dq_s, 2 * p) if is_query else (dk_s, 2 * p - hq)
            turned = jnp.concatenate([source[first, rows, :], source[first + 1, rows, :]], axis=1)
            scale = lax.rsqrt(head_mean(x * x, ones) + EPSILON)
            straight = turned * cos + partner(turned * sin)
            unit = x * scale
            which = 0 if is_query else 1
            gain_sums[which] += jnp.sum(straight * unit, axis=0, keepdims=True)
            pulled = gain * straight
            dx = scale * (pulled - unit * head_mean(unit * pulled, ones))
            dqkv_ref[j, :, p * 128 : (p + 1) * 128] = dx.astype(BF16)
        for p in range(hkv // 2):
            start = (hq + hkv) * HEAD + p * 128
            dqkv_ref[j, :, start : start + 128] = jnp.concatenate(
                [dv_s[2 * p, rows, :], dv_s[2 * p + 1, rows, :]], axis=1
            ).astype(BF16)
    dgain_ref[0:1, :] = gain_sums[0]
    dgain_ref[1:2, :] = gain_sums[1]


def position_tables(length):
    places = np.arange(length, dtype=np.float32)
    half = HEAD // 2
    freqs = np.float32(ROPE_BASE) ** (-(np.arange(half, dtype=np.float32) * 2.0) / HEAD)
    angles = places[:, None] * freqs.astype(np.float32)[None, :]
    cos = np.cos(angles).astype(np.float32)
    sin = np.sin(angles).astype(np.float32)
    ones = np.kron(np.eye(2), np.ones((HEAD, HEAD)) / HEAD)
    return (
        jnp.asarray(np.concatenate([cos] * 4, axis=1)),
        jnp.asarray(np.concatenate([-sin, sin, -sin, sin], axis=1)),
        jnp.asarray(ones, dtype=BF16),
    )


def attend(sizes, place, length, qkv, gains, tables):
    seqs, rows_in, _ = qkv.shape
    hq, hkv, _ = sizes
    slot = seqs * rows_in
    return pl.pallas_call(
        functools.partial(attend_kernel, sizes),
        out_shape=(
            jax.ShapeDtypeStruct((seqs, rows_in, hq * HEAD), BF16),
            jax.ShapeDtypeStruct((hq, slot, 1), F32),
        ),
        in_specs=[SMEM, SMEM] + [VMEM] * 6,
        out_specs=(VMEM, VMEM),
        scratch_shapes=[
            pltpu.VMEM((hq, slot, HEAD), BF16),
            pltpu.VMEM((hkv, slot, HEAD), BF16),
            pltpu.VMEM((hkv, slot, HEAD), BF16),
            pltpu.VMEM((hq, slot, HEAD), BF16),
        ],
        compiler_params=pltpu.CompilerParams(vmem_limit_bytes=VMEM_LIMIT),
        cost_estimate=pl.CostEstimate(
            flops=20 * hq * slot * slot * HEAD, bytes_accessed=1 << 23, transcendentals=0
        ),
        name="attend",
    )(place, length, qkv, *gains, *tables)


def attend_back(sizes, place, length, qkv, cot, lse, gains, tables):
    seqs, rows_in, width = qkv.shape
    hq, hkv, _ = sizes
    slot = seqs * rows_in
    return pl.pallas_call(
        functools.partial(attend_back_kernel, sizes),
        out_shape=(
            jax.ShapeDtypeStruct((seqs, rows_in, width), BF16),
            jax.ShapeDtypeStruct((2, 128), F32),
        ),
        in_specs=[SMEM, SMEM] + [VMEM] * 8,
        out_specs=(VMEM, VMEM),
        scratch_shapes=[
            pltpu.VMEM((hq, slot, HEAD), BF16),
            pltpu.VMEM((hkv, slot, HEAD), BF16),
            pltpu.VMEM((hkv, slot, HEAD), BF16),
            pltpu.VMEM((hq, slot, HEAD), BF16),
            pltpu.VMEM((hq, slot, HEAD), F32),
            pltpu.VMEM((hkv, slot, HEAD), F32),
            pltpu.VMEM((hkv, slot, HEAD), F32),
        ],
        compiler_params=pltpu.CompilerParams(vmem_limit_bytes=VMEM_LIMIT),
        cost_estimate=pl.CostEstimate(
            flops=36 * hq * slot * slot * HEAD, bytes_accessed=1 << 23, transcendentals=0
        ),
        name="attend_back",
    )(place, length, qkv, cot, lse, *gains, *tables)


def ffn_kernel(has_sum, mid_ref, cot_ref, gate_ref, up_ref, down_ref, *refs):
    if has_sum:
        sum_ref, acts_ref, pull_ref = refs
    else:
        acts_ref, pull_ref = refs
    model = mid_ref.shape[-1]
    hidden = acts_ref.shape[-1]
    gate_w = gate_ref[...].reshape(hidden, model)
    up_w = up_ref[...].reshape(hidden, model)
    down_w = down_ref[...].reshape(hidden, model)
    mid = mid_ref[...]
    gate = dot(mid, gate_w, NT)
    up = dot(mid, up_w, NT)
    mids_cot = dot(cot_ref[...], down_w, NT)
    sigmoid = jax.nn.sigmoid(gate)
    active = gate * sigmoid
    gate_cot = (mids_cot * up * sigmoid * (1.0 + gate * (1.0 - sigmoid))).astype(BF16)
    up_cot = (mids_cot * active).astype(BF16)
    acts_ref[0] = gate_cot
    acts_ref[1] = up_cot
    acts_ref[2] = (active * up).astype(BF16)
    pulled = dot(gate_cot, gate_w) + dot(up_cot, up_w)
    if has_sum:
        pulled = pulled + sum_ref[...]
    pull_ref[...] = pulled.astype(pull_ref.dtype)


def ffn_both(mid, cot, weights, summed, last):
    tokens, model = mid.shape
    shards, _, part, _ = weights.shape
    hidden = shards * part
    tile = min(256, tokens)

    def weight_spec(kind):
        return pl.BlockSpec(
            (shards, 1, part, model),
            lambda i: (0, kind, 0, 0),
            pipeline_mode=pl.Buffered(buffer_count=1),
        )

    row_spec = pl.BlockSpec((tile, model), lambda i: (i, 0))
    extra = () if summed is None else (summed,)
    return pl.pallas_call(
        functools.partial(ffn_kernel, summed is not None),
        grid=(tokens // tile,),
        out_shape=(
            jax.ShapeDtypeStruct((3, tokens, hidden), BF16),
            jax.ShapeDtypeStruct((tokens, model), BF16 if last else F32),
        ),
        in_specs=[row_spec, row_spec, weight_spec(0), weight_spec(1), weight_spec(2)]
        + [row_spec] * len(extra),
        out_specs=(pl.BlockSpec((3, tile, hidden), lambda i: (0, i, 0)), row_spec),
        compiler_params=pltpu.CompilerParams(vmem_limit_bytes=VMEM_LIMIT),
        cost_estimate=pl.CostEstimate(
            flops=10 * tokens * model * hidden,
            bytes_accessed=4 * tokens * model + 6 * hidden * model,
            transcendentals=0,
        ),
        name="ffn_both",
    )(mid, cot, weights, weights, weights, *extra)


def ffn_grad_kernel(slots, *refs):
    acts = refs[:slots]
    mids = refs[slots : 2 * slots]
    cots = refs[2 * slots : 3 * slots]
    out_ref = refs[3 * slots]
    kind = pl.program_id(0)

    def store(others):
        total = dot(acts[0][0], others[0][...], TN)
        for act, other in zip(acts[1:], others[1:]):
            total = total + dot(act[0], other[...], TN)
        out_ref[...] = total.astype(BF16).reshape(out_ref.shape)

    @pl.when(kind < 2)
    def _():
        store(mids)

    @pl.when(kind == 2)
    def _():
        store(cots)


def ffn_grads(acts, mids, cots, shards):
    slots = len(acts)
    _, tokens, hidden = acts[0].shape
    model = mids[0].shape[-1]
    part = hidden // shards
    tile = 256
    per = tile // part
    whole = pl.BlockSpec(
        (tokens, model), lambda k, i: (0, 0), pipeline_mode=pl.Buffered(buffer_count=1)
    )
    return pl.pallas_call(
        functools.partial(ffn_grad_kernel, slots),
        grid=(3, hidden // tile),
        out_shape=jax.ShapeDtypeStruct((shards, 3, part, model), BF16),
        in_specs=[pl.BlockSpec((1, tokens, tile), lambda k, i: (k, 0, i))] * slots
        + [whole] * (2 * slots),
        out_specs=pl.BlockSpec((per, 1, part, model), lambda k, i: (i, k, 0, 0)),
        compiler_params=pltpu.CompilerParams(vmem_limit_bytes=VMEM_LIMIT),
        cost_estimate=pl.CostEstimate(
            flops=6 * slots * tokens * model * hidden,
            bytes_accessed=4 * slots * tokens * model,
            transcendentals=0,
        ),
        name="ffn_grads",
    )(*acts, *mids, *cots)


def ffn_down_kernel(chunks, *refs):
    acts = refs[:chunks]
    downs = refs[chunks : 2 * chunks]
    out_ref = refs[2 * chunks]
    total = None
    for act, down in zip(acts, downs):
        hidden = act.shape[-1]
        term = dot(act[0], down[...].reshape(hidden, down.shape[-1]))
        total = term if total is None else total + term
    out_ref[...] = total.astype(BF16)


def ffn_down(acts, weights):
    chunks = len(acts)
    _, tokens, hidden = acts[0].shape
    shards, _, part, model = weights[0].shape
    tile = min(256, tokens)
    act_spec = pl.BlockSpec((1, tile, hidden), lambda i: (2, i, 0))
    down_spec = pl.BlockSpec(
        (shards, 1, part, model),
        lambda i: (0, 2, 0, 0),
        pipeline_mode=pl.Buffered(buffer_count=1),
    )
    return pl.pallas_call(
        functools.partial(ffn_down_kernel, chunks),
        grid=(tokens // tile,),
        out_shape=jax.ShapeDtypeStruct((tokens, model), BF16),
        in_specs=[act_spec] * chunks + [down_spec] * chunks,
        out_specs=pl.BlockSpec((tile, model), lambda i: (i, 0)),
        compiler_params=pltpu.CompilerParams(vmem_limit_bytes=VMEM_LIMIT),
        cost_estimate=pl.CostEstimate(
            flops=2 * chunks * tokens * model * hidden,
            bytes_accessed=chunks * hidden * (tokens + model) * 2,
            transcendentals=0,
        ),
        name="ffn_down",
    )(*acts, *weights)


def ring_places(count):
    return (
        [(i, i ^ 1) for i in range(count)],
        [(i, i ^ 2) for i in range(count)],
    )


def seq_gather(rows):
    count = lax.axis_size("seq")
    if count != 4:
        return lax.all_gather(rows, "seq", axis=0)
    over_one, over_two = ring_places(count)
    half = rows.shape[0] // 2
    one = lax.ppermute(rows, "seq", over_one)
    two = lax.ppermute(rows, "seq", over_two)
    top = lax.ppermute(two[:half], "seq", over_one)
    low = lax.ppermute(one[half:], "seq", over_two)
    return jnp.concatenate([rows, one, two, top, low], axis=0).reshape(
        (count,) + rows.shape
    )


def seq_scatter(parts):
    count = lax.axis_size("seq")
    if count != 4:
        return lax.psum_scatter(parts, "seq", scatter_dimension=0).astype(F32)
    over_one, over_two = ring_places(count)
    half = parts.shape[1] // 2
    top = lax.ppermute(
        jnp.concatenate([parts[3, :half], parts[1, :half]], axis=0), "seq", over_one
    )
    low = lax.ppermute(
        jnp.concatenate([parts[3, half:], parts[2, half:]], axis=0), "seq", over_two
    )
    top_on = (parts[2, :half].astype(F32) + top[:half].astype(F32)).astype(BF16)
    low_on = (parts[1, half:].astype(F32) + low[:half].astype(F32)).astype(BF16)
    top_last = lax.ppermute(top_on, "seq", over_two)
    low_last = lax.ppermute(low_on, "seq", over_one)
    first = jnp.concatenate([top[half:], low[half:]], axis=0).astype(F32)
    last = jnp.concatenate([top_last, low_last], axis=0).astype(F32)
    return parts[0].astype(F32) + first + last


def seq_spread(rows):
    count = lax.axis_size("seq")
    parts = seq_gather(rows)
    if count != 4:
        return parts
    place = lax.axis_index("seq")
    return jnp.stack(
        [lax.dynamic_index_in_dim(parts, place ^ j, 0, keepdims=False) for j in range(count)]
    )


def scale_of(values):
    return lax.rsqrt(jnp.mean(values * values, axis=-1, keepdims=True) + EPSILON)


def normed(values, gain):
    return values * scale_of(values) * gain


def normed_back(values, gain, cot):
    scale = scale_of(values)
    pulled = cot * gain
    mean = jnp.mean(values * pulled, axis=-1, keepdims=True)
    return (
        scale * pulled - values * (scale * scale * scale) * mean,
        jnp.sum(cot * values * scale, axis=0),
    )


def own_columns(weight, heads, place):
    width = heads * HEAD
    part = lax.dynamic_slice_in_dim(weight, place * width, width, 1)
    if heads % 2:
        part = jnp.pad(part, ((0, 0), (0, HEAD)))
    return part


def on_device(
    tokens,
    cotangent,
    lengths,
    attn_gain,
    query_weight,
    key_weight,
    value_weight,
    query_gain,
    key_gain,
    out_weight,
    ffn_gain,
    gate_weight,
    up_weight,
    down_weight,
):
    slots, rows, model = tokens.shape
    seqs = lax.axis_size("seq")
    shards = lax.axis_size("fsdp")
    place = lax.axis_index("seq")
    shard = lax.axis_index("fsdp")
    slot_len = rows * seqs
    query_width = query_weight.shape[1]
    kv_width = key_weight.shape[1]
    hq = query_width // seqs // HEAD
    hkv = kv_width // seqs // HEAD
    hkv_held = hkv + hkv % 2
    sizes = (hq, hkv_held, hq // hkv)
    order = (place if seqs == 4 else place * 0).reshape(1)
    tables = position_tables(slot_len)
    gains = (
        jnp.concatenate([query_gain, query_gain]).reshape(1, 2 * HEAD),
        jnp.concatenate([key_gain, key_gain]).reshape(1, 2 * HEAD),
    )

    qkv_own = jnp.concatenate(
        [
            own_columns(query_weight, hq, place),
            own_columns(key_weight, hkv, place),
            own_columns(value_weight, hkv, place),
        ],
        axis=1,
    )
    qkv_weight = lax.all_gather(qkv_own, "fsdp", axis=0, tiled=True)
    per = shards // seqs
    piece = out_weight.shape[0] // seqs
    out_own = None
    for j in range(seqs):
        moves = [
            (s * shards + s * per + h, s * shards + h * seqs + j)
            for s in range(seqs)
            for h in range(per)
        ]
        got = lax.ppermute(out_weight[j * piece : (j + 1) * piece], ("seq", "fsdp"), moves)
        out_own = got if out_own is None else out_own + got
    out_rows = lax.all_gather(out_own, "fsdp", axis=0, tiled=True)
    hidden_own = gate_weight.shape[0] // seqs
    part = hidden_own // CHUNKS
    ffn_weights = []
    for c in range(CHUNKS):
        start = place * hidden_own + c * part
        mine = jnp.stack(
            [
                lax.dynamic_slice_in_dim(w, start, part, 0)
                for w in (gate_weight, up_weight, down_weight)
            ]
        )
        ffn_weights.append(lax.all_gather(mine, "fsdp", axis=0))

    places = place * rows + jnp.arange(rows, dtype=jnp.int32)
    live = (places[None, :] < lengths[:, None]).astype(F32)[..., None]
    inputs = tokens.astype(F32)
    out_cot = cotangent.astype(F32) * live
    normal_in = [normed(inputs[b], attn_gain).astype(BF16) for b in range(slots)]
    normal_full = [seq_gather(v).reshape(slot_len, model) for v in normal_in]

    qkv = []
    attended = []
    log_sums = []
    hidden_res = []
    mid_full = []
    for b in range(slots):
        raw = dot(normal_full[b], qkv_weight).astype(BF16).reshape(seqs, rows, -1)
        mixed, lse = attend(sizes, order, lengths[b : b + 1], raw, gains, tables)
        mixed = mixed.reshape(slot_len, hq * HEAD)
        qkv.append(raw)
        attended.append(mixed)
        log_sums.append(lse)
        proj = dot(mixed, out_rows).astype(BF16).reshape(seqs, rows, model)
        res = inputs[b] + seq_scatter(proj)
        hidden_res.append(res)
        mid = normed(res, ffn_gain).astype(BF16)
        mid_full.append(seq_gather(mid).reshape(slot_len, model))
    cot_full = [seq_gather(out_cot[b].astype(BF16)).reshape(slot_len, model) for b in range(slots)]

    acts = [[None] * slots for _ in range(CHUNKS)]
    pulled = [None] * slots
    for c in range(CHUNKS):
        for b in range(slots):
            acts[c][b], pulled[b] = ffn_both(
                mid_full[b], cot_full[b], ffn_weights[c], pulled[b], c == CHUNKS - 1
            )
    ffn_sums = []
    for c in range(CHUNKS):
        grads = ffn_grads(acts[c], mid_full, cot_full, shards).reshape(shards, 3 * part, model)
        ffn_sums.append(lax.psum_scatter(grads, "fsdp", scatter_dimension=0))

    output = []
    res_cot = []
    res_full = []
    dqkv = []
    grad_ffn_gain = 0.0
    head_gain = 0.0
    for b in range(slots):
        pull, gain_part = normed_back(
            hidden_res[b], ffn_gain, seq_scatter(pulled[b].reshape(seqs, rows, model))
        )
        grad_ffn_gain = grad_ffn_gain + gain_part
        cot = out_cot[b] + pull
        res_cot.append(cot)
        full = seq_gather(cot.astype(BF16)).reshape(slot_len, model)
        res_full.append(full)
        attended_cot = dot(full, out_rows, NT).astype(BF16).reshape(seqs, rows, hq * HEAD)
        back, gain_part = attend_back(
            sizes, order, lengths[b : b + 1], qkv[b], attended_cot, log_sums[b], gains, tables
        )
        head_gain = head_gain + gain_part
        dqkv.append(back.reshape(slot_len, -1))
    for b in range(slots):
        ffn_out = ffn_down([acts[c][b] for c in range(CHUNKS)], ffn_weights)
        total = hidden_res[b] + seq_scatter(ffn_out.reshape(seqs, rows, model))
        output.append((live[b] * total).astype(BF16))

    grad_tokens = []
    grad_attn_gain = 0.0
    for b in range(slots):
        in_cot = seq_scatter(
            dot(dqkv[b], qkv_weight, NT).astype(BF16).reshape(seqs, rows, model)
        )
        pull, gain_part = normed_back(inputs[b], attn_gain, in_cot)
        grad_attn_gain = grad_attn_gain + gain_part
        grad_tokens.append((res_cot[b] + pull).astype(BF16))

    out_grads = sum(dot(attended[b], res_full[b], TN) for b in range(slots)).astype(BF16)
    out_sums = lax.psum_scatter(out_grads, "fsdp", scatter_dimension=0, tiled=True)
    out_parts = []
    for j in range(seqs):
        moves = [
            (s * shards + h * seqs + j, s * shards + s * per + h)
            for s in range(seqs)
            for h in range(per)
        ]
        out_parts.append(lax.ppermute(out_sums, ("seq", "fsdp"), moves))
    grad_out = lax.psum(jnp.concatenate(out_parts, axis=0), "seq").astype(F32)

    qkv_grads = sum(dot(normal_full[b], dqkv[b], TN) for b in range(slots)).astype(BF16)
    qkv_sums = lax.psum_scatter(qkv_grads, "fsdp", scatter_dimension=0, tiled=True)
    qkv_all = jnp.moveaxis(seq_spread(qkv_sums), 0, 1).astype(F32)
    held = qkv_all.shape[0]
    edge = hq * HEAD
    kv_edge = edge + hkv_held * HEAD
    grad_query = qkv_all[..., :edge].reshape(held, query_width)
    grad_key = qkv_all[..., edge : edge + hkv * HEAD].reshape(held, kv_width)
    grad_value = qkv_all[..., kv_edge : kv_edge + hkv * HEAD].reshape(held, kv_width)

    spread = [seq_spread(v).reshape(seqs, 3, part, model) for v in ffn_sums]
    ffn_grad = [
        jnp.stack([v[:, kind] for v in spread], axis=1).reshape(seqs * hidden_own, model).astype(F32)
        for kind in range(3)
    ]

    gain_sums = lax.psum(
        jnp.concatenate(
            [
                grad_attn_gain,
                grad_ffn_gain,
                (head_gain[0, :HEAD] + head_gain[0, HEAD:]),
                (head_gain[1, :HEAD] + head_gain[1, HEAD:]),
            ]
        ),
        ("seq", "fsdp"),
    )

    def own_gain(start, length):
        width = length // shards
        return lax.dynamic_slice_in_dim(gain_sums, start + shard * width, width, 0)

    return (
        jnp.stack(output),
        jnp.stack(grad_tokens),
        own_gain(0, model),
        grad_query,
        grad_key,
        grad_value,
        own_gain(2 * model, HEAD),
        own_gain(2 * model + HEAD, HEAD),
        grad_out,
        own_gain(model, model),
        ffn_grad[0],
        ffn_grad[1],
        ffn_grad[2],
    )


def solution(mesh):
    return jax.shard_map(
        on_device,
        mesh=mesh,
        in_specs=(
            P("fsdp", "seq", None),
            P("fsdp", "seq", None),
            P("fsdp"),
            P(),
            P("fsdp", None),
            P("fsdp", None),
            P("fsdp", None),
            P(),
            P(),
            P("fsdp", None),
            P(),
            P("fsdp", None),
            P("fsdp", None),
            P("fsdp", None),
        ),
        out_specs=(
            P("fsdp", "seq", None),
            P("fsdp", "seq", None),
            P("fsdp"),
            P("fsdp", None),
            P("fsdp", None),
            P("fsdp", None),
            P("fsdp"),
            P("fsdp"),
            P("fsdp", None),
            P("fsdp"),
            P("fsdp", None),
            P("fsdp", None),
            P("fsdp", None),
        ),
        check_vma=False,
    )
```

time: 3210 us -> 1380 us (0.43)
  waiting for transfers between devices: 2080 us -> 656 us
  matrix products: 732 us -> 58.8 us
  Pallas kernels: 0 us -> 362 us
  other arithmetic: 166 us -> 77.8 us
  local copies, waits for them, and re-layouts: 133 us -> 51 us
  starting transfers between devices: 38.2 us -> 98.5 us
    reduce_scatter x2 -> x4, waiting for transfers between devices: 1010 us -> 51.1 us  [the longest x2 51.1 us: on_device(): ffn_sums.append(lax.psum_scatter(grads, 'fsdp', scatter_dimension=0))]
    all_gather x7 -> x4, waiting for transfers between devices: 793 us -> 76.6 us  [the longest x2 76.6 us: on_device(): ffn_weights.append(lax.all_gather(mine, 'fsdp', axis=0))]
    dot_general x33 -> x12, matrix products: 732 us -> 58.8 us  [dot(): return lax.dot_general(a, b, dims, preferred_element_type=F32)]
    ppermute x0 -> x84, waiting for transfers between devices: none -> 528 us  [the longest x8 138 us: seq_scatter(): lax.ppermute(jnp.concatenate([parts[3, half:], parts[2, half:]], axis=0),...]
    pallas_call x0 -> x12, Pallas kernels: none -> 362 us  [the longest x4 126 us: ffn_both(): pl.pallas_call(functools.partial(ffn_kernel, summed is not None), grid=(t...]
    psum x1, waiting for transfers between devices: 200 us -> 0.01 us  [on_device(): grad_out = lax.psum(jnp.concatenate(out_parts, axis=0), 'seq').astype(F32)]
    ppermute x0 -> x84, starting transfers between devices: none -> 97.9 us  [the longest x11 15.9 us: seq_gather(): low = lax.ppermute(one[half:], 'seq', over_two)]
    concatenate x4 -> x18, other arithmetic: 85.8 us -> 3.09 us  [the longest x1 1.11 us: on_device(): grad_out = lax.psum(jnp.concatenate(out_parts, axis=0), 'seq').astype(F32)]
  transfers between devices with their start and end apart: 18 -> 93, of which waited for: 14 -> 61; matrix products, arithmetic and copies ran while one was open for 14% -> 9% of each run, Pallas kernels for 0% -> 15%
where the time goes in v1:
time: 1380 us; the launch traced here: 1370 us
  waiting for transfers between devices  656 us (48%)
  Pallas kernels  362 us (26%)
  starting transfers between devices  98.5 us (7%)
  other arithmetic  77.8 us (6%)
  matrix products  58.8 us (4%)
  blocking collectives  53.5 us (4%)
  local copies, waits for them, and re-layouts  51 us (4%)
  between operations  16.8 us (1%)
    ppermute x8, waiting for transfers between devices, seq_scatter(): lax.ppermute(jnp.concatenate([parts[3, half:], parts[2, half:]], axis=0),...  138 us
    ppermute x11, waiting for transfers between devices, seq_gather(): top = lax.ppermute(two[:half], 'seq', over_one)  132 us
    ppermute x11, waiting for transfers between devices, seq_gather(): two = lax.ppermute(rows, 'seq', over_two)  131 us
    pallas_call x4, Pallas kernels, ffn_both(): pl.pallas_call(functools.partial(ffn_kernel, summed is not None), grid=(t...  126 us
    pallas_call x2, Pallas kernels, attend_back(): pl.pallas_call(functools.partial(attend_back_kernel, sizes), out_shape=(j...  82.8 us
    all_gather x2, waiting for transfers between devices, on_device(): ffn_weights.append(lax.all_gather(mine, 'fsdp', axis=0))  76.6 us
    pallas_call x2, Pallas kernels, ffn_grads(): pl.pallas_call(functools.partial(ffn_grad_kernel, slots), grid=(3, hidden...  72.7 us
    ppermute x8, waiting for transfers between devices, seq_scatter(): top_last = lax.ppermute(top_on, 'seq', over_two)  67.2 us
  transfers between devices with their start and end apart: 93, of which 61 were waited for; matrix products, arithmetic and copies ran while one was open for 9% of the time, Pallas kernels for 15%

profile of v1, /device:TPU:6, one launch (start us, length us, event | category | flops | bytes accessed | tf_op | source)
XLA Modules:
  0.0 1374.8 jit_solution(17908420917781435567)
XLA Ops:
  13.6 18.6 %collective-permute-done.4 = bf16[64,2048]{1,0:T(8,128)(2,1)S(1)} collective-permute-done((bf16[64,2048]{1,0:T(8,128)(2,1)S(1)}, bf16[64,2048]{1,0:T(8,128)(2,1)S(1)}, u32[]{:S(2)}, u32[]{:S(2)}) %collective-permute-start.4) | collective-permute-done | bytes 262176 | tf_op jit(solution)/shard_map/ppermute | solution.py:529
  47.0 11.9 collective-permute-done.25
  64.3 9.6 collective-permute-done.26
  75.6 7.8 convolution_convert_fusion.4
  83.3 26.3 %attend.3 = (bf16[4,256,512]{2,1,0:T(8,128)(2,1)}, f32[8,1024,1]{2,1,0:T(8,128)}) custom-call(s32[1]{0:T(128)} %bitcast.1.place_ref, s32[1]{0:T(128)} %get-tuple-element.171.len_ref, bf16[4,256,768]{2,1,0:T(8,128)(2,1)} %bitcast.402, f32[1,128]{1,0:T(1,128)} %get-tuple-element.174.qg_ref, f32[1,128]{1,0:T(1,128)} %get-tuple-element.175.kg_ref, ...), custom_call_target="tpu_custom_call" | custom-call | flops 10737418240 | bytes 8388608 | tf_op jit(solution)/shard_map/attend/pallas_call | solution.py:195
  109.7 4.3 convolution_convert_fusion
  117.7 11.4 collective-permute-done.29
  134.7 10.2 collective-permute-done.30
  151.4 11.9 collective-permute-done.37
  166.6 32.9 %collective-permute-done.38 = bf16[128,2048]{1,0:T(8,128)(2,1)S(1)} collective-permute-done((bf16[128,2048]{1,0:T(8,128)(2,1)S(1)}, bf16[128,2048]{1,0:T(8,128)(2,1)S(1)}, u32[]{:S(2)}, u32[]{:S(2)}) %collective-permute-start.38) | collective-permute-done | bytes 524320 | tf_op jit(solution)/shard_map/ppermute | solution.py:411
  203.8 10.7 collective-permute-done.34
  216.2 32.6 %ffn_both.6 = (bf16[3,1024,1024]{2,1,0:T(8,128)(2,1)}, f32[1024,2048]{1,0:T(8,128)}) custom-call(bf16[1024,2048]{1,0:T(8,128)(2,1)} %constant_dynamic-update-slice_fusion.20.mid_ref.refs_3_, bf16[1024,2048]{1,0:T(8,128)(2,1)} %copy-done.85, bf16[8,3,128,2048]{3,2,1,0:T(8,128)(2,1)} %bitcast.346, bf16[8,3,128,2048]{3,2,1,0:T(8,128)(2,1)} %bitcast.347, ...), custom_call_target="tpu_custom_call" | custom-call | flops 21474836480 | bytes 20971520 | tf_op jit(solution)/shard_map/ffn_both/pallas_call | solution.py:288
  248.8 76.6 %all-gather.13.cloned.1.call-done = bf16[24,128,2048]{2,1,0:T(8,128)(2,1)} async-done(((bf16[3,128,2048]{2,1,0:T(8,128)(2,1)}), bf16[24,128,2048]{2,1,0:T(8,128)(2,1)}) %all-gather.13.cloned.1.call-update) | async-done | bytes 12582928 | tf_op jit(solution)/shard_map/all_gather | solution.py:543
  325.4 31.0 %ffn_both.7 = (bf16[3,1024,1024]{2,1,0:T(8,128)(2,1)}, bf16[1024,2048]{1,0:T(8,128)(2,1)}) custom-call(bf16[1024,2048]{1,0:T(8,128)(2,1)} %constant_dynamic-update-slice_fusion.20.mid_ref.refs_3_, bf16[1024,2048]{1,0:T(8,128)(2,1)} %copy-done.85, bf16[8,3,128,2048]{3,2,1,0:T(8,128)(2,1)} %bitcast.354, bf16[8,3,128,2048]{3,2,1,0:T(8,128)(2,1)} %bitcast.355, ...), custom_call_target="tpu_custom_call" | custom-call | flops 21474836480 | bytes 20971520 | tf_op jit(solution)/shard_map/ffn_both/pallas_call | solution.py:288
  359.6 24.0 %collective-permute-done.57 = bf16[256,2048]{1,0:T(8,128)(2,1)S(1)} collective-permute-done((bf16[256,2048]{1,0:T(8,128)(2,1)S(1)}, bf16[256,2048]{1,0:T(8,128)(2,1)S(1)}, u32[]{:S(2)}, u32[]{:S(2)}) %collective-permute-start.57) | collective-permute-done | bytes 1048608 | tf_op jit(solution)/shard_map/ppermute | solution.py:427
  386.7 10.8 collective-permute-done.58
  404.5 21.9 %collective-permute-done.61 = bf16[256,2048]{1,0:T(8,128)(2,1)S(1)} collective-permute-done((bf16[256,2048]{1,0:T(8,128)(2,1)S(1)}, bf16[256,2048]{1,0:T(8,128)(2,1)S(1)}, u32[]{:S(2)}, u32[]{:S(2)}) %collective-permute-start.61) | collective-permute-done | bytes 1048608 | tf_op jit(solution)/shard_map/ppermute | solution.py:410
  429.8 8.1 collective-permute-done.62
  441.4 41.3 %attend_back.3 = (bf16[4,256,768]{2,1,0:T(8,128)(2,1)}, f32[2,128]{1,0:T(2,128)}) custom-call(s32[1]{0:T(128)} %bitcast.1.place_ref, s32[1]{0:T(128)} %get-tuple-element.171.len_ref, bf16[4,256,768]{2,1,0:T(8,128)(2,1)} %bitcast.403, bf16[4,256,512]{2,1,0:T(8,128)(2,1)} %bitcast.407, f32[8,1024,1]{2,1,0:T(8,128)} %get-tuple-element.41.lse_ref, ...), custom_call_target="tpu_custom_call" | custom-call | flops 19327352832 | bytes 8388608 | tf_op jit(solution)/shard_map/attend_back/pallas_call | solution.py:221
  482.6 5.1 convolution_convert_fusion.2
  490.2 20.1 %collective-permute-done.65 = bf16[256,2048]{1,0:T(8,128)(2,1)S(1)} collective-permute-done((bf16[256,2048]{1,0:T(8,128)(2,1)S(1)}, bf16[256,2048]{1,0:T(8,128)(2,1)S(1)}, u32[]{:S(2)}, u32[]{:S(2)}) %collective-permute-start.65) | collective-permute-done | bytes 1048608 | tf_op jit(solution)/shard_map/ppermute | solution.py:427
  513.6 9.0 collective-permute-done.66
  527.8 21.1 %collective-permute-done.1 = bf16[256,2048]{1,0:T(8,128)(2,1)S(1)} collective-permute-done((bf16[256,2048]{1,0:T(8,128)(2,1)S(1)}, bf16[256,2048]{1,0:T(8,128)(2,1)S(1)}, u32[]{:S(2)}, u32[]{:S(2)}) %collective-permute-start.1) | collective-permute-done | bytes 1048608 | tf_op jit(solution)/shard_map/ppermute | solution.py:410
  553.6 4.6 collective-permute-done.2
  560.6 4.5 convolution_convert_fusion.5
  565.1 26.4 %attend.2 = (bf16[4,256,512]{2,1,0:T(8,128)(2,1)}, f32[8,1024,1]{2,1,0:T(8,128)}) custom-call(s32[1]{0:T(128)} %bitcast.1.place_ref, s32[1]{0:T(128)} %get-tuple-element.170.len_ref, bf16[4,256,768]{2,1,0:T(8,128)(2,1)} %bitcast.400, f32[1,128]{1,0:T(1,128)} %get-tuple-element.174.qg_ref, f32[1,128]{1,0:T(1,128)} %get-tuple-element.175.kg_ref, ...), custom_call_target="tpu_custom_call" | custom-call | flops 10737418240 | bytes 8388608 | tf_op jit(solution)/shard_map/attend/pallas_call | solution.py:195
  591.5 4.3 convolution_convert_fusion.1
  598.9 19.6 %collective-permute-done.9 = bf16[256,2048]{1,0:T(8,128)(2,1)S(1)} collective-permute-done((bf16[256,2048]{1,0:T(8,128)(2,1)S(1)}, bf16[256,2048]{1,0:T(8,128)(2,1)S(1)}, u32[]{:S(2)}, u32[]{:S(2)}) %collective-permute-start.9) | collective-permute-done | bytes 1048608 | tf_op jit(solution)/shard_map/ppermute | solution.py:427
  625.5 10.7 collective-permute-done.10
  640.9 17.8 %collective-permute-done.17 = bf16[256,2048]{1,0:T(8,128)(2,1)S(1)} collective-permute-done((bf16[256,2048]{1,0:T(8,128)(2,1)S(1)}, bf16[256,2048]{1,0:T(8,128)(2,1)S(1)}, u32[]{:S(2)}, u32[]{:S(2)}) %collective-permute-start.17) | collective-permute-done | bytes 1048608 | tf_op jit(solution)/shard_map/ppermute | solution.py:410
  662.9 25.7 %collective-permute-done.18 = bf16[128,2048]{1,0:T(8,128)(2,1)S(1)} collective-permute-done((bf16[128,2048]{1,0:T(8,128)(2,1)S(1)}, bf16[128,2048]{1,0:T(8,128)(2,1)S(1)}, u32[]{:S(2)}, u32[]{:S(2)}) %collective-permute-start.18) | collective-permute-done | bytes 524320 | tf_op jit(solution)/shard_map/ppermute | solution.py:411
  691.5 7.2 collective-permute-done.14
  702.2 30.9 %ffn_both.4 = (bf16[3,1024,1024]{2,1,0:T(8,128)(2,1)}, f32[1024,2048]{1,0:T(8,128)}) custom-call(bf16[1024,2048]{1,0:T(8,128)(2,1)} %copy-done.84, bf16[1024,2048]{1,0:T(8,128)(2,1)} %constant_dynamic-update-slice_fusion.10.cot_ref.refs_4_, bf16[8,3,128,2048]{3,2,1,0:T(8,128)(2,1)} %bitcast.349, bf16[8,3,128,2048]{3,2,1,0:T(8,128)(2,1)} %bitcast.350, ...), custom_call_target="tpu_custom_call" | custom-call | flops 21474836480 | bytes 20971520 | tf_op jit(solution)/shard_map/ffn_both/pallas_call | solution.py:288
  733.0 31.1 %ffn_both.5 = (bf16[3,1024,1024]{2,1,0:T(8,128)(2,1)}, bf16[1024,2048]{1,0:T(8,128)(2,1)}) custom-call(bf16[1024,2048]{1,0:T(8,128)(2,1)} %copy-done.84, bf16[1024,2048]{1,0:T(8,128)(2,1)} %constant_dynamic-update-slice_fusion.10.cot_ref.refs_4_, bf16[8,3,128,2048]{3,2,1,0:T(8,128)(2,1)} %bitcast.357, bf16[8,3,128,2048]{3,2,1,0:T(8,128)(2,1)} %bitcast.358, ...), custom_call_target="tpu_custom_call" | custom-call | flops 21474836480 | bytes 20971520 | tf_op jit(solution)/shard_map/ffn_both/pallas_call | solution.py:288
  767.9 18.5 %collective-permute-done.45 = bf16[256,2048]{1,0:T(8,128)(2,1)S(1)} collective-permute-done((bf16[256,2048]{1,0:T(8,128)(2,1)S(1)}, bf16[256,2048]{1,0:T(8,128)(2,1)S(1)}, u32[]{:S(2)}, u32[]{:S(2)}) %collective-permute-start.45) | collective-permute-done | bytes 1048608 | tf_op jit(solution)/shard_map/ppermute | solution.py:427
  790.7 11.5 collective-permute-done.46
  809.4 18.6 %collective-permute-done.49 = bf16[256,2048]{1,0:T(8,128)(2,1)S(1)} collective-permute-done((bf16[256,2048]{1,0:T(8,128)(2,1)S(1)}, bf16[256,2048]{1,0:T(8,128)(2,1)S(1)}, u32[]{:S(2)}, u32[]{:S(2)}) %collective-permute-start.49) | collective-permute-done | bytes 1048608 | tf_op jit(solution)/shard_map/ppermute | solution.py:410
  832.7 4.7 collective-permute-done.50
  847.6 9.0 fusion.51
  860.0 41.5 %attend_back.2 = (bf16[4,256,768]{2,1,0:T(8,128)(2,1)}, f32[2,128]{1,0:T(2,128)}) custom-call(s32[1]{0:T(128)} %bitcast.1.place_ref, s32[1]{0:T(128)} %get-tuple-element.170.len_ref, bf16[4,256,768]{2,1,0:T(8,128)(2,1)} %bitcast.401, bf16[4,256,512]{2,1,0:T(8,128)(2,1)} %bitcast.406, f32[8,1024,1]{2,1,0:T(8,128)} %get-tuple-element.38.lse_ref, ...), custom_call_target="tpu_custom_call" | custom-call | flops 19327352832 | bytes 8388608 | tf_op jit(solution)/shard_map/attend_back/pallas_call | solution.py:221
  901.5 7.3 add_convert_fusion
  911.0 5.0 collective-permute-start.72
  916.0 11.9 collective-permute-done.72
  929.0 36.1 %ffn_grads.2 = bf16[8,3,128,2048]{3,2,1,0:T(8,128)(2,1)} custom-call(bf16[3,1024,1024]{2,1,0:T(8,128)(2,1)} %get-tuple-element.30.refs_0_, bf16[3,1024,1024]{2,1,0:T(8,128)(2,1)} %get-tuple-element.34.refs_0_.refs_1_, bf16[1024,2048]{1,0:T(8,128)(2,1)} %copy-done.84, bf16[1024,2048]{1,0:T(8,128)(2,1)} %constant_dynamic-update-slice_fusion.20.mid_ref.refs_3_, ...), custom_call_target="tpu_custom_call" | custom-call | flops 25769803776 | bytes 16777216 | tf_op jit(solution)/shard_map/ffn_grads/pallas_call | solution.py:340
  965.2 36.6 %ffn_grads.3 = bf16[8,3,128,2048]{3,2,1,0:T(8,128)(2,1)} custom-call(bf16[3,1024,1024]{2,1,0:T(8,128)(2,1)} %get-tuple-element.32.refs_1_.refs_0_, bf16[3,1024,1024]{2,1,0:T(8,128)(2,1)} %get-tuple-element.36.refs_1_, bf16[1024,2048]{1,0:T(8,128)(2,1)} %copy-done.84, bf16[1024,2048]{1,0:T(8,128)(2,1)} %constant_dynamic-update-slice_fusion.20.mid_ref.refs_3_, ...), custom_call_target="tpu_custom_call" | custom-call | flops 25769803776 | bytes 16777216 | tf_op jit(solution)/shard_map/ffn_grads/pallas_call | solution.py:340
  1001.8 14.2 %ffn_down.3 = bf16[1024,2048]{1,0:T(8,128)(2,1)} custom-call(bf16[3,1024,1024]{2,1,0:T(8,128)(2,1)} %get-tuple-element.34.refs_0_.refs_1_, bf16[3,1024,1024]{2,1,0:T(8,128)(2,1)} %get-tuple-element.36.refs_1_, bf16[8,3,128,2048]{3,2,1,0:T(8,128)(2,1)} %bitcast.352, bf16[8,3,128,2048]{3,2,1,0:T(8,128)(2,1)} %bitcast.360), custom_call_target="tpu_custom_call" | custom-call | flops 8589934592 | bytes 12582912 | tf_op jit(solution)/shard_map/ffn_down/pallas_call | solution.py:380
  1018.1 7.7 collective-permute-start.40
  1025.7 15.7 %collective-permute-done.41 = bf16[256,2048]{1,0:T(8,128)(2,1)S(1)} collective-permute-done((bf16[256,2048]{1,0:T(8,128)(2,1)S(1)}, bf16[256,2048]{1,0:T(8,128)(2,1)S(1)}, u32[]{:S(2)}, u32[]{:S(2)}) %collective-permute-start.41) | collective-permute-done | bytes 1048608 | tf_op jit(solution)/shard_map/ppermute | solution.py:427
  1041.4 4.5 collective-permute-done.40
  1051.7 7.6 collective-permute-done.42
  1063.5 14.3 %ffn_down.2 = bf16[1024,2048]{1,0:T(8,128)(2,1)} custom-call(bf16[3,1024,1024]{2,1,0:T(8,128)(2,1)} %get-tuple-element.30.refs_0_, bf16[3,1024,1024]{2,1,0:T(8,128)(2,1)} %get-tuple-element.32.refs_1_.refs_0_, bf16[8,3,128,2048]{3,2,1,0:T(8,128)(2,1)} %bitcast.353, bf16[8,3,128,2048]{3,2,1,0:T(8,128)(2,1)} %bitcast.361), custom_call_target="tpu_custom_call" | custom-call | flops 8589934592 | bytes 12582912 | tf_op jit(solution)/shard_map/ffn_down/pallas_call | solution.py:380
  1088.4 17.6 %collective-permute-done.21 = bf16[256,2048]{1,0:T(8,128)(2,1)S(1)} collective-permute-done((bf16[256,2048]{1,0:T(8,128)(2,1)S(1)}, bf16[256,2048]{1,0:T(8,128)(2,1)S(1)}, u32[]{:S(2)}, u32[]{:S(2)}) %collective-permute-start.21) | collective-permute-done | bytes 1048608 | tf_op jit(solution)/shard_map/ppermute | solution.py:427
  1110.3 7.3 fusion.1
  1117.7 10.8 collective-permute-done.53
  1132.6 7.0 collective-permute-done.22
  1146.9 53.5 %psum.14 = f32[4224]{0:T(1024)S(1)} all-reduce(f32[4224]{0:T(1024)S(1)} %concatenate.223), channel_id=1, replica_groups=mesh['seq'=4,'fsdp'=8] {'seq','fsdp'}, use_global_device_ids=true, to_apply=%region_12.0 | all-reduce | flops 4224 | bytes 33792 | tf_op jit(solution)/shard_map/psum | solution.py:647
  1201.7 6.0 fusion.4
  1228.6 51.1 %reduce-scatter.11.cloned.1.call-done = bf16[1,384,2048]{2,1,0:T(8,128)(2,1)} async-done(((bf16[8,384,2048]{2,1,0:T(8,128)(2,1)}), bf16[1,384,2048]{2,1,0:T(8,128)(2,1)}) %reduce-scatter.11.cloned.1.call-update) | async-done | bytes 1572880 | tf_op jit(solution)/shard_map/reduce_scatter | solution.py:581
  1292.5 24.7 %collective-permute-done.81 = bf16[384,2048]{1,0:T(8,128)(2,1)S(1)} collective-permute-done((bf16[384,2048]{1,0:T(8,128)(2,1)}, bf16[384,2048]{1,0:T(8,128)(2,1)S(1)}, u32[]{:S(2)}, u32[]{:S(2)}) %collective-permute-start.81) | collective-permute-done | bytes 1572896 | tf_op jit(solution)/shard_map/ppermute | solution.py:410
  1321.4 13.3 collective-permute-done.78
  1336.2 11.6 collective-permute-done.82
  1352.8 4.7 bitcast_convert_fusion.2
  1357.9 4.7 bitcast_convert_fusion.1
  1363.0 4.7 bitcast_convert_fusion
  (595 shorter events, 236.6 us)
Async XLA Ops:
  7.2 68.4 %all-gather.7.cloned.1.call-start = ((), (), s32[]{:S(2)}) async-start(), calls=%async_computation.4 | async-start | bytes 3538944 | tf_op jit(solution)/shard_map/all_gather | solution.py:519
  10.1 99.6 %all-gather.9.cloned.1.call-start = ((), (), s32[]{:S(2)}) async-start(), calls=%async_computation.5 | async-start | bytes 2359296 | tf_op jit(solution)/shard_map/all_gather | solution.py:531
  11.0 21.2 %collective-permute-start.4 = (bf16[64,2048]{1,0:T(8,128)(2,1)S(1)}, bf16[64,2048]{1,0:T(8,128)(2,1)S(1)}, u32[]{:S(2)}, u32[]{:S(2)}) collective-permute-start(bf16[64,2048]{1,0:T(8,128)(2,1)S(1)} %get-tuple-element.151), channel_id=1, source_target_pairs={{0,0},{1,4},{10,8},{11,12},{20,16},{21,20},{30,24},{31,28}} | collective-permute-start | bytes 786440 | tf_op jit(solution)/shard_map/ppermute | solution.py:529
  12.3 20.0 %collective-permute-start.7 = (bf16[64,2048]{1,0:T(8,128)(2,1)S(1)}, bf16[64,2048]{1,0:T(8,128)(2,1)S(1)}, u32[]{:S(2)}, u32[]{:S(2)}) collective-permute-start(bf16[64,2048]{1,0:T(8,128)(2,1)S(1)} %get-tuple-element.152), channel_id=1, source_target_pairs={{0,3},{1,7},{10,11},{11,15},{20,19},{21,23},{30,27},{31,31}} | collective-permute-start | bytes 786440 | tf_op jit(solution)/shard_map/ppermute | solution.py:529
  12.9 19.3 %collective-permute-start.6 = (bf16[64,2048]{1,0:T(8,128)(2,1)S(1)}, bf16[64,2048]{1,0:T(8,128)(2,1)S(1)}, u32[]{:S(2)}, u32[]{:S(2)}) collective-permute-start(bf16[64,2048]{1,0:T(8,128)(2,1)S(1)} %get-tuple-element.153), channel_id=1, source_target_pairs={{0,2},{1,6},{10,10},{11,14},{20,18},{21,22},{30,26},{31,30}} | collective-permute-start | bytes 786440 | tf_op jit(solution)/shard_map/ppermute | solution.py:529
  33.0 183.2 %all-gather.11.cloned.1.call-start = ((), (), s32[]{:S(2)}) async-start(), calls=%async_computation.11 | async-start | bytes 14155776 | tf_op jit(solution)/shard_map/all_gather | solution.py:543
  38.2 287.2 %all-gather.13.cloned.1.call-start = ((), (), s32[]{:S(2)}) async-start(), calls=%async_computation.12 | async-start | bytes 14155776 | tf_op jit(solution)/shard_map/all_gather | solution.py:543
  40.8 868.1 %reduce-scatter.7.cloned.1.call-start = ((), (), s32[]{:S(2)}) async-start(), calls=%async_computation.7 | async-start | bytes 2359296 | tf_op jit(solution)/shard_map/reduce_scatter | solution.py:620
  43.7 15.2 %collective-permute-start.25 = (bf16[256,2048]{1,0:T(8,128)(2,1)S(1)}, bf16[256,2048]{1,0:T(8,128)(2,1)S(1)}, u32[]{:S(2)}, u32[]{:S(2)}) collective-permute-start(bf16[256,2048]{1,0:T(8,128)(2,1)S(1)} %get-tuple-element.73), channel_id=1, source_target_pairs={{0,16},{8,24},{16,0},{24,8},{1,17},{9,25},{17,1},{25,9},{2,18},{10... | collective-permute-start | bytes 3145736 | tf_op jit(solution)/shard_map/ppermute | solution.py:410
  43.8 16.3 %collective-permute-start.24 = (bf16[256,2048]{1,0:T(8,128)(2,1)S(1)}, bf16[256,2048]{1,0:T(8,128)(2,1)S(1)}, u32[]{:S(2)}, u32[]{:S(2)}) collective-permute-start(bf16[256,2048]{1,0:T(8,128)(2,1)S(1)} %get-tuple-element.73), channel_id=1, source_target_pairs={{0,8},{8,0},{16,24},{24,16},{1,9},{9,1},{17,25},{25,17},{2,10},{10... | collective-permute-start | bytes 3145736 | tf_op jit(solution)/shard_map/ppermute | solution.py:409
  130.0 14.9 %collective-permute-start.30 = (bf16[128,2048]{1,0:T(8,128)(2,1)S(1)}, bf16[128,2048]{1,0:T(8,128)(2,1)S(1)}, u32[]{:S(2)}, u32[]{:S(2)}) collective-permute-start(bf16[128,2048]{1,0:T(8,128)(2,1)S(1)} %get-tuple-element.138), channel_id=1, source_target_pairs={{0,16},{8,24},{16,0},{24,8},{1,17},{9,25},{17,1},{25,9},{2,18},{10... | collective-permute-start | bytes 1572872 | tf_op jit(solution)/shard_map/ppermute | solution.py:432
  131.7 15.3 %collective-permute-start.31 = (bf16[128,2048]{1,0:T(8,128)(2,1)S(1)}, bf16[128,2048]{1,0:T(8,128)(2,1)S(1)}, u32[]{:S(2)}, u32[]{:S(2)}) collective-permute-start(bf16[128,2048]{1,0:T(8,128)(2,1)S(1)} %get-tuple-element.139), channel_id=1, source_target_pairs={{0,8},{8,0},{16,24},{24,16},{1,9},{9,1},{17,25},{25,17},{2,10},{10... | collective-permute-start | bytes 1572872 | tf_op jit(solution)/shard_map/ppermute | solution.py:433
  134.5 28.8 %collective-permute-start.37 = (bf16[256,2048]{1,0:T(8,128)(2,1)S(1)}, bf16[256,2048]{1,0:T(8,128)(2,1)S(1)}, u32[]{:S(2)}, u32[]{:S(2)}) collective-permute-start(bf16[256,2048]{1,0:T(8,128)(2,1)S(1)} %get-tuple-element.67), channel_id=1, source_target_pairs={{0,16},{8,24},{16,0},{24,8},{1,17},{9,25},{17,1},{25,9},{2,18},{10... | collective-permute-start | bytes 3145736 | tf_op jit(solution)/shard_map/ppermute | solution.py:410
  134.6 31.2 %collective-permute-start.36 = (bf16[256,2048]{1,0:T(8,128)(2,1)S(1)}, bf16[256,2048]{1,0:T(8,128)(2,1)S(1)}, u32[]{:S(2)}, u32[]{:S(2)}) collective-permute-start(bf16[256,2048]{1,0:T(8,128)(2,1)S(1)} %get-tuple-element.67), channel_id=1, source_target_pairs={{0,8},{8,0},{16,24},{24,16},{1,9},{9,1},{17,25},{25,17},{2,10},{10... | collective-permute-start | bytes 3145736 | tf_op jit(solution)/shard_map/ppermute | solution.py:409
  149.1 50.3 %collective-permute-start.33 = (bf16[256,2048]{1,0:T(8,128)(2,1)S(1)}, bf16[256,2048]{1,0:T(8,128)(2,1)S(1)}, u32[]{:S(2)}, u32[]{:S(2)}) collective-permute-start(bf16[256,2048]{1,0:T(8,128)(2,1)S(1)} %get-tuple-element.69), channel_id=1, source_target_pairs={{0,16},{8,24},{16,0},{24,8},{1,17},{9,25},{17,1},{25,9},{2,18},{10... | collective-permute-start | bytes 3145736 | tf_op jit(solution)/shard_map/ppermute | solution.py:410
  149.2 50.8 %collective-permute-start.32 = (bf16[256,2048]{1,0:T(8,128)(2,1)S(1)}, bf16[256,2048]{1,0:T(8,128)(2,1)S(1)}, u32[]{:S(2)}, u32[]{:S(2)}) collective-permute-start(bf16[256,2048]{1,0:T(8,128)(2,1)S(1)} %get-tuple-element.69), channel_id=1, source_target_pairs={{0,8},{8,0},{16,24},{24,16},{1,9},{9,1},{17,25},{25,17},{2,10},{10... | collective-permute-start | bytes 3145736 | tf_op jit(solution)/shard_map/ppermute | solution.py:409
  163.3 36.1 %collective-permute-start.38 = (bf16[128,2048]{1,0:T(8,128)(2,1)S(1)}, bf16[128,2048]{1,0:T(8,128)(2,1)S(1)}, u32[]{:S(2)}, u32[]{:S(2)}) collective-permute-start(bf16[128,2048]{1,0:T(8,128)(2,1)S(1)} %slice.613), channel_id=1, source_target_pairs={{0,8},{8,0},{16,24},{24,16},{1,9},{9,1},{17,25},{25,17},{2,10},{10... | collective-permute-start | bytes 1572872 | tf_op jit(solution)/shard_map/ppermute | solution.py:411
  165.8 34.1 %collective-permute-start.39 = (bf16[128,2048]{1,0:T(8,128)(2,1)S(1)}, bf16[128,2048]{1,0:T(8,128)(2,1)S(1)}, u32[]{:S(2)}, u32[]{:S(2)}) collective-permute-start(bf16[128,2048]{1,0:T(8,128)(2,1)S(1)} %slice.614), channel_id=1, source_target_pairs={{0,16},{8,24},{16,0},{24,8},{1,17},{9,25},{17,1},{25,9},{2,18},{10... | collective-permute-start | bytes 1572872 | tf_op jit(solution)/shard_map/ppermute | solution.py:412
  199.5 14.9 %collective-permute-start.34 = (bf16[128,2048]{1,0:T(8,128)(2,1)S(1)}, bf16[128,2048]{1,0:T(8,128)(2,1)S(1)}, u32[]{:S(2)}, u32[]{:S(2)}) collective-permute-start(bf16[128,2048]{1,0:T(8,128)(2,1)S(1)} %slice.610), channel_id=1, source_target_pairs={{0,8},{8,0},{16,24},{24,16},{1,9},{9,1},{17,25},{25,17},{2,10},{10... | collective-permute-start | bytes 1572872 | tf_op jit(solution)/shard_map/ppermute | solution.py:411
  200.1 15.2 %collective-permute-start.35 = (bf16[128,2048]{1,0:T(8,128)(2,1)S(1)}, bf16[128,2048]{1,0:T(8,128)(2,1)S(1)}, u32[]{:S(2)}, u32[]{:S(2)}) collective-permute-start(bf16[128,2048]{1,0:T(8,128)(2,1)S(1)} %slice.611), channel_id=1, source_target_pairs={{0,16},{8,24},{16,0},{24,8},{1,17},{9,25},{17,1},{25,9},{2,18},{10... | collective-permute-start | bytes 1572872 | tf_op jit(solution)/shard_map/ppermute | solution.py:412
  358.2 25.4 %collective-permute-start.57 = (bf16[256,2048]{1,0:T(8,128)(2,1)S(1)}, bf16[256,2048]{1,0:T(8,128)(2,1)S(1)}, u32[]{:S(2)}, u32[]{:S(2)}) collective-permute-start(bf16[256,2048]{1,0:T(8,128)(2,1)S(1)} %pad_maximum_fusion.26), channel_id=1, source_target_pairs={{0,16},{8,24},{16,0},{24,8},{1,17},{9,25},{17,1},{25,9},{2,18},{10... | collective-permute-start | bytes 3145736 | tf_op jit(solution)/shard_map/ppermute | solution.py:427
  359.0 25.1 %collective-permute-start.56 = (bf16[256,2048]{1,0:T(8,128)(2,1)S(1)}, bf16[256,2048]{1,0:T(8,128)(2,1)S(1)}, u32[]{:S(2)}, u32[]{:S(2)}) collective-permute-start(bf16[256,2048]{1,0:T(8,128)(2,1)S(1)} %pad_maximum_fusion.25), channel_id=1, source_target_pairs={{0,8},{8,0},{16,24},{24,16},{1,9},{9,1},{17,25},{25,17},{2,10},{10... | collective-permute-start | bytes 3145736 | tf_op jit(solution)/shard_map/ppermute | solution.py:424
  403.4 23.0 %collective-permute-start.61 = (bf16[256,2048]{1,0:T(8,128)(2,1)S(1)}, bf16[256,2048]{1,0:T(8,128)(2,1)S(1)}, u32[]{:S(2)}, u32[]{:S(2)}) collective-permute-start(bf16[256,2048]{1,0:T(8,128)(2,1)S(1)} %get-tuple-element.107), channel_id=1, source_target_pairs={{0,16},{8,24},{16,0},{24,8},{1,17},{9,25},{17,1},{25,9},{2,18},{10... | collective-permute-start | bytes 3145736 | tf_op jit(solution)/shard_map/ppermute | solution.py:410
  403.9 23.2 %collective-permute-start.60 = (bf16[256,2048]{1,0:T(8,128)(2,1)S(1)}, bf16[256,2048]{1,0:T(8,128)(2,1)S(1)}, u32[]{:S(2)}, u32[]{:S(2)}) collective-permute-start(bf16[256,2048]{1,0:T(8,128)(2,1)S(1)} %get-tuple-element.107), channel_id=1, source_target_pairs={{0,8},{8,0},{16,24},{24,16},{1,9},{9,1},{17,25},{25,17},{2,10},{10... | collective-permute-start | bytes 3145736 | tf_op jit(solution)/shard_map/ppermute | solution.py:409
  488.0 22.4 %collective-permute-start.65 = (bf16[256,2048]{1,0:T(8,128)(2,1)S(1)}, bf16[256,2048]{1,0:T(8,128)(2,1)S(1)}, u32[]{:S(2)}, u32[]{:S(2)}) collective-permute-start(bf16[256,2048]{1,0:T(8,128)(2,1)S(1)} %pad_maximum_fusion.28), channel_id=1, source_target_pairs={{0,16},{8,24},{16,0},{24,8},{1,17},{9,25},{17,1},{25,9},{2,18},{10... | collective-permute-start | bytes 3145736 | tf_op jit(solution)/shard_map/ppermute | solution.py:427
  489.6 22.9 %collective-permute-start.64 = (bf16[256,2048]{1,0:T(8,128)(2,1)S(1)}, bf16[256,2048]{1,0:T(8,128)(2,1)S(1)}, u32[]{:S(2)}, u32[]{:S(2)}) collective-permute-start(bf16[256,2048]{1,0:T(8,128)(2,1)S(1)} %pad_maximum_fusion.27), channel_id=1, source_target_pairs={{0,8},{8,0},{16,24},{24,16},{1,9},{9,1},{17,25},{25,17},{2,10},{10... | collective-permute-start | bytes 3145736 | tf_op jit(solution)/shard_map/ppermute | solution.py:424
  526.1 22.8 %collective-permute-start.1 = (bf16[256,2048]{1,0:T(8,128)(2,1)S(1)}, bf16[256,2048]{1,0:T(8,128)(2,1)S(1)}, u32[]{:S(2)}, u32[]{:S(2)}) collective-permute-start(bf16[256,2048]{1,0:T(8,128)(2,1)S(1)} %get-tuple-element.63), channel_id=1, source_target_pairs={{0,16},{8,24},{16,0},{24,8},{1,17},{9,25},{17,1},{25,9},{2,18},{10... | collective-permute-start | bytes 3145736 | tf_op jit(solution)/shard_map/ppermute | solution.py:410
  527.2 22.1 %collective-permute-start = (bf16[256,2048]{1,0:T(8,128)(2,1)S(1)}, bf16[256,2048]{1,0:T(8,128)(2,1)S(1)}, u32[]{:S(2)}, u32[]{:S(2)}) collective-permute-start(bf16[256,2048]{1,0:T(8,128)(2,1)S(1)} %get-tuple-element.63), channel_id=1, source_target_pairs={{0,8},{8,0},{16,24},{24,16},{1,9},{9,1},{17,25},{25,17},{2,10},{10... | collective-permute-start | bytes 3145736 | tf_op jit(solution)/shard_map/ppermute | solution.py:409
  596.1 22.3 %collective-permute-start.9 = (bf16[256,2048]{1,0:T(8,128)(2,1)S(1)}, bf16[256,2048]{1,0:T(8,128)(2,1)S(1)}, u32[]{:S(2)}, u32[]{:S(2)}) collective-permute-start(bf16[256,2048]{1,0:T(8,128)(2,1)S(1)} %pad_maximum_fusion.10), channel_id=1, source_target_pairs={{0,16},{8,24},{16,0},{24,8},{1,17},{9,25},{17,1},{25,9},{2,18},{10... | collective-permute-start | bytes 3145736 | tf_op jit(solution)/shard_map/ppermute | solution.py:427
  598.3 22.7 %collective-permute-start.8 = (bf16[256,2048]{1,0:T(8,128)(2,1)S(1)}, bf16[256,2048]{1,0:T(8,128)(2,1)S(1)}, u32[]{:S(2)}, u32[]{:S(2)}) collective-permute-start(bf16[256,2048]{1,0:T(8,128)(2,1)S(1)} %pad_maximum_fusion.9), channel_id=1, source_target_pairs={{0,8},{8,0},{16,24},{24,16},{1,9},{9,1},{17,25},{25,17},{2,10},{10... | collective-permute-start | bytes 3145736 | tf_op jit(solution)/shard_map/ppermute | solution.py:424
  621.3 14.9 %collective-permute-start.10 = (bf16[128,2048]{1,0:T(8,128)(2,1)S(1)}, bf16[128,2048]{1,0:T(8,128)(2,1)S(1)}, u32[]{:S(2)}, u32[]{:S(2)}) collective-permute-start(bf16[128,2048]{1,0:T(8,128)(2,1)S(1)} %get-tuple-element.108), channel_id=1, source_target_pairs={{0,16},{8,24},{16,0},{24,8},{1,17},{9,25},{17,1},{25,9},{2,18},{10... | collective-permute-start | bytes 1572872 | tf_op jit(solution)/shard_map/ppermute | solution.py:432
  621.4 14.9 %collective-permute-start.11 = (bf16[128,2048]{1,0:T(8,128)(2,1)S(1)}, bf16[128,2048]{1,0:T(8,128)(2,1)S(1)}, u32[]{:S(2)}, u32[]{:S(2)}) collective-permute-start(bf16[128,2048]{1,0:T(8,128)(2,1)S(1)} %get-tuple-element.109), channel_id=1, source_target_pairs={{0,8},{8,0},{16,24},{24,16},{1,9},{9,1},{17,25},{25,17},{2,10},{10... | collective-permute-start | bytes 1572872 | tf_op jit(solution)/shard_map/ppermute | solution.py:433
  622.0 36.7 %collective-permute-start.17 = (bf16[256,2048]{1,0:T(8,128)(2,1)S(1)}, bf16[256,2048]{1,0:T(8,128)(2,1)S(1)}, u32[]{:S(2)}, u32[]{:S(2)}) collective-permute-start(bf16[256,2048]{1,0:T(8,128)(2,1)S(1)} %copy-done.76), channel_id=1, source_target_pairs={{0,16},{8,24},{16,0},{24,8},{1,17},{9,25},{17,1},{25,9},{2,18},{10... | collective-permute-start | bytes 3145736 | tf_op jit(solution)/shard_map/ppermute | solution.py:410
  623.9 35.4 %collective-permute-start.16 = (bf16[256,2048]{1,0:T(8,128)(2,1)S(1)}, bf16[256,2048]{1,0:T(8,128)(2,1)S(1)}, u32[]{:S(2)}, u32[]{:S(2)}) collective-permute-start(bf16[256,2048]{1,0:T(8,128)(2,1)S(1)} %copy-done.76), channel_id=1, source_target_pairs={{0,8},{8,0},{16,24},{24,16},{1,9},{9,1},{17,25},{25,17},{2,10},{10... | collective-permute-start | bytes 3145736 | tf_op jit(solution)/shard_map/ppermute | solution.py:409
  638.5 50.9 %collective-permute-start.13 = (bf16[256,2048]{1,0:T(8,128)(2,1)S(1)}, bf16[256,2048]{1,0:T(8,128)(2,1)S(1)}, u32[]{:S(2)}, u32[]{:S(2)}) collective-permute-start(bf16[256,2048]{1,0:T(8,128)(2,1)S(1)} %get-tuple-element.59), channel_id=1, source_target_pairs={{0,16},{8,24},{16,0},{24,8},{1,17},{9,25},{17,1},{25,9},{2,18},{10... | collective-permute-start | bytes 3145736 | tf_op jit(solution)/shard_map/ppermute | solution.py:410
  640.4 50.6 %collective-permute-start.12 = (bf16[256,2048]{1,0:T(8,128)(2,1)S(1)}, bf16[256,2048]{1,0:T(8,128)(2,1)S(1)}, u32[]{:S(2)}, u32[]{:S(2)}) collective-permute-start(bf16[256,2048]{1,0:T(8,128)(2,1)S(1)} %get-tuple-element.59), channel_id=1, source_target_pairs={{0,8},{8,0},{16,24},{24,16},{1,9},{9,1},{17,25},{25,17},{2,10},{10... | collective-permute-start | bytes 3145736 | tf_op jit(solution)/shard_map/ppermute | solution.py:409
  658.7 29.8 %collective-permute-start.18 = (bf16[128,2048]{1,0:T(8,128)(2,1)S(1)}, bf16[128,2048]{1,0:T(8,128)(2,1)S(1)}, u32[]{:S(2)}, u32[]{:S(2)}) collective-permute-start(bf16[128,2048]{1,0:T(8,128)(2,1)S(1)} %slice.582), channel_id=1, source_target_pairs={{0,8},{8,0},{16,24},{24,16},{1,9},{9,1},{17,25},{25,17},{2,10},{10... | collective-permute-start | bytes 1572872 | tf_op jit(solution)/shard_map/ppermute | solution.py:411
  659.4 30.7 %collective-permute-start.19 = (bf16[128,2048]{1,0:T(8,128)(2,1)S(1)}, bf16[128,2048]{1,0:T(8,128)(2,1)S(1)}, u32[]{:S(2)}, u32[]{:S(2)}) collective-permute-start(bf16[128,2048]{1,0:T(8,128)(2,1)S(1)} %slice.583), channel_id=1, source_target_pairs={{0,16},{8,24},{16,0},{24,8},{1,17},{9,25},{17,1},{25,9},{2,18},{10... | collective-permute-start | bytes 1572872 | tf_op jit(solution)/shard_map/ppermute | solution.py:412
  765.9 20.5 %collective-permute-start.45 = (bf16[256,2048]{1,0:T(8,128)(2,1)S(1)}, bf16[256,2048]{1,0:T(8,128)(2,1)S(1)}, u32[]{:S(2)}, u32[]{:S(2)}) collective-permute-start(bf16[256,2048]{1,0:T(8,128)(2,1)S(1)} %pad_maximum_fusion.22), channel_id=1, source_target_pairs={{0,16},{8,24},{16,0},{24,8},{1,17},{9,25},{17,1},{25,9},{2,18},{10... | collective-permute-start | bytes 3145736 | tf_op jit(solution)/shard_map/ppermute | solution.py:427
  766.4 20.5 %collective-permute-start.44 = (bf16[256,2048]{1,0:T(8,128)(2,1)S(1)}, bf16[256,2048]{1,0:T(8,128)(2,1)S(1)}, u32[]{:S(2)}, u32[]{:S(2)}) collective-permute-start(bf16[256,2048]{1,0:T(8,128)(2,1)S(1)} %pad_maximum_fusion.21), channel_id=1, source_target_pairs={{0,8},{8,0},{16,24},{24,16},{1,9},{9,1},{17,25},{25,17},{2,10},{10... | collective-permute-start | bytes 3145736 | tf_op jit(solution)/shard_map/ppermute | solution.py:424
  807.6 20.5 %collective-permute-start.49 = (bf16[256,2048]{1,0:T(8,128)(2,1)S(1)}, bf16[256,2048]{1,0:T(8,128)(2,1)S(1)}, u32[]{:S(2)}, u32[]{:S(2)}) collective-permute-start(bf16[256,2048]{1,0:T(8,128)(2,1)S(1)} %get-tuple-element.55), channel_id=1, source_target_pairs={{0,16},{8,24},{16,0},{24,8},{1,17},{9,25},{17,1},{25,9},{2,18},{10... | collective-permute-start | bytes 3145736 | tf_op jit(solution)/shard_map/ppermute | solution.py:410
  807.8 24.3 %collective-permute-start.48 = (bf16[256,2048]{1,0:T(8,128)(2,1)S(1)}, bf16[256,2048]{1,0:T(8,128)(2,1)S(1)}, u32[]{:S(2)}, u32[]{:S(2)}) collective-permute-start(bf16[256,2048]{1,0:T(8,128)(2,1)S(1)} %get-tuple-element.55), channel_id=1, source_target_pairs={{0,8},{8,0},{16,24},{24,16},{1,9},{9,1},{17,25},{25,17},{2,10},{10... | collective-permute-start | bytes 3145736 | tf_op jit(solution)/shard_map/ppermute | solution.py:409
  847.3 360.4 %reduce-scatter.5.cloned.1.call-start = ((), (), s32[]{:S(2)}) async-start(), calls=%async_computation.6 | async-start | bytes 3538944 | tf_op jit(solution)/shard_map/reduce_scatter | solution.py:632
  908.8 302.4 %all-reduce.2.cloned.1.call-start = ((), (), s32[]{:S(2)}) async-start(), calls=%async_computation.8 | async-start | bytes 2097152 | tf_op jit(solution)/shard_map/psum | solution.py:629
  911.0 16.9 %collective-permute-start.72 = (bf16[64,2048]{1,0:T(8,128)(2,1)}, bf16[64,2048]{1,0:T(8,128)(2,1)S(1)}, u32[]{:S(2)}, u32[]{:S(2)}) collective-permute-start(bf16[64,2048]{1,0:T(8,128)(2,1)} %reduce-scatter.7.cloned.1.call-done), channel_id=1, source_target_pairs={{0,0},{4,1},{8,10},{12,11},{16,20},{20,21},{24,30},{28,31}} | collective-permute-start | bytes 786440 | tf_op jit(solution)/shard_map/ppermute | solution.py:628
  929.0 297.6 %reduce-scatter.9.cloned.1.call-start = ((), (), s32[]{:S(2)}) async-start(), calls=%async_computation.9 | async-start | bytes 14155776 | tf_op jit(solution)/shard_map/reduce_scatter | solution.py:581
  965.2 314.5 %reduce-scatter.11.cloned.1.call-start = ((), (), s32[]{:S(2)}) async-start(), calls=%async_computation.10 | async-start | bytes 14155776 | tf_op jit(solution)/shard_map/reduce_scatter | solution.py:581
  1017.8 23.5 %collective-permute-start.41 = (bf16[256,2048]{1,0:T(8,128)(2,1)S(1)}, bf16[256,2048]{1,0:T(8,128)(2,1)S(1)}, u32[]{:S(2)}, u32[]{:S(2)}) collective-permute-start(bf16[256,2048]{1,0:T(8,128)(2,1)S(1)} %pad_maximum_fusion.20), channel_id=1, source_target_pairs={{0,16},{8,24},{16,0},{24,8},{1,17},{9,25},{17,1},{25,9},{2,18},{10... | collective-permute-start | bytes 3145736 | tf_op jit(solution)/shard_map/ppermute | solution.py:427
  1018.1 27.8 %collective-permute-start.40 = (bf16[256,2048]{1,0:T(8,128)(2,1)S(1)}, bf16[256,2048]{1,0:T(8,128)(2,1)S(1)}, u32[]{:S(2)}, u32[]{:S(2)}) collective-permute-start(bf16[256,2048]{1,0:T(8,128)(2,1)S(1)} %pad_maximum_fusion.19), channel_id=1, source_target_pairs={{0,8},{8,0},{16,24},{24,16},{1,9},{9,1},{17,25},{25,17},{2,10},{10... | collective-permute-start | bytes 3145736 | tf_op jit(solution)/shard_map/ppermute | solution.py:424
  1079.8 26.2 %collective-permute-start.21 = (bf16[256,2048]{1,0:T(8,128)(2,1)S(1)}, bf16[256,2048]{1,0:T(8,128)(2,1)S(1)}, u32[]{:S(2)}, u32[]{:S(2)}) collective-permute-start(bf16[256,2048]{1,0:T(8,128)(2,1)S(1)} %pad_maximum_fusion.14), channel_id=1, source_target_pairs={{0,16},{8,24},{16,0},{24,8},{1,17},{9,25},{17,1},{25,9},{2,18},{10... | collective-permute-start | bytes 3145736 | tf_op jit(solution)/shard_map/ppermute | solution.py:427
  1080.8 26.2 %collective-permute-start.20 = (bf16[256,2048]{1,0:T(8,128)(2,1)S(1)}, bf16[256,2048]{1,0:T(8,128)(2,1)S(1)}, u32[]{:S(2)}, u32[]{:S(2)}) collective-permute-start(bf16[256,2048]{1,0:T(8,128)(2,1)S(1)} %pad_maximum_fusion.13), channel_id=1, source_target_pairs={{0,8},{8,0},{16,24},{24,16},{1,9},{9,1},{17,25},{25,17},{2,10},{10... | collective-permute-start | bytes 3145736 | tf_op jit(solution)/shard_map/ppermute | solution.py:424
  1086.3 42.1 %collective-permute-start.53 = (bf16[256,2048]{1,0:T(8,128)(2,1)S(1)}, bf16[256,2048]{1,0:T(8,128)(2,1)S(1)}, u32[]{:S(2)}, u32[]{:S(2)}) collective-permute-start(bf16[256,2048]{1,0:T(8,128)(2,1)S(1)} %pad_maximum_fusion.24), channel_id=1, source_target_pairs={{0,16},{8,24},{16,0},{24,8},{1,17},{9,25},{17,1},{25,9},{2,18},{10... | collective-permute-start | bytes 3145736 | tf_op jit(solution)/shard_map/ppermute | solution.py:427
  1087.9 41.6 %collective-permute-start.52 = (bf16[256,2048]{1,0:T(8,128)(2,1)S(1)}, bf16[256,2048]{1,0:T(8,128)(2,1)S(1)}, u32[]{:S(2)}, u32[]{:S(2)}) collective-permute-start(bf16[256,2048]{1,0:T(8,128)(2,1)S(1)} %pad_maximum_fusion.23), channel_id=1, source_target_pairs={{0,8},{8,0},{16,24},{24,16},{1,9},{9,1},{17,25},{25,17},{2,10},{10... | collective-permute-start | bytes 3145736 | tf_op jit(solution)/shard_map/ppermute | solution.py:424
  1107.4 32.2 %collective-permute-start.22 = (bf16[128,2048]{1,0:T(8,128)(2,1)S(1)}, bf16[128,2048]{1,0:T(8,128)(2,1)S(1)}, u32[]{:S(2)}, u32[]{:S(2)}) collective-permute-start(bf16[128,2048]{1,0:T(8,128)(2,1)S(1)} %get-tuple-element.100), channel_id=1, source_target_pairs={{0,16},{8,24},{16,0},{24,8},{1,17},{9,25},{17,1},{25,9},{2,18},{10... | collective-permute-start | bytes 1572872 | tf_op jit(solution)/shard_map/ppermute | solution.py:432
  1108.6 31.6 %collective-permute-start.23 = (bf16[128,2048]{1,0:T(8,128)(2,1)S(1)}, bf16[128,2048]{1,0:T(8,128)(2,1)S(1)}, u32[]{:S(2)}, u32[]{:S(2)}) collective-permute-start(bf16[128,2048]{1,0:T(8,128)(2,1)S(1)} %get-tuple-element.101), channel_id=1, source_target_pairs={{0,8},{8,0},{16,24},{24,16},{1,9},{9,1},{17,25},{25,17},{2,10},{10... | collective-permute-start | bytes 1572872 | tf_op jit(solution)/shard_map/ppermute | solution.py:433
  1129.9 15.4 %collective-permute-start.54 = (bf16[128,2048]{1,0:T(8,128)(2,1)S(1)}, bf16[128,2048]{1,0:T(8,128)(2,1)S(1)}, u32[]{:S(2)}, u32[]{:S(2)}) collective-permute-start(bf16[128,2048]{1,0:T(8,128)(2,1)S(1)} %get-tuple-element.88), channel_id=1, source_target_pairs={{0,16},{8,24},{16,0},{24,8},{1,17},{9,25},{17,1},{25,9},{2,18},{10... | collective-permute-start | bytes 1572872 | tf_op jit(solution)/shard_map/ppermute | solution.py:432
  1226.6 61.6 %collective-permute-start.77 = (bf16[384,2048]{1,0:T(8,128)(2,1)}, bf16[384,2048]{1,0:T(8,128)(2,1)S(1)}, u32[]{:S(2)}, u32[]{:S(2)}) collective-permute-start(bf16[384,2048]{1,0:T(8,128)(2,1)} %bitcast.388), channel_id=1, source_target_pairs={{0,16},{8,24},{16,0},{24,8},{1,17},{9,25},{17,1},{25,9},{2,18},{10... | collective-permute-start | bytes 4718600 | tf_op jit(solution)/shard_map/ppermute | solution.py:410
  1226.9 62.9 %collective-permute-start.76 = (bf16[384,2048]{1,0:T(8,128)(2,1)}, bf16[384,2048]{1,0:T(8,128)(2,1)}, u32[]{:S(2)}, u32[]{:S(2)}) collective-permute-start(bf16[384,2048]{1,0:T(8,128)(2,1)} %bitcast.389), channel_id=1, source_target_pairs={{0,8},{8,0},{16,24},{24,16},{1,9},{9,1},{17,25},{25,17},{2,10},{10... | collective-permute-start | bytes 4718600 | tf_op jit(solution)/shard_map/ppermute | solution.py:409
  1279.7 37.5 %collective-permute-start.81 = (bf16[384,2048]{1,0:T(8,128)(2,1)}, bf16[384,2048]{1,0:T(8,128)(2,1)S(1)}, u32[]{:S(2)}, u32[]{:S(2)}) collective-permute-start(bf16[384,2048]{1,0:T(8,128)(2,1)} %bitcast.390), channel_id=1, source_target_pairs={{0,16},{8,24},{16,0},{24,8},{1,17},{9,25},{17,1},{25,9},{2,18},{10... | collective-permute-start | bytes 4718600 | tf_op jit(solution)/shard_map/ppermute | solution.py:410
  1280.2 37.7 %collective-permute-start.80 = (bf16[384,2048]{1,0:T(8,128)(2,1)}, bf16[384,2048]{1,0:T(8,128)(2,1)S(1)}, u32[]{:S(2)}, u32[]{:S(2)}) collective-permute-start(bf16[384,2048]{1,0:T(8,128)(2,1)} %bitcast.391), channel_id=1, source_target_pairs={{0,8},{8,0},{16,24},{24,16},{1,9},{9,1},{17,25},{25,17},{2,10},{10... | collective-permute-start | bytes 4718600 | tf_op jit(solution)/shard_map/ppermute | solution.py:409
  1288.3 46.4 %collective-permute-start.78 = (bf16[192,2048]{1,0:T(8,128)(2,1)S(1)}, bf16[192,2048]{1,0:T(8,128)(2,1)S(1)}, u32[]{:S(2)}, u32[]{:S(2)}) collective-permute-start(bf16[192,2048]{1,0:T(8,128)(2,1)S(1)} %slice.677), channel_id=1, source_target_pairs={{0,8},{8,0},{16,24},{24,16},{1,9},{9,1},{17,25},{25,17},{2,10},{10... | collective-permute-start | bytes 2359304 | tf_op jit(solution)/shard_map/ppermute | solution.py:411
  1291.0 43.7 %collective-permute-start.79 = (bf16[192,2048]{1,0:T(8,128)(2,1)S(1)}, bf16[192,2048]{1,0:T(8,128)(2,1)S(1)}, u32[]{:S(2)}, u32[]{:S(2)}) collective-permute-start(bf16[192,2048]{1,0:T(8,128)(2,1)S(1)} %slice.678), channel_id=1, source_target_pairs={{0,16},{8,24},{16,0},{24,8},{1,17},{9,25},{17,1},{25,9},{2,18},{10... | collective-permute-start | bytes 2359304 | tf_op jit(solution)/shard_map/ppermute | solution.py:412
  1317.3 30.6 %collective-permute-start.82 = (bf16[192,2048]{1,0:T(8,128)(2,1)S(1)}, bf16[192,2048]{1,0:T(8,128)(2,1)S(1)}, u32[]{:S(2)}, u32[]{:S(2)}) collective-permute-start(bf16[192,2048]{1,0:T(8,128)(2,1)S(1)} %slice.680), channel_id=1, source_target_pairs={{0,8},{8,0},{16,24},{24,16},{1,9},{9,1},{17,25},{25,17},{2,10},{10... | collective-permute-start | bytes 2359304 | tf_op jit(solution)/shard_map/ppermute | solution.py:411
  1318.0 31.1 %collective-permute-start.83 = (bf16[192,2048]{1,0:T(8,128)(2,1)S(1)}, bf16[192,2048]{1,0:T(8,128)(2,1)S(1)}, u32[]{:S(2)}, u32[]{:S(2)}) collective-permute-start(bf16[192,2048]{1,0:T(8,128)(2,1)S(1)} %slice.681), channel_id=1, source_target_pairs={{0,16},{8,24},{16,0},{24,8},{1,17},{9,25},{17,1},{25,9},{2,18},{10... | collective-permute-start | bytes 2359304 | tf_op jit(solution)/shard_map/ppermute | solution.py:412
  (156 other events, 3732.9 us)
Sparse Core Ops, SparseCore 0:
  10.3 45.6 all-gather.6
  58.1 31.7 all-gather.8
  92.1 116.2 all-gather.10
  210.4 114.9 all-gather.12
  847.4 33.9 reduce-scatter.6
  908.9 50.2 reduce-scatter.4
  962.3 51.9 all-reduce.1
  1016.6 132.0 reduce-scatter.8
  1151.0 128.6 reduce-scatter.10

commit v2 on v1

--- a/solution.py
+++ b/solution.py
@@ -21,7 +21,8 @@
 VMEM_LIMIT = 58 << 20
 HEAD = 64
 BLOCK = 256
-CHUNKS = 2
+CHUNKS = 4
+ANY = pl.BlockSpec(memory_space=pl.ANY)
 
 
 def dot(a, b, dims=NN):
@@ -70,7 +71,7 @@
 
 
 def attend_kernel(
-    sizes, place_ref, len_ref, qkv_ref, qg_ref, kg_ref, cos_ref, sin_ref, ones_ref,
+    sizes, place_ref, len_ref, qkv_ref, qg_ref, kg_ref, cos_ref, sin_ref, ones_ref, after_ref,
     out_ref, lse_ref, q_s, k_s, v_s, o_s,
 ):
     hq, hkv, group = sizes
@@ -108,7 +109,7 @@
 
 def attend_back_kernel(
     sizes, place_ref, len_ref, qkv_ref, cot_ref, lse_ref, qg_ref, kg_ref, cos_ref, sin_ref,
-    ones_ref, dqkv_ref, dgain_ref, q_s, k_s, v_s, cot_s, dq_s, dk_s, dv_s,
+    ones_ref, after_ref, dqkv_ref, dgain_ref, q_s, k_s, v_s, cot_s, dq_s, dk_s, dv_s,
 ):
     hq, hkv, group = sizes
     seqs, rows_in, _ = qkv_ref.shape
@@ -188,7 +189,7 @@
     )
 
 
-def attend(sizes, place, length, qkv, gains, tables):
+def attend(sizes, place, length, qkv, gains, tables, after):
     seqs, rows_in, _ = qkv.shape
     hq, hkv, _ = sizes
     slot = seqs * rows_in
@@ -198,7 +199,7 @@
             jax.ShapeDtypeStruct((seqs, rows_in, hq * HEAD), BF16),
             jax.ShapeDtypeStruct((hq, slot, 1), F32),
         ),
-        in_specs=[SMEM, SMEM] + [VMEM] * 6,
+        in_specs=[SMEM, SMEM] + [VMEM] * 6 + [ANY],
         out_specs=(VMEM, VMEM),
         scratch_shapes=[
             pltpu.VMEM((hq, slot, HEAD), BF16),
@@ -208,13 +209,13 @@
         ],
         compiler_params=pltpu.CompilerParams(vmem_limit_bytes=VMEM_LIMIT),
         cost_estimate=pl.CostEstimate(
-            flops=20 * hq * slot * slot * HEAD, bytes_accessed=1 << 23, transcendentals=0
+            flops=56 * hq * slot * slot * HEAD, bytes_accessed=1 << 23, transcendentals=0
         ),
         name="attend",
-    )(place, length, qkv, *gains, *tables)
-
-
-def attend_back(sizes, place, length, qkv, cot, lse, gains, tables):
+    )(place, length, qkv, *gains, *tables, after)
+
+
+def attend_back(sizes, place, length, qkv, cot, lse, gains, tables, after):
     seqs, rows_in, width = qkv.shape
     hq, hkv, _ = sizes
     slot = seqs * rows_in
@@ -224,7 +225,7 @@
             jax.ShapeDtypeStruct((seqs, rows_in, width), BF16),
             jax.ShapeDtypeStruct((2, 128), F32),
         ),
-        in_specs=[SMEM, SMEM] + [VMEM] * 8,
+        in_specs=[SMEM, SMEM] + [VMEM] * 8 + [ANY],
         out_specs=(VMEM, VMEM),
         scratch_shapes=[
             pltpu.VMEM((hq, slot, HEAD), BF16),
@@ -237,17 +238,17 @@
         ],
         compiler_params=pltpu.CompilerParams(vmem_limit_bytes=VMEM_LIMIT),
         cost_estimate=pl.CostEstimate(
-            flops=36 * hq * slot * slot * HEAD, bytes_accessed=1 << 23, transcendentals=0
+            flops=88 * hq * slot * slot * HEAD, bytes_accessed=1 << 23, transcendentals=0
         ),
         name="attend_back",
-    )(place, length, qkv, cot, lse, *gains, *tables)
+    )(place, length, qkv, cot, lse, *gains, *tables, after)
 
 
 def ffn_kernel(has_sum, mid_ref, cot_ref, gate_ref, up_ref, down_ref, *refs):
     if has_sum:
-        sum_ref, acts_ref, pull_ref = refs
+        sum_ref, after_ref, acts_ref, pull_ref = refs
     else:
-        acts_ref, pull_ref = refs
+        after_ref, acts_ref, pull_ref = refs
     model = mid_ref.shape[-1]
     hidden = acts_ref.shape[-1]
     gate_w = gate_ref[...].reshape(hidden, model)
@@ -270,7 +271,7 @@
     pull_ref[...] = pulled.astype(pull_ref.dtype)
 
 
-def ffn_both(mid, cot, weights, summed, last):
+def ffn_both(mid, cot, weights, summed, last, after):
     tokens, model = mid.shape
     shards, _, part, _ = weights.shape
     hidden = shards * part
@@ -293,23 +294,24 @@
             jax.ShapeDtypeStruct((tokens, model), BF16 if last else F32),
         ),
         in_specs=[row_spec, row_spec, weight_spec(0), weight_spec(1), weight_spec(2)]
-        + [row_spec] * len(extra),
+        + [row_spec] * len(extra)
+        + [ANY],
         out_specs=(pl.BlockSpec((3, tile, hidden), lambda i: (0, i, 0)), row_spec),
         compiler_params=pltpu.CompilerParams(vmem_limit_bytes=VMEM_LIMIT),
         cost_estimate=pl.CostEstimate(
-            flops=10 * tokens * model * hidden,
+            flops=16 * tokens * model * hidden,
             bytes_accessed=4 * tokens * model + 6 * hidden * model,
             transcendentals=0,
         ),
         name="ffn_both",
-    )(mid, cot, weights, weights, weights, *extra)
+    )(mid, cot, weights, weights, weights, *extra, after)
 
 
 def ffn_grad_kernel(slots, *refs):
     acts = refs[:slots]
     mids = refs[slots : 2 * slots]
     cots = refs[2 * slots : 3 * slots]
-    out_ref = refs[3 * slots]
+    out_ref = refs[3 * slots + 1]
     kind = pl.program_id(0)
 
     def store(others):
@@ -327,7 +329,7 @@
         store(cots)
 
 
-def ffn_grads(acts, mids, cots, shards):
+def ffn_grads(acts, mids, cots, shards, after):
     slots = len(acts)
     _, tokens, hidden = acts[0].shape
     model = mids[0].shape[-1]
@@ -342,22 +344,23 @@
         grid=(3, hidden // tile),
         out_shape=jax.ShapeDtypeStruct((shards, 3, part, model), BF16),
         in_specs=[pl.BlockSpec((1, tokens, tile), lambda k, i: (k, 0, i))] * slots
-        + [whole] * (2 * slots),
+        + [whole] * (2 * slots)
+        + [ANY],
         out_specs=pl.BlockSpec((per, 1, part, model), lambda k, i: (i, k, 0, 0)),
         compiler_params=pltpu.CompilerParams(vmem_limit_bytes=VMEM_LIMIT),
         cost_estimate=pl.CostEstimate(
-            flops=6 * slots * tokens * model * hidden,
+            flops=9 * slots * tokens * model * hidden,
             bytes_accessed=4 * slots * tokens * model,
             transcendentals=0,
         ),
         name="ffn_grads",
-    )(*acts, *mids, *cots)
+    )(*acts, *mids, *cots, after)
 
 
 def ffn_down_kernel(chunks, *refs):
     acts = refs[:chunks]
     downs = refs[chunks : 2 * chunks]
-    out_ref = refs[2 * chunks]
+    out_ref = refs[2 * chunks + 1]
     total = None
     for act, down in zip(acts, downs):
         hidden = act.shape[-1]
@@ -366,7 +369,7 @@
     out_ref[...] = total.astype(BF16)
 
 
-def ffn_down(acts, weights):
+def ffn_down(acts, weights, after):
     chunks = len(acts)
     _, tokens, hidden = acts[0].shape
     shards, _, part, model = weights[0].shape
@@ -381,16 +384,46 @@
         functools.partial(ffn_down_kernel, chunks),
         grid=(tokens // tile,),
         out_shape=jax.ShapeDtypeStruct((tokens, model), BF16),
-        in_specs=[act_spec] * chunks + [down_spec] * chunks,
+        in_specs=[act_spec] * chunks + [down_spec] * chunks + [ANY],
         out_specs=pl.BlockSpec((tile, model), lambda i: (i, 0)),
         compiler_params=pltpu.CompilerParams(vmem_limit_bytes=VMEM_LIMIT),
         cost_estimate=pl.CostEstimate(
-            flops=2 * chunks * tokens * model * hidden,
+            flops=4 * chunks * tokens * model * hidden,
             bytes_accessed=chunks * hidden * (tokens + model) * 2,
             transcendentals=0,
         ),
         name="ffn_down",
-    )(*acts, *weights)
+    )(*acts, *weights, after)
+
+
+def place_kernel(place_ref, parts_ref, *refs):
+    for kind, out_ref in enumerate(refs[-3:]):
+        out_ref[0, 0] = parts_ref[0, kind].astype(F32)
+
+
+def place_parts(place, parts, chunk, held):
+    seqs, _, part, model = parts.shape
+    out = jax.ShapeDtypeStruct((seqs, CHUNKS, part, model), F32)
+    out_spec = pl.BlockSpec(
+        (1, 1, part, model), lambda j, at: (jnp.bitwise_xor(at[0], j), chunk, 0, 0)
+    )
+    return pl.pallas_call(
+        place_kernel,
+        out_shape=(out,) * 3,
+        grid_spec=pltpu.PrefetchScalarGridSpec(
+            num_scalar_prefetch=1,
+            grid=(seqs,),
+            in_specs=[pl.BlockSpec((1, 3, part, model), lambda j, at: (j, 0, 0, 0))]
+            + [ANY] * len(held),
+            out_specs=(out_spec,) * 3,
+        ),
+        input_output_aliases={2 + k: k for k in range(len(held))},
+        compiler_params=pltpu.CompilerParams(vmem_limit_bytes=VMEM_LIMIT),
+        cost_estimate=pl.CostEstimate(
+            flops=0, bytes_accessed=18 * seqs * part * model, transcendentals=0
+        ),
+        name="place_parts",
+    )(place, parts, *held)
 
 
 def ring_places(count):
@@ -447,6 +480,38 @@
     )
 
 
+def out_home(sums):
+    seqs = lax.axis_size("seq")
+    shards = lax.axis_size("fsdp")
+    per = shards // seqs
+    held = []
+    for j in range(seqs):
+        moves = [
+            (s * shards + h * seqs + j, s * shards + s * per + h)
+            for s in range(seqs)
+            for h in range(per)
+        ]
+        held.append(lax.ppermute(sums, ("seq", "fsdp"), moves))
+    held = jnp.concatenate(held, axis=0)
+    if seqs != 4:
+        return lax.psum(held, "seq")
+
+    def hop(values, start, end):
+        moves = [
+            ((s ^ start) * shards + s * per + h, (s ^ end) * shards + s * per + h)
+            for s in range(seqs)
+            for h in range(per)
+        ]
+        return lax.ppermute(values, ("seq", "fsdp"), moves)
+
+    half = held.shape[0] // 2
+    one = hop(held, 0, 1)
+    two = hop(held, 0, 2)
+    top = hop(two[:half], 2, 3)
+    low = hop(one[half:], 1, 3)
+    return held + one + two + jnp.concatenate([top, low], axis=0)
+
+
 def scale_of(values):
     return lax.rsqrt(jnp.mean(values * values, axis=-1, keepdims=True) + EPSILON)
 
@@ -463,6 +528,10 @@
         scale * pulled - values * (scale * scale * scale) * mean,
         jnp.sum(cot * values * scale, axis=0),
     )
+
+
+def follow(values, earlier):
+    return lax.optimization_barrier((values, *earlier))[0]
 
 
 def own_columns(weight, heads, place):
@@ -508,6 +577,12 @@
         jnp.concatenate([key_gain, key_gain]).reshape(1, 2 * HEAD),
     )
 
+    places = place * rows + jnp.arange(rows, dtype=jnp.int32)
+    live = (places[None, :] < lengths[:, None]).astype(F32)[..., None]
+    inputs = tokens.astype(F32)
+    out_cot = cotangent.astype(F32) * live
+    normal_in = [normed(inputs[b], attn_gain).astype(BF16) for b in range(slots)]
+
     qkv_own = jnp.concatenate(
         [
             own_columns(query_weight, hq, place),
@@ -517,6 +592,8 @@
         axis=1,
     )
     qkv_weight = lax.all_gather(qkv_own, "fsdp", axis=0, tiled=True)
+    normal_full = [seq_gather(v).reshape(slot_len, model) for v in normal_in]
+    out_weight = follow(out_weight, normal_full[:1])
     per = shards // seqs
     piece = out_weight.shape[0] // seqs
     out_own = None
@@ -542,13 +619,7 @@
         )
         ffn_weights.append(lax.all_gather(mine, "fsdp", axis=0))
 
-    places = place * rows + jnp.arange(rows, dtype=jnp.int32)
-    live = (places[None, :] < lengths[:, None]).astype(F32)[..., None]
-    inputs = tokens.astype(F32)
-    out_cot = cotangent.astype(F32) * live
-    normal_in = [normed(inputs[b], attn_gain).astype(BF16) for b in range(slots)]
-    normal_full = [seq_gather(v).reshape(slot_len, model) for v in normal_in]
-
+    after = order
     qkv = []
     attended = []
     log_sums = []
@@ -556,12 +627,14 @@
     mid_full = []
     for b in range(slots):
         raw = dot(normal_full[b], qkv_weight).astype(BF16).reshape(seqs, rows, -1)
-        mixed, lse = attend(sizes, order, lengths[b : b + 1], raw, gains, tables)
+        mixed, lse = attend(sizes, order, lengths[b : b + 1], raw, gains, tables, after)
+        after = mixed
         mixed = mixed.reshape(slot_len, hq * HEAD)
         qkv.append(raw)
         attended.append(mixed)
         log_sums.append(lse)
-        proj = dot(mixed, out_rows).astype(BF16).reshape(seqs, rows, model)
+    for b in range(slots):
+        proj = dot(attended[b], out_rows).astype(BF16).reshape(seqs, rows, model)
         res = inputs[b] + seq_scatter(proj)
         hidden_res.append(res)
         mid = normed(res, ffn_gain).astype(BF16)
@@ -570,15 +643,37 @@
 
     acts = [[None] * slots for _ in range(CHUNKS)]
     pulled = [None] * slots
-    for c in range(CHUNKS):
+    ffn_parts = []
+    ffn_sums = []
+
+    def ffn_step(b, c, after):
+        acts[c][b], pulled[b] = ffn_both(
+            mid_full[b], cot_full[b], ffn_weights[c], pulled[b], c == CHUNKS - 1, after
+        )
+        return acts[c][b]
+
+    def grad_step(c, after):
+        ffn_parts.append(ffn_grads(acts[c], mid_full, cot_full, shards, after))
+        return ffn_parts[-1]
+
+    def sum_next(*earlier):
+        sent = ffn_parts[len(ffn_sums)].reshape(shards, 3 * part, model)
+        sent = follow(sent, [*ffn_sums[-1:], *earlier])
+        ffn_sums.append(lax.psum_scatter(sent, "fsdp", scatter_dimension=0))
+
+    early = CHUNKS // 2
+    for b in range(slots):
+        for c in range(early):
+            after = ffn_step(b, c, after)
+    after = grad_step(0, after)
+    sum_next()
+    for c in range(early, CHUNKS):
         for b in range(slots):
-            acts[c][b], pulled[b] = ffn_both(
-                mid_full[b], cot_full[b], ffn_weights[c], pulled[b], c == CHUNKS - 1
-            )
-    ffn_sums = []
-    for c in range(CHUNKS):
-        grads = ffn_grads(acts[c], mid_full, cot_full, shards).reshape(shards, 3 * part, model)
-        ffn_sums.append(lax.psum_scatter(grads, "fsdp", scatter_dimension=0))
+            after = ffn_step(b, c, after)
+    for c in range(1, CHUNKS):
+        after = grad_step(c, after)
+    for _ in range(early - 1):
+        sum_next()
 
     output = []
     res_cot = []
@@ -597,14 +692,21 @@
         res_full.append(full)
         attended_cot = dot(full, out_rows, NT).astype(BF16).reshape(seqs, rows, hq * HEAD)
         back, gain_part = attend_back(
-            sizes, order, lengths[b : b + 1], qkv[b], attended_cot, log_sums[b], gains, tables
+            sizes, order, lengths[b : b + 1], qkv[b], attended_cot, log_sums[b], gains, tables,
+            after,
         )
+        after = back
+        sum_next(back)
         head_gain = head_gain + gain_part
         dqkv.append(back.reshape(slot_len, -1))
     for b in range(slots):
-        ffn_out = ffn_down([acts[c][b] for c in range(CHUNKS)], ffn_weights)
+        ffn_out = ffn_down([acts[c][b] for c in range(CHUNKS)], ffn_weights, after)
+        after = ffn_out
         total = hidden_res[b] + seq_scatter(ffn_out.reshape(seqs, rows, model))
         output.append((live[b] * total).astype(BF16))
+
+    while len(ffn_sums) < CHUNKS:
+        sum_next()
 
     grad_tokens = []
     grad_attn_gain = 0.0
@@ -617,60 +719,53 @@
         grad_tokens.append((res_cot[b] + pull).astype(BF16))
 
     out_grads = sum(dot(attended[b], res_full[b], TN) for b in range(slots)).astype(BF16)
+    out_grads = follow(out_grads, ffn_sums[-1:])
     out_sums = lax.psum_scatter(out_grads, "fsdp", scatter_dimension=0, tiled=True)
-    out_parts = []
-    for j in range(seqs):
-        moves = [
-            (s * shards + h * seqs + j, s * shards + s * per + h)
-            for s in range(seqs)
-            for h in range(per)
-        ]
-        out_parts.append(lax.ppermute(out_sums, ("seq", "fsdp"), moves))
-    grad_out = lax.psum(jnp.concatenate(out_parts, axis=0), "seq").astype(F32)
-
-    qkv_grads = sum(dot(normal_full[b], dqkv[b], TN) for b in range(slots)).astype(BF16)
+    grad_out = out_home(out_sums).astype(F32)
+
+    head_sums = jnp.pad(
+        (head_gain[:, :HEAD] + head_gain[:, HEAD:]).reshape(2, shards, 1, HEAD // shards),
+        ((0, 0), (0, 0), (0, 0), (0, model // shards - HEAD // shards)),
+    ).reshape(2, model)
+    gain_columns = jnp.stack(
+        [grad_attn_gain, grad_ffn_gain, head_sums[0], head_sums[1]], axis=1
+    ).astype(BF16)
+    qkv_grads = jnp.concatenate(
+        [
+            sum(dot(normal_full[b], dqkv[b], TN) for b in range(slots)).astype(BF16),
+            jnp.pad(gain_columns, ((0, 0), (0, 124))),
+        ],
+        axis=1,
+    )
+    qkv_grads = follow(qkv_grads, [out_sums])
     qkv_sums = lax.psum_scatter(qkv_grads, "fsdp", scatter_dimension=0, tiled=True)
     qkv_all = jnp.moveaxis(seq_spread(qkv_sums), 0, 1).astype(F32)
     held = qkv_all.shape[0]
     edge = hq * HEAD
     kv_edge = edge + hkv_held * HEAD
+    last_edge = kv_edge + hkv_held * HEAD
     grad_query = qkv_all[..., :edge].reshape(held, query_width)
     grad_key = qkv_all[..., edge : edge + hkv * HEAD].reshape(held, kv_width)
     grad_value = qkv_all[..., kv_edge : kv_edge + hkv * HEAD].reshape(held, kv_width)
-
-    spread = [seq_spread(v).reshape(seqs, 3, part, model) for v in ffn_sums]
-    ffn_grad = [
-        jnp.stack([v[:, kind] for v in spread], axis=1).reshape(seqs * hidden_own, model).astype(F32)
-        for kind in range(3)
-    ]
-
-    gain_sums = lax.psum(
-        jnp.concatenate(
-            [
-                grad_attn_gain,
-                grad_ffn_gain,
-                (head_gain[0, :HEAD] + head_gain[0, HEAD:]),
-                (head_gain[1, :HEAD] + head_gain[1, HEAD:]),
-            ]
-        ),
-        ("seq", "fsdp"),
-    )
-
-    def own_gain(start, length):
-        width = length // shards
-        return lax.dynamic_slice_in_dim(gain_sums, start + shard * width, width, 0)
+    gain_sums = jnp.sum(qkv_all[..., last_edge : last_edge + 4], axis=1)
+
+    ffn_grad = ()
+    for c in range(CHUNKS):
+        parts = seq_gather(ffn_sums[c]).reshape(seqs, 3, part, model)
+        ffn_grad = place_parts(order, parts, c, ffn_grad)
+    ffn_grad = [v.reshape(seqs * hidden_own, model) for v in ffn_grad]
 
     return (
         jnp.stack(output),
         jnp.stack(grad_tokens),
-        own_gain(0, model),
+        gain_sums[:, 0],
         grad_query,
         grad_key,
         grad_value,
-        own_gain(2 * model, HEAD),
-        own_gain(2 * model + HEAD, HEAD),
+        gain_sums[: HEAD // shards, 2],
+        gain_sums[: HEAD // shards, 3],
         grad_out,
-        own_gain(model, model),
+        gain_sums[:, 1],
         ffn_grad[0],
         ffn_grad[1],
         ffn_grad[2],

time: 1380 us -> 1200 us (0.87)
  waiting for transfers between devices: 656 us -> 362 us
  local copies, waits for them, and re-layouts: 51 us -> 113 us
  Pallas kernels: 362 us -> 416 us
  blocking collectives: 53.5 us -> 0 us
  other arithmetic: 77.8 us -> 104 us
  starting transfers between devices: 98.5 us -> 120 us
    ppermute x8, waiting for transfers between devices: 138 us -> 28.8 us  [seq_scatter(): lax.ppermute(jnp.concatenate([parts[3, half:], parts[2, half:]], axis=0),...]
    all_gather x2 -> x4, waiting for transfers between devices: 76.6 us -> 0.02 us  [on_device(): ffn_weights.append(lax.all_gather(mine, 'fsdp', axis=0))]
    ppermute x11 -> x13, waiting for transfers between devices: 132 us -> 64.8 us  [seq_gather(): top = lax.ppermute(two[:half], 'seq', over_one)]
    psum x1 -> x0, blocking collectives: 53.5 us -> none  [on_device(): lax.psum(jnp.concatenate([grad_attn_gain, grad_ffn_gain, head_gain[0, :HE...]
    reduce_scatter x2 -> x4, waiting for transfers between devices: 51.1 us -> 0.01 us  [sum_next(): ffn_sums.append(lax.psum_scatter(sent, 'fsdp', scatter_dimension=0))]
    ppermute x8, waiting for transfers between devices: 67.2 us -> 18 us  [seq_scatter(): top_last = lax.ppermute(top_on, 'seq', over_two)]
    ppermute x11 -> x13, waiting for transfers between devices: 9.67 us -> 42.5 us  [seq_gather(): low = lax.ppermute(one[half:], 'seq', over_two)]
    ppermute x8, waiting for transfers between devices: 12.5 us -> 43.4 us  [seq_scatter(): lax.ppermute(jnp.concatenate([parts[3, :half], parts[1, :half]], axis=0),...]
  transfers between devices with their start and end apart: 93 -> 108, of which waited for: 61 -> 50; matrix products, arithmetic and copies ran while one was open for 9% -> 19% of each run, Pallas kernels for 15% -> 35%
where the time goes in v2:
time: 1200 us; the launch traced here: 1190 us
  Pallas kernels  416 us (35%)
  waiting for transfers between devices  362 us (30%)
  starting transfers between devices  120 us (10%)
  local copies, waits for them, and re-layouts  113 us (9%)
  other arithmetic  104 us (9%)
  matrix products  59.3 us (5%)
  between operations  16.8 us (1%)
    pallas_call x8, Pallas kernels, ffn_both(): pl.pallas_call(functools.partial(ffn_kernel, summed is not None), grid=(t...  145 us
    ppermute x13, waiting for transfers between devices, seq_gather(): two = lax.ppermute(rows, 'seq', over_two)  124 us
    pallas_call x4, Pallas kernels, ffn_grads(): pl.pallas_call(functools.partial(ffn_grad_kernel, slots), grid=(3, hidden...  86.8 us
    pallas_call x2, Pallas kernels, attend_back(): pl.pallas_call(functools.partial(attend_back_kernel, sizes), out_shape=(j...  82.2 us
    ppermute x13, waiting for transfers between devices, seq_gather(): top = lax.ppermute(two[:half], 'seq', over_one)  64.8 us
    dot_general x12, matrix products, dot(): return lax.dot_general(a, b, dims, preferred_element_type=F32)  59.3 us
    unnamed x324, local copies, waits for them, and re-layouts  54.3 us
    pallas_call x2, Pallas kernels, attend(): pl.pallas_call(functools.partial(attend_kernel, sizes), out_shape=(jax.Sh...  52.9 us
  transfers between devices with their start and end apart: 108, of which 50 were waited for; matrix products, arithmetic and copies ran while one was open for 19% of the time, Pallas kernels for 35%

profile of v2, /device:TPU:6, one launch (start us, length us, event | category | flops | bytes accessed | tf_op | source)
XLA Modules:
  0.0 1190.1 jit_solution(12922936452179637101)
XLA Ops:
  16.6 24.3 %collective-permute-done.1 = bf16[256,2048]{1,0:T(8,128)(2,1)S(1)} collective-permute-done((bf16[256,2048]{1,0:T(8,128)(2,1)S(1)}, bf16[256,2048]{1,0:T(8,128)(2,1)S(1)}, u32[]{:S(2)}, u32[]{:S(2)}) %collective-permute-start.1) | collective-permute-done | bytes 1048608 | tf_op jit(solution)/shard_map/ppermute | solution.py:443
  43.0 10.9 collective-permute-done.2
  57.8 17.6 %collective-permute-done.4 = bf16[64,2048]{1,0:T(8,128)(2,1)S(1)} collective-permute-done((bf16[64,2048]{1,0:T(8,128)(2,1)S(1)}, bf16[64,2048]{1,0:T(8,128)(2,1)S(1)}, u32[]{:S(2)}, u32[]{:S(2)}) %collective-permute-start.4) | collective-permute-done | bytes 262176 | tf_op jit(solution)/shard_map/ppermute | solution.py:606
  88.1 17.7 %collective-permute-done.21 = bf16[256,2048]{1,0:T(8,128)(2,1)S(1)} collective-permute-done((bf16[256,2048]{1,0:T(8,128)(2,1)}, bf16[256,2048]{1,0:T(8,128)(2,1)S(1)}, u32[]{:S(2)}, u32[]{:S(2)}) %collective-permute-start.21) | collective-permute-done | bytes 1048608 | tf_op jit(solution)/shard_map/ppermute | solution.py:443
  111.1 7.0 collective-permute-done.22
  120.3 7.8 convolution_convert_fusion.5
  128.1 26.6 %attend.2 = (bf16[4,256,512]{2,1,0:T(8,128)(2,1)}, f32[8,1024,1]{2,1,0:T(8,128)}) custom-call(s32[1]{0:T(128)} %bitcast.1.place_ref.after_ref, s32[1]{0:T(128)} %get-tuple-element.225.len_ref, bf16[4,256,768]{2,1,0:T(8,128)(2,1)} %bitcast.453, f32[1,128]{1,0:T(1,128)} %get-tuple-element.229.qg_ref, f32[1,128]{1,0:T(1,128)} %get-tuple-element.230.kg_ref, ...), custom_call_target="tpu_custom_call" | custom-call | flops 30064771072 | bytes 8388608 | tf_op jit(solution)/shard_map/attend/pallas_call | solution.py:196
  154.7 4.3 convolution_convert_fusion.1
  164.9 6.8 convolution_convert_fusion.4
  171.7 26.3 %attend.3 = (bf16[4,256,512]{2,1,0:T(8,128)(2,1)}, f32[8,1024,1]{2,1,0:T(8,128)}) custom-call(s32[1]{0:T(128)} %bitcast.1.place_ref.after_ref, s32[1]{0:T(128)} %get-tuple-element.226.len_ref, bf16[4,256,768]{2,1,0:T(8,128)(2,1)} %bitcast.451, f32[1,128]{1,0:T(1,128)} %get-tuple-element.229.qg_ref, f32[1,128]{1,0:T(1,128)} %get-tuple-element.230.kg_ref, ...), custom_call_target="tpu_custom_call" | custom-call | flops 30064771072 | bytes 8388608 | tf_op jit(solution)/shard_map/attend/pallas_call | solution.py:196
  214.4 17.3 %collective-permute-done.25 = bf16[256,2048]{1,0:T(8,128)(2,1)} collective-permute-done((bf16[256,2048]{1,0:T(8,128)(2,1)}, bf16[256,2048]{1,0:T(8,128)(2,1)}, u32[]{:S(2)}, u32[]{:S(2)}) %collective-permute-start.25) | collective-permute-done | bytes 1048608 | tf_op jit(solution)/shard_map/ppermute | solution.py:460
  237.2 16.9 %collective-permute-done.17 = bf16[256,2048]{1,0:T(8,128)(2,1)S(1)} collective-permute-done((bf16[256,2048]{1,0:T(8,128)(2,1)}, bf16[256,2048]{1,0:T(8,128)(2,1)S(1)}, u32[]{:S(2)}, u32[]{:S(2)}) %collective-permute-start.17) | collective-permute-done | bytes 1048608 | tf_op jit(solution)/shard_map/ppermute | solution.py:443
  257.2 19.4 %collective-permute-done.33 = bf16[256,2048]{1,0:T(8,128)(2,1)S(1)} collective-permute-done((bf16[256,2048]{1,0:T(8,128)(2,1)}, bf16[256,2048]{1,0:T(8,128)(2,1)S(1)}, u32[]{:S(2)}, u32[]{:S(2)}) %collective-permute-start.33) | collective-permute-done | bytes 1048608 | tf_op jit(solution)/shard_map/ppermute | solution.py:443
  290.4 8.6 collective-permute-done.26
  314.9 8.1 collective-permute-done.34
  327.1 35.5 %collective-permute-done.35 = bf16[128,2048]{1,0:T(8,128)(2,1)S(1)} collective-permute-done((bf16[128,2048]{1,0:T(8,128)(2,1)S(1)}, bf16[128,2048]{1,0:T(8,128)(2,1)S(1)}, u32[]{:S(2)}, u32[]{:S(2)}) %collective-permute-start.35) | collective-permute-done | bytes 524320 | tf_op jit(solution)/shard_map/ppermute | solution.py:445
  370.9 7.5 collective-permute-done.14
  379.2 7.4 collective-permute-done.30
  388.3 17.6 %ffn_both.8 = (bf16[3,1024,512]{2,1,0:T(8,128)(2,1)}, f32[1024,2048]{1,0:T(8,128)}) custom-call(bf16[1024,2048]{1,0:T(8,128)(2,1)} %copy-done.92, bf16[1024,2048]{1,0:T(8,128)(2,1)} %constant_dynamic-update-slice_fusion.10.cot_ref.refs_4_, bf16[8,3,64,2048]{3,2,1,0:T(8,128)(2,1)} %bitcast.419, bf16[8,3,64,2048]{3,2,1,0:T(8,128)(2,1)} %bitcast.420, ...), custom_call_target="tpu_custom_call" | custom-call | flops 17179869184 | bytes 14680064 | tf_op jit(solution)/shard_map/ffn_both/pallas_call | solution.py:289
  405.9 18.3 %ffn_both.9 = (bf16[3,1024,512]{2,1,0:T(8,128)(2,1)}, f32[1024,2048]{1,0:T(8,128)}) custom-call(bf16[1024,2048]{1,0:T(8,128)(2,1)} %copy-done.92, bf16[1024,2048]{1,0:T(8,128)(2,1)} %constant_dynamic-update-slice_fusion.10.cot_ref.refs_4_, bf16[8,3,64,2048]{3,2,1,0:T(8,128)(2,1)} %bitcast.427, bf16[8,3,64,2048]{3,2,1,0:T(8,128)(2,1)} %bitcast.428, ...), custom_call_target="tpu_custom_call" | custom-call | flops 17179869184 | bytes 14680064 | tf_op jit(solution)/shard_map/ffn_both/pallas_call | solution.py:289
  424.2 17.6 %ffn_both.10 = (bf16[3,1024,512]{2,1,0:T(8,128)(2,1)}, f32[1024,2048]{1,0:T(8,128)}) custom-call(bf16[1024,2048]{1,0:T(8,128)(2,1)} %constant_dynamic-update-slice_fusion.20.mid_ref.refs_3_, bf16[1024,2048]{1,0:T(8,128)(2,1)} %constant_dynamic-update-slice_fusion.25.cot_ref.refs_5_, bf16[8,3,64,2048]{3,2,1,0:T(8,128)(2,1)} %bitcast.422, ...), custom_call_target="tpu_custom_call" | custom-call | flops 17179869184 | bytes 14680064 | tf_op jit(solution)/shard_map/ffn_both/pallas_call | solution.py:289
  441.8 18.7 %ffn_both.11 = (bf16[3,1024,512]{2,1,0:T(8,128)(2,1)}, f32[1024,2048]{1,0:T(8,128)}) custom-call(bf16[1024,2048]{1,0:T(8,128)(2,1)} %constant_dynamic-update-slice_fusion.20.mid_ref.refs_3_, bf16[1024,2048]{1,0:T(8,128)(2,1)} %constant_dynamic-update-slice_fusion.25.cot_ref.refs_5_, bf16[8,3,64,2048]{3,2,1,0:T(8,128)(2,1)} %bitcast.430, ...), custom_call_target="tpu_custom_call" | custom-call | flops 17179869184 | bytes 14680064 | tf_op jit(solution)/shard_map/ffn_both/pallas_call | solution.py:289
  460.5 21.6 %ffn_grads.4.refs_1_ = bf16[8,3,64,2048]{3,2,1,0:T(8,128)(2,1)} custom-call(bf16[3,1024,512]{2,1,0:T(8,128)(2,1)} %get-tuple-element.58.refs_1_.refs_0_, bf16[3,1024,512]{2,1,0:T(8,128)(2,1)} %get-tuple-element.62.refs_1_.refs_0_, bf16[1024,2048]{1,0:T(8,128)(2,1)} %copy-done.92, bf16[1024,2048]{1,0:T(8,128)(2,1)} %constant_dynamic-update-slice_fusion.20.mid_ref.refs_3_, ...), custom_call_target="tpu_custom_call" | custom-call | flops 19327352832 | bytes 16777216 | tf_op jit(solution)/shard_map/ffn_grads/pallas_call | solution.py:342
  482.2 18.4 %ffn_both.12 = (bf16[3,1024,512]{2,1,0:T(8,128)(2,1)}, f32[1024,2048]{1,0:T(8,128)}) custom-call(bf16[1024,2048]{1,0:T(8,128)(2,1)} %copy-done.92, bf16[1024,2048]{1,0:T(8,128)(2,1)} %constant_dynamic-update-slice_fusion.10.cot_ref.refs_4_, bf16[8,3,64,2048]{3,2,1,0:T(8,128)(2,1)} %bitcast.435, bf16[8,3,64,2048]{3,2,1,0:T(8,128)(2,1)} %bitcast.436, ...), custom_call_target="tpu_custom_call" | custom-call | flops 17179869184 | bytes 14680064 | tf_op jit(solution)/shard_map/ffn_both/pallas_call | solution.py:289
  500.5 18.5 %ffn_both.13 = (bf16[3,1024,512]{2,1,0:T(8,128)(2,1)}, f32[1024,2048]{1,0:T(8,128)}) custom-call(bf16[1024,2048]{1,0:T(8,128)(2,1)} %constant_dynamic-update-slice_fusion.20.mid_ref.refs_3_, bf16[1024,2048]{1,0:T(8,128)(2,1)} %constant_dynamic-update-slice_fusion.25.cot_ref.refs_5_, bf16[8,3,64,2048]{3,2,1,0:T(8,128)(2,1)} %bitcast.438, ...), custom_call_target="tpu_custom_call" | custom-call | flops 17179869184 | bytes 14680064 | tf_op jit(solution)/shard_map/ffn_both/pallas_call | solution.py:289
  519.0 18.0 %ffn_both.14 = (bf16[3,1024,512]{2,1,0:T(8,128)(2,1)}, bf16[1024,2048]{1,0:T(8,128)(2,1)}) custom-call(bf16[1024,2048]{1,0:T(8,128)(2,1)} %copy-done.92, bf16[1024,2048]{1,0:T(8,128)(2,1)} %constant_dynamic-update-slice_fusion.10.cot_ref.refs_4_, bf16[8,3,64,2048]{3,2,1,0:T(8,128)(2,1)} %bitcast.443, bf16[8,3,64,2048]{3,2,1,0:T(8,128)(2,1)} %bitcast.444, ...), custom_call_target="tpu_custom_call" | custom-call | flops 17179869184 | bytes 14680064 | tf_op jit(solution)/shard_map/ffn_both/pallas_call | solution.py:289
  541.5 18.1 %ffn_both.15 = (bf16[3,1024,512]{2,1,0:T(8,128)(2,1)}, bf16[1024,2048]{1,0:T(8,128)(2,1)}) custom-call(bf16[1024,2048]{1,0:T(8,128)(2,1)} %constant_dynamic-update-slice_fusion.20.mid_ref.refs_3_, bf16[1024,2048]{1,0:T(8,128)(2,1)} %constant_dynamic-update-slice_fusion.25.cot_ref.refs_5_, bf16[8,3,64,2048]{3,2,1,0:T(8,128)(2,1)} %bitcast.446, ...), custom_call_target="tpu_custom_call" | custom-call | flops 17179869184 | bytes 14680064 | tf_op jit(solution)/shard_map/ffn_both/pallas_call | solution.py:289
  565.1 21.7 %ffn_grads.5.refs_6_ = bf16[8,3,64,2048]{3,2,1,0:T(8,128)(2,1)} custom-call(bf16[3,1024,512]{2,1,0:T(8,128)(2,1)} %get-tuple-element.60.refs_0_.refs_1_, bf16[3,1024,512]{2,1,0:T(8,128)(2,1)} %get-tuple-element.64.refs_6_.refs_1_, bf16[1024,2048]{1,0:T(8,128)(2,1)} %copy-done.92, bf16[1024,2048]{1,0:T(8,128)(2,1)} %constant_dynamic-update-slice_fusion.20.mid_ref.refs_3_, ...), custom_call_target="tpu_custom_call" | custom-call | flops 19327352832 | bytes 16777216 | tf_op jit(solution)/shard_map/ffn_grads/pallas_call | solution.py:342
  605.5 4.9 collective-permute-done.38
  612.0 4.7 multiply_reduce_fusion.1
  620.2 21.7 %ffn_grads.6.refs_6_ = bf16[8,3,64,2048]{3,2,1,0:T(8,128)(2,1)} custom-call(bf16[3,1024,512]{2,1,0:T(8,128)(2,1)} %get-tuple-element.65.refs_1_.refs_0_.refs_2_, bf16[3,1024,512]{2,1,0:T(8,128)(2,1)} %get-tuple-element.68.refs_1_.refs_2_, bf16[1024,2048]{1,0:T(8,128)(2,1)} %copy-done.92, ...), custom_call_target="tpu_custom_call" | custom-call | flops 19327352832 | bytes 16777216 | tf_op jit(solution)/shard_map/ffn_grads/pallas_call | solution.py:342
  644.8 21.8 %ffn_grads.7.after_ref = bf16[8,3,64,2048]{3,2,1,0:T(8,128)(2,1)} custom-call(bf16[3,1024,512]{2,1,0:T(8,128)(2,1)} %get-tuple-element.69.refs_1_.refs_0_.refs_3_, bf16[3,1024,512]{2,1,0:T(8,128)(2,1)} %get-tuple-element.75.refs_6_.refs_1_.refs_3_, bf16[1024,2048]{1,0:T(8,128)(2,1)} %copy-done.92, ...), custom_call_target="tpu_custom_call" | custom-call | flops 19327352832 | bytes 16777216 | tf_op jit(solution)/shard_map/ffn_grads/pallas_call | solution.py:342
  678.3 5.5 convolution_convert_fusion.6
  683.8 41.2 %attend_back.2 = (bf16[4,256,768]{2,1,0:T(8,128)(2,1)}, f32[2,128]{1,0:T(2,128)}) custom-call(s32[1]{0:T(128)} %bitcast.1.place_ref.after_ref, s32[1]{0:T(128)} %get-tuple-element.225.len_ref, bf16[4,256,768]{2,1,0:T(8,128)(2,1)} %bitcast.454, bf16[4,256,512]{2,1,0:T(8,128)(2,1)} %bitcast.460, f32[8,1024,1]{2,1,0:T(8,128)} %get-tuple-element.74.lse_ref, ...), custom_call_target="tpu_custom_call" | custom-call | flops 47244640256 | bytes 8388608 | tf_op jit(solution)/shard_map/attend_back/pallas_call | solution.py:222
  725.6 4.4 constant_dynamic-update-slice_fusion.34
  732.3 19.9 %collective-permute-done.41 = bf16[256,2048]{1,0:T(8,128)(2,1)S(1)} collective-permute-done((bf16[256,2048]{1,0:T(8,128)(2,1)}, bf16[256,2048]{1,0:T(8,128)(2,1)S(1)}, u32[]{:S(2)}, u32[]{:S(2)}) %collective-permute-start.41) | collective-permute-done | bytes 1048608 | tf_op jit(solution)/shard_map/ppermute | solution.py:443
  764.5 5.6 convolution_convert_fusion.7
  770.1 41.0 %attend_back.3 = (bf16[4,256,768]{2,1,0:T(8,128)(2,1)}, f32[2,128]{1,0:T(2,128)}) custom-call(s32[1]{0:T(128)} %bitcast.1.place_ref.after_ref, s32[1]{0:T(128)} %get-tuple-element.226.len_ref, bf16[4,256,768]{2,1,0:T(8,128)(2,1)} %bitcast.452, bf16[4,256,512]{2,1,0:T(8,128)(2,1)} %bitcast.459, f32[8,1024,1]{2,1,0:T(8,128)} %get-tuple-element.72.lse_ref, ...), custom_call_target="tpu_custom_call" | custom-call | flops 47244640256 | bytes 8388608 | tf_op jit(solution)/shard_map/attend_back/pallas_call | solution.py:222
  811.2 14.5 %ffn_down.2.refs_8_ = bf16[1024,2048]{1,0:T(8,128)(2,1)} custom-call(bf16[3,1024,512]{2,1,0:T(8,128)(2,1)} %get-tuple-element.58.refs_1_.refs_0_, bf16[3,1024,512]{2,1,0:T(8,128)(2,1)} %get-tuple-element.60.refs_0_.refs_1_, bf16[3,1024,512]{2,1,0:T(8,128)(2,1)} %get-tuple-element.65.refs_1_.refs_0_.refs_2_, ...), custom_call_target="tpu_custom_call" | custom-call | flops 17179869184 | bytes 12582912 | tf_op jit(solution)/shard_map/ffn_down/pallas_call | solution.py:383
  848.4 14.5 %ffn_down.3 = bf16[1024,2048]{1,0:T(8,128)(2,1)} custom-call(bf16[3,1024,512]{2,1,0:T(8,128)(2,1)} %get-tuple-element.62.refs_1_.refs_0_, bf16[3,1024,512]{2,1,0:T(8,128)(2,1)} %get-tuple-element.64.refs_6_.refs_1_, bf16[3,1024,512]{2,1,0:T(8,128)(2,1)} %get-tuple-element.68.refs_1_.refs_2_, bf16[3,1024,512]{2,1,0:T(8,128)(2,1)} %get-tuple-element.75.refs_6_.refs_1_.refs_3_, ...), custom_call_target="tpu_custom_call" | custom-call | flops 17179869184 | bytes 12582912 | tf_op jit(solution)/shard_map/ffn_down/pallas_call | solution.py:383
  872.5 6.4 fusion.57
  879.0 5.2 add_convert_fusion
  888.8 11.5 collective-permute-done.65
  903.8 6.6 collective-permute-done.64
  914.5 18.4 %collective-permute-done.52 = bf16[256,2048]{1,0:T(8,128)(2,1)S(1)} collective-permute-done((bf16[256,2048]{1,0:T(8,128)(2,1)S(1)}, bf16[256,2048]{1,0:T(8,128)(2,1)S(1)}, u32[]{:S(2)}, u32[]{:S(2)}) %collective-permute-start.52) | collective-permute-done | bytes 1048608 | tf_op jit(solution)/shard_map/ppermute | solution.py:457
  937.1 18.4 %collective-permute-done.56 = bf16[256,2048]{1,0:T(8,128)(2,1)} collective-permute-done((bf16[256,2048]{1,0:T(8,128)(2,1)}, bf16[256,2048]{1,0:T(8,128)(2,1)}, u32[]{:S(2)}, u32[]{:S(2)}) %collective-permute-start.56) | collective-permute-done | bytes 1048608 | tf_op jit(solution)/shard_map/ppermute | solution.py:457
  971.1 5.5 collective-permute-done.67
  976.6 4.7 fusion.23
  981.7 7.1 fusion.4
  989.0 7.2 fusion.1
  998.3 4.7 fusion.9
  1013.7 11.1 collective-permute-done.93
  1029.3 7.7 collective-permute-done.94
  1039.5 5.0 place_parts.4
  1044.6 6.6 collective-permute-done.89
  1061.4 5.0 place_parts.5
  1073.0 5.6 collective-permute-start.81
  1086.2 5.0 place_parts.6
  1092.4 4.8 collective-permute-done.81
  1097.3 4.8 collective-permute-done.80
  1103.1 10.0 collective-permute-start.83
  1120.7 5.0 place_parts.7
  1125.7 17.6 %collective-permute-start.69 = (bf16[256,896]{0,1:T(8,128)(2,1)}, bf16[256,896]{0,1:T(8,128)(2,1)S(1)}, u32[]{:S(2)}, u32[]{:S(2)}) collective-permute-start(bf16[256,896]{0,1:T(8,128)(2,1)} %reduce-scatter.17.cloned.1.call-done), channel_id=1, source_target_pairs={{0,16},{8,24},{16,0},{24,8},{1,17},{9,25},{17,1},{25,9},{2,18},{10... | collective-permute-start | bytes 1376264 | tf_op jit(solution)/shard_map/ppermute | solution.py:443
  1167.4 4.3 convert_bitcast_fusion
  (675 shorter events, 327.0 us)
Async XLA Ops:
  7.2 113.1 %all-gather.11.cloned.1.call-start = ((), (), s32[]{:S(2)}) async-start(), calls=%async_computation.6 | async-start | bytes 3538944 | tf_op jit(solution)/shard_map/all_gather | solution.py:594
  10.1 144.6 %all-gather.13.cloned.1.call-start = ((), (), s32[]{:S(2)}) async-start(), calls=%async_computation.7 | async-start | bytes 2359296 | tf_op jit(solution)/shard_map/all_gather | solution.py:608
  16.0 24.9 %collective-permute-start.1 = (bf16[256,2048]{1,0:T(8,128)(2,1)S(1)}, bf16[256,2048]{1,0:T(8,128)(2,1)S(1)}, u32[]{:S(2)}, u32[]{:S(2)}) collective-permute-start(bf16[256,2048]{1,0:T(8,128)(2,1)S(1)} %get-tuple-element.124), channel_id=1, source_target_pairs={{0,16},{8,24},{16,0},{24,8},{1,17},{9,25},{17,1},{25,9},{2,18},{10... | collective-permute-start | bytes 3145736 | tf_op jit(solution)/shard_map/ppermute | solution.py:443
  16.5 25.0 %collective-permute-start = (bf16[256,2048]{1,0:T(8,128)(2,1)S(1)}, bf16[256,2048]{1,0:T(8,128)(2,1)S(1)}, u32[]{:S(2)}, u32[]{:S(2)}) collective-permute-start(bf16[256,2048]{1,0:T(8,128)(2,1)S(1)} %get-tuple-element.124), channel_id=1, source_target_pairs={{0,8},{8,0},{16,24},{24,16},{1,9},{9,1},{17,25},{25,17},{2,10},{10... | collective-permute-start | bytes 3145736 | tf_op jit(solution)/shard_map/ppermute | solution.py:442
  76.2 312.1 %all-gather.15.cloned.1.call-start = ((), (), s32[]{:S(2)}) async-start(), calls=%async_computation.14 | async-start | bytes 7077888 | tf_op jit(solution)/shard_map/all_gather | solution.py:620
  81.1 324.8 %all-gather.17.cloned.1.call-start = ((), (), s32[]{:S(2)}) async-start(), calls=%async_computation.15 | async-start | bytes 7077888 | tf_op jit(solution)/shard_map/all_gather | solution.py:620
  82.2 399.9 %all-gather.19.cloned.1.call-start = ((), (), s32[]{:S(2)}) async-start(), calls=%async_computation.16 | async-start | bytes 7077888 | tf_op jit(solution)/shard_map/all_gather | solution.py:620
  82.3 24.7 %collective-permute-start.20 = (bf16[256,2048]{1,0:T(8,128)(2,1)}, bf16[256,2048]{1,0:T(8,128)(2,1)S(1)}, u32[]{:S(2)}, u32[]{:S(2)}) collective-permute-start(bf16[256,2048]{1,0:T(8,128)(2,1)} %get-tuple-element.130), channel_id=1, source_target_pairs={{0,8},{8,0},{16,24},{24,16},{1,9},{9,1},{17,25},{25,17},{2,10},{10... | collective-permute-start | bytes 3145736 | tf_op jit(solution)/shard_map/ppermute | solution.py:442
  83.4 435.6 %all-gather.21.cloned.1.call-start = ((), (), s32[]{:S(2)}) async-start(), calls=%async_computation.17 | async-start | bytes 7077888 | tf_op jit(solution)/shard_map/all_gather | solution.py:620
  161.1 50.0 %collective-permute-start.9 = (bf16[256,2048]{1,0:T(8,128)(2,1)S(1)}, bf16[256,2048]{1,0:T(8,128)(2,1)S(1)}, u32[]{:S(2)}, u32[]{:S(2)}) collective-permute-start(bf16[256,2048]{1,0:T(8,128)(2,1)S(1)} %pad_maximum_fusion.4), channel_id=1, source_target_pairs={{0,16},{8,24},{16,0},{24,8},{1,17},{9,25},{17,1},{25,9},{2,18},{10... | collective-permute-start | bytes 3145736 | tf_op jit(solution)/shard_map/ppermute | solution.py:460
  163.2 49.6 %collective-permute-start.8 = (bf16[256,2048]{1,0:T(8,128)(2,1)S(1)}, bf16[256,2048]{1,0:T(8,128)(2,1)}, u32[]{:S(2)}, u32[]{:S(2)}) collective-permute-start(bf16[256,2048]{1,0:T(8,128)(2,1)S(1)} %pad_maximum_fusion.3), channel_id=1, source_target_pairs={{0,8},{8,0},{16,24},{24,16},{1,9},{9,1},{17,25},{25,17},{2,10},{10... | collective-permute-start | bytes 3145736 | tf_op jit(solution)/shard_map/ppermute | solution.py:457
  205.3 26.4 %collective-permute-start.25 = (bf16[256,2048]{1,0:T(8,128)(2,1)}, bf16[256,2048]{1,0:T(8,128)(2,1)}, u32[]{:S(2)}, u32[]{:S(2)}) collective-permute-start(bf16[256,2048]{1,0:T(8,128)(2,1)} %pad_maximum_fusion.8), channel_id=1, source_target_pairs={{0,16},{8,24},{16,0},{24,8},{1,17},{9,25},{17,1},{25,9},{2,18},{10... | collective-permute-start | bytes 3145736 | tf_op jit(solution)/shard_map/ppermute | solution.py:460
  206.8 27.3 %collective-permute-start.24 = (bf16[256,2048]{1,0:T(8,128)(2,1)}, bf16[256,2048]{1,0:T(8,128)(2,1)}, u32[]{:S(2)}, u32[]{:S(2)}) collective-permute-start(bf16[256,2048]{1,0:T(8,128)(2,1)} %pad_maximum_fusion.7), channel_id=1, source_target_pairs={{0,8},{8,0},{16,24},{24,16},{1,9},{9,1},{17,25},{25,17},{2,10},{10... | collective-permute-start | bytes 3145736 | tf_op jit(solution)/shard_map/ppermute | solution.py:457
  210.3 43.8 %collective-permute-start.17 = (bf16[256,2048]{1,0:T(8,128)(2,1)}, bf16[256,2048]{1,0:T(8,128)(2,1)S(1)}, u32[]{:S(2)}, u32[]{:S(2)}) collective-permute-start(bf16[256,2048]{1,0:T(8,128)(2,1)} %get-tuple-element.112), channel_id=1, source_target_pairs={{0,16},{8,24},{16,0},{24,8},{1,17},{9,25},{17,1},{25,9},{2,18},{10... | collective-permute-start | bytes 3145736 | tf_op jit(solution)/shard_map/ppermute | solution.py:443
  211.2 44.4 %collective-permute-start.16 = (bf16[256,2048]{1,0:T(8,128)(2,1)}, bf16[256,2048]{1,0:T(8,128)(2,1)S(1)}, u32[]{:S(2)}, u32[]{:S(2)}) collective-permute-start(bf16[256,2048]{1,0:T(8,128)(2,1)} %get-tuple-element.112), channel_id=1, source_target_pairs={{0,8},{8,0},{16,24},{24,16},{1,9},{9,1},{17,25},{25,17},{2,10},{10... | collective-permute-start | bytes 3145736 | tf_op jit(solution)/shard_map/ppermute | solution.py:442
  212.8 63.8 %collective-permute-start.33 = (bf16[256,2048]{1,0:T(8,128)(2,1)}, bf16[256,2048]{1,0:T(8,128)(2,1)S(1)}, u32[]{:S(2)}, u32[]{:S(2)}) collective-permute-start(bf16[256,2048]{1,0:T(8,128)(2,1)} %get-tuple-element.180), channel_id=1, source_target_pairs={{0,16},{8,24},{16,0},{24,8},{1,17},{9,25},{17,1},{25,9},{2,18},{10... | collective-permute-start | bytes 3145736 | tf_op jit(solution)/shard_map/ppermute | solution.py:443
  214.4 372.4 %reduce-scatter.7.cloned.1.call-start = ((), (), s32[]{:S(2)}) async-start(), calls=%async_computation.8 | async-start | bytes 7077888 | tf_op jit(solution)/shard_map/reduce_scatter | solution.py:662
  231.7 47.7 %collective-permute-start.32 = (bf16[256,2048]{1,0:T(8,128)(2,1)}, bf16[256,2048]{1,0:T(8,128)(2,1)S(1)}, u32[]{:S(2)}, u32[]{:S(2)}) collective-permute-start(bf16[256,2048]{1,0:T(8,128)(2,1)} %get-tuple-element.180), channel_id=1, source_target_pairs={{0,8},{8,0},{16,24},{24,16},{1,9},{9,1},{17,25},{25,17},{2,10},{10... | collective-permute-start | bytes 3145736 | tf_op jit(solution)/shard_map/ppermute | solution.py:442
  234.1 53.7 %collective-permute-start.10 = (bf16[128,2048]{1,0:T(8,128)(2,1)S(1)}, bf16[128,2048]{1,0:T(8,128)(2,1)S(1)}, u32[]{:S(2)}, u32[]{:S(2)}) collective-permute-start(bf16[128,2048]{1,0:T(8,128)(2,1)S(1)} %get-tuple-element.183), channel_id=1, source_target_pairs={{0,16},{8,24},{16,0},{24,8},{1,17},{9,25},{17,1},{25,9},{2,18},{10... | collective-permute-start | bytes 1572872 | tf_op jit(solution)/shard_map/ppermute | solution.py:465
  254.1 35.2 %collective-permute-start.11 = (bf16[128,2048]{1,0:T(8,128)(2,1)S(1)}, bf16[128,2048]{1,0:T(8,128)(2,1)S(1)}, u32[]{:S(2)}, u32[]{:S(2)}) collective-permute-start(bf16[128,2048]{1,0:T(8,128)(2,1)S(1)} %get-tuple-element.184), channel_id=1, source_target_pairs={{0,8},{8,0},{16,24},{24,16},{1,9},{9,1},{17,25},{25,17},{2,10},{10... | collective-permute-start | bytes 1572872 | tf_op jit(solution)/shard_map/ppermute | solution.py:466
  255.5 43.5 %collective-permute-start.26 = (bf16[128,2048]{1,0:T(8,128)(2,1)S(1)}, bf16[128,2048]{1,0:T(8,128)(2,1)S(1)}, u32[]{:S(2)}, u32[]{:S(2)}) collective-permute-start(bf16[128,2048]{1,0:T(8,128)(2,1)S(1)} %get-tuple-element.189), channel_id=1, source_target_pairs={{0,16},{8,24},{16,0},{24,8},{1,17},{9,25},{17,1},{25,9},{2,18},{10... | collective-permute-start | bytes 1572872 | tf_op jit(solution)/shard_map/ppermute | solution.py:465
  276.6 23.9 %collective-permute-start.27 = (bf16[128,2048]{1,0:T(8,128)(2,1)S(1)}, bf16[128,2048]{1,0:T(8,128)(2,1)S(1)}, u32[]{:S(2)}, u32[]{:S(2)}) collective-permute-start(bf16[128,2048]{1,0:T(8,128)(2,1)S(1)} %get-tuple-element.190), channel_id=1, source_target_pairs={{0,8},{8,0},{16,24},{24,16},{1,9},{9,1},{17,25},{25,17},{2,10},{10... | collective-permute-start | bytes 1572872 | tf_op jit(solution)/shard_map/ppermute | solution.py:466
  279.4 32.3 %collective-permute-start.18 = (bf16[128,2048]{1,0:T(8,128)(2,1)S(1)}, bf16[128,2048]{1,0:T(8,128)(2,1)S(1)}, u32[]{:S(2)}, u32[]{:S(2)}) collective-permute-start(bf16[128,2048]{1,0:T(8,128)(2,1)S(1)} %slice.606), channel_id=1, source_target_pairs={{0,8},{8,0},{16,24},{24,16},{1,9},{9,1},{17,25},{25,17},{2,10},{10... | collective-permute-start | bytes 1572872 | tf_op jit(solution)/shard_map/ppermute | solution.py:444
  287.8 25.1 %collective-permute-start.19 = (bf16[128,2048]{1,0:T(8,128)(2,1)S(1)}, bf16[128,2048]{1,0:T(8,128)(2,1)S(1)}, u32[]{:S(2)}, u32[]{:S(2)}) collective-permute-start(bf16[128,2048]{1,0:T(8,128)(2,1)S(1)} %slice.607), channel_id=1, source_target_pairs={{0,16},{8,24},{16,0},{24,8},{1,17},{9,25},{17,1},{25,9},{2,18},{10... | collective-permute-start | bytes 1572872 | tf_op jit(solution)/shard_map/ppermute | solution.py:445
  289.3 33.7 %collective-permute-start.34 = (bf16[128,2048]{1,0:T(8,128)(2,1)S(1)}, bf16[128,2048]{1,0:T(8,128)(2,1)S(1)}, u32[]{:S(2)}, u32[]{:S(2)}) collective-permute-start(bf16[128,2048]{1,0:T(8,128)(2,1)S(1)} %slice.625), channel_id=1, source_target_pairs={{0,8},{8,0},{16,24},{24,16},{1,9},{9,1},{17,25},{25,17},{2,10},{10... | collective-permute-start | bytes 1572872 | tf_op jit(solution)/shard_map/ppermute | solution.py:444
  306.2 57.3 %collective-permute-start.13 = (bf16[256,2048]{1,0:T(8,128)(2,1)S(1)}, bf16[256,2048]{1,0:T(8,128)(2,1)S(1)}, u32[]{:S(2)}, u32[]{:S(2)}) collective-permute-start(bf16[256,2048]{1,0:T(8,128)(2,1)S(1)} %get-tuple-element.114), channel_id=1, source_target_pairs={{0,16},{8,24},{16,0},{24,8},{1,17},{9,25},{17,1},{25,9},{2,18},{10... | collective-permute-start | bytes 3145736 | tf_op jit(solution)/shard_map/ppermute | solution.py:443
  307.9 56.2 %collective-permute-start.12 = (bf16[256,2048]{1,0:T(8,128)(2,1)S(1)}, bf16[256,2048]{1,0:T(8,128)(2,1)S(1)}, u32[]{:S(2)}, u32[]{:S(2)}) collective-permute-start(bf16[256,2048]{1,0:T(8,128)(2,1)S(1)} %get-tuple-element.114), channel_id=1, source_target_pairs={{0,8},{8,0},{16,24},{24,16},{1,9},{9,1},{17,25},{25,17},{2,10},{10... | collective-permute-start | bytes 3145736 | tf_op jit(solution)/shard_map/ppermute | solution.py:442
  311.7 54.3 %collective-permute-start.28 = (bf16[256,2048]{1,0:T(8,128)(2,1)S(1)}, bf16[256,2048]{1,0:T(8,128)(2,1)S(1)}, u32[]{:S(2)}, u32[]{:S(2)}) collective-permute-start(bf16[256,2048]{1,0:T(8,128)(2,1)S(1)} %get-tuple-element.210), channel_id=1, source_target_pairs={{0,8},{8,0},{16,24},{24,16},{1,9},{9,1},{17,25},{25,17},{2,10},{10... | collective-permute-start | bytes 3145736 | tf_op jit(solution)/shard_map/ppermute | solution.py:442
  312.9 54.5 %collective-permute-start.29 = (bf16[256,2048]{1,0:T(8,128)(2,1)S(1)}, bf16[256,2048]{1,0:T(8,128)(2,1)S(1)}, u32[]{:S(2)}, u32[]{:S(2)}) collective-permute-start(bf16[256,2048]{1,0:T(8,128)(2,1)S(1)} %get-tuple-element.210), channel_id=1, source_target_pairs={{0,16},{8,24},{16,0},{24,8},{1,17},{9,25},{17,1},{25,9},{2,18},{10... | collective-permute-start | bytes 3145736 | tf_op jit(solution)/shard_map/ppermute | solution.py:443
  323.0 39.7 %collective-permute-start.35 = (bf16[128,2048]{1,0:T(8,128)(2,1)S(1)}, bf16[128,2048]{1,0:T(8,128)(2,1)S(1)}, u32[]{:S(2)}, u32[]{:S(2)}) collective-permute-start(bf16[128,2048]{1,0:T(8,128)(2,1)S(1)} %slice.626), channel_id=1, source_target_pairs={{0,16},{8,24},{16,0},{24,8},{1,17},{9,25},{17,1},{25,9},{2,18},{10... | collective-permute-start | bytes 1572872 | tf_op jit(solution)/shard_map/ppermute | solution.py:445
  482.1 242.9 %reduce-scatter.9.cloned.1.call-start = ((), (), s32[]{:S(2)}) async-start(), calls=%async_computation.9 | async-start | bytes 7077888 | tf_op jit(solution)/shard_map/reduce_scatter | solution.py:662
  538.9 47.9 %collective-permute-start.45 = (bf16[256,2048]{1,0:T(8,128)(2,1)S(1)}, bf16[256,2048]{1,0:T(8,128)(2,1)}, u32[]{:S(2)}, u32[]{:S(2)}) collective-permute-start(bf16[256,2048]{1,0:T(8,128)(2,1)S(1)} %pad_maximum_fusion.14), channel_id=1, source_target_pairs={{0,16},{8,24},{16,0},{24,8},{1,17},{9,25},{17,1},{25,9},{2,18},{10... | collective-permute-start | bytes 3145736 | tf_op jit(solution)/shard_map/ppermute | solution.py:460
  540.6 46.3 %collective-permute-start.44 = (bf16[256,2048]{1,0:T(8,128)(2,1)S(1)}, bf16[256,2048]{1,0:T(8,128)(2,1)}, u32[]{:S(2)}, u32[]{:S(2)}) collective-permute-start(bf16[256,2048]{1,0:T(8,128)(2,1)S(1)} %pad_maximum_fusion.13), channel_id=1, source_target_pairs={{0,8},{8,0},{16,24},{24,16},{1,9},{9,1},{17,25},{25,17},{2,10},{10... | collective-permute-start | bytes 3145736 | tf_op jit(solution)/shard_map/ppermute | solution.py:457
  562.3 29.2 %collective-permute-start.37 = (bf16[256,2048]{1,0:T(8,128)(2,1)}, bf16[256,2048]{1,0:T(8,128)(2,1)}, u32[]{:S(2)}, u32[]{:S(2)}) collective-permute-start(bf16[256,2048]{1,0:T(8,128)(2,1)} %pad_maximum_fusion.12), channel_id=1, source_target_pairs={{0,16},{8,24},{16,0},{24,8},{1,17},{9,25},{17,1},{25,9},{2,18},{10... | collective-permute-start | bytes 3145736 | tf_op jit(solution)/shard_map/ppermute | solution.py:460
  565.0 26.5 %collective-permute-start.36 = (bf16[256,2048]{1,0:T(8,128)(2,1)}, bf16[256,2048]{1,0:T(8,128)(2,1)S(1)}, u32[]{:S(2)}, u32[]{:S(2)}) collective-permute-start(bf16[256,2048]{1,0:T(8,128)(2,1)} %pad_maximum_fusion.11), channel_id=1, source_target_pairs={{0,8},{8,0},{16,24},{24,16},{1,9},{9,1},{17,25},{25,17},{2,10},{10... | collective-permute-start | bytes 3145736 | tf_op jit(solution)/shard_map/ppermute | solution.py:457
  586.8 224.3 %reduce-scatter.11.cloned.1.call-start = ((), (), s32[]{:S(2)}) async-start(), calls=%async_computation.10 | async-start | bytes 7077888 | tf_op jit(solution)/shard_map/reduce_scatter | solution.py:662
  641.9 26.2 %collective-permute-start.48 = (bf16[256,2048]{1,0:T(8,128)(2,1)}, bf16[256,2048]{1,0:T(8,128)(2,1)S(1)}, u32[]{:S(2)}, u32[]{:S(2)}) collective-permute-start(bf16[256,2048]{1,0:T(8,128)(2,1)} %get-tuple-element.108), channel_id=1, source_target_pairs={{0,8},{8,0},{16,24},{24,16},{1,9},{9,1},{17,25},{25,17},{2,10},{10... | collective-permute-start | bytes 3145736 | tf_op jit(solution)/shard_map/ppermute | solution.py:442
  644.3 29.5 %collective-permute-start.50 = (bf16[128,2048]{1,0:T(8,128)(2,1)}, bf16[128,2048]{1,0:T(8,128)(2,1)S(1)}, u32[]{:S(2)}, u32[]{:S(2)}) collective-permute-start(bf16[128,2048]{1,0:T(8,128)(2,1)} %slice.649), channel_id=1, source_target_pairs={{0,8},{8,0},{16,24},{24,16},{1,9},{9,1},{17,25},{25,17},{2,10},{10... | collective-permute-start | bytes 1572872 | tf_op jit(solution)/shard_map/ppermute | solution.py:444
  725.0 212.0 %reduce-scatter.13.cloned.1.call-start = ((), (), s32[]{:S(2)}) async-start(), calls=%async_computation.11 | async-start | bytes 7077888 | tf_op jit(solution)/shard_map/reduce_scatter | solution.py:662
  811.2 191.9 %reduce-scatter.15.cloned.1.call-start = ((), (), s32[]{:S(2)}) async-start(), calls=%async_computation.12 | async-start | bytes 2359296 | tf_op jit(solution)/shard_map/reduce_scatter | solution.py:723
  829.0 85.0 %collective-permute-start.53 = (bf16[256,2048]{1,0:T(8,128)(2,1)}, bf16[256,2048]{1,0:T(8,128)(2,1)}, u32[]{:S(2)}, u32[]{:S(2)}) collective-permute-start(bf16[256,2048]{1,0:T(8,128)(2,1)} %pad_maximum_fusion.16), channel_id=1, source_target_pairs={{0,16},{8,24},{16,0},{24,8},{1,17},{9,25},{17,1},{25,9},{2,18},{10... | collective-permute-start | bytes 3145736 | tf_op jit(solution)/shard_map/ppermute | solution.py:460
  836.6 49.9 %collective-permute-start.61 = (bf16[256,2048]{1,0:T(8,128)(2,1)}, bf16[256,2048]{1,0:T(8,128)(2,1)}, u32[]{:S(2)}, u32[]{:S(2)}) collective-permute-start(bf16[256,2048]{1,0:T(8,128)(2,1)} %pad_maximum_fusion.20), channel_id=1, source_target_pairs={{0,16},{8,24},{16,0},{24,8},{1,17},{9,25},{17,1},{25,9},{2,18},{10... | collective-permute-start | bytes 3145736 | tf_op jit(solution)/shard_map/ppermute | solution.py:460
  838.9 49.1 %collective-permute-start.60 = (bf16[256,2048]{1,0:T(8,128)(2,1)}, bf16[256,2048]{1,0:T(8,128)(2,1)}, u32[]{:S(2)}, u32[]{:S(2)}) collective-permute-start(bf16[256,2048]{1,0:T(8,128)(2,1)} %pad_maximum_fusion.19), channel_id=1, source_target_pairs={{0,8},{8,0},{16,24},{24,16},{1,9},{9,1},{17,25},{25,17},{2,10},{10... | collective-permute-start | bytes 3145736 | tf_op jit(solution)/shard_map/ppermute | solution.py:457
  847.2 53.1 %collective-permute-start.65 = (bf16[256,2048]{1,0:T(8,128)(2,1)}, bf16[256,2048]{1,0:T(8,128)(2,1)}, u32[]{:S(2)}, u32[]{:S(2)}) collective-permute-start(bf16[256,2048]{1,0:T(8,128)(2,1)} %pad_maximum_fusion.22), channel_id=1, source_target_pairs={{0,16},{8,24},{16,0},{24,8},{1,17},{9,25},{17,1},{25,9},{2,18},{10... | collective-permute-start | bytes 3145736 | tf_op jit(solution)/shard_map/ppermute | solution.py:460
  884.2 26.2 %collective-permute-start.64 = (bf16[256,2048]{1,0:T(8,128)(2,1)S(1)}, bf16[256,2048]{1,0:T(8,128)(2,1)S(1)}, u32[]{:S(2)}, u32[]{:S(2)}) collective-permute-start(bf16[256,2048]{1,0:T(8,128)(2,1)S(1)} %pad_maximum_fusion.21), channel_id=1, source_target_pairs={{0,8},{8,0},{16,24},{24,16},{1,9},{9,1},{17,25},{25,17},{2,10},{10... | collective-permute-start | bytes 3145736 | tf_op jit(solution)/shard_map/ppermute | solution.py:457
  886.6 46.3 %collective-permute-start.52 = (bf16[256,2048]{1,0:T(8,128)(2,1)S(1)}, bf16[256,2048]{1,0:T(8,128)(2,1)S(1)}, u32[]{:S(2)}, u32[]{:S(2)}) collective-permute-start(bf16[256,2048]{1,0:T(8,128)(2,1)S(1)} %pad_maximum_fusion.15), channel_id=1, source_target_pairs={{0,8},{8,0},{16,24},{24,16},{1,9},{9,1},{17,25},{25,17},{2,10},{10... | collective-permute-start | bytes 3145736 | tf_op jit(solution)/shard_map/ppermute | solution.py:457
  887.9 45.8 %collective-permute-start.57 = (bf16[256,2048]{1,0:T(8,128)(2,1)S(1)}, bf16[256,2048]{1,0:T(8,128)(2,1)S(1)}, u32[]{:S(2)}, u32[]{:S(2)}) collective-permute-start(bf16[256,2048]{1,0:T(8,128)(2,1)S(1)} %pad_maximum_fusion.18), channel_id=1, source_target_pairs={{0,16},{8,24},{16,0},{24,8},{1,17},{9,25},{17,1},{25,9},{2,18},{10... | collective-permute-start | bytes 3145736 | tf_op jit(solution)/shard_map/ppermute | solution.py:460
  900.3 55.1 %collective-permute-start.56 = (bf16[256,2048]{1,0:T(8,128)(2,1)}, bf16[256,2048]{1,0:T(8,128)(2,1)}, u32[]{:S(2)}, u32[]{:S(2)}) collective-permute-start(bf16[256,2048]{1,0:T(8,128)(2,1)} %pad_maximum_fusion.17), channel_id=1, source_target_pairs={{0,8},{8,0},{16,24},{24,16},{1,9},{9,1},{17,25},{25,17},{2,10},{10... | collective-permute-start | bytes 3145736 | tf_op jit(solution)/shard_map/ppermute | solution.py:457
  910.4 57.2 %collective-permute-start.62 = (bf16[128,2048]{1,0:T(8,128)(2,1)}, bf16[128,2048]{1,0:T(8,128)(2,1)S(1)}, u32[]{:S(2)}, u32[]{:S(2)}) collective-permute-start(bf16[128,2048]{1,0:T(8,128)(2,1)} %get-tuple-element.131), channel_id=1, source_target_pairs={{0,16},{8,24},{16,0},{24,8},{1,17},{9,25},{17,1},{25,9},{2,18},{10... | collective-permute-start | bytes 1572872 | tf_op jit(solution)/shard_map/ppermute | solution.py:465
  914.0 54.2 %collective-permute-start.63 = (bf16[128,2048]{1,0:T(8,128)(2,1)}, bf16[128,2048]{1,0:T(8,128)(2,1)S(1)}, u32[]{:S(2)}, u32[]{:S(2)}) collective-permute-start(bf16[128,2048]{1,0:T(8,128)(2,1)} %get-tuple-element.132), channel_id=1, source_target_pairs={{0,8},{8,0},{16,24},{24,16},{1,9},{9,1},{17,25},{25,17},{2,10},{10... | collective-permute-start | bytes 1572872 | tf_op jit(solution)/shard_map/ppermute | solution.py:466
  932.9 36.2 %collective-permute-start.66 = (bf16[128,2048]{1,0:T(8,128)(2,1)}, bf16[128,2048]{1,0:T(8,128)(2,1)S(1)}, u32[]{:S(2)}, u32[]{:S(2)}) collective-permute-start(bf16[128,2048]{1,0:T(8,128)(2,1)} %get-tuple-element.137), channel_id=1, source_target_pairs={{0,16},{8,24},{16,0},{24,8},{1,17},{9,25},{17,1},{25,9},{2,18},{10... | collective-permute-start | bytes 1572872 | tf_op jit(solution)/shard_map/ppermute | solution.py:465
  933.7 42.8 %collective-permute-start.67 = (bf16[128,2048]{1,0:T(8,128)(2,1)}, bf16[128,2048]{1,0:T(8,128)(2,1)S(1)}, u32[]{:S(2)}, u32[]{:S(2)}) collective-permute-start(bf16[128,2048]{1,0:T(8,128)(2,1)} %get-tuple-element.138), channel_id=1, source_target_pairs={{0,8},{8,0},{16,24},{24,16},{1,9},{9,1},{17,25},{25,17},{2,10},{10... | collective-permute-start | bytes 1572872 | tf_op jit(solution)/shard_map/ppermute | solution.py:466
  937.0 188.6 %reduce-scatter.17.cloned.1.call-start = ((), (), s32[]{:S(2)}) async-start(), calls=%async_computation.13 | async-start | bytes 4128768 | tf_op jit(solution)/shard_map/reduce_scatter | solution.py:741
  955.4 42.9 %collective-permute-start.54 = (bf16[128,2048]{1,0:T(8,128)(2,1)}, bf16[128,2048]{1,0:T(8,128)(2,1)}, u32[]{:S(2)}, u32[]{:S(2)}) collective-permute-start(bf16[128,2048]{1,0:T(8,128)(2,1)} %get-tuple-element.143), channel_id=1, source_target_pairs={{0,16},{8,24},{16,0},{24,8},{1,17},{9,25},{17,1},{25,9},{2,18},{10... | collective-permute-start | bytes 1572872 | tf_op jit(solution)/shard_map/ppermute | solution.py:465
  967.6 30.7 %collective-permute-start.55 = (bf16[128,2048]{1,0:T(8,128)(2,1)}, bf16[128,2048]{1,0:T(8,128)(2,1)}, u32[]{:S(2)}, u32[]{:S(2)}) collective-permute-start(bf16[128,2048]{1,0:T(8,128)(2,1)} %get-tuple-element.144), channel_id=1, source_target_pairs={{0,8},{8,0},{16,24},{24,16},{1,9},{9,1},{17,25},{25,17},{2,10},{10... | collective-permute-start | bytes 1572872 | tf_op jit(solution)/shard_map/ppermute | solution.py:466
  968.2 35.0 %collective-permute-start.58 = (bf16[128,2048]{1,0:T(8,128)(2,1)}, bf16[128,2048]{1,0:T(8,128)(2,1)}, u32[]{:S(2)}, u32[]{:S(2)}) collective-permute-start(bf16[128,2048]{1,0:T(8,128)(2,1)} %get-tuple-element.149), channel_id=1, source_target_pairs={{0,16},{8,24},{16,0},{24,8},{1,17},{9,25},{17,1},{25,9},{2,18},{10... | collective-permute-start | bytes 1572872 | tf_op jit(solution)/shard_map/ppermute | solution.py:465
  969.1 34.0 %collective-permute-start.59 = (bf16[128,2048]{1,0:T(8,128)(2,1)}, bf16[128,2048]{1,0:T(8,128)(2,1)}, u32[]{:S(2)}, u32[]{:S(2)}) collective-permute-start(bf16[128,2048]{1,0:T(8,128)(2,1)} %get-tuple-element.150), channel_id=1, source_target_pairs={{0,8},{8,0},{16,24},{24,16},{1,9},{9,1},{17,25},{25,17},{2,10},{10... | collective-permute-start | bytes 1572872 | tf_op jit(solution)/shard_map/ppermute | solution.py:466
  1026.5 24.7 %collective-permute-start.89 = (bf16[192,2048]{1,0:T(8,128)(2,1)S(1)}, bf16[192,2048]{1,0:T(8,128)(2,1)S(1)}, u32[]{:S(2)}, u32[]{:S(2)}) collective-permute-start(bf16[192,2048]{1,0:T(8,128)(2,1)S(1)} %bitcast.409), channel_id=1, source_target_pairs={{0,16},{8,24},{16,0},{24,8},{1,17},{9,25},{17,1},{25,9},{2,18},{10... | collective-permute-start | bytes 2359304 | tf_op jit(solution)/shard_map/ppermute | solution.py:443
  1073.0 24.2 %collective-permute-start.81 = (bf16[192,2048]{1,0:T(8,128)(2,1)}, bf16[192,2048]{1,0:T(8,128)(2,1)S(1)}, u32[]{:S(2)}, u32[]{:S(2)}) collective-permute-start(bf16[192,2048]{1,0:T(8,128)(2,1)} %bitcast.104), channel_id=1, source_target_pairs={{0,16},{8,24},{16,0},{24,8},{1,17},{9,25},{17,1},{25,9},{2,18},{10... | collective-permute-start | bytes 2359304 | tf_op jit(solution)/shard_map/ppermute | solution.py:443
  1082.9 31.4 %collective-permute-start.77 = (bf16[256,2048]{1,0:T(8,128)(2,1)}, bf16[256,2048]{1,0:T(8,128)(2,1)S(1)}, u32[]{:S(2)}, u32[]{:S(2)}) collective-permute-start(bf16[256,2048]{1,0:T(8,128)(2,1)} %constant_dynamic-update-slice_fusion.45), channel_id=1, source_target_pairs={{0,16},{1,17},{10,26},{11,27},{20,4},{21,5},{30,14},{31,15}} | collective-permute-start | bytes 3145736 | tf_op jit(solution)/shard_map/ppermute | solution.py:505
  1083.6 32.8 %collective-permute-start.76 = (bf16[256,2048]{1,0:T(8,128)(2,1)}, bf16[256,2048]{1,0:T(8,128)(2,1)S(1)}, u32[]{:S(2)}, u32[]{:S(2)}) collective-permute-start(bf16[256,2048]{1,0:T(8,128)(2,1)} %constant_dynamic-update-slice_fusion.45), channel_id=1, source_target_pairs={{0,8},{1,9},{10,2},{11,3},{20,28},{21,29},{30,22},{31,23}} | collective-permute-start | bytes 3145736 | tf_op jit(solution)/shard_map/ppermute | solution.py:505
  1115.1 28.1 %collective-permute-start.78 = (bf16[128,2048]{1,0:T(8,128)(2,1)}, bf16[128,2048]{1,0:T(8,128)(2,1)}, u32[]{:S(2)}, u32[]{:S(2)}) collective-permute-start(bf16[128,2048]{1,0:T(8,128)(2,1)} %slice.707), channel_id=1, source_target_pairs={{16,24},{17,25},{26,18},{27,19},{4,12},{5,13},{14,6},{15,7}} | collective-permute-start | bytes 1572872 | tf_op jit(solution)/shard_map/ppermute | solution.py:505
  1117.3 28.5 %collective-permute-start.79 = (bf16[128,2048]{1,0:T(8,128)(2,1)}, bf16[128,2048]{1,0:T(8,128)(2,1)}, u32[]{:S(2)}, u32[]{:S(2)}) collective-permute-start(bf16[128,2048]{1,0:T(8,128)(2,1)} %slice.708), channel_id=1, source_target_pairs={{8,24},{9,25},{2,18},{3,19},{28,12},{29,13},{22,6},{23,7}} | collective-permute-start | bytes 1572872 | tf_op jit(solution)/shard_map/ppermute | solution.py:505
  1125.7 26.8 %collective-permute-start.69 = (bf16[256,896]{0,1:T(8,128)(2,1)}, bf16[256,896]{0,1:T(8,128)(2,1)S(1)}, u32[]{:S(2)}, u32[]{:S(2)}) collective-permute-start(bf16[256,896]{0,1:T(8,128)(2,1)} %reduce-scatter.17.cloned.1.call-done), channel_id=1, source_target_pairs={{0,16},{8,24},{16,0},{24,8},{1,17},{9,25},{17,1},{25,9},{2,18},{10... | collective-permute-start | bytes 1376264 | tf_op jit(solution)/shard_map/ppermute | solution.py:443
  (180 other events, 2033.9 us)
Sparse Core Ops, SparseCore 0:
  10.3 39.4 all-gather.10
  76.4 27.2 all-gather.12
  105.3 64.2 all-gather.14
  171.1 63.3 all-gather.16
  236.0 63.3 all-gather.18
  300.9 63.3 all-gather.20
  482.2 68.0 reduce-scatter.6
  586.9 68.4 reduce-scatter.8
  725.1 67.9 reduce-scatter.10
  811.3 67.9 reduce-scatter.12
  937.1 33.8 reduce-scatter.14
  1003.3 43.1 reduce-scatter.16

commit v3 on v2

--- a/solution.py
+++ b/solution.py
@@ -21,12 +21,225 @@
 VMEM_LIMIT = 58 << 20
 HEAD = 64
 BLOCK = 256
-CHUNKS = 4
+CHUNKS = 2
 ANY = pl.BlockSpec(memory_space=pl.ANY)
 
 
 def dot(a, b, dims=NN):
     return lax.dot_general(a, b, dims, preferred_element_type=F32)
+
+
+def over_one(place):
+    return place + 1 - 2 * (place % 2)
+
+
+def over_two(place):
+    return (place + 2) % 4
+
+
+def send(source, target, device, out_sem, in_sem):
+    return pltpu.make_async_remote_copy(
+        src_ref=source,
+        dst_ref=target,
+        send_sem=out_sem,
+        recv_sem=in_sem,
+        device_id={"seq": device},
+        device_id_type=pl.DeviceIdType.MESH,
+    )
+
+
+def gather_job(source, target, scratch):
+    outs, ins, here = scratch
+    place = lax.axis_index("seq")
+    one, two = over_one(place), over_two(place)
+    half = source.shape[0] // 2
+    own = pltpu.make_async_copy(source, target.at[0], here.at[0])
+    first = send(source, target.at[1], one, outs.at[0], ins.at[0])
+    second = send(source, target.at[2], two, outs.at[1], ins.at[1])
+    top = pl.ds(0, half)
+    low = pl.ds(half, half)
+    third = send(target.at[2, top], target.at[3, top], one, outs.at[2], ins.at[2])
+    fourth = send(target.at[1, low], target.at[3, low], two, outs.at[3], ins.at[3])
+
+    def begin():
+        own.start()
+        first.start()
+        second.start()
+
+    def middle():
+        second.wait_recv()
+        third.start()
+        first.wait_recv()
+        fourth.start()
+
+    def finish():
+        third.wait_recv()
+        fourth.wait_recv()
+        for copy in (first, second, third, fourth):
+            copy.wait_send()
+        own.wait()
+
+    return begin, middle, finish
+
+
+def scatter_job(parts, total, scratch):
+    outs, ins, here, got_one, got_two, kept, own, last, summed = scratch
+    place = lax.axis_index("seq")
+    one, two = over_one(place), over_two(place)
+    half = parts.shape[1] // 2
+    top = pl.ds(0, half)
+    low = pl.ds(half, half)
+    sends = [
+        send(parts.at[3, top], got_one.at[0], one, outs.at[0], ins.at[0]),
+        send(parts.at[3, low], got_two.at[0], two, outs.at[1], ins.at[1]),
+        send(parts.at[1, top], got_one.at[1], one, outs.at[2], ins.at[2]),
+        send(parts.at[2, low], got_two.at[1], two, outs.at[3], ins.at[3]),
+        send(kept.at[0], last.at[0], two, outs.at[4], ins.at[4]),
+        send(kept.at[1], last.at[1], one, outs.at[5], ins.at[5]),
+    ]
+    loads = [
+        pltpu.make_async_copy(parts.at[2, top], kept.at[0], here.at[0]),
+        pltpu.make_async_copy(parts.at[1, low], kept.at[1], here.at[1]),
+        pltpu.make_async_copy(parts.at[0], own, here.at[2]),
+    ]
+    store = pltpu.make_async_copy(summed, total, here.at[3])
+
+    def begin():
+        for copy in sends[:4]:
+            copy.start()
+        for copy in loads:
+            copy.start()
+
+    def middle():
+        for k, got in enumerate((got_one, got_two)):
+            loads[k].wait()
+            sends[k].wait_recv()
+            kept[k] = (kept[k].astype(F32) + got[0].astype(F32)).astype(BF16)
+            sends[4 + k].start()
+
+    def finish():
+        loads[2].wait()
+        for k, got in enumerate((got_one, got_two)):
+            sends[2 + k].wait_recv()
+            sends[4 + k].wait_recv()
+            rows = slice(k * half, (k + 1) * half)
+            summed[rows, :] = (
+                own[rows, :].astype(F32) + got[1].astype(F32) + last[k].astype(F32)
+            )
+        store.start()
+        for copy in sends:
+            copy.wait_send()
+        store.wait()
+
+    return begin, middle, finish
+
+
+def job_scratch(job):
+    kind, array = job
+    if kind == "gather":
+        return [
+            pltpu.SemaphoreType.DMA((4,)),
+            pltpu.SemaphoreType.DMA((4,)),
+            pltpu.SemaphoreType.DMA((1,)),
+        ]
+    _, rows, width = array.shape
+    halves = pltpu.VMEM((2, rows // 2, width), BF16)
+    return [
+        pltpu.SemaphoreType.DMA((6,)),
+        pltpu.SemaphoreType.DMA((6,)),
+        pltpu.SemaphoreType.DMA((4,)),
+        halves,
+        halves,
+        halves,
+        pltpu.VMEM((rows, width), BF16),
+        halves,
+        pltpu.VMEM((rows, width), F32),
+    ]
+
+
+def job_result(job):
+    kind, array = job
+    if kind == "gather":
+        return jax.ShapeDtypeStruct((4,) + array.shape, BF16)
+    return jax.ShapeDtypeStruct(array.shape[1:], F32)
+
+
+def plain_job(job):
+    kind, array = job
+    if kind == "gather":
+        return lax.all_gather(array, "seq", axis=0)
+    return lax.psum_scatter(array, "seq", scatter_dimension=0).astype(F32)
+
+
+def meet():
+    place = lax.axis_index("seq")
+    barrier = pltpu.get_barrier_semaphore()
+    for device in (over_one(place), over_two(place)):
+        pl.semaphore_signal(
+            barrier, inc=1, device_id={"seq": device}, device_id_type=pl.DeviceIdType.MESH
+        )
+    pl.semaphore_wait(barrier, 2)
+
+
+def call(
+    body, operands, in_specs, out_shape, out_specs, jobs, number, after=None,
+    grid=(), scratch=(), cost=None, name=None,
+):
+    plain = lax.axis_size("seq") != 4
+    results = [plain_job(job) for job in jobs] if plain else []
+    inside = [] if plain else jobs
+    extra = [] if after is None else [after]
+    job_shapes = [job_scratch(job) for job in inside]
+    n_in = len(operands)
+    n_out = len(out_shape)
+
+    def kernel(*refs):
+        ins = refs[:n_in]
+        rest = refs[n_in + len(extra) :]
+        sources, rest = rest[: len(inside)], rest[len(inside) :]
+        outs, rest = rest[:n_out], rest[n_out:]
+        targets, rest = rest[: len(inside)], rest[len(inside) :]
+        held, rest = rest[: len(scratch)], rest[len(scratch) :]
+        phases = []
+        for job, source, target, shapes in zip(inside, sources, targets, job_shapes):
+            mine, rest = rest[: len(shapes)], rest[len(shapes) :]
+            make = gather_job if job[0] == "gather" else scatter_job
+            phases.append(make(source, target, mine))
+
+        def hook(k):
+            if k == 0 and phases:
+                meet()
+            for phase in phases:
+                phase[k]()
+
+        body(hook, ins, outs, held)
+
+    given = {}
+    if inside:
+        given = {"collective_id": number, "has_side_effects": True}
+    made = pl.pallas_call(
+        kernel,
+        grid=grid,
+        out_shape=tuple(out_shape) + tuple(job_result(job) for job in inside),
+        in_specs=list(in_specs) + [ANY] * (len(extra) + len(inside)),
+        out_specs=tuple(out_specs) + (ANY,) * len(inside),
+        scratch_shapes=list(scratch) + [shape for shapes in job_shapes for shape in shapes],
+        compiler_params=pltpu.CompilerParams(vmem_limit_bytes=VMEM_LIMIT, **given),
+        cost_estimate=cost,
+        name=name,
+    )(*operands, *extra, *[job[1] for job in inside])
+    return made[:n_out], list(made[n_out:]) + results
+
+
+def transfer(jobs, number, after=None):
+    if lax.axis_size("seq") != 4:
+        return [plain_job(job) for job in jobs]
+
+    def body(hook, ins, outs, held):
+        for k in range(3):
+            hook(k)
+
+    return call(body, [], [], [], [], jobs, number, after, name="transfer")[1]
 
 
 def partner(v):
@@ -40,11 +253,19 @@
     return dot(high, ones) + dot(rest, ones)
 
 
+def true_chunk(place, c, count):
+    if count != 4:
+        return c
+    low = 1 - place % 2 if c % 2 else place % 2
+    high = 1 - place // 2 if c // 2 else place // 2
+    return low + 2 * high
+
+
 def prepare_heads(sizes, place, qkv_ref, qg_ref, kg_ref, cos_ref, sin_ref, ones, q_s, k_s, v_s):
     hq, hkv, _ = sizes
     seqs, rows_in, _ = qkv_ref.shape
     for c in range(seqs):
-        j = jnp.bitwise_xor(place, c)
+        j = true_chunk(place, c, seqs)
         rows = slice(c * rows_in, (c + 1) * rows_in)
         cos = cos_ref[rows, :]
         sin = sin_ref[rows, :]
@@ -70,13 +291,14 @@
     return lax.broadcasted_iota(jnp.int32, (block, keys), 1) <= bound
 
 
-def attend_kernel(
-    sizes, place_ref, len_ref, qkv_ref, qg_ref, kg_ref, cos_ref, sin_ref, ones_ref, after_ref,
-    out_ref, lse_ref, q_s, k_s, v_s, o_s,
-):
+def attend_kernel(sizes, hook, ins, outs, held):
+    len_ref, qkv_ref, qg_ref, kg_ref, cos_ref, sin_ref, ones_ref = ins
+    out_ref, lse_ref = outs
+    q_s, k_s, v_s, o_s = held
+    hook(0)
     hq, hkv, group = sizes
     seqs, rows_in, _ = qkv_ref.shape
-    place = place_ref[0]
+    place = lax.axis_index("seq")
     prepare_heads(
         sizes, place, qkv_ref, qg_ref, kg_ref, cos_ref, sin_ref, ones_ref[...], q_s, k_s, v_s
     )
@@ -98,26 +320,30 @@
             return 0
 
         lax.fori_loop(0, hq, one_head, 0)
+        if i == seqs * rows_in // BLOCK - 2:
+            hook(1)
     for c in range(seqs):
-        j = jnp.bitwise_xor(place, c)
+        j = true_chunk(place, c, seqs)
         rows = slice(c * rows_in, (c + 1) * rows_in)
         for p in range(hq // 2):
             out_ref[j, :, p * 128 : (p + 1) * 128] = jnp.concatenate(
                 [o_s[2 * p, rows, :], o_s[2 * p + 1, rows, :]], axis=1
             )
-
-
-def attend_back_kernel(
-    sizes, place_ref, len_ref, qkv_ref, cot_ref, lse_ref, qg_ref, kg_ref, cos_ref, sin_ref,
-    ones_ref, after_ref, dqkv_ref, dgain_ref, q_s, k_s, v_s, cot_s, dq_s, dk_s, dv_s,
-):
+    hook(2)
+
+
+def attend_back_kernel(sizes, hook, ins, outs, held):
+    len_ref, qkv_ref, cot_ref, lse_ref, qg_ref, kg_ref, cos_ref, sin_ref, ones_ref = ins
+    dqkv_ref, dgain_ref = outs
+    q_s, k_s, v_s, cot_s, dq_s, dk_s, dv_s = held
+    hook(0)
     hq, hkv, group = sizes
     seqs, rows_in, _ = qkv_ref.shape
-    place = place_ref[0]
+    place = lax.axis_index("seq")
     ones = ones_ref[...]
     prepare_heads(sizes, place, qkv_ref, qg_ref, kg_ref, cos_ref, sin_ref, ones, q_s, k_s, v_s)
     for c in range(seqs):
-        j = jnp.bitwise_xor(place, c)
+        j = true_chunk(place, c, seqs)
         for h in range(hq):
             cot_s[h, c * rows_in : (c + 1) * rows_in, :] = cot_ref[
                 j, :, h * HEAD : (h + 1) * HEAD
@@ -145,9 +371,11 @@
             return 0
 
         lax.fori_loop(0, hq, one_head, 0)
+        if i == seqs * rows_in // BLOCK - 2:
+            hook(1)
     gain_sums = [jnp.zeros((1, 128), F32), jnp.zeros((1, 128), F32)]
     for c in range(seqs):
-        j = jnp.bitwise_xor(place, c)
+        j = true_chunk(place, c, seqs)
         rows = slice(c * rows_in, (c + 1) * rows_in)
         cos = cos_ref[rows, :]
         sin = sin_ref[rows, :]
@@ -172,6 +400,7 @@
             ).astype(BF16)
     dgain_ref[0:1, :] = gain_sums[0]
     dgain_ref[1:2, :] = gain_sums[1]
+    hook(2)
 
 
 def position_tables(length):
@@ -189,45 +418,52 @@
     )
 
 
-def attend(sizes, place, length, qkv, gains, tables, after):
+def attend(sizes, length, qkv, gains, tables, jobs, number, after):
     seqs, rows_in, _ = qkv.shape
     hq, hkv, _ = sizes
     slot = seqs * rows_in
-    return pl.pallas_call(
+    return call(
         functools.partial(attend_kernel, sizes),
-        out_shape=(
+        [length, qkv, *gains, *tables],
+        [SMEM] + [VMEM] * 6,
+        [
             jax.ShapeDtypeStruct((seqs, rows_in, hq * HEAD), BF16),
             jax.ShapeDtypeStruct((hq, slot, 1), F32),
-        ),
-        in_specs=[SMEM, SMEM] + [VMEM] * 6 + [ANY],
-        out_specs=(VMEM, VMEM),
-        scratch_shapes=[
+        ],
+        [VMEM, VMEM],
+        jobs,
+        number,
+        after,
+        scratch=[
             pltpu.VMEM((hq, slot, HEAD), BF16),
             pltpu.VMEM((hkv, slot, HEAD), BF16),
             pltpu.VMEM((hkv, slot, HEAD), BF16),
             pltpu.VMEM((hq, slot, HEAD), BF16),
         ],
-        compiler_params=pltpu.CompilerParams(vmem_limit_bytes=VMEM_LIMIT),
-        cost_estimate=pl.CostEstimate(
+        cost=pl.CostEstimate(
             flops=56 * hq * slot * slot * HEAD, bytes_accessed=1 << 23, transcendentals=0
         ),
         name="attend",
-    )(place, length, qkv, *gains, *tables, after)
-
-
-def attend_back(sizes, place, length, qkv, cot, lse, gains, tables, after):
+    )
+
+
+def attend_back(sizes, length, qkv, cot, lse, gains, tables, jobs, number, after):
     seqs, rows_in, width = qkv.shape
     hq, hkv, _ = sizes
     slot = seqs * rows_in
-    return pl.pallas_call(
+    return call(
         functools.partial(attend_back_kernel, sizes),
-        out_shape=(
+        [length, qkv, cot, lse, *gains, *tables],
+        [SMEM] + [VMEM] * 8,
+        [
             jax.ShapeDtypeStruct((seqs, rows_in, width), BF16),
             jax.ShapeDtypeStruct((2, 128), F32),
-        ),
-        in_specs=[SMEM, SMEM] + [VMEM] * 8 + [ANY],
-        out_specs=(VMEM, VMEM),
-        scratch_shapes=[
+        ],
+        [VMEM, VMEM],
+        jobs,
+        number,
+        after,
+        scratch=[
             pltpu.VMEM((hq, slot, HEAD), BF16),
             pltpu.VMEM((hkv, slot, HEAD), BF16),
             pltpu.VMEM((hkv, slot, HEAD), BF16),
@@ -236,19 +472,25 @@
             pltpu.VMEM((hkv, slot, HEAD), F32),
             pltpu.VMEM((hkv, slot, HEAD), F32),
         ],
-        compiler_params=pltpu.CompilerParams(vmem_limit_bytes=VMEM_LIMIT),
-        cost_estimate=pl.CostEstimate(
+        cost=pl.CostEstimate(
             flops=88 * hq * slot * slot * HEAD, bytes_accessed=1 << 23, transcendentals=0
         ),
         name="attend_back",
-    )(place, length, qkv, cot, lse, *gains, *tables, after)
-
-
-def ffn_kernel(has_sum, mid_ref, cot_ref, gate_ref, up_ref, down_ref, *refs):
-    if has_sum:
-        sum_ref, after_ref, acts_ref, pull_ref = refs
-    else:
-        after_ref, acts_ref, pull_ref = refs
+    )
+
+
+def hooked(hook, step, steps, work):
+    pl.when(step == 0)(lambda: hook(0))
+    pl.when(step == (2 * steps) // 3)(lambda: hook(1))
+    work()
+    pl.when(step == steps - 1)(lambda: hook(2))
+
+
+def ffn_kernel(steps, hook, ins, outs, held):
+    hooked(hook, pl.program_id(0), steps, lambda: ffn_tile(*ins[:5], ins[5:], *outs))
+
+
+def ffn_tile(mid_ref, cot_ref, gate_ref, up_ref, down_ref, sums, acts_ref, pull_ref):
     model = mid_ref.shape[-1]
     hidden = acts_ref.shape[-1]
     gate_w = gate_ref[...].reshape(hidden, model)
@@ -266,12 +508,12 @@
     acts_ref[1] = up_cot
     acts_ref[2] = (active * up).astype(BF16)
     pulled = dot(gate_cot, gate_w) + dot(up_cot, up_w)
-    if has_sum:
+    for sum_ref in sums:
         pulled = pulled + sum_ref[...]
     pull_ref[...] = pulled.astype(pull_ref.dtype)
 
 
-def ffn_both(mid, cot, weights, summed, last, after):
+def ffn_both(mid, cot, weights, summed, last, jobs, number, after):
     tokens, model = mid.shape
     shards, _, part, _ = weights.shape
     hidden = shards * part
@@ -286,32 +528,34 @@
 
     row_spec = pl.BlockSpec((tile, model), lambda i: (i, 0))
     extra = () if summed is None else (summed,)
-    return pl.pallas_call(
-        functools.partial(ffn_kernel, summed is not None),
-        grid=(tokens // tile,),
-        out_shape=(
+    return call(
+        functools.partial(ffn_kernel, tokens // tile),
+        [mid, cot, weights, weights, weights, *extra],
+        [row_spec, row_spec, weight_spec(0), weight_spec(1), weight_spec(2)]
+        + [row_spec] * len(extra),
+        [
             jax.ShapeDtypeStruct((3, tokens, hidden), BF16),
             jax.ShapeDtypeStruct((tokens, model), BF16 if last else F32),
-        ),
-        in_specs=[row_spec, row_spec, weight_spec(0), weight_spec(1), weight_spec(2)]
-        + [row_spec] * len(extra)
-        + [ANY],
-        out_specs=(pl.BlockSpec((3, tile, hidden), lambda i: (0, i, 0)), row_spec),
-        compiler_params=pltpu.CompilerParams(vmem_limit_bytes=VMEM_LIMIT),
-        cost_estimate=pl.CostEstimate(
+        ],
+        [pl.BlockSpec((3, tile, hidden), lambda i: (0, i, 0)), row_spec],
+        jobs,
+        number,
+        after,
+        grid=(tokens // tile,),
+        cost=pl.CostEstimate(
             flops=16 * tokens * model * hidden,
             bytes_accessed=4 * tokens * model + 6 * hidden * model,
             transcendentals=0,
         ),
         name="ffn_both",
-    )(mid, cot, weights, weights, weights, *extra, after)
-
-
-def ffn_grad_kernel(slots, *refs):
-    acts = refs[:slots]
-    mids = refs[slots : 2 * slots]
-    cots = refs[2 * slots : 3 * slots]
-    out_ref = refs[3 * slots + 1]
+    )
+
+
+def ffn_grad_kernel(slots, tiles, hook, ins, outs, held):
+    acts = ins[:slots]
+    mids = ins[slots : 2 * slots]
+    cots = ins[2 * slots :]
+    (out_ref,) = outs
     kind = pl.program_id(0)
 
     def store(others):
@@ -320,16 +564,14 @@
             total = total + dot(act[0], other[...], TN)
         out_ref[...] = total.astype(BF16).reshape(out_ref.shape)
 
-    @pl.when(kind < 2)
-    def _():
-        store(mids)
-
-    @pl.when(kind == 2)
-    def _():
-        store(cots)
-
-
-def ffn_grads(acts, mids, cots, shards, after):
+    def work():
+        pl.when(kind < 2)(lambda: store(mids))
+        pl.when(kind == 2)(lambda: store(cots))
+
+    hooked(hook, kind * tiles + pl.program_id(1), 3 * tiles, work)
+
+
+def ffn_grads(acts, mids, cots, shards, jobs, number, after):
     slots = len(acts)
     _, tokens, hidden = acts[0].shape
     model = mids[0].shape[-1]
@@ -339,37 +581,43 @@
     whole = pl.BlockSpec(
         (tokens, model), lambda k, i: (0, 0), pipeline_mode=pl.Buffered(buffer_count=1)
     )
-    return pl.pallas_call(
-        functools.partial(ffn_grad_kernel, slots),
+    return call(
+        functools.partial(ffn_grad_kernel, slots, hidden // tile),
+        [*acts, *mids, *cots],
+        [pl.BlockSpec((1, tokens, tile), lambda k, i: (k, 0, i))] * slots
+        + [whole] * (2 * slots),
+        [jax.ShapeDtypeStruct((shards, 3, part, model), BF16)],
+        [pl.BlockSpec((per, 1, part, model), lambda k, i: (i, k, 0, 0))],
+        jobs,
+        number,
+        after,
         grid=(3, hidden // tile),
-        out_shape=jax.ShapeDtypeStruct((shards, 3, part, model), BF16),
-        in_specs=[pl.BlockSpec((1, tokens, tile), lambda k, i: (k, 0, i))] * slots
-        + [whole] * (2 * slots)
-        + [ANY],
-        out_specs=pl.BlockSpec((per, 1, part, model), lambda k, i: (i, k, 0, 0)),
-        compiler_params=pltpu.CompilerParams(vmem_limit_bytes=VMEM_LIMIT),
-        cost_estimate=pl.CostEstimate(
+        cost=pl.CostEstimate(
             flops=9 * slots * tokens * model * hidden,
             bytes_accessed=4 * slots * tokens * model,
             transcendentals=0,
         ),
         name="ffn_grads",
-    )(*acts, *mids, *cots, after)
-
-
-def ffn_down_kernel(chunks, *refs):
-    acts = refs[:chunks]
-    downs = refs[chunks : 2 * chunks]
-    out_ref = refs[2 * chunks + 1]
-    total = None
-    for act, down in zip(acts, downs):
-        hidden = act.shape[-1]
-        term = dot(act[0], down[...].reshape(hidden, down.shape[-1]))
-        total = term if total is None else total + term
-    out_ref[...] = total.astype(BF16)
-
-
-def ffn_down(acts, weights, after):
+    )
+
+
+def ffn_down_kernel(chunks, steps, hook, ins, outs, held):
+    acts = ins[:chunks]
+    downs = ins[chunks:]
+    (out_ref,) = outs
+
+    def work():
+        total = None
+        for act, down in zip(acts, downs):
+            hidden = act.shape[-1]
+            term = dot(act[0], down[...].reshape(hidden, down.shape[-1]))
+            total = term if total is None else total + term
+        out_ref[...] = total.astype(BF16)
+
+    hooked(hook, pl.program_id(0), steps, work)
+
+
+def ffn_down(acts, weights, jobs, number, after):
     chunks = len(acts)
     _, tokens, hidden = acts[0].shape
     shards, _, part, model = weights[0].shape
@@ -380,20 +628,23 @@
         lambda i: (0, 2, 0, 0),
         pipeline_mode=pl.Buffered(buffer_count=1),
     )
-    return pl.pallas_call(
-        functools.partial(ffn_down_kernel, chunks),
+    return call(
+        functools.partial(ffn_down_kernel, chunks, tokens // tile),
+        [*acts, *weights],
+        [act_spec] * chunks + [down_spec] * chunks,
+        [jax.ShapeDtypeStruct((tokens, model), BF16)],
+        [pl.BlockSpec((tile, model), lambda i: (i, 0))],
+        jobs,
+        number,
+        after,
         grid=(tokens // tile,),
-        out_shape=jax.ShapeDtypeStruct((tokens, model), BF16),
-        in_specs=[act_spec] * chunks + [down_spec] * chunks + [ANY],
-        out_specs=pl.BlockSpec((tile, model), lambda i: (i, 0)),
-        compiler_params=pltpu.CompilerParams(vmem_limit_bytes=VMEM_LIMIT),
-        cost_estimate=pl.CostEstimate(
+        cost=pl.CostEstimate(
             flops=4 * chunks * tokens * model * hidden,
             bytes_accessed=chunks * hidden * (tokens + model) * 2,
             transcendentals=0,
         ),
         name="ffn_down",
-    )(*acts, *weights, after)
+    )
 
 
 def place_kernel(place_ref, parts_ref, *refs):
@@ -446,27 +697,6 @@
     return jnp.concatenate([rows, one, two, top, low], axis=0).reshape(
         (count,) + rows.shape
     )
-
-
-def seq_scatter(parts):
-    count = lax.axis_size("seq")
-    if count != 4:
-        return lax.psum_scatter(parts, "seq", scatter_dimension=0).astype(F32)
-    over_one, over_two = ring_places(count)
-    half = parts.shape[1] // 2
-    top = lax.ppermute(
-        jnp.concatenate([parts[3, :half], parts[1, :half]], axis=0), "seq", over_one
-    )
-    low = lax.ppermute(
-        jnp.concatenate([parts[3, half:], parts[2, half:]], axis=0), "seq", over_two
-    )
-    top_on = (parts[2, :half].astype(F32) + top[:half].astype(F32)).astype(BF16)
-    low_on = (parts[1, half:].astype(F32) + low[:half].astype(F32)).astype(BF16)
-    top_last = lax.ppermute(top_on, "seq", over_two)
-    low_last = lax.ppermute(low_on, "seq", over_one)
-    first = jnp.concatenate([top[half:], low[half:]], axis=0).astype(F32)
-    last = jnp.concatenate([top_last, low_last], axis=0).astype(F32)
-    return parts[0].astype(F32) + first + last
 
 
 def seq_spread(rows):
@@ -577,10 +807,13 @@
         jnp.concatenate([key_gain, key_gain]).reshape(1, 2 * HEAD),
     )
 
+    flat = (slot_len, model)
+    chunked = (seqs, rows, model)
     places = place * rows + jnp.arange(rows, dtype=jnp.int32)
     live = (places[None, :] < lengths[:, None]).astype(F32)[..., None]
     inputs = tokens.astype(F32)
     out_cot = cotangent.astype(F32) * live
+    out_low = [out_cot[b].astype(BF16) for b in range(slots)]
     normal_in = [normed(inputs[b], attn_gain).astype(BF16) for b in range(slots)]
 
     qkv_own = jnp.concatenate(
@@ -592,8 +825,6 @@
         axis=1,
     )
     qkv_weight = lax.all_gather(qkv_own, "fsdp", axis=0, tiled=True)
-    normal_full = [seq_gather(v).reshape(slot_len, model) for v in normal_in]
-    out_weight = follow(out_weight, normal_full[:1])
     per = shards // seqs
     piece = out_weight.shape[0] // seqs
     out_own = None
@@ -619,104 +850,122 @@
         )
         ffn_weights.append(lax.all_gather(mine, "fsdp", axis=0))
 
-    after = order
-    qkv = []
-    attended = []
-    log_sums = []
-    hidden_res = []
-    mid_full = []
-    for b in range(slots):
-        raw = dot(normal_full[b], qkv_weight).astype(BF16).reshape(seqs, rows, -1)
-        mixed, lse = attend(sizes, order, lengths[b : b + 1], raw, gains, tables, after)
-        after = mixed
-        mixed = mixed.reshape(slot_len, hq * HEAD)
-        qkv.append(raw)
-        attended.append(mixed)
-        log_sums.append(lse)
-    for b in range(slots):
-        proj = dot(attended[b], out_rows).astype(BF16).reshape(seqs, rows, model)
-        res = inputs[b] + seq_scatter(proj)
-        hidden_res.append(res)
-        mid = normed(res, ffn_gain).astype(BF16)
-        mid_full.append(seq_gather(mid).reshape(slot_len, model))
-    cot_full = [seq_gather(out_cot[b].astype(BF16)).reshape(slot_len, model) for b in range(slots)]
+    def project(full):
+        return dot(full.reshape(flat), qkv_weight).astype(BF16).reshape(seqs, rows, -1)
+
+    def leave(mixed):
+        return dot(mixed.reshape(slot_len, -1), out_rows).astype(BF16).reshape(chunked)
+
+    def enter_ffn(b, total):
+        res = inputs[b] + total
+        return res, normed(res, ffn_gain).astype(BF16)
+
+    def heads(b, raw, jobs, number, after):
+        return attend(sizes, lengths[b : b + 1], raw, gains, tables, jobs, number, after)
+
+    normal_full = [None] * slots
+    cot_full = [None] * slots
+    mid_full = [None] * slots
+    (normal_full[0],) = transfer([("gather", normal_in[0])], 1)
+    qkv_0 = project(normal_full[0])
+    (mixed_0, lse_0), (normal_full[1],) = heads(
+        0, qkv_0, [("gather", normal_in[1])], 2, normal_full[0]
+    )
+    qkv_1 = project(normal_full[1])
+    (mixed_1, lse_1), (total_0,) = heads(1, qkv_1, [("scatter", leave(mixed_0))], 3, mixed_0)
+    qkv = [qkv_0, qkv_1]
+    log_sums = [lse_0, lse_1]
+    attended = [v.reshape(slot_len, hq * HEAD) for v in (mixed_0, mixed_1)]
+    res_0, mid_0 = enter_ffn(0, total_0)
+    mid_full[0], cot_full[0] = [
+        v.reshape(flat)
+        for v in transfer([("gather", mid_0), ("gather", out_low[0])], 4, mixed_1)
+    ]
 
     acts = [[None] * slots for _ in range(CHUNKS)]
     pulled = [None] * slots
-    ffn_parts = []
-    ffn_sums = []
-
-    def ffn_step(b, c, after):
-        acts[c][b], pulled[b] = ffn_both(
-            mid_full[b], cot_full[b], ffn_weights[c], pulled[b], c == CHUNKS - 1, after
+
+    def ffn_step(b, c, jobs, number, after):
+        (acts[c][b], pulled[b]), results = ffn_both(
+            mid_full[b], cot_full[b], ffn_weights[c], pulled[b], c == CHUNKS - 1,
+            jobs, number, after,
         )
-        return acts[c][b]
-
-    def grad_step(c, after):
-        ffn_parts.append(ffn_grads(acts[c], mid_full, cot_full, shards, after))
-        return ffn_parts[-1]
-
-    def sum_next(*earlier):
-        sent = ffn_parts[len(ffn_sums)].reshape(shards, 3 * part, model)
-        sent = follow(sent, [*ffn_sums[-1:], *earlier])
-        ffn_sums.append(lax.psum_scatter(sent, "fsdp", scatter_dimension=0))
-
-    early = CHUNKS // 2
-    for b in range(slots):
-        for c in range(early):
-            after = ffn_step(b, c, after)
-    after = grad_step(0, after)
-    sum_next()
-    for c in range(early, CHUNKS):
-        for b in range(slots):
-            after = ffn_step(b, c, after)
-    for c in range(1, CHUNKS):
-        after = grad_step(c, after)
-    for _ in range(early - 1):
-        sum_next()
-
-    output = []
-    res_cot = []
-    res_full = []
-    dqkv = []
-    grad_ffn_gain = 0.0
-    head_gain = 0.0
-    for b in range(slots):
-        pull, gain_part = normed_back(
-            hidden_res[b], ffn_gain, seq_scatter(pulled[b].reshape(seqs, rows, model))
+        return results
+
+    def grad_step(c, jobs, number, after):
+        (grads,), results = ffn_grads(
+            acts[c], mid_full, cot_full, shards, jobs, number, after
         )
-        grad_ffn_gain = grad_ffn_gain + gain_part
+        return grads.reshape(shards, 3 * part, model), results
+
+    def leave_ffn(b, jobs, number, after):
+        (out,), results = ffn_down(
+            [acts[c][b] for c in range(CHUNKS)], ffn_weights, jobs, number, after
+        )
+        return out.reshape(chunked), results
+
+    total_1, full = ffn_step(
+        0, 0, [("scatter", leave(mixed_1)), ("gather", out_low[1])], 5, mid_full[0]
+    )
+    cot_full[1] = full.reshape(flat)
+    res_1, mid_1 = enter_ffn(1, total_1)
+    hidden_res = [res_0, res_1]
+    (full,) = ffn_step(0, 1, [("gather", mid_1)], 6, acts[0][0])
+    mid_full[1] = full.reshape(flat)
+    (mid_total_0,) = ffn_step(1, 0, [("scatter", pulled[0].reshape(chunked))], 7, acts[1][0])
+
+    def pull_mid(b, total):
+        pull, gain_part = normed_back(hidden_res[b], ffn_gain, total)
         cot = out_cot[b] + pull
-        res_cot.append(cot)
-        full = seq_gather(cot.astype(BF16)).reshape(slot_len, model)
-        res_full.append(full)
+        return cot, cot.astype(BF16), gain_part
+
+    res_cot_0, low_0, ffn_gain_0 = pull_mid(0, mid_total_0)
+    grads_0, (res_full_0,) = grad_step(0, [("gather", low_0)], 8, acts[0][1])
+    ffn_sums = [lax.psum_scatter(grads_0, "fsdp", scatter_dimension=0)]
+    out_0, _ = leave_ffn(0, [], 0, grads_0)
+    (out_total_0,) = ffn_step(1, 1, [("scatter", out_0)], 9, out_0)
+    grads_1, (mid_total_1,) = grad_step(
+        1, [("scatter", pulled[1].reshape(chunked))], 10, acts[1][1]
+    )
+    ffn_sums.append(
+        lax.psum_scatter(follow(grads_1, ffn_sums), "fsdp", scatter_dimension=0)
+    )
+    res_cot_1, low_1, ffn_gain_1 = pull_mid(1, mid_total_1)
+    grad_ffn_gain = ffn_gain_0 + ffn_gain_1
+
+    def back(b, full, jobs, number, after):
         attended_cot = dot(full, out_rows, NT).astype(BF16).reshape(seqs, rows, hq * HEAD)
-        back, gain_part = attend_back(
-            sizes, order, lengths[b : b + 1], qkv[b], attended_cot, log_sums[b], gains, tables,
-            after,
+        (cots, gain_part), results = attend_back(
+            sizes, lengths[b : b + 1], qkv[b], attended_cot, log_sums[b], gains, tables,
+            jobs, number, after,
         )
-        after = back
-        sum_next(back)
-        head_gain = head_gain + gain_part
-        dqkv.append(back.reshape(slot_len, -1))
-    for b in range(slots):
-        ffn_out = ffn_down([acts[c][b] for c in range(CHUNKS)], ffn_weights, after)
-        after = ffn_out
-        total = hidden_res[b] + seq_scatter(ffn_out.reshape(seqs, rows, model))
-        output.append((live[b] * total).astype(BF16))
-
-    while len(ffn_sums) < CHUNKS:
-        sum_next()
-
+        return cots.reshape(slot_len, -1), gain_part, results
+
+    def pull_heads(cots):
+        return dot(cots, qkv_weight, NT).astype(BF16).reshape(chunked)
+
+    dqkv_0, heads_gain_0, (res_full_1,) = back(
+        0, res_full_0.reshape(flat), [("gather", low_1)], 11, grads_1
+    )
+    dqkv_1, heads_gain_1, (in_total_0,) = back(
+        1, res_full_1.reshape(flat), [("scatter", pull_heads(dqkv_0))], 12, dqkv_0
+    )
+    head_gain = heads_gain_0 + heads_gain_1
+    dqkv = [dqkv_0, dqkv_1]
+    res_full = [v.reshape(flat) for v in (res_full_0, res_full_1)]
+    out_1, (in_total_1,) = leave_ffn(1, [("scatter", pull_heads(dqkv_1))], 13, dqkv_1)
+    (out_total_1,) = transfer([("scatter", out_1)], 14, out_1)
+
+    output = [
+        (live[b] * (hidden_res[b] + total)).astype(BF16)
+        for b, total in enumerate((out_total_0, out_total_1))
+    ]
     grad_tokens = []
     grad_attn_gain = 0.0
-    for b in range(slots):
-        in_cot = seq_scatter(
-            dot(dqkv[b], qkv_weight, NT).astype(BF16).reshape(seqs, rows, model)
-        )
+    for b, (in_cot, cot) in enumerate(((in_total_0, res_cot_0), (in_total_1, res_cot_1))):
         pull, gain_part = normed_back(inputs[b], attn_gain, in_cot)
         grad_attn_gain = grad_attn_gain + gain_part
-        grad_tokens.append((res_cot[b] + pull).astype(BF16))
+        grad_tokens.append((cot + pull).astype(BF16))
 
     out_grads = sum(dot(attended[b], res_full[b], TN) for b in range(slots)).astype(BF16)
     out_grads = follow(out_grads, ffn_sums[-1:])
@@ -732,7 +981,7 @@
     ).astype(BF16)
     qkv_grads = jnp.concatenate(
         [
-            sum(dot(normal_full[b], dqkv[b], TN) for b in range(slots)).astype(BF16),
+            sum(dot(normal_full[b].reshape(flat), dqkv[b], TN) for b in range(slots)).astype(BF16),
             jnp.pad(gain_columns, ((0, 0), (0, 124))),
         ],
         axis=1,

time: 1200 us -> 1050 us (0.88); the launches traced: 1190 us -> 1030 us
  Pallas kernels: 416 us -> 643 us
  waiting for transfers between devices: 362 us -> 154 us
  starting transfers between devices: 120 us -> 43.3 us
  local copies, waits for them, and re-layouts: 113 us -> 57.9 us
  other arithmetic: 104 us -> 51 us
    pallas_call x18 -> x15, Pallas kernels: 396 us -> 628 us  [call(): pl.pallas_call(kernel, grid=grid, out_shape=tuple(out_shape) + tuple((job...]
    ppermute x13 -> x3, waiting for transfers between devices: 124 us -> 5 us  [seq_gather(): two = lax.ppermute(rows, 'seq', over_two)]
    ppermute x32 -> x0, waiting for transfers between devices: 101 us -> none  [the longest x8 43.4 us: seq_scatter(): lax.ppermute(jnp.concatenate([parts[3, :half], parts[1, :half]], axis=0),...]
    reduce_scatter x4 -> x2, waiting for transfers between devices: 0.01 us -> 68.5 us  [the longest x1 62.9 us: on_device(): ffn_sums = [lax.psum_scatter(grads_0, 'fsdp', scatter_dimension=0)]]
    ppermute x13 -> x3, waiting for transfers between devices: 42.5 us -> 1.22 us  [seq_gather(): low = lax.ppermute(one[half:], 'seq', over_two)]
    ppermute x13 -> x3, waiting for transfers between devices: 64.8 us -> 31.3 us  [seq_gather(): top = lax.ppermute(two[:half], 'seq', over_one)]
    ppermute x32 -> x0, starting transfers between devices: 31.7 us -> none  [the longest x8 9.53 us: seq_scatter(): top_last = lax.ppermute(top_on, 'seq', over_two)]
    convert_element_type x12 -> x5, other arithmetic: 41.9 us -> 10.4 us  [the longest x2 6.23 us: pull_mid(): return (cot, cot.astype(BF16), gain_part)]
  transfers between devices with their start and end apart: 108 -> 32, of which waited for: 50 -> 10; matrix products, arithmetic and copies ran while one was open for 19% -> 12% of each run, Pallas kernels for 35% -> 51%
where the time goes in v3:
time: 1050 us; the launch traced here: 1030 us
  Pallas kernels  643 us (61%)
  waiting for transfers between devices  154 us (15%)
  matrix products  60.5 us (6%)
  local copies, waits for them, and re-layouts  57.9 us (6%)
  other arithmetic  51 us (5%)
  starting transfers between devices  43.3 us (4%)
  between operations  15.5 us (1%)
    pallas_call x15, Pallas kernels, call(): pl.pallas_call(kernel, grid=grid, out_shape=tuple(out_shape) + tuple((job...  628 us
    reduce_scatter x1, waiting for transfers between devices, on_device(): ffn_sums = [lax.psum_scatter(grads_0, 'fsdp', scatter_dimension=0)]  62.9 us
    dot_general x12, matrix products, dot(): return lax.dot_general(a, b, dims, preferred_element_type=F32)  60.5 us
    unnamed x145, local copies, waits for them, and re-layouts  32.4 us
    ppermute x3, waiting for transfers between devices, seq_gather(): top = lax.ppermute(two[:half], 'seq', over_one)  31.3 us
    ppermute x3, waiting for transfers between devices, seq_gather(): one = lax.ppermute(rows, 'seq', over_one)  26.1 us
  transfers between devices with their start and end apart: 32, of which 10 were waited for; matrix products, arithmetic and copies ran while one was open for 12% of the time, Pallas kernels for 51%

profile of v3, /device:TPU:6, one launch (start us, length us, event | category | flops | bytes accessed | tf_op | source)
XLA Modules:
  0.0 1026.0 jit_solution(9321423061329629391)
XLA Ops:
  13.6 18.6 %collective-permute-done = bf16[64,2048]{1,0:T(8,128)(2,1)S(1)} collective-permute-done((bf16[64,2048]{1,0:T(8,128)(2,1)S(1)}, bf16[64,2048]{1,0:T(8,128)(2,1)S(1)}, u32[]{:S(2)}, u32[]{:S(2)}) %collective-permute-start) | collective-permute-done | bytes 262176 | tf_op jit(solution)/shard_map/ppermute | solution.py:837
  33.0 2.1 dynamic-slice_bitcast_fusion.5
  38.3 2.5 pad_maximum_fusion.3
  45.2 33.0 %transfer.3.refs_7_ = bf16[4,256,2048]{2,1,0:T(8,128)(2,1)} custom-call(bf16[256,2048]{1,0:T(8,128)(2,1)} %get-tuple-element.120.refs_0_), custom_call_target="tpu_custom_call" | custom-call | tf_op jit(solution)/shard_map/transfer/pallas_call | solution.py:220
  80.1 2.0 copy-done.13
  83.8 7.8 convolution_convert_fusion.5
  91.6 40.3 %attend.2 = (bf16[4,256,512]{2,1,0:T(8,128)(2,1)}, f32[8,1024,1]{2,1,0:T(8,128)}, bf16[4,256,2048]{2,1,0:T(8,128)(2,1)}) custom-call(s32[1]{0:T(128)} %get-tuple-element.155.refs_0_, bf16[4,256,768]{2,1,0:T(8,128)(2,1)} %bitcast.252, f32[1,128]{1,0:T(1,128)} %get-tuple-element.161.refs_2_.refs_4_, f32[1,128]{1,0:T(1,128)} %get-tuple-element.162.refs_3_.refs_5_, ...), custom_call_target="tpu_custom_call" | custom-call | flops 30064771072 | bytes 8388608 | tf_op jit(solution)/shard_map/attend/pallas_call | solution.py:220
  131.9 6.4 convolution_convert_fusion.1
  138.4 4.5 convolution_convert_fusion.4
  142.8 37.4 %attend.3 = (bf16[4,256,512]{2,1,0:T(8,128)(2,1)}, f32[8,1024,1]{2,1,0:T(8,128)}, f32[256,2048]{1,0:T(8,128)}) custom-call(s32[1]{0:T(128)} %get-tuple-element.156.refs_0_, bf16[4,256,768]{2,1,0:T(8,128)(2,1)} %bitcast.250, f32[1,128]{1,0:T(1,128)} %get-tuple-element.161.refs_2_.refs_4_, f32[1,128]{1,0:T(1,128)} %get-tuple-element.162.refs_3_.refs_5_, ...), custom_call_target="tpu_custom_call" | custom-call | flops 30064771072 | bytes 8388608 | tf_op jit(solution)/shard_map/attend/pallas_call | solution.py:220
  180.2 1.9 multiply_reduce_fusion.9
  184.7 64.8 %transfer.4 = (bf16[4,256,2048]{2,1,0:T(8,128)(2,1)}, bf16[4,256,2048]{2,1,0:T(8,128)(2,1)}) custom-call(bf16[4,256,512]{2,1,0:T(8,128)(2,1)} %get-tuple-element.58.refs_0_, bf16[256,2048]{1,0:T(8,128)(2,1)} %multiply_convert_fusion.3.refs_1_, bf16[256,2048]{1,0:T(8,128)(2,1)} %get-tuple-element.128.refs_2_), custom_call_target="tpu_custom_call" | custom-call | tf_op jit(solution)/shard_map/transfer/pallas_call | solution.py:220
  249.5 4.4 convolution_convert_fusion
  253.9 69.8 %ffn_both.4 = (bf16[3,1024,1024]{2,1,0:T(8,128)(2,1)}, f32[1024,2048]{1,0:T(8,128)}, f32[256,2048]{1,0:T(8,128)}, bf16[4,256,2048]{2,1,0:T(8,128)(2,1)}) custom-call(bf16[1024,2048]{1,0:T(8,128)(2,1)} %bitcast.224, bf16[1024,2048]{1,0:T(8,128)(2,1)} %bitcast.229, bf16[8,3,128,2048]{3,2,1,0:T(8,128)(2,1)} %bitcast.208, bf16[8,3,128,2048]{3,2,1,0:T(8,128)(2,1)} %bitcast.209, ...), custom_call_target="tpu_custom_call" | custom-call | flops 34359738368 | bytes 20971520 | tf_op jit(solution)/shard_map/ffn_both/pallas_call | solution.py:220
  323.7 2.0 multiply_reduce_fusion.8
  328.3 42.8 %ffn_both.5 = (bf16[3,1024,1024]{2,1,0:T(8,128)(2,1)}, bf16[1024,2048]{1,0:T(8,128)(2,1)}, bf16[4,256,2048]{2,1,0:T(8,128)(2,1)}) custom-call(bf16[1024,2048]{1,0:T(8,128)(2,1)} %bitcast.226, bf16[1024,2048]{1,0:T(8,128)(2,1)} %bitcast.230, bf16[8,3,128,2048]{3,2,1,0:T(8,128)(2,1)} %bitcast.216, bf16[8,3,128,2048]{3,2,1,0:T(8,128)(2,1)} %bitcast.217, ...), custom_call_target="tpu_custom_call" | custom-call | flops 34359738368 | bytes 20971520 | tf_op jit(solution)/shard_map/ffn_both/pallas_call | solution.py:220
  371.1 38.3 %ffn_both.6 = (bf16[3,1024,1024]{2,1,0:T(8,128)(2,1)}, f32[1024,2048]{1,0:T(8,128)}, f32[256,2048]{1,0:T(8,128)}) custom-call(bf16[1024,2048]{1,0:T(8,128)(2,1)} %bitcast.238, bf16[1024,2048]{1,0:T(8,128)(2,1)} %bitcast.234, bf16[8,3,128,2048]{3,2,1,0:T(8,128)(2,1)} %bitcast.211, bf16[8,3,128,2048]{3,2,1,0:T(8,128)(2,1)} %bitcast.212, ...), custom_call_target="tpu_custom_call" | custom-call | flops 34359738368 | bytes 20971520 | tf_op jit(solution)/shard_map/ffn_both/pallas_call | solution.py:220
  409.4 2.3 multiply_reduce_fusion.1
  412.2 3.9 fusion.19
  416.1 40.9 %ffn_grads.2 = (bf16[8,3,128,2048]{3,2,1,0:T(8,128)(2,1)}, bf16[4,256,2048]{2,1,0:T(8,128)(2,1)}) custom-call(bf16[3,1024,1024]{2,1,0:T(8,128)(2,1)} %get-tuple-element.62.refs_6_.refs_0_, bf16[3,1024,1024]{2,1,0:T(8,128)(2,1)} %get-tuple-element.69.refs_1_.refs_6_.refs_0_, bf16[1024,2048]{1,0:T(8,128)(2,1)} %bitcast.227, bf16[1024,2048]{1,0:T(8,128)(2,1)} %bitcast.239, ...), custom_call_target="tpu_custom_call" | custom-call | flops 38654705664 | bytes 16777216 | tf_op jit(solution)/shard_map/ffn_grads/pallas_call | solution.py:220
  457.1 14.2 %ffn_down.2 = bf16[1024,2048]{1,0:T(8,128)(2,1)} custom-call(bf16[3,1024,1024]{2,1,0:T(8,128)(2,1)} %get-tuple-element.62.refs_6_.refs_0_, bf16[3,1024,1024]{2,1,0:T(8,128)(2,1)} %get-tuple-element.66.refs_5_.refs_1_.refs_0_, bf16[8,3,128,2048]{3,2,1,0:T(8,128)(2,1)} %bitcast.214, bf16[8,3,128,2048]{3,2,1,0:T(8,128)(2,1)} %bitcast.219, ...), custom_call_target="tpu_custom_call" | custom-call | flops 17179869184 | bytes 12582912 | tf_op jit(solution)/shard_map/ffn_down/pallas_call | solution.py:220
  471.3 39.9 %ffn_both.7 = (bf16[3,1024,1024]{2,1,0:T(8,128)(2,1)}, bf16[1024,2048]{1,0:T(8,128)(2,1)}, f32[256,2048]{1,0:T(8,128)}) custom-call(bf16[1024,2048]{1,0:T(8,128)(2,1)} %bitcast.240, bf16[1024,2048]{1,0:T(8,128)(2,1)} %bitcast.236, bf16[8,3,128,2048]{3,2,1,0:T(8,128)(2,1)} %bitcast.220, bf16[8,3,128,2048]{3,2,1,0:T(8,128)(2,1)} %bitcast.221, ...), custom_call_target="tpu_custom_call" | custom-call | flops 34359738368 | bytes 20971520 | tf_op jit(solution)/shard_map/ffn_both/pallas_call | solution.py:220
  511.3 43.8 %ffn_grads.3 = (bf16[8,3,128,2048]{3,2,1,0:T(8,128)(2,1)}, f32[256,2048]{1,0:T(8,128)}) custom-call(bf16[3,1024,1024]{2,1,0:T(8,128)(2,1)} %get-tuple-element.66.refs_5_.refs_1_.refs_0_, bf16[3,1024,1024]{2,1,0:T(8,128)(2,1)} %get-tuple-element.73.refs_1_.refs_6_, bf16[1024,2048]{1,0:T(8,128)(2,1)} %bitcast.228, bf16[1024,2048]{1,0:T(8,128)(2,1)} %bitcast.241, ...), custom_call_target="tpu_custom_call" | custom-call | flops 38654705664 | bytes 16777216 | tf_op jit(solution)/shard_map/ffn_grads/pallas_call | solution.py:220
  555.0 62.9 %reduce-scatter.5.cloned.1.call-done = bf16[1,384,2048]{2,1,0:T(8,128)(2,1)} async-done(((bf16[8,384,2048]{2,1,0:T(8,128)(2,1)}), bf16[1,384,2048]{2,1,0:T(8,128)(2,1)}) %reduce-scatter.5.cloned.1.call-update) | async-done | bytes 1572880 | tf_op jit(solution)/shard_map/reduce_scatter | solution.py:924
  619.5 2.3 multiply_reduce_fusion
  622.3 5.1 convolution_convert_fusion.7
  627.4 2.3 fusion.18
  629.8 41.8 %attend_back.2 = (bf16[4,256,768]{2,1,0:T(8,128)(2,1)}, f32[2,128]{1,0:T(2,128)}, bf16[4,256,2048]{2,1,0:T(8,128)(2,1)}) custom-call(s32[1]{0:T(128)} %get-tuple-element.155.refs_0_, bf16[4,256,768]{2,1,0:T(8,128)(2,1)} %bitcast.253, bf16[4,256,512]{2,1,0:T(8,128)(2,1)} %bitcast.258, f32[8,1024,1]{2,1,0:T(8,128)} %get-tuple-element.75.refs_3_, ...), custom_call_target="tpu_custom_call" | custom-call | flops 47244640256 | bytes 8388608 | tf_op jit(solution)/shard_map/attend_back/pallas_call | solution.py:220
  671.6 5.7 convolution_convert_fusion.6
  677.3 5.2 convolution_convert_fusion.3
  682.5 44.8 %attend_back.3 = (bf16[4,256,768]{2,1,0:T(8,128)(2,1)}, f32[2,128]{1,0:T(2,128)}, f32[256,2048]{1,0:T(8,128)}) custom-call(s32[1]{0:T(128)} %get-tuple-element.156.refs_0_, bf16[4,256,768]{2,1,0:T(8,128)(2,1)} %bitcast.251, bf16[4,256,512]{2,1,0:T(8,128)(2,1)} %bitcast.259, f32[8,1024,1]{2,1,0:T(8,128)} %get-tuple-element.80.refs_3_, ...), custom_call_target="tpu_custom_call" | custom-call | flops 47244640256 | bytes 8388608 | tf_op jit(solution)/shard_map/attend_back/pallas_call | solution.py:220
  728.3 4.8 fusion.28
  733.1 5.0 convolution_convert_fusion.2
  738.1 3.9 fusion.1
  742.0 5.7 reduce-scatter.7.cloned.1.call-done
  747.7 41.2 %ffn_down.3 = (bf16[1024,2048]{1,0:T(8,128)(2,1)}, f32[256,2048]{1,0:T(8,128)}) custom-call(bf16[3,1024,1024]{2,1,0:T(8,128)(2,1)} %get-tuple-element.69.refs_1_.refs_6_.refs_0_, bf16[3,1024,1024]{2,1,0:T(8,128)(2,1)} %get-tuple-element.73.refs_1_.refs_6_, bf16[8,3,128,2048]{3,2,1,0:T(8,128)(2,1)} %bitcast.215, bf16[8,3,128,2048]{3,2,1,0:T(8,128)(2,1)} %bitcast.223, ...), custom_call_target="tpu_custom_call" | custom-call | flops 17179869184 | bytes 12582912 | tf_op jit(solution)/shard_map/ffn_down/pallas_call | solution.py:220
  789.0 3.5 multiply_reduce_fusion.3
  792.9 3.8 fusion.27
  796.7 4.0 fusion
  800.7 2.2 pad_maximum_fusion
  803.6 35.2 %transfer.5 = f32[256,2048]{1,0:T(8,128)} custom-call(bf16[4,256,2048]{2,1,0:T(8,128)(2,1)} %bitcast.180, bf16[4,256,2048]{2,1,0:T(8,128)(2,1)} %bitcast.181), custom_call_target="tpu_custom_call" | custom-call | tf_op jit(solution)/shard_map/transfer/pallas_call | solution.py:220
  838.9 2.0 fusion.6
  841.8 3.8 fusion.8
  852.3 26.0 %collective-permute-done.20 = bf16[384,2048]{1,0:T(8,128)(2,1)S(1)} collective-permute-done((bf16[384,2048]{1,0:T(8,128)(2,1)S(1)}, bf16[384,2048]{1,0:T(8,128)(2,1)S(1)}, u32[]{:S(2)}, u32[]{:S(2)}) %collective-permute-start.20) | collective-permute-done | bytes 1572896 | tf_op jit(solution)/shard_map/ppermute | solution.py:693
  879.6 2.3 collective-permute-start.17
  883.3 10.5 %collective-permute-start.8 = (bf16[64,2048]{1,0:T(8,128)(2,1)S(1)}, bf16[64,2048]{1,0:T(8,128)(2,1)S(1)}, u32[]{:S(2)}, u32[]{:S(2)}) collective-permute-start(bf16[64,2048]{1,0:T(8,128)(2,1)S(1)} %copy-done.55), channel_id=1, source_target_pairs={{0,0},{4,1},{8,10},{12,11},{16,20},{20,21},{24,30},{28,31}} | collective-permute-start | bytes 786440 | tf_op jit(solution)/shard_map/ppermute | solution.py:724
  895.2 3.5 collective-permute-done.8
  898.7 2.9 collective-permute-start.22
  905.9 23.3 %collective-permute-done.22 = bf16[192,2048]{1,0:T(8,128)(2,1)S(1)} collective-permute-done((bf16[192,2048]{1,0:T(8,128)(2,1)S(1)}, bf16[192,2048]{1,0:T(8,128)(2,1)S(1)}, u32[]{:S(2)}, u32[]{:S(2)}) %collective-permute-start.22) | collective-permute-done | bytes 786464 | tf_op jit(solution)/shard_map/ppermute | solution.py:695
  931.8 7.7 place_parts.2
  939.5 5.5 collective-permute-start.18
  945.3 2.7 constant_dynamic-update-slice_fusion.13
  955.0 5.7 collective-permute-done.18
  963.7 7.7 place_parts.3
  971.4 7.9 collective-permute-start.5
  979.3 3.4 fusion.14
  983.5 5.0 collective-permute-done.5
  988.7 2.0 collective-permute-start.7
  992.2 2.4 collective-permute-done.6
  996.0 3.6 reshape.315
  999.6 3.8 constant_dynamic-slice_fusion.3
  1003.5 4.3 convert_bitcast_fusion
  1010.3 2.6 copy.44
  1012.9 3.8 copy.53
  (256 shorter events, 65.4 us)
Async XLA Ops:
  7.2 76.6 %all-gather.7.cloned.1.call-start = ((), (), s32[]{:S(2)}) async-start(), calls=%async_computation.4 | async-start | bytes 3538944 | tf_op jit(solution)/shard_map/all_gather | solution.py:827
  10.1 121.8 %all-gather.9.cloned.1.call-start = ((), (), s32[]{:S(2)}) async-start(), calls=%async_computation.5 | async-start | bytes 2359296 | tf_op jit(solution)/shard_map/all_gather | solution.py:839
  10.3 3.4 collective-permute-start.1
  11.0 21.2 %collective-permute-start = (bf16[64,2048]{1,0:T(8,128)(2,1)S(1)}, bf16[64,2048]{1,0:T(8,128)(2,1)S(1)}, u32[]{:S(2)}, u32[]{:S(2)}) collective-permute-start(bf16[64,2048]{1,0:T(8,128)(2,1)S(1)} %get-tuple-element.136), channel_id=1, source_target_pairs={{0,0},{1,4},{10,8},{11,12},{20,16},{21,20},{30,24},{31,28}} | collective-permute-start | bytes 786440 | tf_op jit(solution)/shard_map/ppermute | solution.py:837
  12.3 20.0 %collective-permute-start.3 = (bf16[64,2048]{1,0:T(8,128)(2,1)S(1)}, bf16[64,2048]{1,0:T(8,128)(2,1)S(1)}, u32[]{:S(2)}, u32[]{:S(2)}) collective-permute-start(bf16[64,2048]{1,0:T(8,128)(2,1)S(1)} %get-tuple-element.137), channel_id=1, source_target_pairs={{0,3},{1,7},{10,11},{11,15},{20,19},{21,23},{30,27},{31,31}} | collective-permute-start | bytes 786440 | tf_op jit(solution)/shard_map/ppermute | solution.py:837
  12.9 19.3 %collective-permute-start.2 = (bf16[64,2048]{1,0:T(8,128)(2,1)S(1)}, bf16[64,2048]{1,0:T(8,128)(2,1)S(1)}, u32[]{:S(2)}, u32[]{:S(2)}) collective-permute-start(bf16[64,2048]{1,0:T(8,128)(2,1)S(1)} %get-tuple-element.138), channel_id=1, source_target_pairs={{0,2},{1,6},{10,10},{11,14},{20,18},{21,22},{30,26},{31,30}} | collective-permute-start | bytes 786440 | tf_op jit(solution)/shard_map/ppermute | solution.py:837
  33.0 220.9 %all-gather.13.cloned.1.call-start = ((), (), s32[]{:S(2)}) async-start(), calls=%async_computation.11 | async-start | bytes 14155776 | tf_op jit(solution)/shard_map/all_gather | solution.py:851
  38.2 290.0 %all-gather.11.cloned.1.call-start = ((), (), s32[]{:S(2)}) async-start(), calls=%async_computation.10 | async-start | bytes 14155776 | tf_op jit(solution)/shard_map/all_gather | solution.py:851
  40.8 577.1 %reduce-scatter.5.cloned.1.call-start = ((), (), s32[]{:S(2)}) async-start(), calls=%async_computation.6 | async-start | bytes 14155776 | tf_op jit(solution)/shard_map/reduce_scatter | solution.py:924
  45.2 33.1 %copy-start.48 = (f32[64]{0:T(128)S(1)}, f32[64]{0:T(128)}, u32[]{:S(2)}) copy-start(f32[64]{0:T(128)} %param.24) | copy-start | bytes 772
  45.2 33.1 %copy-start.49 = (f32[64]{0:T(128)S(1)}, f32[64]{0:T(128)}, u32[]{:S(2)}) copy-start(f32[64]{0:T(128)} %param.25) | copy-start | bytes 772
  45.2 33.7 %copy-start.43 = (s32[2]{0:T(128)S(1)}, s32[2]{0:T(128)}, u32[]{:S(2)}) copy-start(s32[2]{0:T(128)} %param.19) | copy-start | bytes 28
  45.2 34.3 %copy-start.25 = (bf16[2,256,2048]{2,1,0:T(8,128)(2,1)S(1)}, bf16[2,256,2048]{2,1,0:T(8,128)(2,1)}, u32[]{:S(2)}) copy-start(bf16[2,256,2048]{2,1,0:T(8,128)(2,1)} %param.18) | copy-start | bytes 6291460
  131.9 6.5 copy-start.50
  131.9 6.5 copy-start.56
  142.8 37.4 %copy-start.3 = (f32[2,256,2048]{2,1,0:T(8,128)S(1)}, f32[2,256,2048]{2,1,0:T(8,128)}, u32[]{:S(2)}) copy-start(f32[2,256,2048]{2,1,0:T(8,128)} %copy-done.2) | copy-start | bytes 12582916
  184.7 64.8 %copy-start.22 = (bf16[4,256,512]{2,1,0:T(8,128)(2,1)S(1)}, bf16[4,256,512]{2,1,0:T(8,128)(2,1)}, u32[]{:S(2)}) copy-start(bf16[4,256,512]{2,1,0:T(8,128)(2,1)} %get-tuple-element.58.refs_0_) | copy-start | bytes 3145732
  184.7 64.8 %copy-start.53 = (bf16[512,2048]{1,0:T(8,128)(2,1)S(1)}, bf16[512,2048]{1,0:T(8,128)(2,1)}, u32[]{:S(2)}) copy-start(bf16[512,2048]{1,0:T(8,128)(2,1)} %all-gather.9.cloned.1.call-done) | copy-start | bytes 6291460
  253.9 69.9 %copy-start.4 = (f32[2,256,2048]{2,1,0:T(8,128)S(1)}, f32[2,256,2048]{2,1,0:T(8,128)}, u32[]{:S(2)}) copy-start(f32[2,256,2048]{2,1,0:T(8,128)} %copy-done.2) | copy-start | bytes 12582916
  326.3 44.7 %copy-start.41 = (f32[256]{0:T(256)}, f32[256]{0:T(256)S(1)}, u32[]{:S(2)}) copy-start(f32[256]{0:T(256)S(1)} %get-tuple-element.152) | copy-start | bytes 3076
  371.0 38.3 %copy-start.11 = (f32[256,2048]{1,0:T(8,128)S(1)}, f32[256,2048]{1,0:T(8,128)}, u32[]{:S(2)}) copy-start(f32[256,2048]{1,0:T(8,128)} %copy-done.10) | copy-start | bytes 6291460
  457.1 290.6 %reduce-scatter.7.cloned.1.call-start = ((), (), s32[]{:S(2)}) async-start(), calls=%async_computation.7 | async-start | bytes 14155776 | tf_op jit(solution)/shard_map/reduce_scatter | solution.py:931
  617.9 185.0 %reduce-scatter.9.cloned.1.call-start = ((), (), s32[]{:S(2)}) async-start(), calls=%async_computation.8 | async-start | bytes 2359296 | tf_op jit(solution)/shard_map/reduce_scatter | solution.py:972
  622.3 5.1 copy-start.15
  622.3 5.1 copy-start.18
  622.3 5.1 copy-start.44
  629.7 41.8 %copy-start.54 = (bf16[512,2048]{1,0:T(8,128)(2,1)S(1)}, bf16[512,2048]{1,0:T(8,128)(2,1)}, u32[]{:S(2)}) copy-start(bf16[512,2048]{1,0:T(8,128)(2,1)} %all-gather.9.cloned.1.call-done) | copy-start | bytes 6291460
  671.5 5.7 copy-start.51
  671.5 5.7 copy-start.58
  682.5 44.8 %copy-start.47 = (f32[2,128]{1,0:T(2,128)S(1)}, f32[2,128]{1,0:T(2,128)}, u32[]{:S(2)}) copy-start(f32[2,128]{1,0:T(2,128)} %get-tuple-element.86) | copy-start | bytes 3076
  682.5 45.7 %copy-start.29 = (bf16[4,256,512]{2,1,0:T(8,128)(2,1)S(1)}, bf16[4,256,512]{2,1,0:T(8,128)(2,1)}, u32[]{:S(2)}) copy-start(bf16[4,256,512]{2,1,0:T(8,128)(2,1)} %get-tuple-element.56.refs_7_) | copy-start | bytes 3145732
  733.1 5.0 copy-start.21
  733.1 5.0 copy-start.23
  747.7 223.7 %reduce-scatter.11.cloned.1.call-start = ((), (), s32[]{:S(2)}) async-start(), calls=%async_computation.9 | async-start | bytes 4128768 | tf_op jit(solution)/shard_map/reduce_scatter | solution.py:990
  747.7 41.2 %copy-start.5 = (f32[2,256,2048]{2,1,0:T(8,128)S(1)}, f32[2,256,2048]{2,1,0:T(8,128)}, u32[]{:S(2)}) copy-start(f32[2,256,2048]{2,1,0:T(8,128)} %copy-done.2) | copy-start | bytes 12582916
  747.7 41.2 %copy-start.34 = (f32[2048]{0:T(1024)S(1)}, f32[2048]{0:T(1024)}, u32[]{:S(2)}) copy-start(f32[2048]{0:T(1024)} %param.20) | copy-start | bytes 24580
  747.7 41.2 %copy-start.38 = (f32[256]{0:T(256)S(1)}, f32[256]{0:T(256)}, u32[]{:S(2)}) copy-start(f32[256]{0:T(256)} %copy-done.37) | copy-start | bytes 3076
  747.7 41.2 %copy-start.40 = (f32[256]{0:T(256)S(1)}, f32[256]{0:T(256)}, u32[]{:S(2)}) copy-start(f32[256]{0:T(256)} %copy-done.39) | copy-start | bytes 3076
  803.6 35.3 %copy-start.12 = (f32[256,2048]{1,0:T(8,128)S(1)}, f32[256,2048]{1,0:T(8,128)}, u32[]{:S(2)}) copy-start(f32[256,2048]{1,0:T(8,128)} %copy-done.10) | copy-start | bytes 6291460
  803.6 37.3 %copy-start.17 = (f32[256,2048]{1,0:T(8,128)S(1)}, f32[256,2048]{1,0:T(8,128)}, u32[]{:S(2)}) copy-start(f32[256,2048]{1,0:T(8,128)} %get-tuple-element.84) | copy-start | bytes 6291460
  841.8 6.0 copy-start.9
  841.8 6.0 copy-start.16
  845.7 37.6 %collective-permute-start.21 = (bf16[384,2048]{1,0:T(8,128)(2,1)S(1)}, bf16[384,2048]{1,0:T(8,128)(2,1)S(1)}, u32[]{:S(2)}, u32[]{:S(2)}) collective-permute-start(bf16[384,2048]{1,0:T(8,128)(2,1)S(1)} %bitcast.197), channel_id=1, source_target_pairs={{0,16},{8,24},{16,0},{24,8},{1,17},{9,25},{17,1},{25,9},{2,18},{10... | collective-permute-start | bytes 4718600 | tf_op jit(solution)/shard_map/ppermute | solution.py:694
  846.3 32.1 %collective-permute-start.20 = (bf16[384,2048]{1,0:T(8,128)(2,1)S(1)}, bf16[384,2048]{1,0:T(8,128)(2,1)S(1)}, u32[]{:S(2)}, u32[]{:S(2)}) collective-permute-start(bf16[384,2048]{1,0:T(8,128)(2,1)S(1)} %bitcast.198), channel_id=1, source_target_pairs={{0,8},{8,0},{16,24},{24,16},{1,9},{9,1},{17,25},{25,17},{2,10},{10... | collective-permute-start | bytes 4718600 | tf_op jit(solution)/shard_map/ppermute | solution.py:693
  852.3 29.6 %copy-start.55 = (bf16[64,2048]{1,0:T(8,128)(2,1)S(1)}, bf16[64,2048]{1,0:T(8,128)(2,1)}, u32[]{:S(2)}) copy-start(bf16[64,2048]{1,0:T(8,128)(2,1)} %reduce-scatter.9.cloned.1.call-done) | copy-start | bytes 786436
  879.6 59.8 %collective-permute-start.17 = (bf16[384,2048]{1,0:T(8,128)(2,1)}, bf16[384,2048]{1,0:T(8,128)(2,1)S(1)}, u32[]{:S(2)}, u32[]{:S(2)}) collective-permute-start(bf16[384,2048]{1,0:T(8,128)(2,1)} %bitcast.51), channel_id=1, source_target_pairs={{0,16},{8,24},{16,0},{24,8},{1,17},{9,25},{17,1},{25,9},{2,18},{10... | collective-permute-start | bytes 4718600 | tf_op jit(solution)/shard_map/ppermute | solution.py:694
  881.9 63.1 %collective-permute-start.16 = (bf16[384,2048]{1,0:T(8,128)(2,1)}, bf16[384,2048]{1,0:T(8,128)(2,1)S(1)}, u32[]{:S(2)}, u32[]{:S(2)}) collective-permute-start(bf16[384,2048]{1,0:T(8,128)(2,1)} %bitcast.51), channel_id=1, source_target_pairs={{0,8},{8,0},{16,24},{24,16},{1,9},{9,1},{17,25},{25,17},{2,10},{10... | collective-permute-start | bytes 4718600 | tf_op jit(solution)/shard_map/ppermute | solution.py:693
  881.9 20.3 %collective-permute-start.10 = (bf16[64,2048]{1,0:T(8,128)(2,1)S(1)}, bf16[64,2048]{1,0:T(8,128)(2,1)S(1)}, u32[]{:S(2)}, u32[]{:S(2)}) collective-permute-start(bf16[64,2048]{1,0:T(8,128)(2,1)S(1)} %copy-done.55), channel_id=1, source_target_pairs={{2,0},{6,1},{10,10},{14,11},{18,20},{22,21},{26,30},{30,31}} | collective-permute-start | bytes 786440 | tf_op jit(solution)/shard_map/ppermute | solution.py:724
  882.6 19.7 %collective-permute-start.9 = (bf16[64,2048]{1,0:T(8,128)(2,1)S(1)}, bf16[64,2048]{1,0:T(8,128)(2,1)S(1)}, u32[]{:S(2)}, u32[]{:S(2)}) collective-permute-start(bf16[64,2048]{1,0:T(8,128)(2,1)S(1)} %copy-done.55), channel_id=1, source_target_pairs={{1,0},{5,1},{9,10},{13,11},{17,20},{21,21},{25,30},{29,31}} | collective-permute-start | bytes 786440 | tf_op jit(solution)/shard_map/ppermute | solution.py:724
  883.3 15.4 %collective-permute-start.8 = (bf16[64,2048]{1,0:T(8,128)(2,1)S(1)}, bf16[64,2048]{1,0:T(8,128)(2,1)S(1)}, u32[]{:S(2)}, u32[]{:S(2)}) collective-permute-start(bf16[64,2048]{1,0:T(8,128)(2,1)S(1)} %copy-done.55), channel_id=1, source_target_pairs={{0,0},{4,1},{8,10},{12,11},{16,20},{20,21},{24,30},{28,31}} | collective-permute-start | bytes 786440 | tf_op jit(solution)/shard_map/ppermute | solution.py:724
  898.7 30.4 %collective-permute-start.22 = (bf16[192,2048]{1,0:T(8,128)(2,1)S(1)}, bf16[192,2048]{1,0:T(8,128)(2,1)S(1)}, u32[]{:S(2)}, u32[]{:S(2)}) collective-permute-start(bf16[192,2048]{1,0:T(8,128)(2,1)S(1)} %slice.164), channel_id=1, source_target_pairs={{0,8},{8,0},{16,24},{24,16},{1,9},{9,1},{17,25},{25,17},{2,10},{10... | collective-permute-start | bytes 2359304 | tf_op jit(solution)/shard_map/ppermute | solution.py:695
  902.3 28.5 %collective-permute-start.23 = (bf16[192,2048]{1,0:T(8,128)(2,1)S(1)}, bf16[192,2048]{1,0:T(8,128)(2,1)S(1)}, u32[]{:S(2)}, u32[]{:S(2)}) collective-permute-start(bf16[192,2048]{1,0:T(8,128)(2,1)S(1)} %slice.165), channel_id=1, source_target_pairs={{0,16},{8,24},{16,0},{24,8},{1,17},{9,25},{17,1},{25,9},{2,18},{10... | collective-permute-start | bytes 2359304 | tf_op jit(solution)/shard_map/ppermute | solution.py:696
  902.3 2.1 collective-permute-start.11
  905.1 44.2 %collective-permute-start.13 = (bf16[256,2048]{1,0:T(8,128)(2,1)}, bf16[256,2048]{1,0:T(8,128)(2,1)S(1)}, u32[]{:S(2)}, u32[]{:S(2)}) collective-permute-start(bf16[256,2048]{1,0:T(8,128)(2,1)} %constant_dynamic-update-slice_fusion.5), channel_id=1, source_target_pairs={{0,16},{1,17},{10,26},{11,27},{20,4},{21,5},{30,14},{31,15}} | collective-permute-start | bytes 3145736 | tf_op jit(solution)/shard_map/ppermute | solution.py:735
  929.1 22.4 %collective-permute-start.12 = (bf16[256,2048]{1,0:T(8,128)(2,1)}, bf16[256,2048]{1,0:T(8,128)(2,1)S(1)}, u32[]{:S(2)}, u32[]{:S(2)}) collective-permute-start(bf16[256,2048]{1,0:T(8,128)(2,1)} %constant_dynamic-update-slice_fusion.5), channel_id=1, source_target_pairs={{0,8},{1,9},{10,2},{11,3},{20,28},{21,29},{30,22},{31,23}} | collective-permute-start | bytes 3145736 | tf_op jit(solution)/shard_map/ppermute | solution.py:735
  939.5 21.1 %collective-permute-start.18 = (bf16[192,2048]{1,0:T(8,128)(2,1)S(1)}, bf16[192,2048]{1,0:T(8,128)(2,1)S(1)}, u32[]{:S(2)}, u32[]{:S(2)}) collective-permute-start(bf16[192,2048]{1,0:T(8,128)(2,1)S(1)} %slice.162), channel_id=1, source_target_pairs={{0,8},{8,0},{16,24},{24,16},{1,9},{9,1},{17,25},{25,17},{2,10},{10... | collective-permute-start | bytes 2359304 | tf_op jit(solution)/shard_map/ppermute | solution.py:695
  945.1 17.7 %collective-permute-start.19 = (bf16[192,2048]{1,0:T(8,128)(2,1)S(1)}, bf16[192,2048]{1,0:T(8,128)(2,1)S(1)}, u32[]{:S(2)}, u32[]{:S(2)}) collective-permute-start(bf16[192,2048]{1,0:T(8,128)(2,1)S(1)} %slice.163), channel_id=1, source_target_pairs={{0,16},{8,24},{16,0},{24,8},{1,17},{9,25},{17,1},{25,9},{2,18},{10... | collective-permute-start | bytes 2359304 | tf_op jit(solution)/shard_map/ppermute | solution.py:696
  950.2 29.1 %collective-permute-start.14 = (bf16[128,2048]{1,0:T(8,128)(2,1)}, bf16[128,2048]{1,0:T(8,128)(2,1)S(1)}, u32[]{:S(2)}, u32[]{:S(2)}) collective-permute-start(bf16[128,2048]{1,0:T(8,128)(2,1)} %slice.159), channel_id=1, source_target_pairs={{16,24},{17,25},{26,18},{27,19},{4,12},{5,13},{14,6},{15,7}} | collective-permute-start | bytes 1572872 | tf_op jit(solution)/shard_map/ppermute | solution.py:735
  952.4 27.0 %collective-permute-start.15 = (bf16[128,2048]{1,0:T(8,128)(2,1)}, bf16[128,2048]{1,0:T(8,128)(2,1)}, u32[]{:S(2)}, u32[]{:S(2)}) collective-permute-start(bf16[128,2048]{1,0:T(8,128)(2,1)} %slice.160), channel_id=1, source_target_pairs={{8,24},{9,25},{2,18},{3,19},{28,12},{29,13},{22,6},{23,7}} | collective-permute-start | bytes 1572872 | tf_op jit(solution)/shard_map/ppermute | solution.py:735
  971.4 11.3 %copy-start.31 = (bf16[256,896]{0,1:T(8,128)(2,1)S(1)}, bf16[256,896]{0,1:T(8,128)(2,1)}, u32[]{:S(2)}) copy-start(bf16[256,896]{0,1:T(8,128)(2,1)} %reduce-scatter.11.cloned.1.call-done) | copy-start | bytes 1376260
  971.4 17.1 %collective-permute-start.5 = (bf16[256,896]{0,1:T(8,128)(2,1)}, bf16[256,896]{0,1:T(8,128)(2,1)S(1)}, u32[]{:S(2)}, u32[]{:S(2)}) collective-permute-start(bf16[256,896]{0,1:T(8,128)(2,1)} %reduce-scatter.11.cloned.1.call-done), channel_id=1, source_target_pairs={{0,16},{8,24},{16,0},{24,8},{1,17},{9,25},{17,1},{25,9},{2,18},{10... | collective-permute-start | bytes 1376264 | tf_op jit(solution)/shard_map/ppermute | solution.py:694
  979.3 9.3 collective-permute-start.4
  988.5 6.1 collective-permute-start.6
  988.7 6.7 collective-permute-start.7
  (30 other events, 78.3 us)
Sparse Core Ops, SparseCore 0:
  10.3 45.6 all-gather.6
  58.1 31.7 all-gather.8
  92.1 116.2 all-gather.12
  210.4 114.9 all-gather.10
  457.2 160.6 reduce-scatter.4
  620.0 127.5 reduce-scatter.6
  750.5 33.9 reduce-scatter.8
  803.1 45.5 reduce-scatter.10

commit v4 on v3

--- a/solution.py
+++ b/solution.py
@@ -48,7 +48,9 @@
     )
 
 
-def gather_job(source, target, scratch):
+def gather_job(sources, targets, scratch):
+    (source,) = sources
+    (target,) = targets
     outs, ins, here = scratch
     place = lax.axis_index("seq")
     one, two = over_one(place), over_two(place)
@@ -79,10 +81,12 @@
             copy.wait_send()
         own.wait()
 
-    return begin, middle, finish
-
-
-def scatter_job(parts, total, scratch):
+    return no_greeting, begin, middle, finish
+
+
+def scatter_job(sources, targets, scratch):
+    (parts,) = sources
+    (total,) = targets
     outs, ins, here, got_one, got_two, kept, own, last, summed = scratch
     place = lax.axis_index("seq")
     one, two = over_one(place), over_two(place)
@@ -131,54 +135,258 @@
             copy.wait_send()
         store.wait()
 
-    return begin, middle, finish
+    return no_greeting, begin, middle, finish
+
+
+def no_greeting(barrier):
+    return 0
+
+
+def nothing():
+    pass
+
+
+def greet(barrier, device):
+    pl.semaphore_signal(
+        barrier, inc=1, device_id=device, device_id_type=pl.DeviceIdType.MESH
+    )
+
+
+def deal_job(sources, targets, scratch):
+    (source,) = sources
+    (target,) = targets
+    outs, ins, here = scratch
+    rows = target.shape[0]
+    count = source.shape[0] // rows
+    place = lax.axis_index("seq")
+    shard = lax.axis_index("fsdp")
+    per = lax.axis_size("fsdp") // count
+    part = shard % per
+    is_source = shard // per == place
+    to_self = jnp.logical_and(is_source, shard // count == part)
+    origin = place * per + shard // count
+
+    def copy(j):
+        return pltpu.make_async_remote_copy(
+            src_ref=source.at[pl.ds(j * rows, rows)],
+            dst_ref=target,
+            send_sem=outs.at[j],
+            recv_sem=ins.at[0],
+            device_id={"fsdp": part * count + j},
+            device_id_type=pl.DeviceIdType.MESH,
+        )
+
+    def local(j):
+        return pltpu.make_async_copy(source.at[pl.ds(j * rows, rows)], target, here.at[0])
+
+    def greeting(barrier):
+        pl.when(origin != shard)(lambda: greet(barrier, {"fsdp": origin}))
+        return jnp.where(is_source, count, 0) - jnp.where(to_self, 1, 0)
+
+    def each(act_remote, act_local):
+        for j in range(count):
+            mine = part * count + j == shard
+            pl.when(jnp.logical_and(is_source, mine))(lambda j=j: act_local(local(j)))
+            pl.when(jnp.logical_and(is_source, jnp.logical_not(mine)))(
+                lambda j=j: act_remote(copy(j))
+            )
+
+    def begin():
+        each(lambda c: c.start(), lambda c: c.start())
+
+    def finish():
+        each(lambda c: c.wait_send(), lambda c: c.wait())
+        pl.when(origin != shard)(lambda: copy(0).wait_recv())
+
+    return greeting, begin, nothing, finish
+
+
+def home_job(sources, targets, scratch):
+    (source,) = sources
+    (target,) = targets
+    outs, ins, here = scratch
+    rows = source.shape[0]
+    count = target.shape[0] // rows
+    place = lax.axis_index("seq")
+    shard = lax.axis_index("fsdp")
+    per = lax.axis_size("fsdp") // count
+    piece = shard % count
+    owner = place * per + shard // count
+    spot = pl.ds(pl.multiple_of(piece * rows, rows), rows)
+
+    def copy(s):
+        return pltpu.make_async_remote_copy(
+            src_ref=source,
+            dst_ref=target.at[spot],
+            send_sem=outs.at[s],
+            recv_sem=ins.at[piece],
+            device_id={"seq": s, "fsdp": owner},
+            device_id_type=pl.DeviceIdType.MESH,
+        )
+
+    def arrival(j):
+        return pltpu.make_async_remote_copy(
+            src_ref=source,
+            dst_ref=target.at[pl.ds(j * rows, rows)],
+            send_sem=outs.at[0],
+            recv_sem=ins.at[j],
+            device_id={"seq": place, "fsdp": owner},
+            device_id_type=pl.DeviceIdType.MESH,
+        )
+
+    own = pltpu.make_async_copy(source, target.at[spot], here.at[0])
+
+    def is_self(s):
+        return jnp.logical_and(owner == shard, place == s)
+
+    def comes_from(j):
+        return shard // per, (shard % per) * count + j
+
+    def from_self(j):
+        seq, fsdp = comes_from(j)
+        return jnp.logical_and(seq == place, fsdp == shard)
+
+    def greeting(barrier):
+        for j in range(count):
+            seq, fsdp = comes_from(j)
+            pl.when(jnp.logical_not(from_self(j)))(
+                lambda seq=seq, fsdp=fsdp: greet(barrier, {"seq": seq, "fsdp": fsdp})
+            )
+        return jnp.where(owner == shard, count - 1, count)
+
+    def begin():
+        pl.when(owner == shard)(own.start)
+        for s in range(count):
+            pl.when(jnp.logical_not(is_self(s)))(lambda s=s: copy(s).start())
+
+    def finish():
+        pl.when(owner == shard)(own.wait)
+        for s in range(count):
+            pl.when(jnp.logical_not(is_self(s)))(lambda s=s: copy(s).wait_send())
+        for j in range(count):
+            pl.when(jnp.logical_not(from_self(j)))(lambda j=j: arrival(j).wait_recv())
+
+    return greeting, begin, nothing, finish
+
+
+def own_job(sources, targets, scratch):
+    (here,) = scratch
+    place = lax.axis_index("seq")
+    count = lax.axis_size("seq")
+    part = targets[0].shape[1]
+    copies = []
+    for c, target in enumerate(targets):
+        for k, source in enumerate(sources):
+            start = place * (source.shape[0] // count) + c * part
+            spot = pl.ds(pl.multiple_of(start, part), part)
+            copies.append(
+                pltpu.make_async_copy(
+                    source.at[spot], target.at[k], here.at[c * len(sources) + k]
+                )
+            )
+
+    def begin():
+        for copy in copies:
+            copy.start()
+
+    def finish():
+        for copy in copies:
+            copy.wait()
+
+    return no_greeting, begin, nothing, finish
+
+
+MAKERS = {
+    "gather": gather_job,
+    "scatter": scatter_job,
+    "deal": deal_job,
+    "home": home_job,
+    "own": own_job,
+}
 
 
 def job_scratch(job):
-    kind, array = job
+    kind, *arrays = job
+    if kind == "scatter":
+        _, rows, width = arrays[0].shape
+        halves = pltpu.VMEM((2, rows // 2, width), BF16)
+        return [
+            pltpu.SemaphoreType.DMA((6,)),
+            pltpu.SemaphoreType.DMA((6,)),
+            pltpu.SemaphoreType.DMA((4,)),
+            halves,
+            halves,
+            halves,
+            pltpu.VMEM((rows, width), BF16),
+            halves,
+            pltpu.VMEM((rows, width), F32),
+        ]
+    if kind == "own":
+        return [pltpu.SemaphoreType.DMA((CHUNKS * len(arrays),))]
+    return [
+        pltpu.SemaphoreType.DMA((4,)),
+        pltpu.SemaphoreType.DMA((4,)),
+        pltpu.SemaphoreType.DMA((1,)),
+    ]
+
+
+def job_results(job):
+    kind, *arrays = job
+    shape = arrays[0].shape
     if kind == "gather":
-        return [
-            pltpu.SemaphoreType.DMA((4,)),
-            pltpu.SemaphoreType.DMA((4,)),
-            pltpu.SemaphoreType.DMA((1,)),
-        ]
-    _, rows, width = array.shape
-    halves = pltpu.VMEM((2, rows // 2, width), BF16)
+        return [jax.ShapeDtypeStruct((4,) + shape, BF16)]
+    if kind == "scatter":
+        return [jax.ShapeDtypeStruct(shape[1:], F32)]
+    if kind == "deal":
+        return [jax.ShapeDtypeStruct((shape[0] // 4,) + shape[1:], BF16)]
+    if kind == "home":
+        return [jax.ShapeDtypeStruct((shape[0] * 4,) + shape[1:], BF16)]
+    part = shape[0] // lax.axis_size("seq") // CHUNKS
+    return [jax.ShapeDtypeStruct((len(arrays), part) + shape[1:], BF16)] * CHUNKS
+
+
+def plain_job(job):
+    kind, *arrays = job
+    seqs = lax.axis_size("seq")
+    shards = lax.axis_size("fsdp")
+    per = shards // seqs
+    ends = [(s, h, s * shards + s * per + h) for s in range(seqs) for h in range(per)]
+    if kind == "gather":
+        return [lax.all_gather(arrays[0], "seq", axis=0)]
+    if kind == "scatter":
+        return [lax.psum_scatter(arrays[0], "seq", scatter_dimension=0).astype(F32)]
+    if kind == "deal":
+        rows = arrays[0].shape[0] // seqs
+        total = None
+        for j in range(seqs):
+            moves = [(end, s * shards + h * seqs + j) for s, h, end in ends]
+            got = lax.ppermute(arrays[0][j * rows : (j + 1) * rows], ("seq", "fsdp"), moves)
+            total = got if total is None else total + got
+        return [total]
+    if kind == "home":
+        held = []
+        for j in range(seqs):
+            moves = [(s * shards + h * seqs + j, end) for s, h, end in ends]
+            held.append(lax.ppermute(arrays[0], ("seq", "fsdp"), moves))
+        return [lax.psum(jnp.concatenate(held, axis=0), "seq")]
+    own_rows = arrays[0].shape[0] // seqs
+    part = own_rows // CHUNKS
+    start = lax.axis_index("seq") * own_rows
     return [
-        pltpu.SemaphoreType.DMA((6,)),
-        pltpu.SemaphoreType.DMA((6,)),
-        pltpu.SemaphoreType.DMA((4,)),
-        halves,
-        halves,
-        halves,
-        pltpu.VMEM((rows, width), BF16),
-        halves,
-        pltpu.VMEM((rows, width), F32),
+        jnp.stack([lax.dynamic_slice_in_dim(w, start + c * part, part, 0) for w in arrays])
+        for c in range(CHUNKS)
     ]
 
 
-def job_result(job):
-    kind, array = job
-    if kind == "gather":
-        return jax.ShapeDtypeStruct((4,) + array.shape, BF16)
-    return jax.ShapeDtypeStruct(array.shape[1:], F32)
-
-
-def plain_job(job):
-    kind, array = job
-    if kind == "gather":
-        return lax.all_gather(array, "seq", axis=0)
-    return lax.psum_scatter(array, "seq", scatter_dimension=0).astype(F32)
-
-
-def meet():
+def meet(greetings):
     place = lax.axis_index("seq")
     barrier = pltpu.get_barrier_semaphore()
     for device in (over_one(place), over_two(place)):
-        pl.semaphore_signal(
-            barrier, inc=1, device_id={"seq": device}, device_id_type=pl.DeviceIdType.MESH
-        )
-    pl.semaphore_wait(barrier, 2)
+        greet(barrier, {"seq": device})
+    peers = 2
+    for greeting in greetings:
+        peers = peers + greeting(barrier)
+    pl.semaphore_wait(barrier, peers)
 
 
 def call(
@@ -186,54 +394,62 @@
     grid=(), scratch=(), cost=None, name=None,
 ):
     plain = lax.axis_size("seq") != 4
-    results = [plain_job(job) for job in jobs] if plain else []
+    results = [v for job in jobs for v in plain_job(job)] if plain else []
     inside = [] if plain else jobs
     extra = [] if after is None else [after]
     job_shapes = [job_scratch(job) for job in inside]
+    job_outs = [job_results(job) for job in inside]
     n_in = len(operands)
     n_out = len(out_shape)
 
     def kernel(*refs):
-        ins = refs[:n_in]
-        rest = refs[n_in + len(extra) :]
-        sources, rest = rest[: len(inside)], rest[len(inside) :]
-        outs, rest = rest[:n_out], rest[n_out:]
-        targets, rest = rest[: len(inside)], rest[len(inside) :]
-        held, rest = rest[: len(scratch)], rest[len(scratch) :]
-        phases = []
-        for job, source, target, shapes in zip(inside, sources, targets, job_shapes):
-            mine, rest = rest[: len(shapes)], rest[len(shapes) :]
-            make = gather_job if job[0] == "gather" else scatter_job
-            phases.append(make(source, target, mine))
+        refs = list(refs)
+
+        def take(count):
+            taken, refs[:] = refs[:count], refs[count:]
+            return taken
+
+        ins = take(n_in)
+        take(len(extra))
+        sources = [take(len(job) - 1) for job in inside]
+        outs = take(n_out)
+        targets = [take(len(shapes)) for shapes in job_outs]
+        held = take(len(scratch))
+        phases = [
+            MAKERS[job[0]](source, target, take(len(shapes)))
+            for job, source, target, shapes in zip(inside, sources, targets, job_shapes)
+        ]
 
         def hook(k):
             if k == 0 and phases:
-                meet()
+                meet([phase[0] for phase in phases])
             for phase in phases:
-                phase[k]()
+                phase[k + 1]()
 
         body(hook, ins, outs, held)
 
     given = {}
     if inside:
         given = {"collective_id": number, "has_side_effects": True}
+    arrays = [array for job in inside for array in job[1:]]
+    shapes = [shape for shapes in job_outs for shape in shapes]
     made = pl.pallas_call(
         kernel,
         grid=grid,
-        out_shape=tuple(out_shape) + tuple(job_result(job) for job in inside),
-        in_specs=list(in_specs) + [ANY] * (len(extra) + len(inside)),
-        out_specs=tuple(out_specs) + (ANY,) * len(inside),
+        out_shape=tuple(out_shape) + tuple(shapes),
+        in_specs=list(in_specs) + [ANY] * (len(extra) + len(arrays)),
+        out_specs=tuple(out_specs) + (ANY,) * len(shapes),
         scratch_shapes=list(scratch) + [shape for shapes in job_shapes for shape in shapes],
         compiler_params=pltpu.CompilerParams(vmem_limit_bytes=VMEM_LIMIT, **given),
         cost_estimate=cost,
         name=name,
-    )(*operands, *extra, *[job[1] for job in inside])
-    return made[:n_out], list(made[n_out:]) + results
+    )(*operands, *extra, *arrays)
+    return list(made[:n_out]), list(made[n_out:]) + results
 
 
 def transfer(jobs, number, after=None):
     if lax.axis_size("seq") != 4:
-        return [plain_job(job) for job in jobs]
+        return [v for job in jobs for v in plain_job(job)]
 
     def body(hook, ins, outs, held):
         for k in range(3):
@@ -481,7 +697,7 @@
 
 def hooked(hook, step, steps, work):
     pl.when(step == 0)(lambda: hook(0))
-    pl.when(step == (2 * steps) // 3)(lambda: hook(1))
+    pl.when(step == (3 * steps) // 4)(lambda: hook(1))
     work()
     pl.when(step == steps - 1)(lambda: hook(2))
 
@@ -677,69 +893,53 @@
     )(place, parts, *held)
 
 
-def ring_places(count):
-    return (
-        [(i, i ^ 1) for i in range(count)],
-        [(i, i ^ 2) for i in range(count)],
-    )
-
-
-def seq_gather(rows):
-    count = lax.axis_size("seq")
-    if count != 4:
-        return lax.all_gather(rows, "seq", axis=0)
-    over_one, over_two = ring_places(count)
-    half = rows.shape[0] // 2
-    one = lax.ppermute(rows, "seq", over_one)
-    two = lax.ppermute(rows, "seq", over_two)
-    top = lax.ppermute(two[:half], "seq", over_one)
-    low = lax.ppermute(one[half:], "seq", over_two)
-    return jnp.concatenate([rows, one, two, top, low], axis=0).reshape(
-        (count,) + rows.shape
-    )
-
-
-def seq_spread(rows):
-    count = lax.axis_size("seq")
-    parts = seq_gather(rows)
-    if count != 4:
-        return parts
-    place = lax.axis_index("seq")
-    return jnp.stack(
-        [lax.dynamic_index_in_dim(parts, place ^ j, 0, keepdims=False) for j in range(count)]
-    )
-
-
-def out_home(sums):
-    seqs = lax.axis_size("seq")
-    shards = lax.axis_size("fsdp")
-    per = shards // seqs
-    held = []
-    for j in range(seqs):
-        moves = [
-            (s * shards + h * seqs + j, s * shards + s * per + h)
-            for s in range(seqs)
-            for h in range(per)
-        ]
-        held.append(lax.ppermute(sums, ("seq", "fsdp"), moves))
-    held = jnp.concatenate(held, axis=0)
-    if seqs != 4:
-        return lax.psum(held, "seq")
-
-    def hop(values, start, end):
-        moves = [
-            ((s ^ start) * shards + s * per + h, (s ^ end) * shards + s * per + h)
-            for s in range(seqs)
-            for h in range(per)
-        ]
-        return lax.ppermute(values, ("seq", "fsdp"), moves)
-
-    half = held.shape[0] // 2
-    one = hop(held, 0, 1)
-    two = hop(held, 0, 2)
-    top = hop(two[:half], 2, 3)
-    low = hop(one[half:], 1, 3)
-    return held + one + two + jnp.concatenate([top, low], axis=0)
+def place_heads_kernel(place_ref, parts_ref, query_ref, key_ref, value_ref, rest_ref):
+    edge = query_ref.shape[1]
+    width = key_ref.shape[1]
+    part = parts_ref[0].astype(F32)
+    query_ref[...] = part[:, :edge]
+    key_ref[...] = part[:, edge : edge + width]
+    value_ref[...] = part[:, edge + width : edge + 2 * width]
+    rest = part[:, edge + 2 * width :]
+
+    @pl.when(pl.program_id(0) == 0)
+    def _():
+        rest_ref[...] = rest
+
+    @pl.when(pl.program_id(0) > 0)
+    def _():
+        rest_ref[...] += rest
+
+
+def place_heads(place, parts, edge, width):
+    seqs, rows, total = parts.shape
+    rest = total - edge - 2 * width
+
+    def column_spec(size):
+        return pl.BlockSpec((rows, size), lambda j, at: (0, jnp.bitwise_xor(at[0], j)))
+
+    return pl.pallas_call(
+        place_heads_kernel,
+        out_shape=[
+            jax.ShapeDtypeStruct((rows, seqs * edge), F32),
+            jax.ShapeDtypeStruct((rows, seqs * width), F32),
+            jax.ShapeDtypeStruct((rows, seqs * width), F32),
+            jax.ShapeDtypeStruct((rows, rest), F32),
+        ],
+        grid_spec=pltpu.PrefetchScalarGridSpec(
+            num_scalar_prefetch=1,
+            grid=(seqs,),
+            in_specs=[pl.BlockSpec((1, rows, total), lambda j, at: (j, 0, 0))],
+            out_specs=[
+                column_spec(edge),
+                column_spec(width),
+                column_spec(width),
+                pl.BlockSpec((rows, rest), lambda j, at: (0, 0)),
+            ],
+        ),
+        compiler_params=pltpu.CompilerParams(vmem_limit_bytes=VMEM_LIMIT),
+        name="place_heads",
+    )(place, parts)
 
 
 def scale_of(values):
@@ -825,30 +1025,16 @@
         axis=1,
     )
     qkv_weight = lax.all_gather(qkv_own, "fsdp", axis=0, tiled=True)
-    per = shards // seqs
-    piece = out_weight.shape[0] // seqs
-    out_own = None
-    for j in range(seqs):
-        moves = [
-            (s * shards + s * per + h, s * shards + h * seqs + j)
-            for s in range(seqs)
-            for h in range(per)
-        ]
-        got = lax.ppermute(out_weight[j * piece : (j + 1) * piece], ("seq", "fsdp"), moves)
-        out_own = got if out_own is None else out_own + got
+    start = [
+        ("gather", normal_in[0]),
+        ("deal", out_weight),
+        ("own", gate_weight, up_weight, down_weight),
+    ]
+    normal_0, out_own, *ffn_own = transfer(start, 1)
     out_rows = lax.all_gather(out_own, "fsdp", axis=0, tiled=True)
     hidden_own = gate_weight.shape[0] // seqs
     part = hidden_own // CHUNKS
-    ffn_weights = []
-    for c in range(CHUNKS):
-        start = place * hidden_own + c * part
-        mine = jnp.stack(
-            [
-                lax.dynamic_slice_in_dim(w, start, part, 0)
-                for w in (gate_weight, up_weight, down_weight)
-            ]
-        )
-        ffn_weights.append(lax.all_gather(mine, "fsdp", axis=0))
+    ffn_weights = [lax.all_gather(own, "fsdp", axis=0) for own in ffn_own]
 
     def project(full):
         return dot(full.reshape(flat), qkv_weight).astype(BF16).reshape(seqs, rows, -1)
@@ -866,7 +1052,7 @@
     normal_full = [None] * slots
     cot_full = [None] * slots
     mid_full = [None] * slots
-    (normal_full[0],) = transfer([("gather", normal_in[0])], 1)
+    normal_full[0] = normal_0
     qkv_0 = project(normal_full[0])
     (mixed_0, lse_0), (normal_full[1],) = heads(
         0, qkv_0, [("gather", normal_in[1])], 2, normal_full[0]
@@ -927,9 +1113,6 @@
     grads_1, (mid_total_1,) = grad_step(
         1, [("scatter", pulled[1].reshape(chunked))], 10, acts[1][1]
     )
-    ffn_sums.append(
-        lax.psum_scatter(follow(grads_1, ffn_sums), "fsdp", scatter_dimension=0)
-    )
     res_cot_1, low_1, ffn_gain_1 = pull_mid(1, mid_total_1)
     grad_ffn_gain = ffn_gain_0 + ffn_gain_1
 
@@ -947,19 +1130,19 @@
     dqkv_0, heads_gain_0, (res_full_1,) = back(
         0, res_full_0.reshape(flat), [("gather", low_1)], 11, grads_1
     )
+    ffn_sums.append(
+        lax.psum_scatter(follow(grads_1, [*ffn_sums, dqkv_0]), "fsdp", scatter_dimension=0)
+    )
     dqkv_1, heads_gain_1, (in_total_0,) = back(
         1, res_full_1.reshape(flat), [("scatter", pull_heads(dqkv_0))], 12, dqkv_0
     )
     head_gain = heads_gain_0 + heads_gain_1
     dqkv = [dqkv_0, dqkv_1]
     res_full = [v.reshape(flat) for v in (res_full_0, res_full_1)]
-    out_1, (in_total_1,) = leave_ffn(1, [("scatter", pull_heads(dqkv_1))], 13, dqkv_1)
-    (out_total_1,) = transfer([("scatter", out_1)], 14, out_1)
-
-    output = [
-        (live[b] * (hidden_res[b] + total)).astype(BF16)
-        for b, total in enumerate((out_total_0, out_total_1))
-    ]
+    out_1, (in_total_1, ffn_parts_0) = leave_ffn(
+        1, [("scatter", pull_heads(dqkv_1)), ("gather", ffn_sums[0])], 13, dqkv_1
+    )
+
     grad_tokens = []
     grad_attn_gain = 0.0
     for b, (in_cot, cot) in enumerate(((in_total_0, res_cot_0), (in_total_1, res_cot_1))):
@@ -968,41 +1151,59 @@
         grad_tokens.append((cot + pull).astype(BF16))
 
     out_grads = sum(dot(attended[b], res_full[b], TN) for b in range(slots)).astype(BF16)
-    out_grads = follow(out_grads, ffn_sums[-1:])
-    out_sums = lax.psum_scatter(out_grads, "fsdp", scatter_dimension=0, tiled=True)
-    grad_out = out_home(out_sums).astype(F32)
-
+    held = model // shards
+    piece = out_grads.shape[0] // shards
+    blocks = held // piece
+    out_grads = jnp.swapaxes(out_grads.reshape(shards, piece, blocks, model // blocks), 1, 2)
     head_sums = jnp.pad(
-        (head_gain[:, :HEAD] + head_gain[:, HEAD:]).reshape(2, shards, 1, HEAD // shards),
-        ((0, 0), (0, 0), (0, 0), (0, model // shards - HEAD // shards)),
+        (head_gain[:, :HEAD] + head_gain[:, HEAD:]).reshape(2, shards, HEAD // shards),
+        ((0, 0), (0, 0), (0, held - HEAD // shards)),
     ).reshape(2, model)
     gain_columns = jnp.stack(
         [grad_attn_gain, grad_ffn_gain, head_sums[0], head_sums[1]], axis=1
     ).astype(BF16)
-    qkv_grads = jnp.concatenate(
+    attn_grads = jnp.concatenate(
         [
             sum(dot(normal_full[b].reshape(flat), dqkv[b], TN) for b in range(slots)).astype(BF16),
             jnp.pad(gain_columns, ((0, 0), (0, 124))),
+            out_grads.reshape(model, model // blocks),
         ],
         axis=1,
     )
-    qkv_grads = follow(qkv_grads, [out_sums])
-    qkv_sums = lax.psum_scatter(qkv_grads, "fsdp", scatter_dimension=0, tiled=True)
-    qkv_all = jnp.moveaxis(seq_spread(qkv_sums), 0, 1).astype(F32)
-    held = qkv_all.shape[0]
+    attn_sums = lax.psum_scatter(
+        follow(attn_grads, ffn_sums[1:]), "fsdp", scatter_dimension=0, tiled=True
+    )
+    out_edge = attn_sums.shape[1] - model // blocks
+    out_sums = jnp.swapaxes(
+        attn_sums[:, out_edge:].reshape(blocks, piece, model // blocks), 0, 1
+    ).reshape(piece, model)
+
+    out_total_1, ffn_parts_1 = transfer(
+        [("scatter", out_1), ("gather", ffn_sums[1])], 14, in_total_1
+    )
+    output = [
+        (live[b] * (hidden_res[b] + total)).astype(BF16)
+        for b, total in enumerate((out_total_0, out_total_1))
+    ]
+    ffn_grad = ()
+    for c, parts in enumerate((ffn_parts_0, ffn_parts_1)):
+        ffn_grad = place_parts(order, parts.reshape(seqs, 3, part, model), c, ffn_grad)
+    ffn_grad = [v.reshape(seqs * hidden_own, model) for v in ffn_grad]
+
+    heads_all, grad_out = transfer(
+        [("gather", attn_sums[:, :out_edge]), ("home", out_sums)], 15, out_total_1
+    )
     edge = hq * HEAD
-    kv_edge = edge + hkv_held * HEAD
-    last_edge = kv_edge + hkv_held * HEAD
-    grad_query = qkv_all[..., :edge].reshape(held, query_width)
-    grad_key = qkv_all[..., edge : edge + hkv * HEAD].reshape(held, kv_width)
-    grad_value = qkv_all[..., kv_edge : kv_edge + hkv * HEAD].reshape(held, kv_width)
-    gain_sums = jnp.sum(qkv_all[..., last_edge : last_edge + 4], axis=1)
-
-    ffn_grad = ()
-    for c in range(CHUNKS):
-        parts = seq_gather(ffn_sums[c]).reshape(seqs, 3, part, model)
-        ffn_grad = place_parts(order, parts, c, ffn_grad)
-    ffn_grad = [v.reshape(seqs * hidden_own, model) for v in ffn_grad]
+    width = hkv_held * HEAD
+    if hkv == hkv_held:
+        grad_query, grad_key, grad_value, gain_sums = place_heads(order, heads_all, edge, width)
+    else:
+        heads_all = jnp.moveaxis(heads_all, 0, 1).astype(F32)
+        last = edge + width
+        grad_query = heads_all[..., :edge].reshape(held, query_width)
+        grad_key = heads_all[..., edge : edge + hkv * HEAD].reshape(held, kv_width)
+        grad_value = heads_all[..., last : last + hkv * HEAD].reshape(held, kv_width)
+        gain_sums = jnp.sum(heads_all[..., last + width :], axis=1)
 
     return (
         jnp.stack(output),
@@ -1013,7 +1214,7 @@
         grad_value,
         gain_sums[: HEAD // shards, 2],
         gain_sums[: HEAD // shards, 3],
-        grad_out,
+        grad_out.astype(F32),
         gain_sums[:, 1],
         ffn_grad[0],
         ffn_grad[1],

time: 1050 us -> 1100 us (1.048); the launches traced: 1030 us -> 1100 us
  Pallas kernels: 643 us -> 931 us
  waiting for transfers between devices: 154 us -> 13 us
  starting transfers between devices: 43.3 us -> 0.28 us
  local copies, waits for them, and re-layouts: 57.9 us -> 27 us
    pallas_call x15 -> x17, Pallas kernels: 628 us -> 914 us  [the longest x16 909 us: call(): pl.pallas_call(kernel, grid=grid, out_shape=tuple(out_shape) + tuple(shap...]
    ppermute x24 -> x0, waiting for transfers between devices: 85.7 us -> none  [the longest x3 31.3 us: seq_gather(): top = lax.ppermute(two[:half], 'seq', over_one)]
    reduce_scatter x1, waiting for transfers between devices: 62.9 us -> 0.02 us  [on_device(): ffn_sums = [lax.psum_scatter(grads_0, 'fsdp', scatter_dimension=0)]]
    ppermute x24 -> x0, starting transfers between devices: 42.8 us -> none  [the longest x4 12.5 us: out_home(): held.append(lax.ppermute(sums, ('seq', 'fsdp'), moves))]
    unnamed x145 -> x112, local copies, waits for them, and re-layouts: 32.4 us -> 11.6 us
    all_gather x2, waiting for transfers between devices: 0.01 us -> 11.6 us  [on_device(): ffn_weights = [lax.all_gather(own, 'fsdp', axis=0) for own in ffn_own]]
  transfers between devices with their start and end apart: 32 -> 7, of which waited for: 10 -> 1; matrix products, arithmetic and copies ran while one was open for 12% -> 10% of each run, Pallas kernels for 51% -> 66%
where the time goes in v4:
time: 1100 us
  Pallas kernels  931 us (85%)
  matrix products  63.6 us (6%)
  other arithmetic  45.9 us (4%)
  local copies, waits for them, and re-layouts  27 us (2%)
  between operations  15.1 us (1%)
  waiting for transfers between devices  13 us (1%)
    pallas_call x16, Pallas kernels, call(): pl.pallas_call(kernel, grid=grid, out_shape=tuple(out_shape) + tuple(shap...  909 us
    dot_general x12, matrix products, dot(): return lax.dot_general(a, b, dims, preferred_element_type=F32)  63.6 us
  transfers between devices with their start and end apart: 7, of which 1 were waited for; matrix products, arithmetic and copies ran while one was open for 10% of the time, Pallas kernels for 66%

profile of v4, /device:TPU:6, one launch (start us, length us, event | category | flops | bytes accessed | tf_op | source)
XLA Modules:
  0.0 1095.8 jit_solution(14571215944651566140)
XLA Ops:
  7.2 1.2 copy-done
  8.4 0.9 constant_dynamic-slice_fusion
  10.2 2.1 convert_element_type.88
  12.7 0.8 multiply_multiply_fusion
  13.5 0.9 copy-done.2
  14.4 1.7 multiply_convert_fusion.4
  16.1 128.9 %transfer.4 = (bf16[4,256,2048]{2,1,0:T(8,128)(2,1)}, bf16[64,2048]{1,0:T(8,128)(2,1)}, bf16[3,128,2048]{2,1,0:T(8,128)(2,1)}, bf16[3,128,2048]{2,1,0:T(8,128)(2,1)}) custom-call(bf16[256,2048]{1,0:T(8,128)(2,1)} %get-tuple-element.148.refs_0_, bf16[256,2048]{1,0:T(8,128)(2,1)} %refs_1_.1, bf16[1024,2048]{1,0:T(8,128)(2,1)} %refs_2_.1, ...), custom_call_target="tpu_custom_call" | custom-call | tf_op jit(solution)/shard_map/transfer/pallas_call | solution.py:436
  148.4 2.0 copy-done.13
  150.4 1.6 fusion.7
  152.0 7.7 convolution_convert_fusion.5
  159.8 44.6 %attend.2 = (bf16[4,256,512]{2,1,0:T(8,128)(2,1)}, f32[8,1024,1]{2,1,0:T(8,128)}, bf16[4,256,2048]{2,1,0:T(8,128)(2,1)}) custom-call(s32[1]{0:T(128)} %get-tuple-element.163.refs_0_, bf16[4,256,768]{2,1,0:T(8,128)(2,1)} %bitcast.218, f32[1,128]{1,0:T(1,128)} %get-tuple-element.169.refs_2_.refs_4_, f32[1,128]{1,0:T(1,128)} %get-tuple-element.170.refs_3_.refs_5_, ...), custom_call_target="tpu_custom_call" | custom-call | flops 30064771072 | bytes 8388608 | tf_op jit(solution)/shard_map/attend/pallas_call | solution.py:436
  204.4 6.4 convolution_convert_fusion.1
  210.8 4.5 convolution_convert_fusion.4
  215.3 40.1 %attend.3 = (bf16[4,256,512]{2,1,0:T(8,128)(2,1)}, f32[8,1024,1]{2,1,0:T(8,128)}, f32[256,2048]{1,0:T(8,128)}) custom-call(s32[1]{0:T(128)} %get-tuple-element.164.refs_0_, bf16[4,256,768]{2,1,0:T(8,128)(2,1)} %bitcast.216, f32[1,128]{1,0:T(1,128)} %get-tuple-element.169.refs_2_.refs_4_, f32[1,128]{1,0:T(1,128)} %get-tuple-element.170.refs_3_.refs_5_, ...), custom_call_target="tpu_custom_call" | custom-call | flops 30064771072 | bytes 8388608 | tf_op jit(solution)/shard_map/attend/pallas_call | solution.py:436
  255.4 1.9 multiply_reduce_fusion.9
  257.3 1.3 copy-done.10
  258.6 1.2 multiply_convert_fusion.3.refs_1_
  259.9 65.2 %transfer.5 = (bf16[4,256,2048]{2,1,0:T(8,128)(2,1)}, bf16[4,256,2048]{2,1,0:T(8,128)(2,1)}) custom-call(bf16[4,256,512]{2,1,0:T(8,128)(2,1)} %get-tuple-element.72.refs_0_, bf16[256,2048]{1,0:T(8,128)(2,1)} %multiply_convert_fusion.3.refs_1_, bf16[256,2048]{1,0:T(8,128)(2,1)} %get-tuple-element.150.refs_2_), custom_call_target="tpu_custom_call" | custom-call | tf_op jit(solution)/shard_map/transfer/pallas_call | solution.py:436
  325.1 4.4 convolution_convert_fusion
  329.4 72.0 %ffn_both.4 = (bf16[3,1024,1024]{2,1,0:T(8,128)(2,1)}, f32[1024,2048]{1,0:T(8,128)}, f32[256,2048]{1,0:T(8,128)}, bf16[4,256,2048]{2,1,0:T(8,128)(2,1)}) custom-call(bf16[1024,2048]{1,0:T(8,128)(2,1)} %bitcast.189, bf16[1024,2048]{1,0:T(8,128)(2,1)} %bitcast.194, bf16[8,3,128,2048]{3,2,1,0:T(8,128)(2,1)} %bitcast.172, bf16[8,3,128,2048]{3,2,1,0:T(8,128)(2,1)} %bitcast.173, ...), custom_call_target="tpu_custom_call" | custom-call | flops 34359738368 | bytes 20971520 | tf_op jit(solution)/shard_map/ffn_both/pallas_call | solution.py:436
  401.4 2.0 multiply_reduce_fusion.8
  404.7 1.2 multiply_convert_fusion.2.refs_7_
  406.0 11.6 %all-gather.11.cloned.1.call-done = bf16[24,128,2048]{2,1,0:T(8,128)(2,1)} async-done(((bf16[3,128,2048]{2,1,0:T(8,128)(2,1)}), bf16[24,128,2048]{2,1,0:T(8,128)(2,1)}) %all-gather.11.cloned.1.call-update) | async-done | bytes 12582928 | tf_op jit(solution)/shard_map/all_gather | solution.py:1037
  417.6 45.7 %ffn_both.5 = (bf16[3,1024,1024]{2,1,0:T(8,128)(2,1)}, bf16[1024,2048]{1,0:T(8,128)(2,1)}, bf16[4,256,2048]{2,1,0:T(8,128)(2,1)}) custom-call(bf16[1024,2048]{1,0:T(8,128)(2,1)} %bitcast.191, bf16[1024,2048]{1,0:T(8,128)(2,1)} %bitcast.195, bf16[8,3,128,2048]{3,2,1,0:T(8,128)(2,1)} %bitcast.180, bf16[8,3,128,2048]{3,2,1,0:T(8,128)(2,1)} %bitcast.181, ...), custom_call_target="tpu_custom_call" | custom-call | flops 34359738368 | bytes 20971520 | tf_op jit(solution)/shard_map/ffn_both/pallas_call | solution.py:436
  463.3 44.4 %ffn_both.6 = (bf16[3,1024,1024]{2,1,0:T(8,128)(2,1)}, f32[1024,2048]{1,0:T(8,128)}, f32[256,2048]{1,0:T(8,128)}) custom-call(bf16[1024,2048]{1,0:T(8,128)(2,1)} %bitcast.204, bf16[1024,2048]{1,0:T(8,128)(2,1)} %bitcast.200, bf16[8,3,128,2048]{3,2,1,0:T(8,128)(2,1)} %bitcast.175, bf16[8,3,128,2048]{3,2,1,0:T(8,128)(2,1)} %bitcast.176, ...), custom_call_target="tpu_custom_call" | custom-call | flops 34359738368 | bytes 20971520 | tf_op jit(solution)/shard_map/ffn_both/pallas_call | solution.py:436
  507.8 2.9 multiply_reduce_fusion.1
  510.6 3.9 fusion.15
  514.5 42.2 %ffn_grads.2 = (bf16[8,3,128,2048]{3,2,1,0:T(8,128)(2,1)}, bf16[4,256,2048]{2,1,0:T(8,128)(2,1)}) custom-call(bf16[3,1024,1024]{2,1,0:T(8,128)(2,1)} %get-tuple-element.78.refs_6_.refs_0_, bf16[3,1024,1024]{2,1,0:T(8,128)(2,1)} %get-tuple-element.85.refs_1_.refs_6_.refs_0_, bf16[1024,2048]{1,0:T(8,128)(2,1)} %bitcast.192, bf16[1024,2048]{1,0:T(8,128)(2,1)} %bitcast.205, ...), custom_call_target="tpu_custom_call" | custom-call | flops 38654705664 | bytes 16777216 | tf_op jit(solution)/shard_map/ffn_grads/pallas_call | solution.py:436
  556.8 14.2 %ffn_down.2 = bf16[1024,2048]{1,0:T(8,128)(2,1)} custom-call(bf16[3,1024,1024]{2,1,0:T(8,128)(2,1)} %get-tuple-element.78.refs_6_.refs_0_, bf16[3,1024,1024]{2,1,0:T(8,128)(2,1)} %get-tuple-element.82.refs_5_.refs_1_.refs_0_, bf16[8,3,128,2048]{3,2,1,0:T(8,128)(2,1)} %bitcast.178, bf16[8,3,128,2048]{3,2,1,0:T(8,128)(2,1)} %bitcast.183, ...), custom_call_target="tpu_custom_call" | custom-call | flops 17179869184 | bytes 12582912 | tf_op jit(solution)/shard_map/ffn_down/pallas_call | solution.py:436
  571.0 43.2 %ffn_both.7 = (bf16[3,1024,1024]{2,1,0:T(8,128)(2,1)}, bf16[1024,2048]{1,0:T(8,128)(2,1)}, f32[256,2048]{1,0:T(8,128)}) custom-call(bf16[1024,2048]{1,0:T(8,128)(2,1)} %bitcast.206, bf16[1024,2048]{1,0:T(8,128)(2,1)} %bitcast.202, bf16[8,3,128,2048]{3,2,1,0:T(8,128)(2,1)} %bitcast.184, bf16[8,3,128,2048]{3,2,1,0:T(8,128)(2,1)} %bitcast.185, ...), custom_call_target="tpu_custom_call" | custom-call | flops 34359738368 | bytes 20971520 | tf_op jit(solution)/shard_map/ffn_both/pallas_call | solution.py:436
  614.3 42.6 %ffn_grads.3 = (bf16[8,3,128,2048]{3,2,1,0:T(8,128)(2,1)}, f32[256,2048]{1,0:T(8,128)}) custom-call(bf16[3,1024,1024]{2,1,0:T(8,128)(2,1)} %get-tuple-element.82.refs_5_.refs_1_.refs_0_, bf16[3,1024,1024]{2,1,0:T(8,128)(2,1)} %get-tuple-element.89.refs_1_.refs_6_, bf16[1024,2048]{1,0:T(8,128)(2,1)} %bitcast.193, bf16[1024,2048]{1,0:T(8,128)(2,1)} %bitcast.207, ...), custom_call_target="tpu_custom_call" | custom-call | flops 38654705664 | bytes 16777216 | tf_op jit(solution)/shard_map/ffn_grads/pallas_call | solution.py:436
  656.9 2.3 multiply_reduce_fusion
  659.7 5.2 convolution_convert_fusion.7
  664.9 2.3 fusion.14
  667.2 42.4 %attend_back.2 = (bf16[4,256,768]{2,1,0:T(8,128)(2,1)}, f32[2,128]{1,0:T(2,128)}, bf16[4,256,2048]{2,1,0:T(8,128)(2,1)}) custom-call(s32[1]{0:T(128)} %get-tuple-element.163.refs_0_, bf16[4,256,768]{2,1,0:T(8,128)(2,1)} %bitcast.219, bf16[4,256,512]{2,1,0:T(8,128)(2,1)} %bitcast.224, f32[8,1024,1]{2,1,0:T(8,128)} %get-tuple-element.91.refs_3_, ...), custom_call_target="tpu_custom_call" | custom-call | flops 47244640256 | bytes 8388608 | tf_op jit(solution)/shard_map/attend_back/pallas_call | solution.py:436
  710.9 4.7 fusion.21
  715.6 3.7 fusion.5
  719.3 3.8 reshape.322
  723.1 1.8 copy.60
  725.0 1.1 copy-done.20
  726.1 5.1 convolution_convert_fusion.6
  731.2 5.0 convolution_convert_fusion.3
  736.2 43.9 %attend_back.3 = (bf16[4,256,768]{2,1,0:T(8,128)(2,1)}, f32[2,128]{1,0:T(2,128)}, f32[256,2048]{1,0:T(8,128)}) custom-call(s32[1]{0:T(128)} %get-tuple-element.164.refs_0_, bf16[4,256,768]{2,1,0:T(8,128)(2,1)} %bitcast.217, bf16[4,256,512]{2,1,0:T(8,128)(2,1)} %bitcast.225, f32[8,1024,1]{2,1,0:T(8,128)} %get-tuple-element.96.refs_3_, ...), custom_call_target="tpu_custom_call" | custom-call | flops 47244640256 | bytes 8388608 | tf_op jit(solution)/shard_map/attend_back/pallas_call | solution.py:436
  780.9 8.0 convolution_convert_fusion.2
  789.0 3.7 fusion.20
  792.7 5.2 fusion.2
  797.9 88.8 %ffn_down.3 = (bf16[1024,2048]{1,0:T(8,128)(2,1)}, f32[256,2048]{1,0:T(8,128)}, bf16[4,384,2048]{2,1,0:T(8,128)(2,1)}) custom-call(bf16[3,1024,1024]{2,1,0:T(8,128)(2,1)} %get-tuple-element.85.refs_1_.refs_6_.refs_0_, bf16[3,1024,1024]{2,1,0:T(8,128)(2,1)} %get-tuple-element.89.refs_1_.refs_6_, bf16[8,3,128,2048]{3,2,1,0:T(8,128)(2,1)} %bitcast.179, ...), custom_call_target="tpu_custom_call" | custom-call | flops 17179869184 | bytes 12582912 | tf_op jit(solution)/shard_map/ffn_down/pallas_call | solution.py:436
  886.8 3.3 multiply_reduce_fusion.3
  890.5 5.9 fusion.4
  897.0 0.9 copy-done.12
  898.0 1.8 fusion.10
  899.8 8.7 place_parts.2
  908.5 4.0 fusion.12
  912.6 1.5 pad_maximum_fusion.1
  914.1 83.1 %transfer.6 = (f32[256,2048]{1,0:T(8,128)}, bf16[4,384,2048]{2,1,0:T(8,128)(2,1)}) custom-call(f32[256,2048]{1,0:T(8,128)} %get-tuple-element.99.refs_0_, bf16[4,256,2048]{2,1,0:T(8,128)(2,1)} %bitcast.160, bf16[384,2048]{1,0:T(8,128)(2,1)} %bitcast.163), custom_call_target="tpu_custom_call" | custom-call | tf_op jit(solution)/shard_map/transfer/pallas_call | solution.py:436
  997.2 8.7 place_parts.3
  1006.2 1.5 pad_maximum_fusion
  1007.7 1.0 slice.95
  1009.6 1.8 slice.94.refs_1_
  1011.4 68.3 %transfer.7 = (bf16[4,256,896]{2,1,0:T(8,128)(2,1)}, bf16[256,2048]{1,0:T(8,128)(2,1)}) custom-call(f32[256,2048]{1,0:T(8,128)} %get-tuple-element.102.refs_0_, bf16[256,896]{1,0:T(8,128)(2,1)} %slice.94.refs_1_, bf16[64,2048]{1,0:T(8,128)(2,1)} %bitcast.167), custom_call_target="tpu_custom_call" | custom-call | tf_op jit(solution)/shard_map/transfer/pallas_call | solution.py:436
  1079.7 4.2 place_heads.1
  1083.9 1.5 slice_reduce_fusion.2
  1085.4 1.8 slice_reduce_fusion
  1087.1 1.6 convert_element_type.112
  (153 shorter events, 11.0 us)
Async XLA Ops:
  7.2 1.2 copy-start
  7.2 144.8 %all-gather.7.cloned.1.call-start = ((), (), s32[]{:S(2)}) async-start(), calls=%async_computation.3 | async-start | bytes 3538944 | tf_op jit(solution)/shard_map/all_gather | solution.py:1027
  10.1 194.2 %all-gather.9.cloned.1.call-start = ((), (), s32[]{:S(2)}) async-start(), calls=%async_computation.4 | async-start | bytes 2359296 | tf_op jit(solution)/shard_map/all_gather | solution.py:1034
  12.3 2.1 copy-start.2
  12.3 2.1 copy-start.27
  13.5 2.6 copy-start.32
  13.5 2.6 copy-start.34
  145.0 1.5 copy-start.43
  145.1 1.4 copy-start.44
  145.1 2.1 copy-start.38
  145.1 2.7 copy-start.23
  145.1 184.3 %all-gather.13.cloned.1.call-start = ((), (), s32[]{:S(2)}) async-start(), calls=%async_computation.9 | async-start | bytes 14155776 | tf_op jit(solution)/shard_map/all_gather | solution.py:1037
  145.9 271.7 %all-gather.11.cloned.1.call-start = ((), (), s32[]{:S(2)}) async-start(), calls=%async_computation.8 | async-start | bytes 14155776 | tf_op jit(solution)/shard_map/all_gather | solution.py:1037
  146.4 563.2 %reduce-scatter.4.cloned.1.call-start = ((), (), s32[]{:S(2)}) async-start(), calls=%async_computation.5 | async-start | bytes 14155776 | tf_op jit(solution)/shard_map/reduce_scatter | solution.py:1110
  147.8 0.6 copy-start.30
  148.4 2.0 copy-start.13
  204.4 6.4 copy-start.46
  204.4 6.4 copy-start.49
  215.3 40.1 %copy-start.3 = (f32[2,256,2048]{2,1,0:T(8,128)S(1)}, f32[2,256,2048]{2,1,0:T(8,128)}, u32[]{:S(2)}) copy-start(f32[2,256,2048]{2,1,0:T(8,128)} %copy-done.2) | copy-start | bytes 12582916
  255.4 3.2 copy-start.26
  257.3 1.3 copy-start.10
  259.9 65.2 %copy-start.21 = (bf16[4,256,512]{2,1,0:T(8,128)(2,1)S(1)}, bf16[4,256,512]{2,1,0:T(8,128)(2,1)}, u32[]{:S(2)}) copy-start(bf16[4,256,512]{2,1,0:T(8,128)(2,1)} %get-tuple-element.72.refs_0_) | copy-start | bytes 3145732
  259.9 65.2 %copy-start.48 = (bf16[512,2048]{1,0:T(8,128)(2,1)S(1)}, bf16[512,2048]{1,0:T(8,128)(2,1)}, u32[]{:S(2)}) copy-start(bf16[512,2048]{1,0:T(8,128)(2,1)} %all-gather.9.cloned.1.call-done) | copy-start | bytes 6291460
  329.4 72.0 %copy-start.4 = (f32[2,256,2048]{2,1,0:T(8,128)S(1)}, f32[2,256,2048]{2,1,0:T(8,128)}, u32[]{:S(2)}) copy-start(f32[2,256,2048]{2,1,0:T(8,128)} %copy-done.2) | copy-start | bytes 12582916
  403.4 1.3 copy-start.7
  404.0 59.3 %copy-start.36 = (f32[256]{0:T(256)}, f32[256]{0:T(256)S(1)}, u32[]{:S(2)}) copy-start(f32[256]{0:T(256)S(1)} %get-tuple-element.160) | copy-start | bytes 3076
  463.3 44.4 %copy-start.11 = (f32[256,2048]{1,0:T(8,128)S(1)}, f32[256,2048]{1,0:T(8,128)}, u32[]{:S(2)}) copy-start(f32[256,2048]{1,0:T(8,128)} %copy-done.10) | copy-start | bytes 6291460
  507.7 2.9 copy-start.14
  556.8 339.6 %reduce-scatter.6.cloned.1.call-start = ((), (), s32[]{:S(2)}) async-start(), calls=%async_computation.6 | async-start | bytes 14155776 | tf_op jit(solution)/shard_map/reduce_scatter | solution.py:1134
  614.3 42.6 %copy-start.8 = (f32[256,2048]{1,0:T(8,128)S(1)}, f32[256,2048]{1,0:T(8,128)}, u32[]{:S(2)}) copy-start(f32[256,2048]{1,0:T(8,128)} %copy-done.7) | copy-start | bytes 6291460
  614.3 42.6 %copy-start.37 = (f32[256]{0:T(256)S(1)}, f32[256]{0:T(256)}, u32[]{:S(2)}) copy-start(f32[256]{0:T(256)} %copy-done.36) | copy-start | bytes 3076
  656.9 2.8 copy-start.18
  659.7 5.2 copy-start.15
  659.7 5.2 copy-start.17
  659.7 5.2 copy-start.39
  709.7 0.7 copy-start.29
  709.7 1.2 copy-start.24
  709.7 298.0 %reduce-scatter.8.cloned.1.call-start = ((), (), s32[]{:S(2)}) async-start(), calls=%async_computation.7 | async-start | bytes 6488064 | tf_op jit(solution)/shard_map/reduce_scatter | solution.py:1173
  710.9 4.7 copy-start.19
  710.9 4.7 copy-start.22
  723.1 2.9 copy-start.20
  726.1 5.1 copy-start.47
  726.1 5.1 copy-start.51
  736.2 43.9 %copy-start.42 = (f32[2,128]{1,0:T(2,128)S(1)}, f32[2,128]{1,0:T(2,128)}, u32[]{:S(2)}) copy-start(f32[2,128]{1,0:T(2,128)} %get-tuple-element.104) | copy-start | bytes 3076
  780.9 8.0 copy-start.45
  780.9 8.0 copy-start.52
  789.0 3.7 copy-start.50
  789.0 3.7 copy-start.53
  797.9 88.8 %copy-start.5 = (f32[2,256,2048]{2,1,0:T(8,128)S(1)}, f32[2,256,2048]{2,1,0:T(8,128)}, u32[]{:S(2)}) copy-start(f32[2,256,2048]{2,1,0:T(8,128)} %copy-done.2) | copy-start | bytes 12582916
  797.9 88.8 %copy-start.28 = (f32[2048]{0:T(1024)S(1)}, f32[2048]{0:T(1024)}, u32[]{:S(2)}) copy-start(f32[2048]{0:T(1024)} %param.20) | copy-start | bytes 24580
  797.9 88.8 %copy-start.33 = (f32[256]{0:T(256)S(1)}, f32[256]{0:T(256)}, u32[]{:S(2)}) copy-start(f32[256]{0:T(256)} %copy-done.32) | copy-start | bytes 3076
  797.9 88.9 %copy-start.35 = (f32[256]{0:T(256)S(1)}, f32[256]{0:T(256)}, u32[]{:S(2)}) copy-start(f32[256]{0:T(256)} %copy-done.34) | copy-start | bytes 3076
  896.4 0.7 copy-start.31
  896.4 1.6 copy-start.12
  899.8 8.7 copy-start.6
  899.8 8.7 copy-start.40
  899.8 8.7 copy-start.41
  997.2 8.7 copy-start.9
  997.2 8.7 copy-start.16
  1079.7 7.5 copy-start.25
  1079.7 9.0 copy-start.1
Sparse Core Ops, SparseCore 0:
  10.3 49.4 all-gather.6
  145.2 37.8 all-gather.8
  184.8 116.2 all-gather.12
  302.6 114.9 all-gather.10
  556.9 132.6 reduce-scatter.3
  709.8 132.1 reduce-scatter.5
  896.5 67.6 reduce-scatter.7

commit v5 on v4

--- a/solution.py
+++ b/solution.py
@@ -51,11 +51,12 @@
 def gather_job(sources, targets, scratch):
     (source,) = sources
     (target,) = targets
-    outs, ins, here = scratch
+    outs, ins, here, held = scratch
     place = lax.axis_index("seq")
     one, two = over_one(place), over_two(place)
     half = source.shape[0] // 2
-    own = pltpu.make_async_copy(source, target.at[0], here.at[0])
+    load = pltpu.make_async_copy(source, held, here.at[0])
+    store = pltpu.make_async_copy(held, target.at[0], here.at[1])
     first = send(source, target.at[1], one, outs.at[0], ins.at[0])
     second = send(source, target.at[2], two, outs.at[1], ins.at[1])
     top = pl.ds(0, half)
@@ -64,11 +65,13 @@
     fourth = send(target.at[1, low], target.at[3, low], two, outs.at[3], ins.at[3])
 
     def begin():
-        own.start()
         first.start()
         second.start()
+        load.start()
 
     def middle():
+        load.wait()
+        store.start()
         second.wait_recv()
         third.start()
         first.wait_recv()
@@ -79,7 +82,7 @@
         fourth.wait_recv()
         for copy in (first, second, third, fourth):
             copy.wait_send()
-        own.wait()
+        store.wait()
 
     return no_greeting, begin, middle, finish
 
@@ -270,30 +273,34 @@
 
 
 def own_job(sources, targets, scratch):
-    (here,) = scratch
+    loaded, stored, held = scratch
     place = lax.axis_index("seq")
     count = lax.axis_size("seq")
     part = targets[0].shape[1]
-    copies = []
+    loads = []
+    stores = []
     for c, target in enumerate(targets):
         for k, source in enumerate(sources):
             start = place * (source.shape[0] // count) + c * part
             spot = pl.ds(pl.multiple_of(start, part), part)
-            copies.append(
-                pltpu.make_async_copy(
-                    source.at[spot], target.at[k], here.at[c * len(sources) + k]
-                )
-            )
+            n = c * len(sources) + k
+            loads.append(pltpu.make_async_copy(source.at[spot], held.at[n], loaded.at[n]))
+            stores.append(pltpu.make_async_copy(held.at[n], target.at[k], stored.at[n]))
 
     def begin():
-        for copy in copies:
-            copy.start()
+        for load in loads:
+            load.start()
+
+    def middle():
+        for load, store in zip(loads, stores):
+            load.wait()
+            store.start()
 
     def finish():
-        for copy in copies:
-            copy.wait()
-
-    return no_greeting, begin, nothing, finish
+        for store in stores:
+            store.wait()
+
+    return no_greeting, begin, middle, finish
 
 
 MAKERS = {
@@ -322,12 +329,20 @@
             pltpu.VMEM((rows, width), F32),
         ]
     if kind == "own":
-        return [pltpu.SemaphoreType.DMA((CHUNKS * len(arrays),))]
-    return [
+        count = CHUNKS * len(arrays)
+        rows, width = arrays[0].shape
+        part = rows // lax.axis_size("seq") // CHUNKS
+        return [
+            pltpu.SemaphoreType.DMA((count,)),
+            pltpu.SemaphoreType.DMA((count,)),
+            pltpu.VMEM((count, part, width), BF16),
+        ]
+    moves = [
         pltpu.SemaphoreType.DMA((4,)),
         pltpu.SemaphoreType.DMA((4,)),
-        pltpu.SemaphoreType.DMA((1,)),
+        pltpu.SemaphoreType.DMA((2,)),
     ]
+    return moves + [pltpu.VMEM(arrays[0].shape, BF16)] if kind == "gather" else moves
 
 
 def job_results(job):
@@ -697,16 +712,15 @@
 
 def hooked(hook, step, steps, work):
     pl.when(step == 0)(lambda: hook(0))
-    pl.when(step == (3 * steps) // 4)(lambda: hook(1))
-    work()
+    work(lambda: pl.when(step == (3 * steps) // 5)(lambda: hook(1)))
     pl.when(step == steps - 1)(lambda: hook(2))
 
 
 def ffn_kernel(steps, hook, ins, outs, held):
-    hooked(hook, pl.program_id(0), steps, lambda: ffn_tile(*ins[:5], ins[5:], *outs))
-
-
-def ffn_tile(mid_ref, cot_ref, gate_ref, up_ref, down_ref, sums, acts_ref, pull_ref):
+    hooked(hook, pl.program_id(0), steps, lambda late: ffn_tile(late, *ins[:5], ins[5:], *outs))
+
+
+def ffn_tile(late, mid_ref, cot_ref, gate_ref, up_ref, down_ref, sums, acts_ref, pull_ref):
     model = mid_ref.shape[-1]
     hidden = acts_ref.shape[-1]
     gate_w = gate_ref[...].reshape(hidden, model)
@@ -716,6 +730,7 @@
     gate = dot(mid, gate_w, NT)
     up = dot(mid, up_w, NT)
     mids_cot = dot(cot_ref[...], down_w, NT)
+    late()
     sigmoid = jax.nn.sigmoid(gate)
     active = gate * sigmoid
     gate_cot = (mids_cot * up * sigmoid * (1.0 + gate * (1.0 - sigmoid))).astype(BF16)
@@ -780,7 +795,8 @@
             total = total + dot(act[0], other[...], TN)
         out_ref[...] = total.astype(BF16).reshape(out_ref.shape)
 
-    def work():
+    def work(late):
+        late()
         pl.when(kind < 2)(lambda: store(mids))
         pl.when(kind == 2)(lambda: store(cots))
 
@@ -822,7 +838,8 @@
     downs = ins[chunks:]
     (out_ref,) = outs
 
-    def work():
+    def work(late):
+        late()
         total = None
         for act, down in zip(acts, downs):
             hidden = act.shape[-1]
@@ -893,7 +910,10 @@
     )(place, parts, *held)
 
 
-def place_heads_kernel(place_ref, parts_ref, query_ref, key_ref, value_ref, rest_ref):
+def place_heads_kernel(
+    place_ref, parts_ref, query_w_ref, key_w_ref, value_w_ref,
+    query_ref, key_ref, value_ref, rest_ref, met_ref,
+):
     edge = query_ref.shape[1]
     width = key_ref.shape[1]
     part = parts_ref[0].astype(F32)
@@ -901,17 +921,27 @@
     key_ref[...] = part[:, edge : edge + width]
     value_ref[...] = part[:, edge + width : edge + 2 * width]
     rest = part[:, edge + 2 * width :]
+    met = jnp.zeros_like(met_ref)
+    for grad_ref, weight_ref in (
+        (query_ref, query_w_ref),
+        (key_ref, key_w_ref),
+        (value_ref, value_w_ref),
+    ):
+        product = grad_ref[...] * weight_ref[...].astype(F32)
+        met = met + jnp.sum(product, axis=1, keepdims=True)
 
     @pl.when(pl.program_id(0) == 0)
     def _():
         rest_ref[...] = rest
+        met_ref[...] = met
 
     @pl.when(pl.program_id(0) > 0)
     def _():
         rest_ref[...] += rest
-
-
-def place_heads(place, parts, edge, width):
+        met_ref[...] += met
+
+
+def place_heads(place, parts, edge, width, weights):
     seqs, rows, total = parts.shape
     rest = total - edge - 2 * width
 
@@ -925,21 +955,28 @@
             jax.ShapeDtypeStruct((rows, seqs * width), F32),
             jax.ShapeDtypeStruct((rows, seqs * width), F32),
             jax.ShapeDtypeStruct((rows, rest), F32),
+            jax.ShapeDtypeStruct((rows, 128), F32),
         ],
         grid_spec=pltpu.PrefetchScalarGridSpec(
             num_scalar_prefetch=1,
             grid=(seqs,),
-            in_specs=[pl.BlockSpec((1, rows, total), lambda j, at: (j, 0, 0))],
+            in_specs=[
+                pl.BlockSpec((1, rows, total), lambda j, at: (j, 0, 0)),
+                column_spec(edge),
+                column_spec(width),
+                column_spec(width),
+            ],
             out_specs=[
                 column_spec(edge),
                 column_spec(width),
                 column_spec(width),
                 pl.BlockSpec((rows, rest), lambda j, at: (0, 0)),
+                pl.BlockSpec((rows, 128), lambda j, at: (0, 0)),
             ],
         ),
         compiler_params=pltpu.CompilerParams(vmem_limit_bytes=VMEM_LIMIT),
         name="place_heads",
-    )(place, parts)
+    )(place, parts, *weights)
 
 
 def scale_of(values):
@@ -1113,6 +1150,8 @@
     grads_1, (mid_total_1,) = grad_step(
         1, [("scatter", pulled[1].reshape(chunked))], 10, acts[1][1]
     )
+    ffn_sums.append(lax.psum_scatter(grads_1, "fsdp", scatter_dimension=0))
+    out_1, _ = leave_ffn(1, [], 0, grads_1)
     res_cot_1, low_1, ffn_gain_1 = pull_mid(1, mid_total_1)
     grad_ffn_gain = ffn_gain_0 + ffn_gain_1
 
@@ -1127,27 +1166,25 @@
     def pull_heads(cots):
         return dot(cots, qkv_weight, NT).astype(BF16).reshape(chunked)
 
-    dqkv_0, heads_gain_0, (res_full_1,) = back(
-        0, res_full_0.reshape(flat), [("gather", low_1)], 11, grads_1
-    )
-    ffn_sums.append(
-        lax.psum_scatter(follow(grads_1, [*ffn_sums, dqkv_0]), "fsdp", scatter_dimension=0)
-    )
-    dqkv_1, heads_gain_1, (in_total_0,) = back(
-        1, res_full_1.reshape(flat), [("scatter", pull_heads(dqkv_0))], 12, dqkv_0
+    dqkv_0, heads_gain_0, (res_full_1, out_total_1) = back(
+        0, res_full_0.reshape(flat), [("gather", low_1), ("scatter", out_1)], 11, out_1
+    )
+    dqkv_1, heads_gain_1, (in_total_0, ffn_parts_0) = back(
+        1,
+        res_full_1.reshape(flat),
+        [("scatter", pull_heads(dqkv_0)), ("gather", ffn_sums[0])],
+        12,
+        dqkv_0,
     )
     head_gain = heads_gain_0 + heads_gain_1
     dqkv = [dqkv_0, dqkv_1]
     res_full = [v.reshape(flat) for v in (res_full_0, res_full_1)]
-    out_1, (in_total_1, ffn_parts_0) = leave_ffn(
-        1, [("scatter", pull_heads(dqkv_1)), ("gather", ffn_sums[0])], 13, dqkv_1
-    )
-
+    in_total_1, ffn_parts_1 = transfer(
+        [("scatter", pull_heads(dqkv_1)), ("gather", ffn_sums[1])], 13, dqkv_1
+    )
     grad_tokens = []
-    grad_attn_gain = 0.0
     for b, (in_cot, cot) in enumerate(((in_total_0, res_cot_0), (in_total_1, res_cot_1))):
-        pull, gain_part = normed_back(inputs[b], attn_gain, in_cot)
-        grad_attn_gain = grad_attn_gain + gain_part
+        pull, _ = normed_back(inputs[b], attn_gain, in_cot)
         grad_tokens.append((cot + pull).astype(BF16))
 
     out_grads = sum(dot(attended[b], res_full[b], TN) for b in range(slots)).astype(BF16)
@@ -1160,27 +1197,22 @@
         ((0, 0), (0, 0), (0, held - HEAD // shards)),
     ).reshape(2, model)
     gain_columns = jnp.stack(
-        [grad_attn_gain, grad_ffn_gain, head_sums[0], head_sums[1]], axis=1
+        [grad_ffn_gain, head_sums[0], head_sums[1]], axis=1
     ).astype(BF16)
     attn_grads = jnp.concatenate(
         [
             sum(dot(normal_full[b].reshape(flat), dqkv[b], TN) for b in range(slots)).astype(BF16),
-            jnp.pad(gain_columns, ((0, 0), (0, 124))),
+            jnp.pad(gain_columns, ((0, 0), (0, 125))),
             out_grads.reshape(model, model // blocks),
         ],
         axis=1,
     )
-    attn_sums = lax.psum_scatter(
-        follow(attn_grads, ffn_sums[1:]), "fsdp", scatter_dimension=0, tiled=True
-    )
+    attn_sums = lax.psum_scatter(attn_grads, "fsdp", scatter_dimension=0, tiled=True)
     out_edge = attn_sums.shape[1] - model // blocks
     out_sums = jnp.swapaxes(
         attn_sums[:, out_edge:].reshape(blocks, piece, model // blocks), 0, 1
     ).reshape(piece, model)
 
-    out_total_1, ffn_parts_1 = transfer(
-        [("scatter", out_1), ("gather", ffn_sums[1])], 14, in_total_1
-    )
     output = [
         (live[b] * (hidden_res[b] + total)).astype(BF16)
         for b, total in enumerate((out_total_0, out_total_1))
@@ -1191,12 +1223,15 @@
     ffn_grad = [v.reshape(seqs * hidden_own, model) for v in ffn_grad]
 
     heads_all, grad_out = transfer(
-        [("gather", attn_sums[:, :out_edge]), ("home", out_sums)], 15, out_total_1
+        [("gather", attn_sums[:, :out_edge]), ("home", out_sums)], 14, in_total_1
     )
     edge = hq * HEAD
     width = hkv_held * HEAD
     if hkv == hkv_held:
-        grad_query, grad_key, grad_value, gain_sums = place_heads(order, heads_all, edge, width)
+        grad_query, grad_key, grad_value, gain_sums, met = place_heads(
+            order, heads_all, edge, width, (query_weight, key_weight, value_weight)
+        )
+        met = met[:, 0]
     else:
         heads_all = jnp.moveaxis(heads_all, 0, 1).astype(F32)
         last = edge + width
@@ -1204,18 +1239,27 @@
         grad_key = heads_all[..., edge : edge + hkv * HEAD].reshape(held, kv_width)
         grad_value = heads_all[..., last : last + hkv * HEAD].reshape(held, kv_width)
         gain_sums = jnp.sum(heads_all[..., last + width :], axis=1)
+        met = sum(
+            jnp.sum(grad * weight.astype(F32), axis=1)
+            for grad, weight in (
+                (grad_query, query_weight),
+                (grad_key, key_weight),
+                (grad_value, value_weight),
+            )
+        )
+    grad_attn_gain = met / lax.dynamic_slice_in_dim(attn_gain, shard * held, held, 0)
 
     return (
         jnp.stack(output),
         jnp.stack(grad_tokens),
-        gain_sums[:, 0],
+        grad_attn_gain,
         grad_query,
         grad_key,
         grad_value,
+        gain_sums[: HEAD // shards, 1],
         gain_sums[: HEAD // shards, 2],
-        gain_sums[: HEAD // shards, 3],
         grad_out.astype(F32),
-        gain_sums[:, 1],
+        gain_sums[:, 0],
         ffn_grad[0],
         ffn_grad[1],
         ffn_grad[2],

time: 1100 us -> 1010 us (0.918)
  Pallas kernels: 931 us -> 847 us
  waiting for transfers between devices: 13 us -> 1.95 us
    pallas_call x16, Pallas kernels: 909 us -> 826 us  [call(): pl.pallas_call(kernel, grid=grid, out_shape=tuple(out_shape) + tuple(shap...]
    all_gather x2, waiting for transfers between devices: 11.6 us -> 0.62 us  [on_device(): ffn_weights = [lax.all_gather(own, 'fsdp', axis=0) for own in ffn_own]]
  transfers between devices with their start and end apart: 7 -> 7, of which waited for: 1 -> 1; matrix products, arithmetic and copies ran while one was open for 10% -> 10% of each run, Pallas kernels for 66% -> 64%
where the time goes in v5:
time: 1010 us; the launch traced here: 1000 us
  Pallas kernels  847 us (84%)
  matrix products  65.9 us (7%)
  other arithmetic  40 us (4%)
  local copies, waits for them, and re-layouts  32.4 us (3%)
  between operations  15 us (1%)
    pallas_call x16, Pallas kernels, call(): pl.pallas_call(kernel, grid=grid, out_shape=tuple(out_shape) + tuple(shap...  826 us
    dot_general x12, matrix products, dot(): return lax.dot_general(a, b, dims, preferred_element_type=F32)  65.9 us
  transfers between devices with their start and end apart: 7, of which 1 were waited for; matrix products, arithmetic and copies ran while one was open for 10% of the time, Pallas kernels for 64%

profile of v5, /device:TPU:6, one launch (start us, length us, event | category | flops | bytes accessed | tf_op | source)
XLA Modules:
  0.0 1003.1 jit_solution(10416263945440448071)
XLA Ops:
  7.2 1.0 constant_dynamic-slice_fusion.2
  8.2 0.9 constant_dynamic-slice_fusion
  10.0 2.1 convert_element_type.88
  14.1 1.7 multiply_convert_fusion.4
  15.9 38.7 %transfer.4 = (bf16[4,256,2048]{2,1,0:T(8,128)(2,1)}, bf16[64,2048]{1,0:T(8,128)(2,1)}, bf16[3,128,2048]{2,1,0:T(8,128)(2,1)}, bf16[3,128,2048]{2,1,0:T(8,128)(2,1)}) custom-call(bf16[256,2048]{1,0:T(8,128)(2,1)} %get-tuple-element.138.refs_0_, bf16[256,2048]{1,0:T(8,128)(2,1)} %refs_1_.1, bf16[1024,2048]{1,0:T(8,128)(2,1)} %refs_2_.1, ...), custom_call_target="tpu_custom_call" | custom-call | tf_op jit(solution)/shard_map/transfer/pallas_call | solution.py:451
  58.2 2.0 copy-done.10
  60.2 1.6 fusion.7
  61.8 7.8 convolution_convert_fusion.5
  69.6 43.8 %attend.2 = (bf16[4,256,512]{2,1,0:T(8,128)(2,1)}, f32[8,1024,1]{2,1,0:T(8,128)}, bf16[4,256,2048]{2,1,0:T(8,128)(2,1)}) custom-call(s32[1]{0:T(128)} %get-tuple-element.153.refs_0_, bf16[4,256,768]{2,1,0:T(8,128)(2,1)} %bitcast.217, f32[1,128]{1,0:T(1,128)} %get-tuple-element.159.refs_2_.refs_4_, f32[1,128]{1,0:T(1,128)} %get-tuple-element.160.refs_3_.refs_5_, ...), custom_call_target="tpu_custom_call" | custom-call | flops 30064771072 | bytes 8388608 | tf_op jit(solution)/shard_map/attend/pallas_call | solution.py:451
  113.4 6.4 convolution_convert_fusion.1
  119.8 4.5 convolution_convert_fusion.4
  124.3 43.1 %attend.3 = (bf16[4,256,512]{2,1,0:T(8,128)(2,1)}, f32[8,1024,1]{2,1,0:T(8,128)}, f32[256,2048]{1,0:T(8,128)}) custom-call(s32[1]{0:T(128)} %get-tuple-element.154.refs_0_, bf16[4,256,768]{2,1,0:T(8,128)(2,1)} %bitcast.215, f32[1,128]{1,0:T(1,128)} %get-tuple-element.159.refs_2_.refs_4_, f32[1,128]{1,0:T(1,128)} %get-tuple-element.160.refs_3_.refs_5_, ...), custom_call_target="tpu_custom_call" | custom-call | flops 30064771072 | bytes 8388608 | tf_op jit(solution)/shard_map/attend/pallas_call | solution.py:451
  167.5 1.9 multiply_reduce_fusion.7
  169.4 1.3 copy-done.4
  170.7 1.2 multiply_convert_fusion.3.refs_1_
  171.9 69.8 %transfer.5 = (bf16[4,256,2048]{2,1,0:T(8,128)(2,1)}, bf16[4,256,2048]{2,1,0:T(8,128)(2,1)}) custom-call(bf16[4,256,512]{2,1,0:T(8,128)(2,1)} %get-tuple-element.70.refs_0_, bf16[256,2048]{1,0:T(8,128)(2,1)} %multiply_convert_fusion.3.refs_1_, bf16[256,2048]{1,0:T(8,128)(2,1)} %get-tuple-element.140.refs_2_), custom_call_target="tpu_custom_call" | custom-call | tf_op jit(solution)/shard_map/transfer/pallas_call | solution.py:451
  241.7 4.4 convolution_convert_fusion
  246.1 76.9 %ffn_both.4 = (bf16[3,1024,1024]{2,1,0:T(8,128)(2,1)}, f32[1024,2048]{1,0:T(8,128)}, f32[256,2048]{1,0:T(8,128)}, bf16[4,256,2048]{2,1,0:T(8,128)(2,1)}) custom-call(bf16[1024,2048]{1,0:T(8,128)(2,1)} %bitcast.187, bf16[1024,2048]{1,0:T(8,128)(2,1)} %bitcast.192, bf16[8,3,128,2048]{3,2,1,0:T(8,128)(2,1)} %bitcast.170, bf16[8,3,128,2048]{3,2,1,0:T(8,128)(2,1)} %bitcast.171, ...), custom_call_target="tpu_custom_call" | custom-call | flops 34359738368 | bytes 20971520 | tf_op jit(solution)/shard_map/ffn_both/pallas_call | solution.py:451
  323.0 1.9 multiply_reduce_fusion.6
  326.2 1.2 multiply_convert_fusion.2.refs_7_
  328.1 46.5 %ffn_both.5 = (bf16[3,1024,1024]{2,1,0:T(8,128)(2,1)}, bf16[1024,2048]{1,0:T(8,128)(2,1)}, bf16[4,256,2048]{2,1,0:T(8,128)(2,1)}) custom-call(bf16[1024,2048]{1,0:T(8,128)(2,1)} %bitcast.189, bf16[1024,2048]{1,0:T(8,128)(2,1)} %bitcast.193, bf16[8,3,128,2048]{3,2,1,0:T(8,128)(2,1)} %bitcast.178, bf16[8,3,128,2048]{3,2,1,0:T(8,128)(2,1)} %bitcast.179, ...), custom_call_target="tpu_custom_call" | custom-call | flops 34359738368 | bytes 20971520 | tf_op jit(solution)/shard_map/ffn_both/pallas_call | solution.py:451
  374.6 44.8 %ffn_both.6 = (bf16[3,1024,1024]{2,1,0:T(8,128)(2,1)}, f32[1024,2048]{1,0:T(8,128)}, f32[256,2048]{1,0:T(8,128)}) custom-call(bf16[1024,2048]{1,0:T(8,128)(2,1)} %bitcast.202, bf16[1024,2048]{1,0:T(8,128)(2,1)} %bitcast.198, bf16[8,3,128,2048]{3,2,1,0:T(8,128)(2,1)} %bitcast.173, bf16[8,3,128,2048]{3,2,1,0:T(8,128)(2,1)} %bitcast.174, ...), custom_call_target="tpu_custom_call" | custom-call | flops 34359738368 | bytes 20971520 | tf_op jit(solution)/shard_map/ffn_both/pallas_call | solution.py:451
  419.4 2.3 multiply_reduce_fusion.1
  422.2 3.9 fusion.15
  426.1 43.9 %ffn_grads.2 = (bf16[8,3,128,2048]{3,2,1,0:T(8,128)(2,1)}, bf16[4,256,2048]{2,1,0:T(8,128)(2,1)}) custom-call(bf16[3,1024,1024]{2,1,0:T(8,128)(2,1)} %get-tuple-element.76.refs_6_.refs_0_, bf16[3,1024,1024]{2,1,0:T(8,128)(2,1)} %get-tuple-element.83.refs_1_.refs_6_.refs_0_, bf16[1024,2048]{1,0:T(8,128)(2,1)} %bitcast.190, bf16[1024,2048]{1,0:T(8,128)(2,1)} %bitcast.203, ...), custom_call_target="tpu_custom_call" | custom-call | flops 38654705664 | bytes 16777216 | tf_op jit(solution)/shard_map/ffn_grads/pallas_call | solution.py:451
  470.1 14.2 %ffn_down.2 = bf16[1024,2048]{1,0:T(8,128)(2,1)} custom-call(bf16[3,1024,1024]{2,1,0:T(8,128)(2,1)} %get-tuple-element.76.refs_6_.refs_0_, bf16[3,1024,1024]{2,1,0:T(8,128)(2,1)} %get-tuple-element.80.refs_5_.refs_1_.refs_0_, bf16[8,3,128,2048]{3,2,1,0:T(8,128)(2,1)} %bitcast.176, bf16[8,3,128,2048]{3,2,1,0:T(8,128)(2,1)} %bitcast.181, ...), custom_call_target="tpu_custom_call" | custom-call | flops 17179869184 | bytes 12582912 | tf_op jit(solution)/shard_map/ffn_down/pallas_call | solution.py:451
  484.3 42.8 %ffn_both.7 = (bf16[3,1024,1024]{2,1,0:T(8,128)(2,1)}, bf16[1024,2048]{1,0:T(8,128)(2,1)}, f32[256,2048]{1,0:T(8,128)}) custom-call(bf16[1024,2048]{1,0:T(8,128)(2,1)} %bitcast.204, bf16[1024,2048]{1,0:T(8,128)(2,1)} %bitcast.200, bf16[8,3,128,2048]{3,2,1,0:T(8,128)(2,1)} %bitcast.182, bf16[8,3,128,2048]{3,2,1,0:T(8,128)(2,1)} %bitcast.183, ...), custom_call_target="tpu_custom_call" | custom-call | flops 34359738368 | bytes 20971520 | tf_op jit(solution)/shard_map/ffn_both/pallas_call | solution.py:451
  527.1 41.8 %ffn_grads.3 = (bf16[8,3,128,2048]{3,2,1,0:T(8,128)(2,1)}, f32[256,2048]{1,0:T(8,128)}) custom-call(bf16[3,1024,1024]{2,1,0:T(8,128)(2,1)} %get-tuple-element.80.refs_5_.refs_1_.refs_0_, bf16[3,1024,1024]{2,1,0:T(8,128)(2,1)} %get-tuple-element.89.refs_1_.refs_6_, bf16[1024,2048]{1,0:T(8,128)(2,1)} %bitcast.191, bf16[1024,2048]{1,0:T(8,128)(2,1)} %bitcast.205, ...), custom_call_target="tpu_custom_call" | custom-call | flops 38654705664 | bytes 16777216 | tf_op jit(solution)/shard_map/ffn_grads/pallas_call | solution.py:451
  569.2 1.4 copy-done.8
  570.6 2.3 multiply_reduce_fusion
  573.5 4.5 fusion.21
  578.0 3.4 convolution_convert_fusion.7
  581.4 2.3 fusion.14
  583.7 14.3 %ffn_down.3 = bf16[1024,2048]{1,0:T(8,128)(2,1)} custom-call(bf16[3,1024,1024]{2,1,0:T(8,128)(2,1)} %get-tuple-element.83.refs_1_.refs_6_.refs_0_, bf16[3,1024,1024]{2,1,0:T(8,128)(2,1)} %get-tuple-element.89.refs_1_.refs_6_, bf16[8,3,128,2048]{3,2,1,0:T(8,128)(2,1)} %bitcast.177, bf16[8,3,128,2048]{3,2,1,0:T(8,128)(2,1)} %bitcast.185, ...), custom_call_target="tpu_custom_call" | custom-call | flops 17179869184 | bytes 12582912 | tf_op jit(solution)/shard_map/ffn_down/pallas_call | solution.py:451
  598.0 73.2 %attend_back.2 = (bf16[4,256,768]{2,1,0:T(8,128)(2,1)}, f32[2,128]{1,0:T(2,128)}, bf16[4,256,2048]{2,1,0:T(8,128)(2,1)}, f32[256,2048]{1,0:T(8,128)}) custom-call(s32[1]{0:T(128)} %get-tuple-element.153.refs_0_, bf16[4,256,768]{2,1,0:T(8,128)(2,1)} %bitcast.218, bf16[4,256,512]{2,1,0:T(8,128)(2,1)} %bitcast.222, f32[8,1024,1]{2,1,0:T(8,128)} %get-tuple-element.88.refs_3_, ...), custom_call_target="tpu_custom_call" | custom-call | flops 47244640256 | bytes 8388608 | tf_op jit(solution)/shard_map/attend_back/pallas_call | solution.py:451
  671.2 5.9 fusion.5
  677.1 3.3 reshape.309
  680.4 1.8 copy.59
  682.3 1.1 copy-done.21
  683.4 5.1 convolution_convert_fusion.6
  688.5 5.0 convolution_convert_fusion.3
  693.5 5.9 fusion.20
  699.4 86.9 %attend_back.3 = (bf16[4,256,768]{2,1,0:T(8,128)(2,1)}, f32[2,128]{1,0:T(2,128)}, f32[256,2048]{1,0:T(8,128)}, bf16[4,384,2048]{2,1,0:T(8,128)(2,1)}) custom-call(s32[1]{0:T(128)} %get-tuple-element.154.refs_0_, bf16[4,256,768]{2,1,0:T(8,128)(2,1)} %bitcast.216, bf16[4,256,512]{2,1,0:T(8,128)(2,1)} %bitcast.221, f32[8,1024,1]{2,1,0:T(8,128)} %get-tuple-element.95.refs_3_, ...), custom_call_target="tpu_custom_call" | custom-call | flops 47244640256 | bytes 8388608 | tf_op jit(solution)/shard_map/attend_back/pallas_call | solution.py:451
  787.6 8.2 fusion.2
  795.8 3.0 fusion.4
  799.5 0.9 copy-done.6
  800.4 2.0 fusion.10
  803.5 1.5 pad_maximum_fusion
  805.0 1.0 copy-done.50
  806.5 5.0 convolution_convert_fusion.2
  811.5 80.6 %transfer.6 = (f32[256,2048]{1,0:T(8,128)}, bf16[4,384,2048]{2,1,0:T(8,128)(2,1)}) custom-call(bf16[1024,768]{1,0:T(8,128)(2,1)} %bitcast.160, bf16[4,256,2048]{2,1,0:T(8,128)(2,1)} %bitcast.155, bf16[384,2048]{1,0:T(8,128)(2,1)} %bitcast.159), custom_call_target="tpu_custom_call" | custom-call | tf_op jit(solution)/shard_map/transfer/pallas_call | solution.py:451
  892.1 7.7 place_parts.2
  899.9 8.7 place_parts.3
  908.6 2.9 multiply_reduce_fusion.3
  913.3 1.4 fusion.12
  914.7 1.5 pad_maximum_fusion.1
  916.2 1.0 slice.95
  918.1 1.8 slice.94.refs_1_
  920.0 65.1 %transfer.7 = (bf16[4,256,896]{2,1,0:T(8,128)(2,1)}, bf16[256,2048]{1,0:T(8,128)(2,1)}) custom-call(f32[256,2048]{1,0:T(8,128)} %get-tuple-element.99.refs_0_, bf16[256,896]{1,0:T(8,128)(2,1)} %slice.94.refs_1_, bf16[64,2048]{1,0:T(8,128)(2,1)} %bitcast.165), custom_call_target="tpu_custom_call" | custom-call | tf_op jit(solution)/shard_map/transfer/pallas_call | solution.py:451
  985.1 4.7 place_heads.1
  989.8 1.6 slice_reduce_fusion
  991.4 1.5 slice_reduce_fusion.2
  992.9 1.0 slice_reduce_fusion.1
  993.9 1.6 convert_element_type.112
  (155 shorter events, 16.9 us)
Async XLA Ops:
  7.2 54.6 %all-gather.7.cloned.1.call-start = ((), (), s32[]{:S(2)}) async-start(), calls=%async_computation.3 | async-start | bytes 3538944 | tf_op jit(solution)/shard_map/all_gather | solution.py:1064
  9.9 103.5 %all-gather.9.cloned.1.call-start = ((), (), s32[]{:S(2)}) async-start(), calls=%async_computation.4 | async-start | bytes 2359296 | tf_op jit(solution)/shard_map/all_gather | solution.py:1071
  12.1 2.1 copy-start
  12.1 2.0 copy-start.30
  13.3 2.6 copy-start.36
  13.3 2.6 copy-start.38
  54.5 1.5 copy-start.45
  54.5 1.4 copy-start.46
  54.5 2.0 copy-start.40
  54.5 3.3 copy-start.24
  54.6 191.5 %all-gather.13.cloned.1.call-start = ((), (), s32[]{:S(2)}) async-start(), calls=%async_computation.9 | async-start | bytes 14155776 | tf_op jit(solution)/shard_map/all_gather | solution.py:1074
  55.3 272.7 %all-gather.11.cloned.1.call-start = ((), (), s32[]{:S(2)}) async-start(), calls=%async_computation.8 | async-start | bytes 14155776 | tf_op jit(solution)/shard_map/all_gather | solution.py:1074
  55.9 643.5 %reduce-scatter.4.cloned.1.call-start = ((), (), s32[]{:S(2)}) async-start(), calls=%async_computation.5 | async-start | bytes 14155776 | tf_op jit(solution)/shard_map/reduce_scatter | solution.py:1147
  57.2 0.6 copy-start.32
  58.2 2.0 copy-start.10
  113.4 6.4 copy-start.48
  113.4 6.4 copy-start.53
  124.3 43.1 %copy-start.1 = (f32[2,256,2048]{2,1,0:T(8,128)S(1)}, f32[2,256,2048]{2,1,0:T(8,128)}, u32[]{:S(2)}) copy-start(f32[2,256,2048]{2,1,0:T(8,128)} %copy-done) | copy-start | bytes 12582916
  167.4 3.2 copy-start.29
  169.4 1.3 copy-start.4
  171.9 69.8 %copy-start.22 = (bf16[4,256,512]{2,1,0:T(8,128)(2,1)S(1)}, bf16[4,256,512]{2,1,0:T(8,128)(2,1)}, u32[]{:S(2)}) copy-start(bf16[4,256,512]{2,1,0:T(8,128)(2,1)} %get-tuple-element.70.refs_0_) | copy-start | bytes 3145732
  171.9 69.8 %copy-start.51 = (bf16[512,2048]{1,0:T(8,128)(2,1)S(1)}, bf16[512,2048]{1,0:T(8,128)(2,1)}, u32[]{:S(2)}) copy-start(bf16[512,2048]{1,0:T(8,128)(2,1)} %all-gather.9.cloned.1.call-done) | copy-start | bytes 6291460
  246.1 76.9 %copy-start.2 = (f32[2,256,2048]{2,1,0:T(8,128)S(1)}, f32[2,256,2048]{2,1,0:T(8,128)}, u32[]{:S(2)}) copy-start(f32[2,256,2048]{2,1,0:T(8,128)} %copy-done) | copy-start | bytes 12582916
  324.9 1.3 copy-start.7
  325.5 0.7 copy-start.34
  374.6 44.8 %copy-start.5 = (f32[256,2048]{1,0:T(8,128)S(1)}, f32[256,2048]{1,0:T(8,128)}, u32[]{:S(2)}) copy-start(f32[256,2048]{1,0:T(8,128)} %copy-done.4) | copy-start | bytes 6291460
  419.4 2.8 copy-start.11
  470.1 341.4 %reduce-scatter.6.cloned.1.call-start = ((), (), s32[]{:S(2)}) async-start(), calls=%async_computation.6 | async-start | bytes 14155776 | tf_op jit(solution)/shard_map/reduce_scatter | solution.py:1153
  569.0 1.6 copy-start.8
  569.0 1.6 copy-start.35
  569.0 4.0 copy-start.27
  569.0 347.2 %reduce-scatter.8.cloned.1.call-start = ((), (), s32[]{:S(2)}) async-start(), calls=%async_computation.7 | async-start | bytes 6488064 | tf_op jit(solution)/shard_map/reduce_scatter | solution.py:1210
  570.6 2.9 copy-start.20
  573.5 4.5 copy-start.52
  578.0 3.4 copy-start.12
  578.0 3.4 copy-start.19
  578.0 3.4 copy-start.41
  598.0 73.2 %copy-start.14 = (f32[512,2048,1]{1,0,2:T(8,128)S(1)}, f32[512,2048,1]{1,0,2:T(8,128)}, u32[]{:S(2)}) copy-start(f32[512,2048,1]{1,0,2:T(8,128)} %fusion.21) | copy-start | bytes 12582916
  598.0 73.2 %copy-start.23 = (bf16[4,256,512]{2,1,0:T(8,128)(2,1)S(1)}, bf16[4,256,512]{2,1,0:T(8,128)(2,1)}, u32[]{:S(2)}) copy-start(bf16[4,256,512]{2,1,0:T(8,128)(2,1)} %get-tuple-element.70.refs_0_) | copy-start | bytes 3145732
  680.4 3.0 copy-start.21
  683.4 5.1 copy-start.49
  683.4 5.1 copy-start.54
  688.5 5.0 copy-start.47
  699.4 86.9 %copy-start.44 = (f32[2,128]{1,0:T(2,128)S(1)}, f32[2,128]{1,0:T(2,128)}, u32[]{:S(2)}) copy-start(f32[2,128]{1,0:T(2,128)} %get-tuple-element.100) | copy-start | bytes 3076
  787.6 8.2 copy-start.15
  798.8 0.7 copy-start.33
  798.8 1.6 copy-start.6
  800.4 2.2 copy-start.9
  800.4 2.9 copy-start.25
  803.3 2.8 copy-start.50
  803.5 3.0 copy-start.26
  899.8 8.7 copy-start.3
  899.8 8.7 copy-start.31
  908.6 3.0 copy-start.13
  908.6 3.5 copy-start.16
  908.6 4.1 copy-start.17
  908.6 4.7 copy-start.18
  908.6 4.7 copy-start.37
  908.6 4.7 copy-start.39
  908.6 4.7 copy-start.42
  908.6 4.7 copy-start.43
  985.1 8.8 copy-start.28
Sparse Core Ops, SparseCore 0:
  10.2 49.3 all-gather.6
  61.2 32.4 all-gather.8
  95.3 116.2 all-gather.12
  213.1 114.9 all-gather.10
  470.2 128.3 reduce-scatter.3
  600.7 127.5 reduce-scatter.5
  798.9 62.9 reduce-scatter.7

commit v6 on v5

--- a/solution.py
+++ b/solution.py
@@ -523,10 +523,15 @@
 
 
 def attend_kernel(sizes, hook, ins, outs, held):
-    len_ref, qkv_ref, qg_ref, kg_ref, cos_ref, sin_ref, ones_ref = ins
-    out_ref, lse_ref = outs
+    len_ref, normal_ref, weight_ref, qg_ref, kg_ref, cos_ref, sin_ref, ones_ref = ins
+    out_ref, lse_ref, qkv_ref = outs
     q_s, k_s, v_s, o_s = held
     hook(0)
+
+    @pl.loop(0, qkv_ref.shape[0])
+    def _(j):
+        qkv_ref[j] = dot(normal_ref[j], weight_ref[...]).astype(BF16)
+
     hq, hkv, group = sizes
     seqs, rows_in, _ = qkv_ref.shape
     place = lax.axis_index("seq")
@@ -564,8 +569,11 @@
 
 
 def attend_back_kernel(sizes, hook, ins, outs, held):
-    len_ref, qkv_ref, cot_ref, lse_ref, qg_ref, kg_ref, cos_ref, sin_ref, ones_ref = ins
-    dqkv_ref, dgain_ref = outs
+    (
+        len_ref, qkv_ref, res_ref, out_w_ref, qkv_w_ref, lse_ref,
+        qg_ref, kg_ref, cos_ref, sin_ref, ones_ref,
+    ) = ins
+    dqkv_ref, dgain_ref, pull_ref = outs
     q_s, k_s, v_s, cot_s, dq_s, dk_s, dv_s = held
     hook(0)
     hq, hkv, group = sizes
@@ -575,10 +583,9 @@
     prepare_heads(sizes, place, qkv_ref, qg_ref, kg_ref, cos_ref, sin_ref, ones, q_s, k_s, v_s)
     for c in range(seqs):
         j = true_chunk(place, c, seqs)
+        cots = dot(res_ref[j], out_w_ref[...], NT).astype(BF16)
         for h in range(hq):
-            cot_s[h, c * rows_in : (c + 1) * rows_in, :] = cot_ref[
-                j, :, h * HEAD : (h + 1) * HEAD
-            ]
+            cot_s[h, c * rows_in : (c + 1) * rows_in, :] = cots[:, h * HEAD : (h + 1) * HEAD]
     dk_s[...] = jnp.zeros_like(dk_s)
     dv_s[...] = jnp.zeros_like(dv_s)
     for i in range(seqs * rows_in // BLOCK):
@@ -631,6 +638,11 @@
             ).astype(BF16)
     dgain_ref[0:1, :] = gain_sums[0]
     dgain_ref[1:2, :] = gain_sums[1]
+
+    @pl.loop(0, seqs)
+    def _(j):
+        pull_ref[j] = dot(dqkv_ref[j], qkv_w_ref[...], NT).astype(BF16)
+
     hook(2)
 
 
@@ -649,19 +661,20 @@
     )
 
 
-def attend(sizes, length, qkv, gains, tables, jobs, number, after):
-    seqs, rows_in, _ = qkv.shape
+def attend(sizes, length, normal, weight, gains, tables, jobs, number, after):
+    seqs, rows_in, _ = normal.shape
     hq, hkv, _ = sizes
     slot = seqs * rows_in
     return call(
         functools.partial(attend_kernel, sizes),
-        [length, qkv, *gains, *tables],
-        [SMEM] + [VMEM] * 6,
+        [length, normal, weight, *gains, *tables],
+        [SMEM] + [VMEM] * 7,
         [
             jax.ShapeDtypeStruct((seqs, rows_in, hq * HEAD), BF16),
             jax.ShapeDtypeStruct((hq, slot, 1), F32),
+            jax.ShapeDtypeStruct((seqs, rows_in, weight.shape[1]), BF16),
         ],
-        [VMEM, VMEM],
+        [VMEM, VMEM, VMEM],
         jobs,
         number,
         after,
@@ -678,19 +691,22 @@
     )
 
 
-def attend_back(sizes, length, qkv, cot, lse, gains, tables, jobs, number, after):
+def attend_back(
+    sizes, length, qkv, res, out_w, qkv_w, lse, gains, tables, jobs, number, after
+):
     seqs, rows_in, width = qkv.shape
     hq, hkv, _ = sizes
     slot = seqs * rows_in
     return call(
         functools.partial(attend_back_kernel, sizes),
-        [length, qkv, cot, lse, *gains, *tables],
-        [SMEM] + [VMEM] * 8,
+        [length, qkv, res, out_w, qkv_w, lse, *gains, *tables],
+        [SMEM] + [VMEM] * 10,
         [
             jax.ShapeDtypeStruct((seqs, rows_in, width), BF16),
             jax.ShapeDtypeStruct((2, 128), F32),
+            jax.ShapeDtypeStruct(res.shape, BF16),
         ],
-        [VMEM, VMEM],
+        [VMEM, VMEM, VMEM],
         jobs,
         number,
         after,
@@ -717,19 +733,34 @@
 
 
 def ffn_kernel(steps, hook, ins, outs, held):
-    hooked(hook, pl.program_id(0), steps, lambda late: ffn_tile(late, *ins[:5], ins[5:], *outs))
-
-
-def ffn_tile(late, mid_ref, cot_ref, gate_ref, up_ref, down_ref, sums, acts_ref, pull_ref):
+    step = pl.program_id(0)
+    weights_ref, loaded = held
+    loads = [
+        pltpu.make_async_copy(ins[2].at[:, k], weights_ref.at[k], loaded.at[k]) for k in range(3)
+    ]
+
+    def first(act):
+        pl.when(step == 0)(act)
+
+    def work(late):
+        for load in loads:
+            first(load.start)
+        ffn_tile(late, first, loads, *ins[:2], weights_ref, ins[3:], *outs)
+
+    hooked(hook, step, steps, work)
+
+
+def ffn_tile(late, first, loads, mid_ref, cot_ref, weights_ref, sums, acts_ref, pull_ref):
     model = mid_ref.shape[-1]
     hidden = acts_ref.shape[-1]
-    gate_w = gate_ref[...].reshape(hidden, model)
-    up_w = up_ref[...].reshape(hidden, model)
-    down_w = down_ref[...].reshape(hidden, model)
+    whole = (hidden, model)
     mid = mid_ref[...]
-    gate = dot(mid, gate_w, NT)
-    up = dot(mid, up_w, NT)
-    mids_cot = dot(cot_ref[...], down_w, NT)
+    first(loads[0].wait)
+    gate = dot(mid, weights_ref[0].reshape(whole), NT)
+    first(loads[1].wait)
+    up = dot(mid, weights_ref[1].reshape(whole), NT)
+    first(loads[2].wait)
+    mids_cot = dot(cot_ref[...], weights_ref[2].reshape(whole), NT)
     late()
     sigmoid = jax.nn.sigmoid(gate)
     active = gate * sigmoid
@@ -738,7 +769,9 @@
     acts_ref[0] = gate_cot
     acts_ref[1] = up_cot
     acts_ref[2] = (active * up).astype(BF16)
-    pulled = dot(gate_cot, gate_w) + dot(up_cot, up_w)
+    pulled = dot(gate_cot, weights_ref[0].reshape(whole)) + dot(
+        up_cot, weights_ref[1].reshape(whole)
+    )
     for sum_ref in sums:
         pulled = pulled + sum_ref[...]
     pull_ref[...] = pulled.astype(pull_ref.dtype)
@@ -750,20 +783,12 @@
     hidden = shards * part
     tile = min(256, tokens)
 
-    def weight_spec(kind):
-        return pl.BlockSpec(
-            (shards, 1, part, model),
-            lambda i: (0, kind, 0, 0),
-            pipeline_mode=pl.Buffered(buffer_count=1),
-        )
-
     row_spec = pl.BlockSpec((tile, model), lambda i: (i, 0))
     extra = () if summed is None else (summed,)
     return call(
         functools.partial(ffn_kernel, tokens // tile),
-        [mid, cot, weights, weights, weights, *extra],
-        [row_spec, row_spec, weight_spec(0), weight_spec(1), weight_spec(2)]
-        + [row_spec] * len(extra),
+        [mid, cot, weights, *extra],
+        [row_spec, row_spec, ANY] + [row_spec] * len(extra),
         [
             jax.ShapeDtypeStruct((3, tokens, hidden), BF16),
             jax.ShapeDtypeStruct((tokens, model), BF16 if last else F32),
@@ -773,6 +798,10 @@
         number,
         after,
         grid=(tokens // tile,),
+        scratch=[
+            pltpu.VMEM((3, shards, part, model), BF16),
+            pltpu.SemaphoreType.DMA((3,)),
+        ],
         cost=pl.CostEstimate(
             flops=16 * tokens * model * hidden,
             bytes_accessed=4 * tokens * model + 6 * hidden * model,
@@ -784,23 +813,33 @@
 
 def ffn_grad_kernel(slots, tiles, hook, ins, outs, held):
     acts = ins[:slots]
-    mids = ins[slots : 2 * slots]
-    cots = ins[2 * slots :]
+    others = ins[slots:]
     (out_ref,) = outs
+    rows_ref, loaded = held
     kind = pl.program_id(0)
-
-    def store(others):
-        total = dot(acts[0][0], others[0][...], TN)
-        for act, other in zip(acts[1:], others[1:]):
-            total = total + dot(act[0], other[...], TN)
+    step = kind * tiles + pl.program_id(1)
+    loads = [
+        pltpu.make_async_copy(other, rows_ref.at[k], loaded.at[k])
+        for k, other in enumerate(others)
+    ]
+
+    def store(first):
+        total = None
+        for k, act in enumerate(acts):
+            term = dot(act[0], rows_ref[first + k], TN)
+            total = term if total is None else total + term
         out_ref[...] = total.astype(BF16).reshape(out_ref.shape)
 
     def work(late):
+        for k, load in enumerate(loads):
+            pl.when(step == 0)(load.start)
+        for k, load in enumerate(loads):
+            pl.when(step == (0 if k < slots else 2 * tiles))(load.wait)
         late()
-        pl.when(kind < 2)(lambda: store(mids))
-        pl.when(kind == 2)(lambda: store(cots))
-
-    hooked(hook, kind * tiles + pl.program_id(1), 3 * tiles, work)
+        pl.when(kind < 2)(lambda: store(0))
+        pl.when(kind == 2)(lambda: store(slots))
+
+    hooked(hook, step, 3 * tiles, work)
 
 
 def ffn_grads(acts, mids, cots, shards, jobs, number, after):
@@ -810,20 +849,21 @@
     part = hidden // shards
     tile = 256
     per = tile // part
-    whole = pl.BlockSpec(
-        (tokens, model), lambda k, i: (0, 0), pipeline_mode=pl.Buffered(buffer_count=1)
-    )
     return call(
         functools.partial(ffn_grad_kernel, slots, hidden // tile),
         [*acts, *mids, *cots],
         [pl.BlockSpec((1, tokens, tile), lambda k, i: (k, 0, i))] * slots
-        + [whole] * (2 * slots),
+        + [ANY] * (2 * slots),
         [jax.ShapeDtypeStruct((shards, 3, part, model), BF16)],
         [pl.BlockSpec((per, 1, part, model), lambda k, i: (i, k, 0, 0))],
         jobs,
         number,
         after,
         grid=(3, hidden // tile),
+        scratch=[
+            pltpu.VMEM((2 * slots, tokens, model), BF16),
+            pltpu.SemaphoreType.DMA((2 * slots,)),
+        ],
         cost=pl.CostEstimate(
             flops=9 * slots * tokens * model * hidden,
             bytes_accessed=4 * slots * tokens * model,
@@ -1073,9 +1113,6 @@
     part = hidden_own // CHUNKS
     ffn_weights = [lax.all_gather(own, "fsdp", axis=0) for own in ffn_own]
 
-    def project(full):
-        return dot(full.reshape(flat), qkv_weight).astype(BF16).reshape(seqs, rows, -1)
-
     def leave(mixed):
         return dot(mixed.reshape(slot_len, -1), out_rows).astype(BF16).reshape(chunked)
 
@@ -1083,19 +1120,20 @@
         res = inputs[b] + total
         return res, normed(res, ffn_gain).astype(BF16)
 
-    def heads(b, raw, jobs, number, after):
-        return attend(sizes, lengths[b : b + 1], raw, gains, tables, jobs, number, after)
+    def heads(b, jobs, number, after):
+        return attend(
+            sizes, lengths[b : b + 1], normal_full[b], qkv_weight, gains, tables,
+            jobs, number, after,
+        )
 
     normal_full = [None] * slots
     cot_full = [None] * slots
     mid_full = [None] * slots
     normal_full[0] = normal_0
-    qkv_0 = project(normal_full[0])
-    (mixed_0, lse_0), (normal_full[1],) = heads(
-        0, qkv_0, [("gather", normal_in[1])], 2, normal_full[0]
-    )
-    qkv_1 = project(normal_full[1])
-    (mixed_1, lse_1), (total_0,) = heads(1, qkv_1, [("scatter", leave(mixed_0))], 3, mixed_0)
+    (mixed_0, lse_0, qkv_0), (normal_full[1],) = heads(
+        0, [("gather", normal_in[1])], 2, normal_full[0]
+    )
+    (mixed_1, lse_1, qkv_1), (total_0,) = heads(1, [("scatter", leave(mixed_0))], 3, mixed_0)
     qkv = [qkv_0, qkv_1]
     log_sums = [lse_0, lse_1]
     attended = [v.reshape(slot_len, hq * HEAD) for v in (mixed_0, mixed_1)]
@@ -1150,69 +1188,54 @@
     grads_1, (mid_total_1,) = grad_step(
         1, [("scatter", pulled[1].reshape(chunked))], 10, acts[1][1]
     )
-    ffn_sums.append(lax.psum_scatter(grads_1, "fsdp", scatter_dimension=0))
+    ffn_sums.append(
+        lax.psum_scatter(grads_1, "fsdp", scatter_dimension=0)
+    )
     out_1, _ = leave_ffn(1, [], 0, grads_1)
     res_cot_1, low_1, ffn_gain_1 = pull_mid(1, mid_total_1)
     grad_ffn_gain = ffn_gain_0 + ffn_gain_1
 
     def back(b, full, jobs, number, after):
-        attended_cot = dot(full, out_rows, NT).astype(BF16).reshape(seqs, rows, hq * HEAD)
-        (cots, gain_part), results = attend_back(
-            sizes, lengths[b : b + 1], qkv[b], attended_cot, log_sums[b], gains, tables,
-            jobs, number, after,
+        return attend_back(
+            sizes, lengths[b : b + 1], qkv[b], full, out_rows, qkv_weight, log_sums[b],
+            gains, tables, jobs, number, after,
         )
-        return cots.reshape(slot_len, -1), gain_part, results
-
-    def pull_heads(cots):
-        return dot(cots, qkv_weight, NT).astype(BF16).reshape(chunked)
-
-    dqkv_0, heads_gain_0, (res_full_1, out_total_1) = back(
-        0, res_full_0.reshape(flat), [("gather", low_1), ("scatter", out_1)], 11, out_1
-    )
-    dqkv_1, heads_gain_1, (in_total_0, ffn_parts_0) = back(
-        1,
-        res_full_1.reshape(flat),
-        [("scatter", pull_heads(dqkv_0)), ("gather", ffn_sums[0])],
-        12,
-        dqkv_0,
+
+    (dqkv_0, heads_gain_0, pull_0), (res_full_1, out_total_1) = back(
+        0, res_full_0, [("gather", low_1), ("scatter", out_1)], 11, out_1
+    )
+    res_full = [v.reshape(flat) for v in (res_full_0, res_full_1)]
+    out_grads = sum(dot(attended[b], res_full[b], TN) for b in range(slots)).astype(BF16)
+    (dqkv_1, heads_gain_1, pull_1), (in_total_0, ffn_parts_0) = back(
+        1, res_full_1, [("scatter", pull_0), ("gather", ffn_sums[0])], 12, out_grads
+    )
+    out_sums = lax.psum_scatter(
+        follow(out_grads, [ffn_sums[1], dqkv_1]), "fsdp", scatter_dimension=0, tiled=True
     )
     head_gain = heads_gain_0 + heads_gain_1
-    dqkv = [dqkv_0, dqkv_1]
-    res_full = [v.reshape(flat) for v in (res_full_0, res_full_1)]
-    in_total_1, ffn_parts_1 = transfer(
-        [("scatter", pull_heads(dqkv_1)), ("gather", ffn_sums[1])], 13, dqkv_1
-    )
+    dqkv = [v.reshape(slot_len, -1) for v in (dqkv_0, dqkv_1)]
+    held = model // shards
+    head_sums = jnp.pad(
+        (head_gain[:, :HEAD] + head_gain[:, HEAD:]).reshape(2, shards, HEAD // shards),
+        ((0, 0), (0, 0), (0, held - HEAD // shards)),
+    ).reshape(2, model)
+    gain_columns = jnp.stack([grad_ffn_gain, head_sums[0], head_sums[1]], axis=1).astype(BF16)
+    qkv_grads = jnp.concatenate(
+        [
+            sum(dot(normal_full[b].reshape(flat), dqkv[b], TN) for b in range(slots)).astype(BF16),
+            jnp.pad(gain_columns, ((0, 0), (0, 125))),
+        ],
+        axis=1,
+    )
+    in_total_1, ffn_parts_1, grad_out = transfer(
+        [("scatter", pull_1), ("gather", ffn_sums[1]), ("home", out_sums)], 13, qkv_grads
+    )
+    qkv_sums = lax.psum_scatter(qkv_grads, "fsdp", scatter_dimension=0, tiled=True)
+    (heads_all,) = transfer([("gather", qkv_sums)], 14, in_total_1)
     grad_tokens = []
     for b, (in_cot, cot) in enumerate(((in_total_0, res_cot_0), (in_total_1, res_cot_1))):
         pull, _ = normed_back(inputs[b], attn_gain, in_cot)
         grad_tokens.append((cot + pull).astype(BF16))
-
-    out_grads = sum(dot(attended[b], res_full[b], TN) for b in range(slots)).astype(BF16)
-    held = model // shards
-    piece = out_grads.shape[0] // shards
-    blocks = held // piece
-    out_grads = jnp.swapaxes(out_grads.reshape(shards, piece, blocks, model // blocks), 1, 2)
-    head_sums = jnp.pad(
-        (head_gain[:, :HEAD] + head_gain[:, HEAD:]).reshape(2, shards, HEAD // shards),
-        ((0, 0), (0, 0), (0, held - HEAD // shards)),
-    ).reshape(2, model)
-    gain_columns = jnp.stack(
-        [grad_ffn_gain, head_sums[0], head_sums[1]], axis=1
-    ).astype(BF16)
-    attn_grads = jnp.concatenate(
-        [
-            sum(dot(normal_full[b].reshape(flat), dqkv[b], TN) for b in range(slots)).astype(BF16),
-            jnp.pad(gain_columns, ((0, 0), (0, 125))),
-            out_grads.reshape(model, model // blocks),
-        ],
-        axis=1,
-    )
-    attn_sums = lax.psum_scatter(attn_grads, "fsdp", scatter_dimension=0, tiled=True)
-    out_edge = attn_sums.shape[1] - model // blocks
-    out_sums = jnp.swapaxes(
-        attn_sums[:, out_edge:].reshape(blocks, piece, model // blocks), 0, 1
-    ).reshape(piece, model)
-
     output = [
         (live[b] * (hidden_res[b] + total)).astype(BF16)
         for b, total in enumerate((out_total_0, out_total_1))
@@ -1222,9 +1245,6 @@
         ffn_grad = place_parts(order, parts.reshape(seqs, 3, part, model), c, ffn_grad)
     ffn_grad = [v.reshape(seqs * hidden_own, model) for v in ffn_grad]
 
-    heads_all, grad_out = transfer(
-        [("gather", attn_sums[:, :out_edge]), ("home", out_sums)], 14, in_total_1
-    )
     edge = hq * HEAD
     width = hkv_held * HEAD
     if hkv == hkv_held:

time: 1010 us -> 980 us (0.970)
  matrix products: 65.9 us -> 37.4 us
  waiting for transfers between devices: 1.95 us -> 14.2 us
  local copies, waits for them, and re-layouts: 32.4 us -> 21.5 us
    dot_general x12 -> x6, matrix products: 65.9 us -> 37.4 us  [dot(): return lax.dot_general(a, b, dims, preferred_element_type=F32)]
    all_gather x2, waiting for transfers between devices: 0.62 us -> 12.8 us  [on_device(): ffn_weights = [lax.all_gather(own, 'fsdp', axis=0) for own in ffn_own]]
  transfers between devices with their start and end apart: 7 -> 8, of which waited for: 1 -> 1; matrix products, arithmetic and copies ran while one was open for 10% -> 7% of each run, Pallas kernels for 64% -> 70%
where the time goes in v6:
time: 980 us; the launch traced here: 975 us
  Pallas kernels  845 us (86%)
  other arithmetic  40.6 us (4%)
  matrix products  37.4 us (4%)
  local copies, waits for them, and re-layouts  21.5 us (2%)
  between operations  15 us (2%)
  waiting for transfers between devices  14.2 us (1%)
    pallas_call x16, Pallas kernels, call(): pl.pallas_call(kernel, grid=grid, out_shape=tuple(out_shape) + tuple(shap...  824 us
    dot_general x6, matrix products, dot(): return lax.dot_general(a, b, dims, preferred_element_type=F32)  37.4 us
  transfers between devices with their start and end apart: 8, of which 1 were waited for; matrix products, arithmetic and copies ran while one was open for 7% of the time, Pallas kernels for 70%

profile of v6, /device:TPU:6, one launch (start us, length us, event | category | flops | bytes accessed | tf_op | source)
XLA Modules:
  0.0 974.7 jit_solution(10301166927586709520)
XLA Ops:
  7.2 1.0 constant_dynamic-slice_fusion.2
  8.2 0.9 constant_dynamic-slice_fusion
  9.1 0.8 pad_maximum_fusion.2
  10.0 2.1 convert_element_type.70
  12.4 0.8 multiply_multiply_fusion
  13.3 0.9 copy-done
  14.2 1.7 multiply_convert_fusion.4
  15.9 38.7 %transfer.4 = (bf16[4,256,2048]{2,1,0:T(8,128)(2,1)}, bf16[64,2048]{1,0:T(8,128)(2,1)}, bf16[3,128,2048]{2,1,0:T(8,128)(2,1)}, bf16[3,128,2048]{2,1,0:T(8,128)(2,1)}) custom-call(bf16[256,2048]{1,0:T(8,128)(2,1)} %get-tuple-element.146.refs_0_, bf16[256,2048]{1,0:T(8,128)(2,1)} %refs_1_.1, bf16[1024,2048]{1,0:T(8,128)(2,1)} %refs_2_.1, ...), custom_call_target="tpu_custom_call" | custom-call | tf_op jit(solution)/shard_map/transfer/pallas_call | solution.py:451
  54.7 0.7 all-gather.13.cloned.1.call-update
  56.0 0.7 maximum_bitcast_fusion
  58.3 2.0 copy-done.10
  60.3 1.6 fusion.5
  61.9 46.3 %attend.2 = (bf16[4,256,512]{2,1,0:T(8,128)(2,1)}, f32[8,1024,1]{2,1,0:T(8,128)}, bf16[4,256,768]{2,1,0:T(8,128)(2,1)}, bf16[4,256,2048]{2,1,0:T(8,128)(2,1)}) custom-call(s32[1]{0:T(128)} %get-tuple-element.161.refs_0_, bf16[4,256,2048]{2,1,0:T(8,128)(2,1)} %get-tuple-element.69.refs_1_.refs_8_, ...), custom_call_target="tpu_custom_call" | custom-call | flops 30064771072 | bytes 8388608 | tf_op jit(solution)/shard_map/attend/pallas_call | solution.py:451
  108.2 6.3 convolution_convert_fusion.1
  114.5 45.4 %attend.3 = (bf16[4,256,512]{2,1,0:T(8,128)(2,1)}, f32[8,1024,1]{2,1,0:T(8,128)}, bf16[4,256,768]{2,1,0:T(8,128)(2,1)}, f32[256,2048]{1,0:T(8,128)}) custom-call(s32[1]{0:T(128)} %get-tuple-element.162.refs_0_, bf16[4,256,2048]{2,1,0:T(8,128)(2,1)} %get-tuple-element.70.refs_1_, bf16[2048,768]{1,0:T(8,128)(2,1)} %all-gather.7.cloned.1.call-done.refs_2_.refs_4_, ...), custom_call_target="tpu_custom_call" | custom-call | flops 30064771072 | bytes 8388608 | tf_op jit(solution)/shard_map/attend/pallas_call | solution.py:451
  160.0 2.0 multiply_reduce_fusion.7
  162.0 1.3 copy-done.4
  163.3 1.2 multiply_convert_fusion.3.refs_1_
  164.5 69.7 %transfer.5 = (bf16[4,256,2048]{2,1,0:T(8,128)(2,1)}, bf16[4,256,2048]{2,1,0:T(8,128)(2,1)}) custom-call(bf16[4,256,512]{2,1,0:T(8,128)(2,1)} %get-tuple-element.74.refs_0_, bf16[256,2048]{1,0:T(8,128)(2,1)} %multiply_convert_fusion.3.refs_1_, bf16[256,2048]{1,0:T(8,128)(2,1)} %get-tuple-element.148.refs_2_), custom_call_target="tpu_custom_call" | custom-call | tf_op jit(solution)/shard_map/transfer/pallas_call | solution.py:451
  234.2 4.4 convolution_convert_fusion
  238.6 72.3 %ffn_both.4 = (bf16[3,1024,1024]{2,1,0:T(8,128)(2,1)}, f32[1024,2048]{1,0:T(8,128)}, f32[256,2048]{1,0:T(8,128)}, bf16[4,256,2048]{2,1,0:T(8,128)(2,1)}) custom-call(bf16[1024,2048]{1,0:T(8,128)(2,1)} %bitcast.138, bf16[1024,2048]{1,0:T(8,128)(2,1)} %bitcast.143, bf16[8,3,128,2048]{3,2,1,0:T(8,128)(2,1)} %bitcast.130, bf16[1024,2048]{1,0:T(8,128)(2,1)} %bitcast.139, ...), custom_call_target="tpu_custom_call" | custom-call | flops 34359738368 | bytes 20971520 | tf_op jit(solution)/shard_map/ffn_both/pallas_call | solution.py:451
  311.0 1.9 multiply_reduce_fusion.6
  313.5 0.7 copy-done.7
  314.2 1.2 multiply_convert_fusion.2.refs_5_
  315.4 12.8 %all-gather.11.cloned.1.call-done = bf16[24,128,2048]{2,1,0:T(8,128)(2,1)} async-done(((bf16[3,128,2048]{2,1,0:T(8,128)(2,1)}), bf16[24,128,2048]{2,1,0:T(8,128)(2,1)}) %all-gather.11.cloned.1.call-update) | async-done | bytes 12582928 | tf_op jit(solution)/shard_map/all_gather | solution.py:1114
  328.2 42.1 %ffn_both.5 = (bf16[3,1024,1024]{2,1,0:T(8,128)(2,1)}, bf16[1024,2048]{1,0:T(8,128)(2,1)}, bf16[4,256,2048]{2,1,0:T(8,128)(2,1)}) custom-call(bf16[1024,2048]{1,0:T(8,128)(2,1)} %bitcast.140, bf16[1024,2048]{1,0:T(8,128)(2,1)} %bitcast.144, bf16[8,3,128,2048]{3,2,1,0:T(8,128)(2,1)} %bitcast.134, f32[1024,2048]{1,0:T(8,128)} %get-tuple-element.79.refs_3_, ...), custom_call_target="tpu_custom_call" | custom-call | flops 34359738368 | bytes 20971520 | tf_op jit(solution)/shard_map/ffn_both/pallas_call | solution.py:451
  370.3 40.7 %ffn_both.6 = (bf16[3,1024,1024]{2,1,0:T(8,128)(2,1)}, f32[1024,2048]{1,0:T(8,128)}, f32[256,2048]{1,0:T(8,128)}) custom-call(bf16[1024,2048]{1,0:T(8,128)(2,1)} %bitcast.152, bf16[1024,2048]{1,0:T(8,128)(2,1)} %bitcast.148, bf16[8,3,128,2048]{3,2,1,0:T(8,128)(2,1)} %bitcast.131, bf16[3,1024,1024]{2,1,0:T(8,128)(2,1)} %get-tuple-element.84.refs_3_.refs_1_.refs_0_, ...), custom_call_target="tpu_custom_call" | custom-call | flops 34359738368 | bytes 20971520 | tf_op jit(solution)/shard_map/ffn_both/pallas_call | solution.py:451
  411.1 2.9 multiply_reduce_fusion.2
  414.0 3.9 fusion.13
  417.9 38.2 %ffn_grads.2 = (bf16[8,3,128,2048]{3,2,1,0:T(8,128)(2,1)}, bf16[4,256,2048]{2,1,0:T(8,128)(2,1)}) custom-call(bf16[3,1024,1024]{2,1,0:T(8,128)(2,1)} %get-tuple-element.80.refs_4_.refs_0_, bf16[3,1024,1024]{2,1,0:T(8,128)(2,1)} %get-tuple-element.87.refs_1_.refs_6_.refs_0_, bf16[1024,2048]{1,0:T(8,128)(2,1)} %bitcast.141, bf16[1024,2048]{1,0:T(8,128)(2,1)} %bitcast.153, ...), custom_call_target="tpu_custom_call" | custom-call | flops 38654705664 | bytes 16777216 | tf_op jit(solution)/shard_map/ffn_grads/pallas_call | solution.py:451
  456.1 14.6 %ffn_down.2 = bf16[1024,2048]{1,0:T(8,128)(2,1)} custom-call(bf16[3,1024,1024]{2,1,0:T(8,128)(2,1)} %get-tuple-element.80.refs_4_.refs_0_, bf16[3,1024,1024]{2,1,0:T(8,128)(2,1)} %get-tuple-element.84.refs_3_.refs_1_.refs_0_, bf16[8,3,128,2048]{3,2,1,0:T(8,128)(2,1)} %bitcast.132, bf16[8,3,128,2048]{3,2,1,0:T(8,128)(2,1)} %bitcast.135, ...), custom_call_target="tpu_custom_call" | custom-call | flops 17179869184 | bytes 12582912 | tf_op jit(solution)/shard_map/ffn_down/pallas_call | solution.py:451
  470.7 38.9 %ffn_both.7 = (bf16[3,1024,1024]{2,1,0:T(8,128)(2,1)}, bf16[1024,2048]{1,0:T(8,128)(2,1)}, f32[256,2048]{1,0:T(8,128)}) custom-call(bf16[1024,2048]{1,0:T(8,128)(2,1)} %bitcast.154, bf16[1024,2048]{1,0:T(8,128)(2,1)} %bitcast.150, bf16[8,3,128,2048]{3,2,1,0:T(8,128)(2,1)} %bitcast.136, f32[1024,2048]{1,0:T(8,128)} %get-tuple-element.86.refs_3_, ...), custom_call_target="tpu_custom_call" | custom-call | flops 34359738368 | bytes 20971520 | tf_op jit(solution)/shard_map/ffn_both/pallas_call | solution.py:451
  509.7 38.8 %ffn_grads.3 = (bf16[8,3,128,2048]{3,2,1,0:T(8,128)(2,1)}, f32[256,2048]{1,0:T(8,128)}) custom-call(bf16[3,1024,1024]{2,1,0:T(8,128)(2,1)} %get-tuple-element.84.refs_3_.refs_1_.refs_0_, bf16[3,1024,1024]{2,1,0:T(8,128)(2,1)} %get-tuple-element.94.refs_1_.refs_6_, bf16[1024,2048]{1,0:T(8,128)(2,1)} %bitcast.142, bf16[1024,2048]{1,0:T(8,128)(2,1)} %bitcast.155, ...), custom_call_target="tpu_custom_call" | custom-call | flops 38654705664 | bytes 16777216 | tf_op jit(solution)/shard_map/ffn_grads/pallas_call | solution.py:451
  548.7 1.3 copy-done.8
  550.0 2.4 multiply_reduce_fusion.1
  553.0 4.4 fusion.18
  557.5 2.3 fusion.12
  559.8 14.2 %ffn_down.3 = bf16[1024,2048]{1,0:T(8,128)(2,1)} custom-call(bf16[3,1024,1024]{2,1,0:T(8,128)(2,1)} %get-tuple-element.87.refs_1_.refs_6_.refs_0_, bf16[3,1024,1024]{2,1,0:T(8,128)(2,1)} %get-tuple-element.94.refs_1_.refs_6_, bf16[8,3,128,2048]{3,2,1,0:T(8,128)(2,1)} %bitcast.133, bf16[8,3,128,2048]{3,2,1,0:T(8,128)(2,1)} %bitcast.137, ...), custom_call_target="tpu_custom_call" | custom-call | flops 17179869184 | bytes 12582912 | tf_op jit(solution)/shard_map/ffn_down/pallas_call | solution.py:451
  574.0 79.5 %attend_back.2 = (bf16[4,256,768]{2,1,0:T(8,128)(2,1)}, f32[2,128]{1,0:T(2,128)}, bf16[4,256,2048]{2,1,0:T(8,128)(2,1)}, bf16[4,256,2048]{2,1,0:T(8,128)(2,1)}, f32[256,2048]{1,0:T(8,128)}) custom-call(s32[1]{0:T(128)} %get-tuple-element.161.refs_0_, bf16[4,256,768]{2,1,0:T(8,128)(2,1)} %get-tuple-element.91.refs_1_, ...), custom_call_target="tpu_custom_call" | custom-call | flops 47244640256 | bytes 8388608 | tf_op jit(solution)/shard_map/attend_back/pallas_call | solution.py:451
  653.5 6.0 fusion.2.refs_11_
  659.5 93.2 %attend_back.3 = (bf16[4,256,768]{2,1,0:T(8,128)(2,1)}, f32[2,128]{1,0:T(2,128)}, bf16[4,256,2048]{2,1,0:T(8,128)(2,1)}, f32[256,2048]{1,0:T(8,128)}, bf16[4,384,2048]{2,1,0:T(8,128)(2,1)}) custom-call(s32[1]{0:T(128)} %get-tuple-element.162.refs_0_, bf16[4,256,768]{2,1,0:T(8,128)(2,1)} %get-tuple-element.99.refs_1_, ...), custom_call_target="tpu_custom_call" | custom-call | flops 47244640256 | bytes 8388608 | tf_op jit(solution)/shard_map/attend_back/pallas_call | solution.py:451
  753.5 0.7 copy-done.46
  754.2 8.6 fusion.19
  763.3 7.7 fusion.1
  771.1 2.2 fusion.3.refs_0_
  773.3 0.6 copy-done.30
  774.0 0.9 copy-done.6
  774.9 2.0 fusion.8
  777.2 0.6 copy-done.23
  778.1 1.5 pad_maximum_fusion
  779.6 7.7 place_parts.2
  787.3 117.3 %transfer.6 = (f32[256,2048]{1,0:T(8,128)}, bf16[4,384,2048]{2,1,0:T(8,128)(2,1)}, bf16[256,2048]{1,0:T(8,128)(2,1)}) custom-call(bf16[2048,896]{1,0:T(8,128)(2,1)} %fusion.3.refs_0_, bf16[4,256,2048]{2,1,0:T(8,128)(2,1)} %get-tuple-element.108.refs_1_, bf16[384,2048]{1,0:T(8,128)(2,1)} %bitcast.124, bf16[64,2048]{1,0:T(8,128)(2,1)} %reduce-scatter.9.cloned.1.call-done.refs_3_), custom_call_target="tpu_custom_call" | custom-call | tf_op jit(solution)/shard_map/transfer/pallas_call | solution.py:451
  904.7 2.8 convert_element_type.88
  907.4 8.7 place_parts.3
  916.2 2.9 multiply_reduce_fusion.3
  919.6 0.6 copy-done.16
  920.9 1.4 fusion.10
  922.3 1.5 pad_maximum_fusion.1
  923.8 34.5 %transfer.7.parts_ref = bf16[4,256,896]{2,1,0:T(8,128)(2,1)} custom-call(f32[256,2048]{1,0:T(8,128)} %get-tuple-element.110.refs_0_, bf16[256,896]{1,0:T(8,128)(2,1)} %reduce-scatter.11.cloned.1.call-done.refs_1_), custom_call_target="tpu_custom_call" | custom-call | tf_op jit(solution)/shard_map/transfer/pallas_call | solution.py:451
  958.3 4.6 place_heads.1
  962.9 1.6 slice_reduce_fusion
  964.5 1.5 slice_reduce_fusion.2
  966.0 1.0 slice_reduce_fusion.1
  967.0 0.7 dynamic-slice_divide_fusion
  (132 shorter events, 7.3 us)
Async XLA Ops:
  7.2 54.7 %all-gather.7.cloned.1.call-start = ((), (), s32[]{:S(2)}) async-start(), calls=%async_computation.4 | async-start | bytes 3538944 | tf_op jit(solution)/shard_map/all_gather | solution.py:1104
  9.9 98.3 %all-gather.9.cloned.1.call-start = ((), (), s32[]{:S(2)}) async-start(), calls=%async_computation.5 | async-start | bytes 2359296 | tf_op jit(solution)/shard_map/all_gather | solution.py:1111
  12.1 2.1 copy-start
  12.1 2.1 copy-start.26
  13.3 2.6 copy-start.33
  13.3 2.6 copy-start.35
  54.5 1.5 copy-start.43
  54.6 1.4 copy-start.44
  54.6 2.1 copy-start.37
  54.6 3.3 copy-start.22
  54.6 184.0 %all-gather.13.cloned.1.call-start = ((), (), s32[]{:S(2)}) async-start(), calls=%async_computation.11 | async-start | bytes 14155776 | tf_op jit(solution)/shard_map/all_gather | solution.py:1114
  55.4 272.9 %all-gather.11.cloned.1.call-start = ((), (), s32[]{:S(2)}) async-start(), calls=%async_computation.10 | async-start | bytes 14155776 | tf_op jit(solution)/shard_map/all_gather | solution.py:1114
  55.9 603.6 %reduce-scatter.5.cloned.1.call-start = ((), (), s32[]{:S(2)}) async-start(), calls=%async_computation.6 | async-start | bytes 14155776 | tf_op jit(solution)/shard_map/reduce_scatter | solution.py:1185
  57.3 0.6 copy-start.29
  58.2 2.0 copy-start.10
  114.5 45.5 %copy-start.1 = (f32[2,256,2048]{2,1,0:T(8,128)S(1)}, f32[2,256,2048]{2,1,0:T(8,128)}, u32[]{:S(2)}) copy-start(f32[2,256,2048]{2,1,0:T(8,128)} %copy-done) | copy-start | bytes 12582916
  160.0 3.3 copy-start.25
  162.0 1.3 copy-start.4
  164.5 69.7 %copy-start.20 = (bf16[4,256,512]{2,1,0:T(8,128)(2,1)S(1)}, bf16[4,256,512]{2,1,0:T(8,128)(2,1)}, u32[]{:S(2)}) copy-start(bf16[4,256,512]{2,1,0:T(8,128)(2,1)} %get-tuple-element.74.refs_0_) | copy-start | bytes 3145732
  164.5 69.7 %copy-start.45 = (bf16[512,2048]{1,0:T(8,128)(2,1)S(1)}, bf16[512,2048]{1,0:T(8,128)(2,1)}, u32[]{:S(2)}) copy-start(bf16[512,2048]{1,0:T(8,128)(2,1)} %all-gather.9.cloned.1.call-done.refs_3_) | copy-start | bytes 6291460
  238.6 72.4 %copy-start.2 = (f32[2,256,2048]{2,1,0:T(8,128)S(1)}, f32[2,256,2048]{2,1,0:T(8,128)}, u32[]{:S(2)}) copy-start(f32[2,256,2048]{2,1,0:T(8,128)} %copy-done) | copy-start | bytes 12582916
  312.9 1.3 copy-start.7
  313.5 0.7 copy-start.31
  370.3 40.8 %copy-start.5 = (f32[256,2048]{1,0:T(8,128)S(1)}, f32[256,2048]{1,0:T(8,128)}, u32[]{:S(2)}) copy-start(f32[256,2048]{1,0:T(8,128)} %copy-done.4) | copy-start | bytes 6291460
  411.1 2.9 copy-start.11
  456.1 296.7 %reduce-scatter.7.cloned.1.call-start = ((), (), s32[]{:S(2)}) async-start(), calls=%async_computation.7 | async-start | bytes 14155776 | tf_op jit(solution)/shard_map/reduce_scatter | solution.py:1192
  548.4 1.6 copy-start.8
  548.4 1.6 copy-start.32
  548.4 4.0 copy-start.24
  548.5 238.8 %reduce-scatter.9.cloned.1.call-start = ((), (), s32[]{:S(2)}) async-start(), calls=%async_computation.8 | async-start | bytes 2359296 | tf_op jit(solution)/shard_map/reduce_scatter | solution.py:1212
  550.0 3.0 copy-start.19
  553.0 4.5 copy-start.12
  553.0 4.5 copy-start.18
  553.0 4.5 copy-start.38
  574.0 79.5 %copy-start.14 = (f32[512,2048,1]{1,0,2:T(8,128)S(1)}, f32[512,2048,1]{1,0,2:T(8,128)}, u32[]{:S(2)}) copy-start(f32[512,2048,1]{1,0,2:T(8,128)} %fusion.18) | copy-start | bytes 12582916
  574.0 79.5 %copy-start.21 = (bf16[4,256,512]{2,1,0:T(8,128)(2,1)S(1)}, bf16[4,256,512]{2,1,0:T(8,128)(2,1)}, u32[]{:S(2)}) copy-start(bf16[4,256,512]{2,1,0:T(8,128)(2,1)} %get-tuple-element.74.refs_0_) | copy-start | bytes 3145732
  752.8 0.7 copy-start.28
  752.8 1.4 copy-start.46
  752.8 171.0 %reduce-scatter.11.cloned.1.call-start = ((), (), s32[]{:S(2)}) async-start(), calls=%async_computation.9 | async-start | bytes 4128768 | tf_op jit(solution)/shard_map/reduce_scatter | solution.py:1233
  754.2 8.6 copy-start.41
  754.2 8.6 copy-start.42
  754.2 9.1 copy-start.47
  773.3 0.7 copy-start.30
  773.3 1.6 copy-start.6
  774.9 2.2 copy-start.9
  774.9 2.9 copy-start.23
  907.4 8.7 copy-start.3
  907.4 8.7 copy-start.27
  916.1 3.0 copy-start.13
  916.2 3.5 copy-start.15
  916.2 4.1 copy-start.16
  916.2 4.7 copy-start.17
  916.2 4.7 copy-start.34
  916.2 4.7 copy-start.36
  916.2 4.7 copy-start.39
  916.2 4.7 copy-start.40
Sparse Core Ops, SparseCore 0:
  10.2 49.3 all-gather.6
  61.2 32.3 all-gather.8
  95.2 116.4 all-gather.12
  213.2 114.9 all-gather.10
  456.2 128.3 reduce-scatter.4
  586.8 127.5 reduce-scatter.6
  753.0 33.9 reduce-scatter.8
  789.3 103.2 reduce-scatter.10

commit v7 on v6

--- a/solution.py
+++ b/solution.py
@@ -204,70 +204,63 @@
     return greeting, begin, nothing, finish
 
 
-def home_job(sources, targets, scratch):
+def swap_job(sources, targets, scratch):
     (source,) = sources
     (target,) = targets
     outs, ins, here = scratch
-    rows = source.shape[0]
-    count = target.shape[0] // rows
+    count, rows, _ = source.shape
     place = lax.axis_index("seq")
     shard = lax.axis_index("fsdp")
     per = lax.axis_size("fsdp") // count
     piece = shard % count
-    owner = place * per + shard // count
     spot = pl.ds(pl.multiple_of(piece * rows, rows), rows)
 
-    def copy(s):
+    def owner(j):
+        return true_chunk(place, j, count) * per + shard // count
+
+    def copy(j):
         return pltpu.make_async_remote_copy(
-            src_ref=source,
+            src_ref=source.at[j],
             dst_ref=target.at[spot],
-            send_sem=outs.at[s],
+            send_sem=outs.at[j],
             recv_sem=ins.at[piece],
-            device_id={"seq": s, "fsdp": owner},
+            device_id={"fsdp": owner(j)},
             device_id_type=pl.DeviceIdType.MESH,
         )
 
-    def arrival(j):
+    def arrival(p):
         return pltpu.make_async_remote_copy(
-            src_ref=source,
-            dst_ref=target.at[pl.ds(j * rows, rows)],
+            src_ref=source.at[0],
+            dst_ref=target.at[pl.ds(p * rows, rows)],
             send_sem=outs.at[0],
-            recv_sem=ins.at[j],
-            device_id={"seq": place, "fsdp": owner},
+            recv_sem=ins.at[p],
+            device_id={"fsdp": owner(0)},
             device_id_type=pl.DeviceIdType.MESH,
         )
 
-    own = pltpu.make_async_copy(source, target.at[spot], here.at[0])
-
-    def is_self(s):
-        return jnp.logical_and(owner == shard, place == s)
-
-    def comes_from(j):
-        return shard // per, (shard % per) * count + j
-
-    def from_self(j):
-        seq, fsdp = comes_from(j)
-        return jnp.logical_and(seq == place, fsdp == shard)
+    def local(j):
+        return pltpu.make_async_copy(source.at[j], target.at[spot], here.at[0])
+
+    def origin(p):
+        return (shard % per) * count + p
+
+    def each(act_remote, act_local):
+        for j in range(count):
+            pl.when(owner(j) != shard)(lambda j=j: act_remote(copy(j)))
+            pl.when(owner(j) == shard)(lambda j=j: act_local(local(j)))
 
     def greeting(barrier):
-        for j in range(count):
-            seq, fsdp = comes_from(j)
-            pl.when(jnp.logical_not(from_self(j)))(
-                lambda seq=seq, fsdp=fsdp: greet(barrier, {"seq": seq, "fsdp": fsdp})
-            )
-        return jnp.where(owner == shard, count - 1, count)
+        for p in range(count):
+            pl.when(origin(p) != shard)(lambda p=p: greet(barrier, {"fsdp": origin(p)}))
+        return jnp.where(shard % per == shard // count, count - 1, count)
 
     def begin():
-        pl.when(owner == shard)(own.start)
-        for s in range(count):
-            pl.when(jnp.logical_not(is_self(s)))(lambda s=s: copy(s).start())
+        each(lambda c: c.start(), lambda c: c.start())
 
     def finish():
-        pl.when(owner == shard)(own.wait)
-        for s in range(count):
-            pl.when(jnp.logical_not(is_self(s)))(lambda s=s: copy(s).wait_send())
-        for j in range(count):
-            pl.when(jnp.logical_not(from_self(j)))(lambda j=j: arrival(j).wait_recv())
+        each(lambda c: c.wait_send(), lambda c: c.wait())
+        for p in range(count):
+            pl.when(origin(p) != shard)(lambda p=p: arrival(p).wait_recv())
 
     return greeting, begin, nothing, finish
 
@@ -307,7 +300,7 @@
     "gather": gather_job,
     "scatter": scatter_job,
     "deal": deal_job,
-    "home": home_job,
+    "swap": swap_job,
     "own": own_job,
 }
 
@@ -354,8 +347,8 @@
         return [jax.ShapeDtypeStruct(shape[1:], F32)]
     if kind == "deal":
         return [jax.ShapeDtypeStruct((shape[0] // 4,) + shape[1:], BF16)]
-    if kind == "home":
-        return [jax.ShapeDtypeStruct((shape[0] * 4,) + shape[1:], BF16)]
+    if kind == "swap":
+        return [jax.ShapeDtypeStruct((shape[0] * shape[1], shape[2]), BF16)]
     part = shape[0] // lax.axis_size("seq") // CHUNKS
     return [jax.ShapeDtypeStruct((len(arrays), part) + shape[1:], BF16)] * CHUNKS
 
@@ -378,12 +371,20 @@
             got = lax.ppermute(arrays[0][j * rows : (j + 1) * rows], ("seq", "fsdp"), moves)
             total = got if total is None else total + got
         return [total]
-    if kind == "home":
-        held = []
-        for j in range(seqs):
-            moves = [(s * shards + h * seqs + j, end) for s, h, end in ends]
-            held.append(lax.ppermute(arrays[0], ("seq", "fsdp"), moves))
-        return [lax.psum(jnp.concatenate(held, axis=0), "seq")]
+    if kind == "swap":
+        total = None
+        for q in range(seqs):
+            for p in range(seqs):
+                moves = [
+                    (s * shards + h * seqs + p, s * shards + q * per + h)
+                    for s in range(seqs)
+                    for h in range(per)
+                ]
+                got = lax.ppermute(arrays[0][q], ("seq", "fsdp"), moves)
+                rows = got.shape[0]
+                got = jnp.pad(got, ((p * rows, (seqs - 1 - p) * rows), (0, 0)))
+                total = got if total is None else total + got
+        return [total]
     own_rows = arrays[0].shape[0] // seqs
     part = own_rows // CHUNKS
     start = lax.axis_index("seq") * own_rows
@@ -406,7 +407,7 @@
 
 def call(
     body, operands, in_specs, out_shape, out_specs, jobs, number, after=None,
-    grid=(), scratch=(), cost=None, name=None,
+    grid=(), scratch=(), cost=None, name=None, late=(),
 ):
     plain = lax.axis_size("seq") != 4
     results = [v for job in jobs for v in plain_job(job)] if plain else []
@@ -430,6 +431,14 @@
         outs = take(n_out)
         targets = [take(len(shapes)) for shapes in job_outs]
         held = take(len(scratch))
+        loaded = take(len(late))
+        marks = take(1) if late else []
+        loads = [
+            pltpu.make_async_copy(ins[n], ref, marks[0].at[k])
+            for k, (n, ref) in enumerate(zip(late, loaded))
+        ]
+        for n, ref in zip(late, loaded):
+            ins[n] = ref
         phases = [
             MAKERS[job[0]](source, target, take(len(shapes)))
             for job, source, target, shapes in zip(inside, sources, targets, job_shapes)
@@ -440,6 +449,11 @@
                 meet([phase[0] for phase in phases])
             for phase in phases:
                 phase[k + 1]()
+            if k == 0:
+                for load in loads:
+                    load.start()
+                for load in loads:
+                    load.wait()
 
         body(hook, ins, outs, held)
 
@@ -447,6 +461,10 @@
     if inside:
         given = {"collective_id": number, "has_side_effects": True}
     arrays = [array for job in inside for array in job[1:]]
+    in_specs = [ANY if n in late else spec for n, spec in enumerate(in_specs)]
+    late_shapes = [pltpu.VMEM(operands[n].shape, operands[n].dtype) for n in late]
+    if late:
+        late_shapes.append(pltpu.SemaphoreType.DMA((len(late),)))
     shapes = [shape for shapes in job_outs for shape in shapes]
     made = pl.pallas_call(
         kernel,
@@ -454,7 +472,9 @@
         out_shape=tuple(out_shape) + tuple(shapes),
         in_specs=list(in_specs) + [ANY] * (len(extra) + len(arrays)),
         out_specs=tuple(out_specs) + (ANY,) * len(shapes),
-        scratch_shapes=list(scratch) + [shape for shapes in job_shapes for shape in shapes],
+        scratch_shapes=list(scratch)
+        + late_shapes
+        + [shape for shapes in job_shapes for shape in shapes],
         compiler_params=pltpu.CompilerParams(vmem_limit_bytes=VMEM_LIMIT, **given),
         cost_estimate=cost,
         name=name,
@@ -688,6 +708,7 @@
             flops=56 * hq * slot * slot * HEAD, bytes_accessed=1 << 23, transcendentals=0
         ),
         name="attend",
+        late=(1, 2),
     )
 
 
@@ -723,6 +744,7 @@
             flops=88 * hq * slot * slot * HEAD, bytes_accessed=1 << 23, transcendentals=0
         ),
         name="attend_back",
+        late=(1, 2, 3, 4, 5),
     )
 
 
@@ -1191,7 +1213,6 @@
     ffn_sums.append(
         lax.psum_scatter(grads_1, "fsdp", scatter_dimension=0)
     )
-    out_1, _ = leave_ffn(1, [], 0, grads_1)
     res_cot_1, low_1, ffn_gain_1 = pull_mid(1, mid_total_1)
     grad_ffn_gain = ffn_gain_0 + ffn_gain_1
 
@@ -1201,37 +1222,43 @@
             gains, tables, jobs, number, after,
         )
 
-    (dqkv_0, heads_gain_0, pull_0), (res_full_1, out_total_1) = back(
-        0, res_full_0, [("gather", low_1), ("scatter", out_1)], 11, out_1
+    (dqkv_0, heads_gain_0, pull_0), (res_full_1,) = back(
+        0, res_full_0, [("gather", low_1)], 11, grads_1
     )
     res_full = [v.reshape(flat) for v in (res_full_0, res_full_1)]
     out_grads = sum(dot(attended[b], res_full[b], TN) for b in range(slots)).astype(BF16)
     (dqkv_1, heads_gain_1, pull_1), (in_total_0, ffn_parts_0) = back(
         1, res_full_1, [("scatter", pull_0), ("gather", ffn_sums[0])], 12, out_grads
     )
-    out_sums = lax.psum_scatter(
-        follow(out_grads, [ffn_sums[1], dqkv_1]), "fsdp", scatter_dimension=0, tiled=True
-    )
     head_gain = heads_gain_0 + heads_gain_1
     dqkv = [v.reshape(slot_len, -1) for v in (dqkv_0, dqkv_1)]
     held = model // shards
+    piece = out_grads.shape[0] // shards
+    blocks = held // piece
+    out_grads = jnp.swapaxes(out_grads.reshape(shards, piece, blocks, model // blocks), 1, 2)
     head_sums = jnp.pad(
         (head_gain[:, :HEAD] + head_gain[:, HEAD:]).reshape(2, shards, HEAD // shards),
         ((0, 0), (0, 0), (0, held - HEAD // shards)),
     ).reshape(2, model)
     gain_columns = jnp.stack([grad_ffn_gain, head_sums[0], head_sums[1]], axis=1).astype(BF16)
-    qkv_grads = jnp.concatenate(
+    attn_grads = jnp.concatenate(
         [
             sum(dot(normal_full[b].reshape(flat), dqkv[b], TN) for b in range(slots)).astype(BF16),
             jnp.pad(gain_columns, ((0, 0), (0, 125))),
+            out_grads.reshape(model, model // blocks),
         ],
         axis=1,
     )
-    in_total_1, ffn_parts_1, grad_out = transfer(
-        [("scatter", pull_1), ("gather", ffn_sums[1]), ("home", out_sums)], 13, qkv_grads
-    )
-    qkv_sums = lax.psum_scatter(qkv_grads, "fsdp", scatter_dimension=0, tiled=True)
-    (heads_all,) = transfer([("gather", qkv_sums)], 14, in_total_1)
+    attn_sums = lax.psum_scatter(attn_grads, "fsdp", scatter_dimension=0, tiled=True)
+    out_1, (in_total_1, ffn_parts_1) = leave_ffn(
+        1, [("scatter", pull_1), ("gather", ffn_sums[1])], 13, attn_grads
+    )
+    (heads_all,) = transfer([("gather", attn_sums)], 14, out_1)
+    out_edge = attn_sums.shape[1] - model // blocks
+    out_pieces = jnp.swapaxes(
+        heads_all[..., out_edge:].reshape(seqs, blocks, piece, model // blocks), 1, 2
+    ).reshape(seqs, piece, model)
+    grad_out, out_total_1 = transfer([("swap", out_pieces), ("scatter", out_1)], 15, out_1)
     grad_tokens = []
     for b, (in_cot, cot) in enumerate(((in_total_0, res_cot_0), (in_total_1, res_cot_1))):
         pull, _ = normed_back(inputs[b], attn_gain, in_cot)
@@ -1249,11 +1276,11 @@
     width = hkv_held * HEAD
     if hkv == hkv_held:
         grad_query, grad_key, grad_value, gain_sums, met = place_heads(
-            order, heads_all, edge, width, (query_weight, key_weight, value_weight)
+            order, heads_all[..., :out_edge], edge, width, (query_weight, key_weight, value_weight)
         )
         met = met[:, 0]
     else:
-        heads_all = jnp.moveaxis(heads_all, 0, 1).astype(F32)
+        heads_all = jnp.moveaxis(heads_all[..., :out_edge], 0, 1).astype(F32)
         last = edge + width
         grad_query = heads_all[..., :edge].reshape(held, query_width)
         grad_key = heads_all[..., edge : edge + hkv * HEAD].reshape(held, kv_width)

time: 980 us -> 946 us (0.965)
  Pallas kernels: 845 us -> 800 us
    pallas_call x16, Pallas kernels: 824 us -> 778 us  [call(): pl.pallas_call(kernel, grid=grid, out_shape=tuple(out_shape) + tuple(shap...]
  transfers between devices with their start and end apart: 8 -> 7, of which waited for: 1 -> 1; matrix products, arithmetic and copies ran while one was open for 7% -> 8% of each run, Pallas kernels for 70% -> 65%
where the time goes in v7:
time: 946 us; the launch traced here: 940 us
  Pallas kernels  800 us (85%)
  other arithmetic  42.9 us (5%)
  matrix products  36.8 us (4%)
  local copies, waits for them, and re-layouts  30.4 us (3%)
  between operations  15 us (2%)
  waiting for transfers between devices  14.8 us (2%)
    pallas_call x16, Pallas kernels, call(): pl.pallas_call(kernel, grid=grid, out_shape=tuple(out_shape) + tuple(shap...  778 us
    dot_general x6, matrix products, dot(): return lax.dot_general(a, b, dims, preferred_element_type=F32)  36.8 us
  transfers between devices with their start and end apart: 7, of which 1 were waited for; matrix products, arithmetic and copies ran while one was open for 8% of the time, Pallas kernels for 65%

profile of v7, /device:TPU:6, one launch (start us, length us, event | category | flops | bytes accessed | tf_op | source)
XLA Modules:
  0.0 940.3 jit_solution(3446836635143589606)
XLA Ops:
  7.2 1.0 constant_dynamic-slice_fusion.2
  8.2 0.9 constant_dynamic-slice_fusion
  9.1 0.8 pad_maximum_fusion.2
  10.0 2.1 convert_element_type.70
  12.4 0.8 multiply_multiply_fusion
  13.3 0.9 copy-done
  14.2 1.7 multiply_convert_fusion.4
  15.9 38.7 %transfer.4 = (bf16[4,256,2048]{2,1,0:T(8,128)(2,1)}, bf16[64,2048]{1,0:T(8,128)(2,1)}, bf16[3,128,2048]{2,1,0:T(8,128)(2,1)}, bf16[3,128,2048]{2,1,0:T(8,128)(2,1)}) custom-call(bf16[256,2048]{1,0:T(8,128)(2,1)} %get-tuple-element.146.refs_0_, bf16[256,2048]{1,0:T(8,128)(2,1)} %refs_1_.1, bf16[1024,2048]{1,0:T(8,128)(2,1)} %refs_2_.1, ...), custom_call_target="tpu_custom_call" | custom-call | tf_op jit(solution)/shard_map/transfer/pallas_call | solution.py:469
  54.7 0.7 all-gather.13.cloned.1.call-update
  58.2 2.0 copy-done.10
  60.3 1.6 fusion.7
  61.9 43.7 %attend.2 = (bf16[4,256,512]{2,1,0:T(8,128)(2,1)}, f32[8,1024,1]{2,1,0:T(8,128)}, bf16[4,256,768]{2,1,0:T(8,128)(2,1)}, bf16[4,256,2048]{2,1,0:T(8,128)(2,1)}) custom-call(s32[1]{0:T(128)} %get-tuple-element.161.refs_0_, bf16[4,256,2048]{2,1,0:T(8,128)(2,1)} %get-tuple-element.69.refs_1_.refs_8_, ...), custom_call_target="tpu_custom_call" | custom-call | flops 30064771072 | bytes 8388608 | tf_op jit(solution)/shard_map/attend/pallas_call | solution.py:469
  105.6 6.8 convolution_convert_fusion.1
  112.3 45.3 %attend.3 = (bf16[4,256,512]{2,1,0:T(8,128)(2,1)}, f32[8,1024,1]{2,1,0:T(8,128)}, bf16[4,256,768]{2,1,0:T(8,128)(2,1)}, f32[256,2048]{1,0:T(8,128)}) custom-call(s32[1]{0:T(128)} %get-tuple-element.162.refs_0_, bf16[4,256,2048]{2,1,0:T(8,128)(2,1)} %get-tuple-element.70.refs_1_, bf16[2048,768]{1,0:T(8,128)(2,1)} %all-gather.7.cloned.1.call-done.refs_2_.refs_4_, ...), custom_call_target="tpu_custom_call" | custom-call | flops 30064771072 | bytes 8388608 | tf_op jit(solution)/shard_map/attend/pallas_call | solution.py:469
  157.7 1.9 multiply_reduce_fusion.7
  159.6 1.3 copy-done.4
  160.9 1.2 multiply_convert_fusion.3.refs_1_
  162.2 70.4 %transfer.5 = (bf16[4,256,2048]{2,1,0:T(8,128)(2,1)}, bf16[4,256,2048]{2,1,0:T(8,128)(2,1)}) custom-call(bf16[4,256,512]{2,1,0:T(8,128)(2,1)} %get-tuple-element.74.refs_0_, bf16[256,2048]{1,0:T(8,128)(2,1)} %multiply_convert_fusion.3.refs_1_, bf16[256,2048]{1,0:T(8,128)(2,1)} %get-tuple-element.148.refs_2_), custom_call_target="tpu_custom_call" | custom-call | tf_op jit(solution)/shard_map/transfer/pallas_call | solution.py:469
  232.6 4.4 convolution_convert_fusion
  237.0 73.1 %ffn_both.4 = (bf16[3,1024,1024]{2,1,0:T(8,128)(2,1)}, f32[1024,2048]{1,0:T(8,128)}, f32[256,2048]{1,0:T(8,128)}, bf16[4,256,2048]{2,1,0:T(8,128)(2,1)}) custom-call(bf16[1024,2048]{1,0:T(8,128)(2,1)} %bitcast.150, bf16[1024,2048]{1,0:T(8,128)(2,1)} %bitcast.155, bf16[8,3,128,2048]{3,2,1,0:T(8,128)(2,1)} %bitcast.142, bf16[1024,2048]{1,0:T(8,128)(2,1)} %bitcast.151, ...), custom_call_target="tpu_custom_call" | custom-call | flops 34359738368 | bytes 20971520 | tf_op jit(solution)/shard_map/ffn_both/pallas_call | solution.py:469
  310.1 2.0 multiply_reduce_fusion.6
  312.7 0.7 copy-done.7
  313.4 1.2 multiply_convert_fusion.2.refs_5_
  314.6 13.5 %all-gather.11.cloned.1.call-done = bf16[24,128,2048]{2,1,0:T(8,128)(2,1)} async-done(((bf16[3,128,2048]{2,1,0:T(8,128)(2,1)}), bf16[24,128,2048]{2,1,0:T(8,128)(2,1)}) %all-gather.11.cloned.1.call-update) | async-done | bytes 12582928 | tf_op jit(solution)/shard_map/all_gather | solution.py:1136
  328.1 42.1 %ffn_both.5 = (bf16[3,1024,1024]{2,1,0:T(8,128)(2,1)}, bf16[1024,2048]{1,0:T(8,128)(2,1)}, bf16[4,256,2048]{2,1,0:T(8,128)(2,1)}) custom-call(bf16[1024,2048]{1,0:T(8,128)(2,1)} %bitcast.152, bf16[1024,2048]{1,0:T(8,128)(2,1)} %bitcast.156, bf16[8,3,128,2048]{3,2,1,0:T(8,128)(2,1)} %bitcast.146, f32[1024,2048]{1,0:T(8,128)} %get-tuple-element.79.refs_3_, ...), custom_call_target="tpu_custom_call" | custom-call | flops 34359738368 | bytes 20971520 | tf_op jit(solution)/shard_map/ffn_both/pallas_call | solution.py:469
  370.2 40.7 %ffn_both.6 = (bf16[3,1024,1024]{2,1,0:T(8,128)(2,1)}, f32[1024,2048]{1,0:T(8,128)}, f32[256,2048]{1,0:T(8,128)}) custom-call(bf16[1024,2048]{1,0:T(8,128)(2,1)} %bitcast.165, bf16[1024,2048]{1,0:T(8,128)(2,1)} %bitcast.161, bf16[8,3,128,2048]{3,2,1,0:T(8,128)(2,1)} %bitcast.143, bf16[3,1024,1024]{2,1,0:T(8,128)(2,1)} %get-tuple-element.84.refs_3_.refs_1_.refs_0_, ...), custom_call_target="tpu_custom_call" | custom-call | flops 34359738368 | bytes 20971520 | tf_op jit(solution)/shard_map/ffn_both/pallas_call | solution.py:469
  411.0 2.3 multiply_reduce_fusion.3
  413.8 3.9 fusion.15
  417.7 38.2 %ffn_grads.2 = (bf16[8,3,128,2048]{3,2,1,0:T(8,128)(2,1)}, bf16[4,256,2048]{2,1,0:T(8,128)(2,1)}) custom-call(bf16[3,1024,1024]{2,1,0:T(8,128)(2,1)} %get-tuple-element.80.refs_4_.refs_0_, bf16[3,1024,1024]{2,1,0:T(8,128)(2,1)} %get-tuple-element.87.refs_1_.refs_6_.refs_0_, bf16[1024,2048]{1,0:T(8,128)(2,1)} %bitcast.153, bf16[1024,2048]{1,0:T(8,128)(2,1)} %bitcast.166, ...), custom_call_target="tpu_custom_call" | custom-call | flops 38654705664 | bytes 16777216 | tf_op jit(solution)/shard_map/ffn_grads/pallas_call | solution.py:469
  456.0 14.4 %ffn_down.2 = bf16[1024,2048]{1,0:T(8,128)(2,1)} custom-call(bf16[3,1024,1024]{2,1,0:T(8,128)(2,1)} %get-tuple-element.80.refs_4_.refs_0_, bf16[3,1024,1024]{2,1,0:T(8,128)(2,1)} %get-tuple-element.84.refs_3_.refs_1_.refs_0_, bf16[8,3,128,2048]{3,2,1,0:T(8,128)(2,1)} %bitcast.144, bf16[8,3,128,2048]{3,2,1,0:T(8,128)(2,1)} %bitcast.147, ...), custom_call_target="tpu_custom_call" | custom-call | flops 17179869184 | bytes 12582912 | tf_op jit(solution)/shard_map/ffn_down/pallas_call | solution.py:469
  470.4 38.9 %ffn_both.7 = (bf16[3,1024,1024]{2,1,0:T(8,128)(2,1)}, bf16[1024,2048]{1,0:T(8,128)(2,1)}, f32[256,2048]{1,0:T(8,128)}) custom-call(bf16[1024,2048]{1,0:T(8,128)(2,1)} %bitcast.167, bf16[1024,2048]{1,0:T(8,128)(2,1)} %bitcast.163, bf16[8,3,128,2048]{3,2,1,0:T(8,128)(2,1)} %bitcast.148, f32[1024,2048]{1,0:T(8,128)} %get-tuple-element.86.refs_3_, ...), custom_call_target="tpu_custom_call" | custom-call | flops 34359738368 | bytes 20971520 | tf_op jit(solution)/shard_map/ffn_both/pallas_call | solution.py:469
  509.2 38.8 %ffn_grads.3 = (bf16[8,3,128,2048]{3,2,1,0:T(8,128)(2,1)}, f32[256,2048]{1,0:T(8,128)}) custom-call(bf16[3,1024,1024]{2,1,0:T(8,128)(2,1)} %get-tuple-element.84.refs_3_.refs_1_.refs_0_, bf16[3,1024,1024]{2,1,0:T(8,128)(2,1)} %get-tuple-element.91.refs_1_.refs_6_, bf16[1024,2048]{1,0:T(8,128)(2,1)} %bitcast.154, bf16[1024,2048]{1,0:T(8,128)(2,1)} %bitcast.168, ...), custom_call_target="tpu_custom_call" | custom-call | flops 38654705664 | bytes 16777216 | tf_op jit(solution)/shard_map/ffn_grads/pallas_call | solution.py:469
  548.6 1.1 copy-done.8
  549.7 2.4 multiply_reduce_fusion.2
  552.7 4.4 fusion.21
  557.1 2.3 fusion.14
  559.5 51.8 %attend_back.2 = (bf16[4,256,768]{2,1,0:T(8,128)(2,1)}, f32[2,128]{1,0:T(2,128)}, bf16[4,256,2048]{2,1,0:T(8,128)(2,1)}, bf16[4,256,2048]{2,1,0:T(8,128)(2,1)}) custom-call(s32[1]{0:T(128)} %get-tuple-element.161.refs_0_, bf16[4,256,768]{2,1,0:T(8,128)(2,1)} %get-tuple-element.92.refs_1_, bf16[4,256,2048]{2,1,0:T(8,128)(2,1)} %get-tuple-element.93.refs_2_, ...), custom_call_target="tpu_custom_call" | custom-call | flops 47244640256 | bytes 8388608 | tf_op jit(solution)/shard_map/attend_back/pallas_call | solution.py:469
  611.3 5.9 fusion.5.refs_11_
  617.2 3.3 reshape.261
  620.6 1.8 copy.59
  622.4 1.2 copy-done.44
  623.6 7.1 fusion.20
  630.7 89.7 %attend_back.3 = (bf16[4,256,768]{2,1,0:T(8,128)(2,1)}, f32[2,128]{1,0:T(2,128)}, bf16[4,256,2048]{2,1,0:T(8,128)(2,1)}, f32[256,2048]{1,0:T(8,128)}, bf16[4,384,2048]{2,1,0:T(8,128)(2,1)}) custom-call(s32[1]{0:T(128)} %get-tuple-element.162.refs_0_, bf16[4,256,768]{2,1,0:T(8,128)(2,1)} %get-tuple-element.99.refs_1_, ...), custom_call_target="tpu_custom_call" | custom-call | flops 47244640256 | bytes 8388608 | tf_op jit(solution)/shard_map/attend_back/pallas_call | solution.py:469
  721.7 8.2 fusion.2
  729.9 3.0 fusion.4.refs_4_
  733.6 0.9 copy-done.6
  734.5 1.8 fusion.10
  736.3 7.9 place_parts.2
  744.2 89.0 %ffn_down.3 = (bf16[1024,2048]{1,0:T(8,128)(2,1)}, f32[256,2048]{1,0:T(8,128)}, bf16[4,384,2048]{2,1,0:T(8,128)(2,1)}) custom-call(bf16[3,1024,1024]{2,1,0:T(8,128)(2,1)} %get-tuple-element.87.refs_1_.refs_6_.refs_0_, bf16[3,1024,1024]{2,1,0:T(8,128)(2,1)} %get-tuple-element.91.refs_1_.refs_6_, bf16[8,3,128,2048]{3,2,1,0:T(8,128)(2,1)} %bitcast.145, ...), custom_call_target="tpu_custom_call" | custom-call | flops 17179869184 | bytes 12582912 | tf_op jit(solution)/shard_map/ffn_down/pallas_call | solution.py:469
  833.3 8.8 place_parts.3
  842.3 2.9 multiply_reduce_fusion.1
  846.9 1.4 fusion.12
  848.3 1.5 pad_maximum_fusion.1
  849.8 23.3 %transfer.6 = bf16[4,256,1408]{2,1,0:T(8,128)(2,1)} custom-call(bf16[4,256,2048]{2,1,0:T(8,128)(2,1)} %bitcast.121, bf16[256,1408]{1,0:T(8,128)(2,1)} %reduce-scatter.8.cloned.1.call-done.refs_1_), custom_call_target="tpu_custom_call" | custom-call | tf_op jit(solution)/shard_map/transfer/pallas_call | solution.py:469
  873.1 2.9 slice.81.parts_ref
  876.0 4.7 place_heads.1
  880.7 1.6 slice_reduce_fusion
  882.2 1.5 slice_reduce_fusion.2
  883.7 0.8 copy.72
  884.6 1.6 reshape.265.refs_1_
  886.2 40.1 %transfer.7 = (bf16[256,2048]{1,0:T(8,128)(2,1)}, f32[256,2048]{1,0:T(8,128)}) custom-call(bf16[4,256,2048]{2,1,0:T(8,128)(2,1)} %bitcast.122, bf16[4,64,2048]{2,1,0:T(8,128)(2,1)} %reshape.265.refs_1_, bf16[4,256,2048]{2,1,0:T(8,128)(2,1)} %bitcast.123), custom_call_target="tpu_custom_call" | custom-call | tf_op jit(solution)/shard_map/transfer/pallas_call | solution.py:469
  926.4 2.9 convert_element_type.88
  929.3 1.8 fusion.11
  931.2 1.5 pad_maximum_fusion
  (132 shorter events, 10.2 us)
Async XLA Ops:
  7.2 54.7 %all-gather.7.cloned.1.call-start = ((), (), s32[]{:S(2)}) async-start(), calls=%async_computation.3 | async-start | bytes 3538944 | tf_op jit(solution)/shard_map/all_gather | solution.py:1126
  9.9 95.7 %all-gather.9.cloned.1.call-start = ((), (), s32[]{:S(2)}) async-start(), calls=%async_computation.4 | async-start | bytes 2359296 | tf_op jit(solution)/shard_map/all_gather | solution.py:1133
  12.1 2.1 copy-start
  12.1 2.1 copy-start.27
  13.3 2.6 copy-start.33
  13.3 2.6 copy-start.35
  54.5 1.5 copy-start.42
  54.5 1.4 copy-start.43
  54.6 2.1 copy-start.37
  54.6 3.3 copy-start.23
  54.6 182.4 %all-gather.13.cloned.1.call-start = ((), (), s32[]{:S(2)}) async-start(), calls=%async_computation.9 | async-start | bytes 14155776 | tf_op jit(solution)/shard_map/all_gather | solution.py:1136
  55.3 272.7 %all-gather.11.cloned.1.call-start = ((), (), s32[]{:S(2)}) async-start(), calls=%async_computation.8 | async-start | bytes 14155776 | tf_op jit(solution)/shard_map/all_gather | solution.py:1136
  55.9 574.8 %reduce-scatter.4.cloned.1.call-start = ((), (), s32[]{:S(2)}) async-start(), calls=%async_computation.5 | async-start | bytes 14155776 | tf_op jit(solution)/shard_map/reduce_scatter | solution.py:1207
  57.3 0.6 copy-start.29
  58.2 2.0 copy-start.10
  112.3 45.3 %copy-start.1 = (f32[2,256,2048]{2,1,0:T(8,128)S(1)}, f32[2,256,2048]{2,1,0:T(8,128)}, u32[]{:S(2)}) copy-start(f32[2,256,2048]{2,1,0:T(8,128)} %copy-done) | copy-start | bytes 12582916
  157.7 3.2 copy-start.25
  159.6 1.3 copy-start.4
  162.2 70.4 %copy-start.21 = (bf16[4,256,512]{2,1,0:T(8,128)(2,1)S(1)}, bf16[4,256,512]{2,1,0:T(8,128)(2,1)}, u32[]{:S(2)}) copy-start(bf16[4,256,512]{2,1,0:T(8,128)(2,1)} %get-tuple-element.74.refs_0_) | copy-start | bytes 3145732
  162.2 70.4 %copy-start.45 = (bf16[512,2048]{1,0:T(8,128)(2,1)S(1)}, bf16[512,2048]{1,0:T(8,128)(2,1)}, u32[]{:S(2)}) copy-start(bf16[512,2048]{1,0:T(8,128)(2,1)} %all-gather.9.cloned.1.call-done.refs_3_) | copy-start | bytes 6291460
  237.0 73.1 %copy-start.2 = (f32[2,256,2048]{2,1,0:T(8,128)S(1)}, f32[2,256,2048]{2,1,0:T(8,128)}, u32[]{:S(2)}) copy-start(f32[2,256,2048]{2,1,0:T(8,128)} %copy-done) | copy-start | bytes 12582916
  312.1 1.3 copy-start.7
  312.7 0.7 copy-start.31
  370.2 40.8 %copy-start.5 = (f32[256,2048]{1,0:T(8,128)S(1)}, f32[256,2048]{1,0:T(8,128)}, u32[]{:S(2)}) copy-start(f32[256,2048]{1,0:T(8,128)} %copy-done.4) | copy-start | bytes 6291460
  411.0 2.8 copy-start.11
  455.9 288.3 %reduce-scatter.6.cloned.1.call-start = ((), (), s32[]{:S(2)}) async-start(), calls=%async_computation.6 | async-start | bytes 14155776 | tf_op jit(solution)/shard_map/reduce_scatter | solution.py:1214
  548.1 1.6 copy-start.8
  548.1 1.6 copy-start.32
  548.1 4.0 copy-start.24
  548.1 301.7 %reduce-scatter.8.cloned.1.call-start = ((), (), s32[]{:S(2)}) async-start(), calls=%async_computation.7 | async-start | bytes 6488064 | tf_op jit(solution)/shard_map/reduce_scatter | solution.py:1252
  549.7 3.0 copy-start.20
  552.7 4.5 copy-start.12
  552.7 4.5 copy-start.18
  552.7 4.5 copy-start.38
  559.5 51.8 %copy-start.13 = (f32[512,2048,1]{1,0,2:T(8,128)S(1)}, f32[512,2048,1]{1,0,2:T(8,128)}, u32[]{:S(2)}) copy-start(f32[512,2048,1]{1,0,2:T(8,128)} %fusion.21) | copy-start | bytes 12582916
  559.5 51.8 %copy-start.22 = (bf16[4,256,512]{2,1,0:T(8,128)(2,1)S(1)}, bf16[4,256,512]{2,1,0:T(8,128)(2,1)}, u32[]{:S(2)}) copy-start(bf16[4,256,512]{2,1,0:T(8,128)(2,1)} %get-tuple-element.74.refs_0_) | copy-start | bytes 3145732
  620.6 3.0 copy-start.44
  630.7 89.8 %copy-start.41 = (f32[2,128]{1,0:T(2,128)S(1)}, f32[2,128]{1,0:T(2,128)}, u32[]{:S(2)}) copy-start(f32[2,128]{1,0:T(2,128)} %get-tuple-element.104) | copy-start | bytes 3076
  721.7 8.2 copy-start.14
  732.9 0.7 copy-start.30
  732.9 1.6 copy-start.6
  833.3 8.9 copy-start.3
  833.3 8.9 copy-start.28
  842.2 3.0 copy-start.15
  842.2 3.5 copy-start.16
  842.2 4.1 copy-start.17
  842.2 4.7 copy-start.19
  842.2 4.7 copy-start.34
  842.2 4.7 copy-start.36
  842.2 4.7 copy-start.39
  842.2 4.7 copy-start.40
  876.0 7.8 slice-start
  886.1 40.2 %copy-start.26 = (f32[256,128]{1,0:T(8,128)S(1)}, f32[256,128]{1,0:T(8,128)}, u32[]{:S(2)}) copy-start(f32[256,128]{1,0:T(8,128)} %get-tuple-element.111) | copy-start | bytes 393220
  926.3 3.1 copy-start.9
Sparse Core Ops, SparseCore 0:
  10.2 49.3 all-gather.6
  61.2 32.4 all-gather.8
  95.3 116.2 all-gather.12
  213.1 114.9 all-gather.10
  456.0 128.3 reduce-scatter.3
  586.6 127.5 reduce-scatter.5
  733.0 62.9 reduce-scatter.7

commit v8 on v7

--- a/solution.py
+++ b/solution.py
@@ -204,50 +204,52 @@
     return greeting, begin, nothing, finish
 
 
-def swap_job(sources, targets, scratch):
+def spread_job(sources, targets, scratch):
     (source,) = sources
-    (target,) = targets
-    outs, ins, here = scratch
-    count, rows, _ = source.shape
+    gathered, target = targets
+    *first, z_outs, z_ins, z_here = scratch
+    _, begin_gather, middle_gather, finish_gather = gather_job(sources, [gathered], first)
+    count = gathered.shape[0]
     place = lax.axis_index("seq")
     shard = lax.axis_index("fsdp")
     per = lax.axis_size("fsdp") // count
     piece = shard % count
-    spot = pl.ds(pl.multiple_of(piece * rows, rows), rows)
 
     def owner(j):
         return true_chunk(place, j, count) * per + shard // count
 
+    def chunk(j):
+        return gathered.at[j] if j else source
+
     def copy(j):
         return pltpu.make_async_remote_copy(
-            src_ref=source.at[j],
-            dst_ref=target.at[spot],
-            send_sem=outs.at[j],
-            recv_sem=ins.at[piece],
+            src_ref=chunk(j),
+            dst_ref=target.at[piece],
+            send_sem=z_outs.at[j],
+            recv_sem=z_ins.at[piece],
             device_id={"fsdp": owner(j)},
             device_id_type=pl.DeviceIdType.MESH,
         )
 
     def arrival(p):
         return pltpu.make_async_remote_copy(
-            src_ref=source.at[0],
-            dst_ref=target.at[pl.ds(p * rows, rows)],
-            send_sem=outs.at[0],
-            recv_sem=ins.at[p],
+            src_ref=source,
+            dst_ref=target.at[p],
+            send_sem=z_outs.at[0],
+            recv_sem=z_ins.at[p],
             device_id={"fsdp": owner(0)},
             device_id_type=pl.DeviceIdType.MESH,
         )
 
     def local(j):
-        return pltpu.make_async_copy(source.at[j], target.at[spot], here.at[0])
+        return pltpu.make_async_copy(chunk(j), target.at[piece], z_here.at[0])
 
     def origin(p):
         return (shard % per) * count + p
 
-    def each(act_remote, act_local):
-        for j in range(count):
-            pl.when(owner(j) != shard)(lambda j=j: act_remote(copy(j)))
-            pl.when(owner(j) == shard)(lambda j=j: act_local(local(j)))
+    def start(j):
+        pl.when(owner(j) != shard)(lambda: copy(j).start())
+        pl.when(owner(j) == shard)(lambda: local(j).start())
 
     def greeting(barrier):
         for p in range(count):
@@ -255,14 +257,24 @@
         return jnp.where(shard % per == shard // count, count - 1, count)
 
     def begin():
-        each(lambda c: c.start(), lambda c: c.start())
+        begin_gather()
+        start(0)
+
+    def middle():
+        middle_gather()
+        start(1)
+        start(2)
 
     def finish():
-        each(lambda c: c.wait_send(), lambda c: c.wait())
+        finish_gather()
+        start(3)
+        for j in range(count):
+            pl.when(owner(j) != shard)(lambda j=j: copy(j).wait_send())
+            pl.when(owner(j) == shard)(lambda j=j: local(j).wait())
         for p in range(count):
             pl.when(origin(p) != shard)(lambda p=p: arrival(p).wait_recv())
 
-    return greeting, begin, nothing, finish
+    return greeting, begin, middle, finish
 
 
 def own_job(sources, targets, scratch):
@@ -300,7 +312,7 @@
     "gather": gather_job,
     "scatter": scatter_job,
     "deal": deal_job,
-    "swap": swap_job,
+    "spread": spread_job,
     "own": own_job,
 }
 
@@ -335,7 +347,16 @@
         pltpu.SemaphoreType.DMA((4,)),
         pltpu.SemaphoreType.DMA((2,)),
     ]
-    return moves + [pltpu.VMEM(arrays[0].shape, BF16)] if kind == "gather" else moves
+    if kind == "deal":
+        return moves
+    moves.append(pltpu.VMEM(arrays[0].shape, BF16))
+    if kind == "spread":
+        moves += [
+            pltpu.SemaphoreType.DMA((4,)),
+            pltpu.SemaphoreType.DMA((4,)),
+            pltpu.SemaphoreType.DMA((1,)),
+        ]
+    return moves
 
 
 def job_results(job):
@@ -347,8 +368,8 @@
         return [jax.ShapeDtypeStruct(shape[1:], F32)]
     if kind == "deal":
         return [jax.ShapeDtypeStruct((shape[0] // 4,) + shape[1:], BF16)]
-    if kind == "swap":
-        return [jax.ShapeDtypeStruct((shape[0] * shape[1], shape[2]), BF16)]
+    if kind == "spread":
+        return [jax.ShapeDtypeStruct((4,) + shape, BF16)] * 2
     part = shape[0] // lax.axis_size("seq") // CHUNKS
     return [jax.ShapeDtypeStruct((len(arrays), part) + shape[1:], BF16)] * CHUNKS
 
@@ -371,20 +392,21 @@
             got = lax.ppermute(arrays[0][j * rows : (j + 1) * rows], ("seq", "fsdp"), moves)
             total = got if total is None else total + got
         return [total]
-    if kind == "swap":
-        total = None
-        for q in range(seqs):
-            for p in range(seqs):
+    if kind == "spread":
+        gathered = lax.all_gather(arrays[0], "seq", axis=0)
+        pieces = []
+        for p in range(seqs):
+            total = None
+            for q in range(seqs):
                 moves = [
                     (s * shards + h * seqs + p, s * shards + q * per + h)
                     for s in range(seqs)
                     for h in range(per)
                 ]
-                got = lax.ppermute(arrays[0][q], ("seq", "fsdp"), moves)
-                rows = got.shape[0]
-                got = jnp.pad(got, ((p * rows, (seqs - 1 - p) * rows), (0, 0)))
+                got = lax.ppermute(gathered[q], ("seq", "fsdp"), moves)
                 total = got if total is None else total + got
-        return [total]
+            pieces.append(total)
+        return [gathered, jnp.stack(pieces)]
     own_rows = arrays[0].shape[0] // seqs
     part = own_rows // CHUNKS
     start = lax.axis_index("seq") * own_rows
@@ -575,7 +597,7 @@
             lse_ref[h, rows, :] = highest + jnp.log(total)
             return 0
 
-        lax.fori_loop(0, hq, one_head, 0)
+        lax.fori_loop(0, hq, one_head, 0, unroll=min(4, hq))
         if i == seqs * rows_in // BLOCK - 2:
             hook(1)
     for c in range(seqs):
@@ -628,7 +650,7 @@
             dv_s[kv, :keys, :] += dot(probs.astype(BF16), cot, TN)
             return 0
 
-        lax.fori_loop(0, hq, one_head, 0)
+        lax.fori_loop(0, hq, one_head, 0, unroll=min(4, hq))
         if i == seqs * rows_in // BLOCK - 2:
             hook(1)
     gain_sums = [jnp.zeros((1, 128), F32), jnp.zeros((1, 128), F32)]
@@ -1250,15 +1272,18 @@
         axis=1,
     )
     attn_sums = lax.psum_scatter(attn_grads, "fsdp", scatter_dimension=0, tiled=True)
-    out_1, (in_total_1, ffn_parts_1) = leave_ffn(
-        1, [("scatter", pull_1), ("gather", ffn_sums[1])], 13, attn_grads
-    )
-    (heads_all,) = transfer([("gather", attn_sums)], 14, out_1)
+    out_1, (in_total_1,) = leave_ffn(1, [("scatter", pull_1)], 13, attn_grads)
+    (out_total_1,) = transfer([("scatter", out_1)], 14, in_total_1)
+    ffn_parts_1 = lax.all_gather(follow(ffn_sums[1], [attn_sums, in_total_1]), "seq", axis=0)
     out_edge = attn_sums.shape[1] - model // blocks
-    out_pieces = jnp.swapaxes(
-        heads_all[..., out_edge:].reshape(seqs, blocks, piece, model // blocks), 1, 2
-    ).reshape(seqs, piece, model)
-    grad_out, out_total_1 = transfer([("swap", out_pieces), ("scatter", out_1)], 15, out_1)
+    heads_all, _, out_parts = transfer(
+        [("gather", attn_sums[:, :out_edge]), ("spread", attn_sums[:, out_edge:])],
+        15,
+        out_total_1,
+    )
+    grad_out = jnp.swapaxes(
+        out_parts.reshape(seqs, blocks, piece, model // blocks), 1, 2
+    ).reshape(held, model)
     grad_tokens = []
     for b, (in_cot, cot) in enumerate(((in_total_0, res_cot_0), (in_total_1, res_cot_1))):
         pull, _ = normed_back(inputs[b], attn_gain, in_cot)
@@ -1269,18 +1294,18 @@
     ]
     ffn_grad = ()
     for c, parts in enumerate((ffn_parts_0, ffn_parts_1)):
-        ffn_grad = place_parts(order, parts.reshape(seqs, 3, part, model), c, ffn_grad)
+        ffn_grad = place_parts(order * (1 - c), parts.reshape(seqs, 3, part, model), c, ffn_grad)
     ffn_grad = [v.reshape(seqs * hidden_own, model) for v in ffn_grad]
 
     edge = hq * HEAD
     width = hkv_held * HEAD
     if hkv == hkv_held:
         grad_query, grad_key, grad_value, gain_sums, met = place_heads(
-            order, heads_all[..., :out_edge], edge, width, (query_weight, key_weight, value_weight)
+            order, heads_all, edge, width, (query_weight, key_weight, value_weight)
         )
         met = met[:, 0]
     else:
-        heads_all = jnp.moveaxis(heads_all[..., :out_edge], 0, 1).astype(F32)
+        heads_all = jnp.moveaxis(heads_all, 0, 1).astype(F32)
         last = edge + width
         grad_query = heads_all[..., :edge].reshape(held, query_width)
         grad_key = heads_all[..., edge : edge + hkv * HEAD].reshape(held, kv_width)

time: 946 us -> 955 us (level)
  waiting for transfers between devices: 14.8 us -> 40.8 us
  Pallas kernels: 800 us -> 788 us
    reduce_scatter x1, waiting for transfers between devices: 0.01 us -> 22.9 us  [on_device(): lax.psum_scatter(attn_grads, 'fsdp', scatter_dimension=0, tiled=True)]
    pallas_call x16, Pallas kernels: 778 us -> 767 us  [call(): pl.pallas_call(kernel, grid=grid, out_shape=tuple(out_shape) + tuple(shap...]
  transfers between devices with their start and end apart: 7 -> 8, of which waited for: 1 -> 2; matrix products, arithmetic and copies ran while one was open for 8% -> 9% of each run, Pallas kernels for 65% -> 69%
where the time goes in v8:
time: 955 us; the launch traced here: 951 us
  Pallas kernels  788 us (83%)
  waiting for transfers between devices  40.8 us (4%)
  other arithmetic  39.7 us (4%)
  matrix products  36.6 us (4%)
  local copies, waits for them, and re-layouts  30.8 us (3%)
  between operations  15.1 us (2%)
    pallas_call x16, Pallas kernels, call(): pl.pallas_call(kernel, grid=grid, out_shape=tuple(out_shape) + tuple(shap...  767 us
    dot_general x6, matrix products, dot(): return lax.dot_general(a, b, dims, preferred_element_type=F32)  36.6 us
    reduce_scatter x1, waiting for transfers between devices, on_device(): lax.psum_scatter(attn_grads, 'fsdp', scatter_dimension=0, tiled=True)  22.9 us
  transfers between devices with their start and end apart: 8, of which 2 were waited for; matrix products, arithmetic and copies ran while one was open for 9% of the time, Pallas kernels for 69%

profile of v8, /device:TPU:6, one launch (start us, length us, event | category | flops | bytes accessed | tf_op | source)
XLA Modules:
  0.0 951.5 jit_solution(7891365652806370382)
XLA Ops:
  7.2 1.0 constant_dynamic-slice_fusion.2
  8.2 0.9 constant_dynamic-slice_fusion
  9.1 0.8 pad_maximum_fusion.2
  10.0 2.1 convert_element_type.79
  12.4 0.9 multiply_multiply_fusion
  13.3 0.8 copy-done
  14.1 1.7 multiply_convert_fusion.4
  15.9 38.7 %transfer.4 = (bf16[4,256,2048]{2,1,0:T(8,128)(2,1)}, bf16[64,2048]{1,0:T(8,128)(2,1)}, bf16[3,128,2048]{2,1,0:T(8,128)(2,1)}, bf16[3,128,2048]{2,1,0:T(8,128)(2,1)}) custom-call(bf16[256,2048]{1,0:T(8,128)(2,1)} %get-tuple-element.146.refs_0_, bf16[256,2048]{1,0:T(8,128)(2,1)} %refs_1_.1, bf16[1024,2048]{1,0:T(8,128)(2,1)} %refs_2_.1, ...), custom_call_target="tpu_custom_call" | custom-call | tf_op jit(solution)/shard_map/transfer/pallas_call | solution.py:491
  58.2 2.0 copy-done.10
  60.2 1.6 fusion.7
  61.8 44.6 %attend.2 = (bf16[4,256,512]{2,1,0:T(8,128)(2,1)}, f32[8,1024,1]{2,1,0:T(8,128)}, bf16[4,256,768]{2,1,0:T(8,128)(2,1)}, bf16[4,256,2048]{2,1,0:T(8,128)(2,1)}) custom-call(s32[1]{0:T(128)} %get-tuple-element.161.refs_0_, bf16[4,256,2048]{2,1,0:T(8,128)(2,1)} %get-tuple-element.69.refs_1_.refs_8_, ...), custom_call_target="tpu_custom_call" | custom-call | flops 30064771072 | bytes 8388608 | tf_op jit(solution)/shard_map/attend/pallas_call | solution.py:491
  106.4 6.4 convolution_convert_fusion.1
  112.9 43.4 %attend.3 = (bf16[4,256,512]{2,1,0:T(8,128)(2,1)}, f32[8,1024,1]{2,1,0:T(8,128)}, bf16[4,256,768]{2,1,0:T(8,128)(2,1)}, f32[256,2048]{1,0:T(8,128)}) custom-call(s32[1]{0:T(128)} %get-tuple-element.162.refs_0_, bf16[4,256,2048]{2,1,0:T(8,128)(2,1)} %get-tuple-element.70.refs_1_, bf16[2048,768]{1,0:T(8,128)(2,1)} %all-gather.9.cloned.1.call-done.refs_2_.refs_4_, ...), custom_call_target="tpu_custom_call" | custom-call | flops 30064771072 | bytes 8388608 | tf_op jit(solution)/shard_map/attend/pallas_call | solution.py:491
  156.3 1.9 multiply_reduce_fusion.7
  158.2 1.3 copy-done.4
  159.5 1.2 multiply_convert_fusion.3.refs_1_
  160.7 69.7 %transfer.5 = (bf16[4,256,2048]{2,1,0:T(8,128)(2,1)}, bf16[4,256,2048]{2,1,0:T(8,128)(2,1)}) custom-call(bf16[4,256,512]{2,1,0:T(8,128)(2,1)} %get-tuple-element.74.refs_0_, bf16[256,2048]{1,0:T(8,128)(2,1)} %multiply_convert_fusion.3.refs_1_, bf16[256,2048]{1,0:T(8,128)(2,1)} %get-tuple-element.148.refs_2_), custom_call_target="tpu_custom_call" | custom-call | tf_op jit(solution)/shard_map/transfer/pallas_call | solution.py:491
  230.5 4.4 convolution_convert_fusion
  234.8 72.4 %ffn_both.4 = (bf16[3,1024,1024]{2,1,0:T(8,128)(2,1)}, f32[1024,2048]{1,0:T(8,128)}, f32[256,2048]{1,0:T(8,128)}, bf16[4,256,2048]{2,1,0:T(8,128)(2,1)}) custom-call(bf16[1024,2048]{1,0:T(8,128)(2,1)} %bitcast.153, bf16[1024,2048]{1,0:T(8,128)(2,1)} %bitcast.158, bf16[8,3,128,2048]{3,2,1,0:T(8,128)(2,1)} %bitcast.145, bf16[1024,2048]{1,0:T(8,128)(2,1)} %bitcast.154, ...), custom_call_target="tpu_custom_call" | custom-call | flops 34359738368 | bytes 20971520 | tf_op jit(solution)/shard_map/ffn_both/pallas_call | solution.py:491
  307.2 1.9 multiply_reduce_fusion.6
  310.4 1.2 multiply_convert_fusion.2.refs_5_
  311.7 16.5 %all-gather.13.cloned.1.call-done = bf16[24,128,2048]{2,1,0:T(8,128)(2,1)} async-done(((bf16[3,128,2048]{2,1,0:T(8,128)(2,1)}), bf16[24,128,2048]{2,1,0:T(8,128)(2,1)}) %all-gather.13.cloned.1.call-update) | async-done | bytes 12582928 | tf_op jit(solution)/shard_map/all_gather | solution.py:1158
  328.2 42.1 %ffn_both.5 = (bf16[3,1024,1024]{2,1,0:T(8,128)(2,1)}, bf16[1024,2048]{1,0:T(8,128)(2,1)}, bf16[4,256,2048]{2,1,0:T(8,128)(2,1)}) custom-call(bf16[1024,2048]{1,0:T(8,128)(2,1)} %bitcast.155, bf16[1024,2048]{1,0:T(8,128)(2,1)} %bitcast.159, bf16[8,3,128,2048]{3,2,1,0:T(8,128)(2,1)} %bitcast.149, f32[1024,2048]{1,0:T(8,128)} %get-tuple-element.79.refs_3_, ...), custom_call_target="tpu_custom_call" | custom-call | flops 34359738368 | bytes 20971520 | tf_op jit(solution)/shard_map/ffn_both/pallas_call | solution.py:491
  370.3 40.7 %ffn_both.6 = (bf16[3,1024,1024]{2,1,0:T(8,128)(2,1)}, f32[1024,2048]{1,0:T(8,128)}, f32[256,2048]{1,0:T(8,128)}) custom-call(bf16[1024,2048]{1,0:T(8,128)(2,1)} %bitcast.167, bf16[1024,2048]{1,0:T(8,128)(2,1)} %bitcast.163, bf16[8,3,128,2048]{3,2,1,0:T(8,128)(2,1)} %bitcast.146, bf16[3,1024,1024]{2,1,0:T(8,128)(2,1)} %get-tuple-element.84.refs_3_.refs_1_.refs_0_, ...), custom_call_target="tpu_custom_call" | custom-call | flops 34359738368 | bytes 20971520 | tf_op jit(solution)/shard_map/ffn_both/pallas_call | solution.py:491
  411.1 2.3 multiply_reduce_fusion.3
  413.9 3.9 fusion.15
  417.8 38.2 %ffn_grads.2 = (bf16[8,3,128,2048]{3,2,1,0:T(8,128)(2,1)}, bf16[4,256,2048]{2,1,0:T(8,128)(2,1)}) custom-call(bf16[3,1024,1024]{2,1,0:T(8,128)(2,1)} %get-tuple-element.80.refs_4_.refs_0_, bf16[3,1024,1024]{2,1,0:T(8,128)(2,1)} %get-tuple-element.87.refs_1_.refs_6_.refs_0_, bf16[1024,2048]{1,0:T(8,128)(2,1)} %bitcast.156, bf16[1024,2048]{1,0:T(8,128)(2,1)} %bitcast.168, ...), custom_call_target="tpu_custom_call" | custom-call | flops 38654705664 | bytes 16777216 | tf_op jit(solution)/shard_map/ffn_grads/pallas_call | solution.py:491
  456.1 14.4 %ffn_down.2 = bf16[1024,2048]{1,0:T(8,128)(2,1)} custom-call(bf16[3,1024,1024]{2,1,0:T(8,128)(2,1)} %get-tuple-element.80.refs_4_.refs_0_, bf16[3,1024,1024]{2,1,0:T(8,128)(2,1)} %get-tuple-element.84.refs_3_.refs_1_.refs_0_, bf16[8,3,128,2048]{3,2,1,0:T(8,128)(2,1)} %bitcast.147, bf16[8,3,128,2048]{3,2,1,0:T(8,128)(2,1)} %bitcast.150, ...), custom_call_target="tpu_custom_call" | custom-call | flops 17179869184 | bytes 12582912 | tf_op jit(solution)/shard_map/ffn_down/pallas_call | solution.py:491
  470.5 38.9 %ffn_both.7 = (bf16[3,1024,1024]{2,1,0:T(8,128)(2,1)}, bf16[1024,2048]{1,0:T(8,128)(2,1)}, f32[256,2048]{1,0:T(8,128)}) custom-call(bf16[1024,2048]{1,0:T(8,128)(2,1)} %bitcast.169, bf16[1024,2048]{1,0:T(8,128)(2,1)} %bitcast.165, bf16[8,3,128,2048]{3,2,1,0:T(8,128)(2,1)} %bitcast.151, f32[1024,2048]{1,0:T(8,128)} %get-tuple-element.86.refs_3_, ...), custom_call_target="tpu_custom_call" | custom-call | flops 34359738368 | bytes 20971520 | tf_op jit(solution)/shard_map/ffn_both/pallas_call | solution.py:491
  509.4 38.8 %ffn_grads.3 = (bf16[8,3,128,2048]{3,2,1,0:T(8,128)(2,1)}, f32[256,2048]{1,0:T(8,128)}) custom-call(bf16[3,1024,1024]{2,1,0:T(8,128)(2,1)} %get-tuple-element.84.refs_3_.refs_1_.refs_0_, bf16[3,1024,1024]{2,1,0:T(8,128)(2,1)} %get-tuple-element.91.refs_1_.refs_6_, bf16[1024,2048]{1,0:T(8,128)(2,1)} %bitcast.157, bf16[1024,2048]{1,0:T(8,128)(2,1)} %bitcast.170, ...), custom_call_target="tpu_custom_call" | custom-call | flops 38654705664 | bytes 16777216 | tf_op jit(solution)/shard_map/ffn_grads/pallas_call | solution.py:491
  548.7 1.1 copy-done.8
  549.8 2.4 multiply_reduce_fusion.2
  552.8 4.4 fusion.21
  557.3 2.3 fusion.14
  559.6 47.6 %attend_back.2 = (bf16[4,256,768]{2,1,0:T(8,128)(2,1)}, f32[2,128]{1,0:T(2,128)}, bf16[4,256,2048]{2,1,0:T(8,128)(2,1)}, bf16[4,256,2048]{2,1,0:T(8,128)(2,1)}) custom-call(s32[1]{0:T(128)} %get-tuple-element.161.refs_0_, bf16[4,256,768]{2,1,0:T(8,128)(2,1)} %get-tuple-element.92.refs_1_, bf16[4,256,2048]{2,1,0:T(8,128)(2,1)} %get-tuple-element.93.refs_2_, ...), custom_call_target="tpu_custom_call" | custom-call | flops 47244640256 | bytes 8388608 | tf_op jit(solution)/shard_map/attend_back/pallas_call | solution.py:491
  607.2 6.0 fusion.5.refs_11_
  613.1 3.3 reshape.261
  616.5 1.8 copy.59
  618.3 1.2 copy-done.45
  619.5 7.3 fusion.20
  626.8 89.8 %attend_back.3 = (bf16[4,256,768]{2,1,0:T(8,128)(2,1)}, f32[2,128]{1,0:T(2,128)}, bf16[4,256,2048]{2,1,0:T(8,128)(2,1)}, f32[256,2048]{1,0:T(8,128)}, bf16[4,384,2048]{2,1,0:T(8,128)(2,1)}) custom-call(s32[1]{0:T(128)} %get-tuple-element.162.refs_0_, bf16[4,256,768]{2,1,0:T(8,128)(2,1)} %get-tuple-element.99.refs_1_, ...), custom_call_target="tpu_custom_call" | custom-call | flops 47244640256 | bytes 8388608 | tf_op jit(solution)/shard_map/attend_back/pallas_call | solution.py:491
  717.9 8.2 fusion.2
  726.1 2.9 fusion.4.refs_4_
  729.1 40.1 %ffn_down.3 = (bf16[1024,2048]{1,0:T(8,128)(2,1)}, f32[256,2048]{1,0:T(8,128)}) custom-call(bf16[3,1024,1024]{2,1,0:T(8,128)(2,1)} %get-tuple-element.87.refs_1_.refs_6_.refs_0_, bf16[3,1024,1024]{2,1,0:T(8,128)(2,1)} %get-tuple-element.91.refs_1_.refs_6_, bf16[8,3,128,2048]{3,2,1,0:T(8,128)(2,1)} %bitcast.148, bf16[8,3,128,2048]{3,2,1,0:T(8,128)(2,1)} %bitcast.152, ...), custom_call_target="tpu_custom_call" | custom-call | flops 17179869184 | bytes 12582912 | tf_op jit(solution)/shard_map/ffn_down/pallas_call | solution.py:491
  769.2 22.9 %reduce-scatter.6.cloned.1.call-done = bf16[256,1408]{1,0:T(8,128)(2,1)} async-done(((bf16[2048,1408]{1,0:T(8,128)(2,1)}), bf16[256,1408]{1,0:T(8,128)(2,1)}) %reduce-scatter.6.cloned.1.call-update) | async-done | bytes 720912 | tf_op jit(solution)/shard_map/reduce_scatter | solution.py:1274
  792.2 1.8 fusion.10
  794.1 54.0 %transfer.6.refs_0_ = f32[256,2048]{1,0:T(8,128)} custom-call(f32[256,2048]{1,0:T(8,128)} %get-tuple-element.107.refs_0_, bf16[4,256,2048]{2,1,0:T(8,128)(2,1)} %bitcast.135), custom_call_target="tpu_custom_call" | custom-call | tf_op jit(solution)/shard_map/transfer/pallas_call | solution.py:491
  848.1 8.7 place_parts.2
  856.8 2.9 multiply_reduce_fusion.1
  860.6 1.5 pad_maximum_fusion
  862.1 1.1 copy-done.19
  864.6 1.3 fusion.12
  865.9 1.5 pad_maximum_fusion.1
  867.4 0.7 slice.95.refs_2_
  868.1 0.8 slice.94.refs_1_
  868.9 53.4 %transfer.7 = (bf16[4,256,896]{2,1,0:T(8,128)(2,1)}, bf16[4,256,512]{2,1,0:T(8,128)(2,1)}, bf16[4,256,512]{2,1,0:T(8,128)(2,1)}) custom-call(f32[256,2048]{1,0:T(8,128)} %transfer.6.refs_0_, bf16[256,896]{1,0:T(8,128)(2,1)} %slice.94.refs_1_, bf16[256,512]{1,0:T(8,128)(2,1)} %slice.95.refs_2_), custom_call_target="tpu_custom_call" | custom-call | tf_op jit(solution)/shard_map/transfer/pallas_call | solution.py:491
  922.4 1.5 convert_bitcast_fusion
  923.9 1.4 copy.60
  925.2 2.2 copy.71
  927.4 4.6 place_heads.1
  932.0 1.5 slice_reduce_fusion.2
  933.5 1.6 slice_reduce_fusion
  935.0 1.0 slice_reduce_fusion.1
  936.7 7.7 place_parts.3
  (136 shorter events, 11.3 us)
Async XLA Ops:
  7.2 54.7 %all-gather.9.cloned.1.call-start = ((), (), s32[]{:S(2)}) async-start(), calls=%async_computation.3 | async-start | bytes 3538944 | tf_op jit(solution)/shard_map/all_gather | solution.py:1148
  9.9 96.5 %all-gather.11.cloned.1.call-start = ((), (), s32[]{:S(2)}) async-start(), calls=%async_computation.4 | async-start | bytes 2359296 | tf_op jit(solution)/shard_map/all_gather | solution.py:1155
  12.1 2.1 copy-start
  12.1 2.1 copy-start.28
  13.3 2.6 copy-start.34
  13.3 2.6 copy-start.36
  54.5 1.5 copy-start.43
  54.5 1.4 copy-start.44
  54.6 2.1 copy-start.38
  54.6 3.3 copy-start.24
  54.6 180.2 %all-gather.15.cloned.1.call-start = ((), (), s32[]{:S(2)}) async-start(), calls=%async_computation.9 | async-start | bytes 14155776 | tf_op jit(solution)/shard_map/all_gather | solution.py:1158
  55.3 272.9 %all-gather.13.cloned.1.call-start = ((), (), s32[]{:S(2)}) async-start(), calls=%async_computation.8 | async-start | bytes 14155776 | tf_op jit(solution)/shard_map/all_gather | solution.py:1158
  55.9 570.9 %reduce-scatter.4.cloned.1.call-start = ((), (), s32[]{:S(2)}) async-start(), calls=%async_computation.5 | async-start | bytes 14155776 | tf_op jit(solution)/shard_map/reduce_scatter | solution.py:1229
  57.3 0.6 copy-start.30
  58.2 2.0 copy-start.10
  112.8 43.4 %copy-start.1 = (f32[2,256,2048]{2,1,0:T(8,128)S(1)}, f32[2,256,2048]{2,1,0:T(8,128)}, u32[]{:S(2)}) copy-start(f32[2,256,2048]{2,1,0:T(8,128)} %copy-done) | copy-start | bytes 12582916
  156.3 3.2 copy-start.27
  158.2 1.3 copy-start.4
  160.7 69.7 %copy-start.22 = (bf16[4,256,512]{2,1,0:T(8,128)(2,1)S(1)}, bf16[4,256,512]{2,1,0:T(8,128)(2,1)}, u32[]{:S(2)}) copy-start(bf16[4,256,512]{2,1,0:T(8,128)(2,1)} %get-tuple-element.74.refs_0_) | copy-start | bytes 3145732
  160.7 69.7 %copy-start.46 = (bf16[512,2048]{1,0:T(8,128)(2,1)S(1)}, bf16[512,2048]{1,0:T(8,128)(2,1)}, u32[]{:S(2)}) copy-start(bf16[512,2048]{1,0:T(8,128)(2,1)} %all-gather.11.cloned.1.call-done.refs_3_) | copy-start | bytes 6291460
  234.8 72.4 %copy-start.2 = (f32[2,256,2048]{2,1,0:T(8,128)S(1)}, f32[2,256,2048]{2,1,0:T(8,128)}, u32[]{:S(2)}) copy-start(f32[2,256,2048]{2,1,0:T(8,128)} %copy-done) | copy-start | bytes 12582916
  309.1 1.3 copy-start.7
  309.8 0.7 copy-start.32
  370.3 40.8 %copy-start.5 = (f32[256,2048]{1,0:T(8,128)S(1)}, f32[256,2048]{1,0:T(8,128)}, u32[]{:S(2)}) copy-start(f32[256,2048]{1,0:T(8,128)} %copy-done.4) | copy-start | bytes 6291460
  411.0 2.8 copy-start.11
  456.0 313.2 %reduce-scatter.8.cloned.1.call-start = ((), (), s32[]{:S(2)}) async-start(), calls=%async_computation.7 | async-start | bytes 14155776 | tf_op jit(solution)/shard_map/reduce_scatter | solution.py:1236
  548.2 1.6 copy-start.8
  548.2 1.6 copy-start.33
  548.2 4.0 copy-start.25
  548.2 243.9 %reduce-scatter.6.cloned.1.call-start = ((), (), s32[]{:S(2)}) async-start(), calls=%async_computation.6 | async-start | bytes 6488064 | tf_op jit(solution)/shard_map/reduce_scatter | solution.py:1274
  549.8 3.0 copy-start.21
  552.8 4.5 copy-start.12
  552.8 4.5 copy-start.20
  552.8 4.5 copy-start.39
  559.6 47.6 %copy-start.15 = (f32[512,2048,1]{1,0,2:T(8,128)S(1)}, f32[512,2048,1]{1,0,2:T(8,128)}, u32[]{:S(2)}) copy-start(f32[512,2048,1]{1,0,2:T(8,128)} %fusion.21) | copy-start | bytes 12582916
  559.6 47.6 %copy-start.23 = (bf16[4,256,512]{2,1,0:T(8,128)(2,1)S(1)}, bf16[4,256,512]{2,1,0:T(8,128)(2,1)}, u32[]{:S(2)}) copy-start(bf16[4,256,512]{2,1,0:T(8,128)(2,1)} %get-tuple-element.74.refs_0_) | copy-start | bytes 3145732
  616.5 3.0 copy-start.45
  626.8 89.8 %copy-start.42 = (f32[2,128]{1,0:T(2,128)S(1)}, f32[2,128]{1,0:T(2,128)}, u32[]{:S(2)}) copy-start(f32[2,128]{1,0:T(2,128)} %get-tuple-element.104) | copy-start | bytes 3076
  717.9 8.2 copy-start.16
  729.0 207.7 %all-gather.17.cloned.1.call-start = ((), (), s32[]{:S(2)}) async-start(), calls=%async_computation.10 | async-start | bytes 7864320 | tf_op jit(solution)/shard_map/all_gather | solution.py:1277
  729.1 63.1 %copy-start.31 = (f32[2,256]{1,0:T(2,128)S(1)}, f32[2,256]{1,0:T(2,128)}, u32[]{:S(2)}) copy-start(f32[2,256]{1,0:T(2,128)} %copy-done.30) | copy-start | bytes 6148
  729.1 63.1 %copy-start.6 = (f32[256,2048]{1,0:T(8,128)S(1)}, f32[256,2048]{1,0:T(8,128)}, u32[]{:S(2)}) copy-start(f32[256,2048]{1,0:T(8,128)} %copy-done.4) | copy-start | bytes 6291460
  848.1 8.7 copy-start.3
  848.1 8.7 copy-start.29
  856.8 2.9 copy-start.9
  856.8 3.5 copy-start.13
  860.3 1.8 copy-start.18
  860.3 3.0 copy-start.19
  860.5 3.4 copy-start.14
  860.6 4.0 copy-start.17
  860.6 4.0 copy-start.35
  860.6 4.0 copy-start.37
  860.6 4.0 copy-start.40
  860.6 4.0 copy-start.41
  865.9 1.5 copy-start.26
Sparse Core Ops, SparseCore 0:
  10.2 49.3 all-gather.8
  61.2 32.8 all-gather.10
  95.8 115.8 all-gather.14
  213.2 114.9 all-gather.12
  456.1 128.3 reduce-scatter.3
  586.7 127.5 reduce-scatter.7
  729.1 62.9 reduce-scatter.5
  794.0 90.4 all-gather.16

commit v9 on v8

--- a/solution.py
+++ b/solution.py
@@ -204,6 +204,74 @@
     return greeting, begin, nothing, finish
 
 
+def line_job(sources, targets, scratch):
+    (source,) = sources
+    (target,) = targets
+    far_out, far_in, near_out, near_in, here = scratch
+    shards = target.shape[0]
+    steps = shards // 2
+    shard = lax.axis_index("fsdp")
+    near = shard + 1 - 2 * (shard % 2)
+
+    def away(start, k):
+        return (start + 2 * k) % shards
+
+    def send_line(origin, spot, device, out_sem, in_sem):
+        return pltpu.make_async_remote_copy(
+            src_ref=origin,
+            dst_ref=target.at[spot],
+            send_sem=out_sem,
+            recv_sem=in_sem,
+            device_id={"fsdp": device},
+            device_id_type=pl.DeviceIdType.MESH,
+        )
+
+    own = pltpu.make_async_copy(source, target.at[shard], here.at[0])
+    far = [
+        send_line(source, shard, away(shard, k), far_out.at[k - 1], far_in.at[k - 1])
+        for k in range(1, steps)
+    ]
+    far_came = [
+        send_line(
+            source, away(shard, steps - k), away(shard, k), far_out.at[k - 1], far_in.at[k - 1]
+        )
+        for k in range(1, steps)
+    ]
+    held = [shard] + [away(shard, steps - k) for k in range(1, steps)]
+    close = [
+        send_line(target.at[spot] if k else source, spot, near, near_out.at[k], near_in.at[k])
+        for k, spot in enumerate(held)
+    ]
+    close_came = [
+        send_line(source, away(near, steps - k) if k else near, near, near_out.at[k], near_in.at[k])
+        for k in range(steps)
+    ]
+
+    def greeting(barrier):
+        for k in range(1, steps):
+            greet(barrier, {"fsdp": away(shard, k)})
+        greet(barrier, {"fsdp": near})
+        return steps
+
+    def begin():
+        own.start()
+        for copy in far:
+            copy.start()
+        close[0].start()
+
+    def finish():
+        for k in range(1, steps):
+            far_came[k - 1].wait_recv()
+            close[k].start()
+        for copy in close_came:
+            copy.wait_recv()
+        for copy in far + close:
+            copy.wait_send()
+        own.wait()
+
+    return greeting, begin, nothing, finish
+
+
 def spread_job(sources, targets, scratch):
     (source,) = sources
     gathered, target = targets
@@ -313,6 +381,7 @@
     "scatter": scatter_job,
     "deal": deal_job,
     "spread": spread_job,
+    "line": line_job,
     "own": own_job,
 }
 
@@ -349,6 +418,9 @@
     ]
     if kind == "deal":
         return moves
+    if kind == "line":
+        steps = lax.axis_size("fsdp") // 2
+        return [pltpu.SemaphoreType.DMA((steps,))] * 4 + [pltpu.SemaphoreType.DMA((1,))]
     moves.append(pltpu.VMEM(arrays[0].shape, BF16))
     if kind == "spread":
         moves += [
@@ -370,6 +442,8 @@
         return [jax.ShapeDtypeStruct((shape[0] // 4,) + shape[1:], BF16)]
     if kind == "spread":
         return [jax.ShapeDtypeStruct((4,) + shape, BF16)] * 2
+    if kind == "line":
+        return [jax.ShapeDtypeStruct((lax.axis_size("fsdp"),) + shape, BF16)]
     part = shape[0] // lax.axis_size("seq") // CHUNKS
     return [jax.ShapeDtypeStruct((len(arrays), part) + shape[1:], BF16)] * CHUNKS
 
@@ -392,6 +466,8 @@
             got = lax.ppermute(arrays[0][j * rows : (j + 1) * rows], ("seq", "fsdp"), moves)
             total = got if total is None else total + got
         return [total]
+    if kind == "line":
+        return [lax.all_gather(arrays[0], "fsdp", axis=0)]
     if kind == "spread":
         gathered = lax.all_gather(arrays[0], "seq", axis=0)
         pieces = []
@@ -934,11 +1010,19 @@
     hooked(hook, pl.program_id(0), steps, work)
 
 
-def ffn_down(acts, weights, jobs, number, after):
+def ffn_down(acts, weights, jobs, number, after, true_order=False):
     chunks = len(acts)
     _, tokens, hidden = acts[0].shape
     shards, _, part, model = weights[0].shape
     tile = min(256, tokens)
+    def spot(i):
+        if not true_order or lax.axis_size("seq") != 4:
+            return i
+        place = lax.axis_index("seq")
+        low = (place % 2 + i % 2) % 2
+        high = (place // 2 + i // 2) % 2
+        return low + 2 * high
+
     act_spec = pl.BlockSpec((1, tile, hidden), lambda i: (2, i, 0))
     down_spec = pl.BlockSpec(
         (shards, 1, part, model),
@@ -950,7 +1034,7 @@
         [*acts, *weights],
         [act_spec] * chunks + [down_spec] * chunks,
         [jax.ShapeDtypeStruct((tokens, model), BF16)],
-        [pl.BlockSpec((tile, model), lambda i: (i, 0))],
+        [pl.BlockSpec((tile, model), lambda i: (spot(i), 0))],
         jobs,
         number,
         after,
@@ -1152,7 +1236,6 @@
         ("own", gate_weight, up_weight, down_weight),
     ]
     normal_0, out_own, *ffn_own = transfer(start, 1)
-    out_rows = lax.all_gather(out_own, "fsdp", axis=0, tiled=True)
     hidden_own = gate_weight.shape[0] // seqs
     part = hidden_own // CHUNKS
     ffn_weights = [lax.all_gather(own, "fsdp", axis=0) for own in ffn_own]
@@ -1174,9 +1257,10 @@
     cot_full = [None] * slots
     mid_full = [None] * slots
     normal_full[0] = normal_0
-    (mixed_0, lse_0, qkv_0), (normal_full[1],) = heads(
-        0, [("gather", normal_in[1])], 2, normal_full[0]
-    )
+    (mixed_0, lse_0, qkv_0), (normal_full[1], out_rows) = heads(
+        0, [("gather", normal_in[1]), ("line", out_own)], 2, normal_full[0]
+    )
+    out_rows = out_rows.reshape(-1, model)
     (mixed_1, lse_1, qkv_1), (total_0,) = heads(1, [("scatter", leave(mixed_0))], 3, mixed_0)
     qkv = [qkv_0, qkv_1]
     log_sums = [lse_0, lse_1]
@@ -1203,9 +1287,9 @@
         )
         return grads.reshape(shards, 3 * part, model), results
 
-    def leave_ffn(b, jobs, number, after):
+    def leave_ffn(b, jobs, number, after, true_order=False):
         (out,), results = ffn_down(
-            [acts[c][b] for c in range(CHUNKS)], ffn_weights, jobs, number, after
+            [acts[c][b] for c in range(CHUNKS)], ffn_weights, jobs, number, after, true_order
         )
         return out.reshape(chunked), results
 
@@ -1272,14 +1356,17 @@
         axis=1,
     )
     attn_sums = lax.psum_scatter(attn_grads, "fsdp", scatter_dimension=0, tiled=True)
-    out_1, (in_total_1,) = leave_ffn(1, [("scatter", pull_1)], 13, attn_grads)
-    (out_total_1,) = transfer([("scatter", out_1)], 14, in_total_1)
-    ffn_parts_1 = lax.all_gather(follow(ffn_sums[1], [attn_sums, in_total_1]), "seq", axis=0)
+    out_1, (in_total_1, ffn_parts_1) = leave_ffn(
+        1, [("scatter", pull_1), ("gather", ffn_sums[1])], 13, attn_grads, True
+    )
+    out_total_1 = lax.psum_scatter(
+        follow(out_1, [attn_sums]), "seq", scatter_dimension=0
+    ).astype(F32)
     out_edge = attn_sums.shape[1] - model // blocks
     heads_all, _, out_parts = transfer(
         [("gather", attn_sums[:, :out_edge]), ("spread", attn_sums[:, out_edge:])],
-        15,
-        out_total_1,
+        14,
+        in_total_1,
     )
     grad_out = jnp.swapaxes(
         out_parts.reshape(seqs, blocks, piece, model // blocks), 1, 2
@@ -1294,7 +1381,7 @@
     ]
     ffn_grad = ()
     for c, parts in enumerate((ffn_parts_0, ffn_parts_1)):
-        ffn_grad = place_parts(order * (1 - c), parts.reshape(seqs, 3, part, model), c, ffn_grad)
+        ffn_grad = place_parts(order, parts.reshape(seqs, 3, part, model), c, ffn_grad)
     ffn_grad = [v.reshape(seqs * hidden_own, model) for v in ffn_grad]
 
     edge = hq * HEAD

time: 955 us -> 924 us (0.968)
  waiting for transfers between devices: 40.8 us -> 4.05 us
    reduce_scatter x1, waiting for transfers between devices: 22.9 us -> 0.02 us  [on_device(): lax.psum_scatter(attn_grads, 'fsdp', scatter_dimension=0, tiled=True)]
    all_gather x2, waiting for transfers between devices: 16.5 us -> 0.01 us  [on_device(): ffn_weights = [lax.all_gather(own, 'fsdp', axis=0) for own in ffn_own]]
    pallas_call x16 -> x15, Pallas kernels: 767 us -> 770 us  [call(): pl.pallas_call(kernel, grid=grid, out_shape=tuple(out_shape) + tuple(shap...]
  transfers between devices with their start and end apart: 8 -> 7, of which waited for: 2 -> 1; matrix products, arithmetic and copies ran while one was open for 9% -> 9% of each run, Pallas kernels for 69% -> 73%
where the time goes in v9:
time: 924 us; the launch traced here: 921 us
  Pallas kernels  792 us (86%)
  other arithmetic  41.2 us (4%)
  matrix products  36.8 us (4%)
  local copies, waits for them, and re-layouts  31.3 us (3%)
  between operations  15 us (2%)
    pallas_call x15, Pallas kernels, call(): pl.pallas_call(kernel, grid=grid, out_shape=tuple(out_shape) + tuple(shap...  770 us
    dot_general x6, matrix products, dot(): return lax.dot_general(a, b, dims, preferred_element_type=F32)  36.8 us
  transfers between devices with their start and end apart: 7, of which 1 were waited for; matrix products, arithmetic and copies ran while one was open for 9% of the time, Pallas kernels for 73%

profile of v9, /device:TPU:6, one launch (start us, length us, event | category | flops | bytes accessed | tf_op | source)
XLA Modules:
  0.0 920.6 jit_solution(9979541083985018489)
XLA Ops:
  7.2 1.0 constant_dynamic-slice_fusion.2
  8.2 0.9 constant_dynamic-slice_fusion
  9.1 0.8 pad_maximum_fusion.2
  10.0 2.1 convert_element_type.85
  12.4 0.9 multiply_multiply_fusion
  13.3 0.9 copy-done
  14.2 1.7 multiply_convert_fusion.3
  15.9 38.7 %transfer.3 = (bf16[4,256,2048]{2,1,0:T(8,128)(2,1)}, bf16[64,2048]{1,0:T(8,128)(2,1)}, bf16[3,128,2048]{2,1,0:T(8,128)(2,1)}, bf16[3,128,2048]{2,1,0:T(8,128)(2,1)}) custom-call(bf16[256,2048]{1,0:T(8,128)(2,1)} %get-tuple-element.150.refs_0_, bf16[256,2048]{1,0:T(8,128)(2,1)} %refs_1_.1, bf16[1024,2048]{1,0:T(8,128)(2,1)} %refs_2_.1, ...), custom_call_target="tpu_custom_call" | custom-call | tf_op jit(solution)/shard_map/transfer/pallas_call | solution.py:567
  57.7 2.0 copy-done.10
  59.7 1.6 fusion.9
  61.3 49.5 %attend.2 = (bf16[4,256,512]{2,1,0:T(8,128)(2,1)}, f32[8,1024,1]{2,1,0:T(8,128)}, bf16[4,256,768]{2,1,0:T(8,128)(2,1)}, bf16[4,256,2048]{2,1,0:T(8,128)(2,1)}, bf16[8,64,2048]{2,1,0:T(8,128)(2,1)}) custom-call(s32[1]{0:T(128)} %get-tuple-element.165.refs_0_, bf16[4,256,2048]{2,1,0:T(8,128)(2,1)} %get-tuple-element.71.refs_1_.refs_8_, ...), custom_call_target="tpu_custom_call" | custom-call | flops 30064771072 | bytes 8388608 | tf_op jit(solution)/shard_map/attend/pallas_call | solution.py:567
  110.8 6.3 convolution_convert_fusion.1
  117.1 43.9 %attend.3 = (bf16[4,256,512]{2,1,0:T(8,128)(2,1)}, f32[8,1024,1]{2,1,0:T(8,128)}, bf16[4,256,768]{2,1,0:T(8,128)(2,1)}, f32[256,2048]{1,0:T(8,128)}) custom-call(s32[1]{0:T(128)} %get-tuple-element.166.refs_0_, bf16[4,256,2048]{2,1,0:T(8,128)(2,1)} %get-tuple-element.73.refs_1_, bf16[2048,768]{1,0:T(8,128)(2,1)} %all-gather.6.cloned.1.call-done.refs_2_.refs_4_, ...), custom_call_target="tpu_custom_call" | custom-call | flops 30064771072 | bytes 8388608 | tf_op jit(solution)/shard_map/attend/pallas_call | solution.py:567
  161.0 2.0 multiply_reduce_fusion.7
  162.9 1.3 copy-done.7
  164.2 1.2 multiply_convert_fusion.2.refs_1_
  165.5 70.4 %transfer.4 = (bf16[4,256,2048]{2,1,0:T(8,128)(2,1)}, bf16[4,256,2048]{2,1,0:T(8,128)(2,1)}) custom-call(bf16[4,256,512]{2,1,0:T(8,128)(2,1)} %get-tuple-element.77.refs_0_, bf16[256,2048]{1,0:T(8,128)(2,1)} %multiply_convert_fusion.2.refs_1_, bf16[256,2048]{1,0:T(8,128)(2,1)} %get-tuple-element.152.refs_2_), custom_call_target="tpu_custom_call" | custom-call | tf_op jit(solution)/shard_map/transfer/pallas_call | solution.py:567
  235.9 4.4 convolution_convert_fusion
  240.3 73.1 %ffn_both.4 = (bf16[3,1024,1024]{2,1,0:T(8,128)(2,1)}, f32[1024,2048]{1,0:T(8,128)}, f32[256,2048]{1,0:T(8,128)}, bf16[4,256,2048]{2,1,0:T(8,128)(2,1)}) custom-call(bf16[1024,2048]{1,0:T(8,128)(2,1)} %bitcast.157, bf16[1024,2048]{1,0:T(8,128)(2,1)} %bitcast.162, bf16[8,3,128,2048]{3,2,1,0:T(8,128)(2,1)} %bitcast.149, bf16[1024,2048]{1,0:T(8,128)(2,1)} %bitcast.158, ...), custom_call_target="tpu_custom_call" | custom-call | flops 34359738368 | bytes 20971520 | tf_op jit(solution)/shard_map/ffn_both/pallas_call | solution.py:567
  313.4 1.9 multiply_reduce_fusion.6
  315.9 0.7 copy-done.4
  316.6 1.2 multiply_convert_fusion.1.refs_5_
  317.9 39.1 %ffn_both.5 = (bf16[3,1024,1024]{2,1,0:T(8,128)(2,1)}, bf16[1024,2048]{1,0:T(8,128)(2,1)}, bf16[4,256,2048]{2,1,0:T(8,128)(2,1)}) custom-call(bf16[1024,2048]{1,0:T(8,128)(2,1)} %bitcast.159, bf16[1024,2048]{1,0:T(8,128)(2,1)} %bitcast.163, bf16[8,3,128,2048]{3,2,1,0:T(8,128)(2,1)} %bitcast.153, f32[1024,2048]{1,0:T(8,128)} %get-tuple-element.82.refs_3_, ...), custom_call_target="tpu_custom_call" | custom-call | flops 34359738368 | bytes 20971520 | tf_op jit(solution)/shard_map/ffn_both/pallas_call | solution.py:567
  356.9 38.6 %ffn_both.6 = (bf16[3,1024,1024]{2,1,0:T(8,128)(2,1)}, f32[1024,2048]{1,0:T(8,128)}, f32[256,2048]{1,0:T(8,128)}) custom-call(bf16[1024,2048]{1,0:T(8,128)(2,1)} %bitcast.172, bf16[1024,2048]{1,0:T(8,128)(2,1)} %bitcast.168, bf16[8,3,128,2048]{3,2,1,0:T(8,128)(2,1)} %bitcast.150, bf16[3,1024,1024]{2,1,0:T(8,128)(2,1)} %get-tuple-element.87.refs_3_.refs_1_.refs_0_, ...), custom_call_target="tpu_custom_call" | custom-call | flops 34359738368 | bytes 20971520 | tf_op jit(solution)/shard_map/ffn_both/pallas_call | solution.py:567
  395.6 2.3 multiply_reduce_fusion.3
  398.4 3.9 fusion.17
  402.3 38.7 %ffn_grads.2 = (bf16[8,3,128,2048]{3,2,1,0:T(8,128)(2,1)}, bf16[4,256,2048]{2,1,0:T(8,128)(2,1)}) custom-call(bf16[3,1024,1024]{2,1,0:T(8,128)(2,1)} %get-tuple-element.83.refs_4_.refs_0_, bf16[3,1024,1024]{2,1,0:T(8,128)(2,1)} %get-tuple-element.90.refs_1_.refs_6_.refs_0_, bf16[1024,2048]{1,0:T(8,128)(2,1)} %bitcast.160, bf16[1024,2048]{1,0:T(8,128)(2,1)} %bitcast.173, ...), custom_call_target="tpu_custom_call" | custom-call | flops 38654705664 | bytes 16777216 | tf_op jit(solution)/shard_map/ffn_grads/pallas_call | solution.py:567
  441.1 14.4 %ffn_down.2 = bf16[1024,2048]{1,0:T(8,128)(2,1)} custom-call(bf16[3,1024,1024]{2,1,0:T(8,128)(2,1)} %get-tuple-element.83.refs_4_.refs_0_, bf16[3,1024,1024]{2,1,0:T(8,128)(2,1)} %get-tuple-element.87.refs_3_.refs_1_.refs_0_, bf16[8,3,128,2048]{3,2,1,0:T(8,128)(2,1)} %bitcast.151, bf16[8,3,128,2048]{3,2,1,0:T(8,128)(2,1)} %bitcast.154, ...), custom_call_target="tpu_custom_call" | custom-call | flops 17179869184 | bytes 12582912 | tf_op jit(solution)/shard_map/ffn_down/pallas_call | solution.py:567
  455.4 36.6 %ffn_both.7 = (bf16[3,1024,1024]{2,1,0:T(8,128)(2,1)}, bf16[1024,2048]{1,0:T(8,128)(2,1)}, f32[256,2048]{1,0:T(8,128)}) custom-call(bf16[1024,2048]{1,0:T(8,128)(2,1)} %bitcast.174, bf16[1024,2048]{1,0:T(8,128)(2,1)} %bitcast.170, bf16[8,3,128,2048]{3,2,1,0:T(8,128)(2,1)} %bitcast.155, f32[1024,2048]{1,0:T(8,128)} %get-tuple-element.89.refs_3_, ...), custom_call_target="tpu_custom_call" | custom-call | flops 34359738368 | bytes 20971520 | tf_op jit(solution)/shard_map/ffn_both/pallas_call | solution.py:567
  492.0 38.3 %ffn_grads.3 = (bf16[8,3,128,2048]{3,2,1,0:T(8,128)(2,1)}, f32[256,2048]{1,0:T(8,128)}) custom-call(bf16[3,1024,1024]{2,1,0:T(8,128)(2,1)} %get-tuple-element.87.refs_3_.refs_1_.refs_0_, bf16[3,1024,1024]{2,1,0:T(8,128)(2,1)} %get-tuple-element.94.refs_1_.refs_6_, bf16[1024,2048]{1,0:T(8,128)(2,1)} %bitcast.161, bf16[1024,2048]{1,0:T(8,128)(2,1)} %bitcast.175, ...), custom_call_target="tpu_custom_call" | custom-call | flops 38654705664 | bytes 16777216 | tf_op jit(solution)/shard_map/ffn_grads/pallas_call | solution.py:567
  530.6 1.3 copy-done.5
  531.9 2.3 multiply_reduce_fusion.2
  534.9 4.4 fusion.23
  539.3 2.3 fusion.16
  541.6 48.1 %attend_back.2 = (bf16[4,256,768]{2,1,0:T(8,128)(2,1)}, f32[2,128]{1,0:T(2,128)}, bf16[4,256,2048]{2,1,0:T(8,128)(2,1)}, bf16[4,256,2048]{2,1,0:T(8,128)(2,1)}) custom-call(s32[1]{0:T(128)} %get-tuple-element.165.refs_0_, bf16[4,256,768]{2,1,0:T(8,128)(2,1)} %get-tuple-element.95.refs_1_, bf16[4,256,2048]{2,1,0:T(8,128)(2,1)} %get-tuple-element.96.refs_2_, ...), custom_call_target="tpu_custom_call" | custom-call | flops 47244640256 | bytes 8388608 | tf_op jit(solution)/shard_map/attend_back/pallas_call | solution.py:567
  589.8 6.3 fusion.5.refs_11_
  596.1 3.3 reshape.267
  599.5 1.8 copy.59
  601.3 1.1 copy-done.44
  602.4 7.1 fusion.22
  609.6 87.1 %attend_back.3 = (bf16[4,256,768]{2,1,0:T(8,128)(2,1)}, f32[2,128]{1,0:T(2,128)}, bf16[4,256,2048]{2,1,0:T(8,128)(2,1)}, f32[256,2048]{1,0:T(8,128)}, bf16[4,384,2048]{2,1,0:T(8,128)(2,1)}) custom-call(s32[1]{0:T(128)} %get-tuple-element.166.refs_0_, bf16[4,256,768]{2,1,0:T(8,128)(2,1)} %get-tuple-element.102.refs_1_, ...), custom_call_target="tpu_custom_call" | custom-call | flops 47244640256 | bytes 8388608 | tf_op jit(solution)/shard_map/attend_back/pallas_call | solution.py:567
  698.0 8.3 fusion.2
  706.3 2.9 fusion.4.refs_4_
  709.3 3.2 reduce-scatter.9.cloned.1.call-done
  712.5 89.9 %ffn_down.3 = (bf16[1024,2048]{1,0:T(8,128)(2,1)}, f32[256,2048]{1,0:T(8,128)}, bf16[4,384,2048]{2,1,0:T(8,128)(2,1)}) custom-call(bf16[3,1024,1024]{2,1,0:T(8,128)(2,1)} %get-tuple-element.90.refs_1_.refs_6_.refs_0_, bf16[3,1024,1024]{2,1,0:T(8,128)(2,1)} %get-tuple-element.94.refs_1_.refs_6_, bf16[8,3,128,2048]{3,2,1,0:T(8,128)(2,1)} %bitcast.152, ...), custom_call_target="tpu_custom_call" | custom-call | flops 17179869184 | bytes 12582912 | tf_op jit(solution)/shard_map/ffn_down/pallas_call | solution.py:567
  803.1 0.9 copy-done.9
  804.0 1.8 fusion.12
  805.8 7.7 place_parts.2
  813.5 8.8 place_parts.3
  822.4 3.0 multiply_reduce_fusion.1
  827.4 1.4 fusion.13
  828.8 1.5 pad_maximum_fusion.1
  830.3 0.7 slice.95.refs_2_
  831.0 0.8 slice.94.refs_1_
  831.8 64.2 %transfer.5 = (bf16[4,256,896]{2,1,0:T(8,128)(2,1)}, bf16[4,256,512]{2,1,0:T(8,128)(2,1)}, bf16[4,256,512]{2,1,0:T(8,128)(2,1)}) custom-call(f32[256,2048]{1,0:T(8,128)} %get-tuple-element.113.refs_0_, bf16[256,896]{1,0:T(8,128)(2,1)} %slice.94.refs_1_, bf16[256,512]{1,0:T(8,128)(2,1)} %slice.95.refs_2_), custom_call_target="tpu_custom_call" | custom-call | tf_op jit(solution)/shard_map/transfer/pallas_call | solution.py:567
  896.0 1.5 convert_bitcast_fusion
  897.5 1.4 copy.60
  898.9 2.2 copy.71
  901.1 4.7 place_heads.1
  905.8 1.5 slice_reduce_fusion.2
  907.3 1.6 slice_reduce_fusion
  908.9 1.0 slice_reduce_fusion.1
  910.6 1.5 fusion.15
  912.1 1.5 pad_maximum_fusion
  (130 shorter events, 10.2 us)
Async XLA Ops:
  7.2 54.1 %all-gather.6.cloned.1.call-start = ((), (), s32[]{:S(2)}) async-start(), calls=%async_computation.4 | async-start | bytes 3538944 | tf_op jit(solution)/shard_map/all_gather | solution.py:1232
  9.9 230.3 %all-gather.10.cloned.1.call-start = ((), (), s32[]{:S(2)}) async-start(), calls=%async_computation.9 | async-start | bytes 14155776 | tf_op jit(solution)/shard_map/all_gather | solution.py:1241
  12.1 2.1 copy-start
  12.1 2.1 copy-start.27
  13.3 2.6 copy-start.33
  13.3 2.6 copy-start.35
  54.5 0.9 copy-start.42
  54.6 0.9 copy-start.43
  54.6 1.5 copy-start.37
  54.6 2.7 copy-start.23
  54.6 263.2 %all-gather.8.cloned.1.call-start = ((), (), s32[]{:S(2)}) async-start(), calls=%async_computation.8 | async-start | bytes 14155776 | tf_op jit(solution)/shard_map/all_gather | solution.py:1241
  55.4 554.2 %reduce-scatter.7.cloned.1.call-start = ((), (), s32[]{:S(2)}) async-start(), calls=%async_computation.5 | async-start | bytes 14155776 | tf_op jit(solution)/shard_map/reduce_scatter | solution.py:1313
  56.7 0.6 copy-start.29
  57.7 2.0 copy-start.10
  117.1 43.9 %copy-start.1 = (f32[2,256,2048]{2,1,0:T(8,128)S(1)}, f32[2,256,2048]{2,1,0:T(8,128)}, u32[]{:S(2)}) copy-start(f32[2,256,2048]{2,1,0:T(8,128)} %copy-done) | copy-start | bytes 12582916
  161.0 3.3 copy-start.26
  162.9 1.3 copy-start.7
  165.5 70.4 %copy-start.21 = (bf16[4,256,512]{2,1,0:T(8,128)(2,1)S(1)}, bf16[4,256,512]{2,1,0:T(8,128)(2,1)}, u32[]{:S(2)}) copy-start(bf16[4,256,512]{2,1,0:T(8,128)(2,1)} %get-tuple-element.77.refs_0_) | copy-start | bytes 3145732
  165.5 70.4 %copy-start.45 = (bf16[8,64,2048]{2,1,0:T(8,128)(2,1)S(1)}, bf16[8,64,2048]{2,1,0:T(8,128)(2,1)}, u32[]{:S(2)}) copy-start(bf16[8,64,2048]{2,1,0:T(8,128)(2,1)} %get-tuple-element.75) | copy-start | bytes 6291460
  240.3 73.1 %copy-start.2 = (f32[2,256,2048]{2,1,0:T(8,128)S(1)}, f32[2,256,2048]{2,1,0:T(8,128)}, u32[]{:S(2)}) copy-start(f32[2,256,2048]{2,1,0:T(8,128)} %copy-done) | copy-start | bytes 12582916
  315.3 1.3 copy-start.4
  315.9 0.7 copy-start.31
  356.9 38.6 %copy-start.8 = (f32[256,2048]{1,0:T(8,128)S(1)}, f32[256,2048]{1,0:T(8,128)}, u32[]{:S(2)}) copy-start(f32[256,2048]{1,0:T(8,128)} %copy-done.7) | copy-start | bytes 6291460
  395.5 2.8 copy-start.11
  441.0 271.5 %reduce-scatter.9.cloned.1.call-start = ((), (), s32[]{:S(2)}) async-start(), calls=%async_computation.6 | async-start | bytes 14155776 | tf_op jit(solution)/shard_map/reduce_scatter | solution.py:1320
  530.3 1.6 copy-start.5
  530.3 1.6 copy-start.32
  530.3 3.9 copy-start.24
  530.4 272.0 %reduce-scatter.11.cloned.1.call-start = ((), (), s32[]{:S(2)}) async-start(), calls=%async_computation.7 | async-start | bytes 6488064 | tf_op jit(solution)/shard_map/reduce_scatter | solution.py:1358
  531.9 2.9 copy-start.20
  534.9 4.5 copy-start.12
  534.9 4.5 copy-start.19
  534.9 4.5 copy-start.38
  541.6 48.1 %copy-start.14 = (f32[512,2048,1]{1,0,2:T(8,128)S(1)}, f32[512,2048,1]{1,0,2:T(8,128)}, u32[]{:S(2)}) copy-start(f32[512,2048,1]{1,0,2:T(8,128)} %fusion.23) | copy-start | bytes 12582916
  541.6 48.1 %copy-start.22 = (bf16[4,256,512]{2,1,0:T(8,128)(2,1)S(1)}, bf16[4,256,512]{2,1,0:T(8,128)(2,1)}, u32[]{:S(2)}) copy-start(bf16[4,256,512]{2,1,0:T(8,128)(2,1)} %get-tuple-element.77.refs_0_) | copy-start | bytes 3145732
  599.5 2.9 copy-start.44
  609.6 87.1 %copy-start.41 = (f32[2,128]{1,0:T(2,128)S(1)}, f32[2,128]{1,0:T(2,128)}, u32[]{:S(2)}) copy-start(f32[2,128]{1,0:T(2,128)} %get-tuple-element.107) | copy-start | bytes 3076
  697.9 8.3 copy-start.15
  709.2 201.3 %reduce-scatter.13.cloned.1.call-start = ((), (), s32[]{:S(2)}) async-start(), calls=%async_computation.10 | async-start | bytes 5242880
  802.4 0.7 copy-start.30
  802.4 1.6 copy-start.9
  813.5 8.8 copy-start.3
  813.5 8.8 copy-start.28
  822.3 3.1 copy-start.13
  822.3 3.8 copy-start.16
  822.3 4.4 copy-start.17
  822.4 5.0 copy-start.18
  822.4 5.0 copy-start.34
  822.4 5.0 copy-start.36
  822.4 5.0 copy-start.39
  822.4 5.0 copy-start.40
  828.7 1.5 copy-start.25
  901.1 9.5 %copy-start.6 = (f32[256,2048]{1,0:T(8,128)S(1)}, f32[256,2048]{1,0:T(8,128)}, u32[]{:S(2)}) copy-start(f32[256,2048]{1,0:T(8,128)} %copy-done.4) | copy-start | bytes 6291460
Sparse Core Ops, SparseCore 0:
  10.2 49.3 all-gather.5
  61.2 133.8 all-gather.9
  196.8 116.3 all-gather.7
  441.1 141.5 reduce-scatter.6
  584.9 127.5 reduce-scatter.8
  715.2 73.0 reduce-scatter.10
  802.6 74.4 reduce-scatter.12

commit v10 on v9

--- a/solution.py
+++ b/solution.py
@@ -686,12 +686,36 @@
     hook(2)
 
 
-def attend_back_kernel(sizes, hook, ins, outs, held):
+def out_weight_grads(grads_ref, shards, slots):
+    width = slots[0][0].shape[-1]
+    model = slots[0][1].shape[-1]
+    tile = min(256, width)
+    piece = width // shards
+    held = model // shards
+    blocks = held // piece
+    columns = model // blocks
+    for t in range(width // tile):
+        total = None
+        for mixed_ref, res_ref in slots:
+            rows = mixed_ref.shape[0] * mixed_ref.shape[1]
+            mixed = mixed_ref[:, :, t * tile : (t + 1) * tile].reshape(rows, tile)
+            term = dot(mixed, res_ref[...].reshape(rows, model), TN)
+            total = term if total is None else total + term
+        total = total.astype(BF16)
+        for p in range(tile // piece):
+            first = (t * (tile // piece) + p) * held
+            for c in range(blocks):
+                grads_ref[first + c * piece : first + (c + 1) * piece, :] = total[
+                    p * piece : (p + 1) * piece, c * columns : (c + 1) * columns
+                ]
+
+
+def attend_back_kernel(sizes, shards, hook, ins, outs, held):
     (
         len_ref, qkv_ref, res_ref, out_w_ref, qkv_w_ref, lse_ref,
-        qg_ref, kg_ref, cos_ref, sin_ref, ones_ref,
+        qg_ref, kg_ref, cos_ref, sin_ref, ones_ref, *others,
     ) = ins
-    dqkv_ref, dgain_ref, pull_ref = outs
+    dqkv_ref, dgain_ref, pull_ref, *out_grads = outs
     q_s, k_s, v_s, cot_s, dq_s, dk_s, dv_s = held
     hook(0)
     hq, hkv, group = sizes
@@ -728,6 +752,11 @@
 
         lax.fori_loop(0, hq, one_head, 0, unroll=min(4, hq))
         if i == seqs * rows_in // BLOCK - 2:
+            for grads_ref in out_grads:
+                before_ref, here_ref, res_before_ref = others
+                out_weight_grads(
+                    grads_ref, shards, ((before_ref, res_before_ref), (here_ref, res_ref))
+                )
             hook(1)
     gain_sums = [jnp.zeros((1, 128), F32), jnp.zeros((1, 128), F32)]
     for c in range(seqs):
@@ -811,21 +840,25 @@
 
 
 def attend_back(
-    sizes, length, qkv, res, out_w, qkv_w, lse, gains, tables, jobs, number, after
+    sizes, length, qkv, res, out_w, qkv_w, lse, gains, tables, jobs, number, after, others=()
 ):
     seqs, rows_in, width = qkv.shape
     hq, hkv, _ = sizes
     slot = seqs * rows_in
+    shards = lax.axis_size("fsdp")
+    model = res.shape[-1]
+    columns = hq * HEAD // shards * model // (model // shards)
     return call(
-        functools.partial(attend_back_kernel, sizes),
-        [length, qkv, res, out_w, qkv_w, lse, *gains, *tables],
-        [SMEM] + [VMEM] * 10,
+        functools.partial(attend_back_kernel, sizes, shards),
+        [length, qkv, res, out_w, qkv_w, lse, *gains, *tables, *others],
+        [SMEM] + [VMEM] * (10 + len(others)),
         [
             jax.ShapeDtypeStruct((seqs, rows_in, width), BF16),
             jax.ShapeDtypeStruct((2, 128), F32),
             jax.ShapeDtypeStruct(res.shape, BF16),
-        ],
-        [VMEM, VMEM, VMEM],
+        ]
+        + [jax.ShapeDtypeStruct((model, columns), BF16)] * bool(others),
+        [VMEM, VMEM, VMEM] + [VMEM] * bool(others),
         jobs,
         number,
         after,
@@ -842,7 +875,7 @@
             flops=88 * hq * slot * slot * HEAD, bytes_accessed=1 << 23, transcendentals=0
         ),
         name="attend_back",
-        late=(1, 2, 3, 4, 5),
+        late=(1, 2, 3, 4, 5) + tuple(range(11, 11 + len(others))),
     )
 
 
@@ -1229,13 +1262,14 @@
         ],
         axis=1,
     )
-    qkv_weight = lax.all_gather(qkv_own, "fsdp", axis=0, tiled=True)
     start = [
         ("gather", normal_in[0]),
         ("deal", out_weight),
         ("own", gate_weight, up_weight, down_weight),
+        ("line", qkv_own),
     ]
-    normal_0, out_own, *ffn_own = transfer(start, 1)
+    normal_0, out_own, *ffn_own, qkv_weight = transfer(start, 1)
+    qkv_weight = qkv_weight.reshape(model, -1)
     hidden_own = gate_weight.shape[0] // seqs
     part = hidden_own // CHUNKS
     ffn_weights = [lax.all_gather(own, "fsdp", axis=0) for own in ffn_own]
@@ -1264,7 +1298,6 @@
     (mixed_1, lse_1, qkv_1), (total_0,) = heads(1, [("scatter", leave(mixed_0))], 3, mixed_0)
     qkv = [qkv_0, qkv_1]
     log_sums = [lse_0, lse_1]
-    attended = [v.reshape(slot_len, hq * HEAD) for v in (mixed_0, mixed_1)]
     res_0, mid_0 = enter_ffn(0, total_0)
     mid_full[0], cot_full[0] = [
         v.reshape(flat)
@@ -1322,26 +1355,28 @@
     res_cot_1, low_1, ffn_gain_1 = pull_mid(1, mid_total_1)
     grad_ffn_gain = ffn_gain_0 + ffn_gain_1
 
-    def back(b, full, jobs, number, after):
+    def back(b, full, jobs, number, after, others=()):
         return attend_back(
             sizes, lengths[b : b + 1], qkv[b], full, out_rows, qkv_weight, log_sums[b],
-            gains, tables, jobs, number, after,
+            gains, tables, jobs, number, after, others,
         )
 
     (dqkv_0, heads_gain_0, pull_0), (res_full_1,) = back(
         0, res_full_0, [("gather", low_1)], 11, grads_1
     )
-    res_full = [v.reshape(flat) for v in (res_full_0, res_full_1)]
-    out_grads = sum(dot(attended[b], res_full[b], TN) for b in range(slots)).astype(BF16)
-    (dqkv_1, heads_gain_1, pull_1), (in_total_0, ffn_parts_0) = back(
-        1, res_full_1, [("scatter", pull_0), ("gather", ffn_sums[0])], 12, out_grads
+    (dqkv_1, heads_gain_1, pull_1, out_grads), (in_total_0, ffn_parts_0) = back(
+        1,
+        res_full_1,
+        [("scatter", pull_0), ("gather", ffn_sums[0])],
+        12,
+        dqkv_0,
+        (mixed_0, mixed_1, res_full_0),
     )
     head_gain = heads_gain_0 + heads_gain_1
     dqkv = [v.reshape(slot_len, -1) for v in (dqkv_0, dqkv_1)]
     held = model // shards
-    piece = out_grads.shape[0] // shards
+    piece = hq * HEAD // shards
     blocks = held // piece
-    out_grads = jnp.swapaxes(out_grads.reshape(shards, piece, blocks, model // blocks), 1, 2)
     head_sums = jnp.pad(
         (head_gain[:, :HEAD] + head_gain[:, HEAD:]).reshape(2, shards, HEAD // shards),
         ((0, 0), (0, 0), (0, held - HEAD // shards)),
@@ -1351,7 +1386,7 @@
         [
             sum(dot(normal_full[b].reshape(flat), dqkv[b], TN) for b in range(slots)).astype(BF16),
             jnp.pad(gain_columns, ((0, 0), (0, 125))),
-            out_grads.reshape(model, model // blocks),
+            out_grads,
         ],
         axis=1,
     )

time: 924 us -> 936 us (1.013)
  waiting for transfers between devices: 4.05 us -> 18.4 us
  matrix products: 36.8 us -> 25.8 us
    reduce_scatter x1, waiting for transfers between devices: 3.22 us -> 17.5 us  [on_device(): ffn_sums.append(lax.psum_scatter(grads_1, 'fsdp', scatter_dimension=0))]
    dot_general x6 -> x4, matrix products: 36.8 us -> 25.8 us  [dot(): return lax.dot_general(a, b, dims, preferred_element_type=F32)]
  transfers between devices with their start and end apart: 7 -> 6, of which waited for: 1 -> 1; matrix products, arithmetic and copies ran while one was open for 9% -> 7% of each run, Pallas kernels for 73% -> 69%
where the time goes in v10:
time: 936 us; the launch traced here: 926 us
  Pallas kernels  797 us (85%)
  other arithmetic  44.9 us (5%)
  matrix products  25.8 us (3%)
  local copies, waits for them, and re-layouts  24.5 us (3%)
  waiting for transfers between devices  18.4 us (2%)
  between operations  15.2 us (2%)
    pallas_call x15, Pallas kernels, call(): pl.pallas_call(kernel, grid=grid, out_shape=tuple(out_shape) + tuple(shap...  775 us
    dot_general x4, matrix products, dot(): return lax.dot_general(a, b, dims, preferred_element_type=F32)  25.8 us
  transfers between devices with their start and end apart: 6, of which 1 were waited for; matrix products, arithmetic and copies ran while one was open for 7% of the time, Pallas kernels for 69%

profile of v10, /device:TPU:6, one launch (start us, length us, event | category | flops | bytes accessed | tf_op | source)
XLA Modules:
  0.0 926.0 jit_solution(1576946484336034872)
XLA Ops:
  7.2 2.1 convert_element_type.82
  9.4 2.0 copy-done
  11.7 1.0 constant_dynamic-slice_fusion.2
  13.3 0.9 constant_dynamic-slice_fusion
  14.2 0.8 pad_maximum_fusion.2.refs_5_
  15.0 3.9 multiply_convert_fusion.3
  18.9 43.7 %transfer.3 = (bf16[4,256,2048]{2,1,0:T(8,128)(2,1)}, bf16[64,2048]{1,0:T(8,128)(2,1)}, bf16[3,128,2048]{2,1,0:T(8,128)(2,1)}, bf16[3,128,2048]{2,1,0:T(8,128)(2,1)}, bf16[8,256,768]{2,1,0:T(8,128)(2,1)}) custom-call(bf16[256,2048]{1,0:T(8,128)(2,1)} %get-tuple-element.154.refs_0_, bf16[256,2048]{1,0:T(8,128)(2,1)} %refs_1_.1, bf16[1024,2048]{1,0:T(8,128)(2,1)} %refs_2_.1, ...), custom_call_target="tpu_custom_call" | custom-call | tf_op jit(solution)/shard_map/transfer/pallas_call | solution.py:567
  62.8 0.7 all-gather.5.cloned.1.call-update
  63.6 0.7 maximum_bitcast_fusion
  64.8 55.2 %attend.2 = (bf16[4,256,512]{2,1,0:T(8,128)(2,1)}, f32[8,1024,1]{2,1,0:T(8,128)}, bf16[4,256,768]{2,1,0:T(8,128)(2,1)}, bf16[4,256,2048]{2,1,0:T(8,128)(2,1)}, bf16[8,64,2048]{2,1,0:T(8,128)(2,1)}) custom-call(s32[1]{0:T(128)} %get-tuple-element.169.refs_0_, bf16[4,256,2048]{2,1,0:T(8,128)(2,1)} %get-tuple-element.73.refs_1_.refs_8_, ...), custom_call_target="tpu_custom_call" | custom-call | flops 30064771072 | bytes 8388608 | tf_op jit(solution)/shard_map/attend/pallas_call | solution.py:567
  120.0 6.3 convolution_convert_fusion.1
  126.3 43.9 %attend.3 = (bf16[4,256,512]{2,1,0:T(8,128)(2,1)}, f32[8,1024,1]{2,1,0:T(8,128)}, bf16[4,256,768]{2,1,0:T(8,128)(2,1)}, f32[256,2048]{1,0:T(8,128)}) custom-call(s32[1]{0:T(128)} %get-tuple-element.170.refs_0_, bf16[4,256,2048]{2,1,0:T(8,128)(2,1)} %get-tuple-element.76.refs_1_, bf16[2048,768]{1,0:T(8,128)(2,1)} %bitcast.153, ...), custom_call_target="tpu_custom_call" | custom-call | flops 30064771072 | bytes 8388608 | tf_op jit(solution)/shard_map/attend/pallas_call | solution.py:567
  170.2 1.9 multiply_reduce_fusion.7
  172.2 1.2 copy-done.7
  173.5 1.2 multiply_convert_fusion.2.refs_1_
  175.0 1.8 fusion.8
  176.9 0.8 copy-done.10
  177.7 70.4 %transfer.4 = (bf16[4,256,2048]{2,1,0:T(8,128)(2,1)}, bf16[4,256,2048]{2,1,0:T(8,128)(2,1)}) custom-call(bf16[4,256,512]{2,1,0:T(8,128)(2,1)} %get-tuple-element.80.refs_0_.refs_12_, bf16[256,2048]{1,0:T(8,128)(2,1)} %multiply_convert_fusion.2.refs_1_, bf16[256,2048]{1,0:T(8,128)(2,1)} %get-tuple-element.156.refs_2_), custom_call_target="tpu_custom_call" | custom-call | tf_op jit(solution)/shard_map/transfer/pallas_call | solution.py:567
  248.1 4.4 convolution_convert_fusion
  252.5 73.0 %ffn_both.4 = (bf16[3,1024,1024]{2,1,0:T(8,128)(2,1)}, f32[1024,2048]{1,0:T(8,128)}, f32[256,2048]{1,0:T(8,128)}, bf16[4,256,2048]{2,1,0:T(8,128)(2,1)}) custom-call(bf16[1024,2048]{1,0:T(8,128)(2,1)} %bitcast.143, bf16[1024,2048]{1,0:T(8,128)(2,1)} %bitcast.148, bf16[8,3,128,2048]{3,2,1,0:T(8,128)(2,1)} %bitcast.135, bf16[1024,2048]{1,0:T(8,128)(2,1)} %bitcast.144, ...), custom_call_target="tpu_custom_call" | custom-call | flops 34359738368 | bytes 20971520 | tf_op jit(solution)/shard_map/ffn_both/pallas_call | solution.py:567
  325.5 1.9 multiply_reduce_fusion.6
  328.0 0.7 copy-done.4
  328.7 1.2 multiply_convert_fusion.1.refs_5_
  329.9 38.6 %ffn_both.5 = (bf16[3,1024,1024]{2,1,0:T(8,128)(2,1)}, bf16[1024,2048]{1,0:T(8,128)(2,1)}, bf16[4,256,2048]{2,1,0:T(8,128)(2,1)}) custom-call(bf16[1024,2048]{1,0:T(8,128)(2,1)} %bitcast.145, bf16[1024,2048]{1,0:T(8,128)(2,1)} %bitcast.149, bf16[8,3,128,2048]{3,2,1,0:T(8,128)(2,1)} %bitcast.139, f32[1024,2048]{1,0:T(8,128)} %get-tuple-element.85.refs_3_, ...), custom_call_target="tpu_custom_call" | custom-call | flops 34359738368 | bytes 20971520 | tf_op jit(solution)/shard_map/ffn_both/pallas_call | solution.py:567
  368.6 38.6 %ffn_both.6 = (bf16[3,1024,1024]{2,1,0:T(8,128)(2,1)}, f32[1024,2048]{1,0:T(8,128)}, f32[256,2048]{1,0:T(8,128)}) custom-call(bf16[1024,2048]{1,0:T(8,128)(2,1)} %bitcast.162, bf16[1024,2048]{1,0:T(8,128)(2,1)} %bitcast.158, bf16[8,3,128,2048]{3,2,1,0:T(8,128)(2,1)} %bitcast.136, bf16[3,1024,1024]{2,1,0:T(8,128)(2,1)} %get-tuple-element.90.refs_3_.refs_1_.refs_0_, ...), custom_call_target="tpu_custom_call" | custom-call | flops 34359738368 | bytes 20971520 | tf_op jit(solution)/shard_map/ffn_both/pallas_call | solution.py:567
  407.2 2.3 multiply_reduce_fusion.3
  410.0 3.9 fusion.16
  413.9 38.7 %ffn_grads.2 = (bf16[8,3,128,2048]{3,2,1,0:T(8,128)(2,1)}, bf16[4,256,2048]{2,1,0:T(8,128)(2,1)}) custom-call(bf16[3,1024,1024]{2,1,0:T(8,128)(2,1)} %get-tuple-element.86.refs_4_.refs_0_, bf16[3,1024,1024]{2,1,0:T(8,128)(2,1)} %get-tuple-element.93.refs_1_.refs_6_.refs_0_, bf16[1024,2048]{1,0:T(8,128)(2,1)} %bitcast.146, bf16[1024,2048]{1,0:T(8,128)(2,1)} %bitcast.163, ...), custom_call_target="tpu_custom_call" | custom-call | flops 38654705664 | bytes 16777216 | tf_op jit(solution)/shard_map/ffn_grads/pallas_call | solution.py:567
  452.7 14.6 %ffn_down.2 = bf16[1024,2048]{1,0:T(8,128)(2,1)} custom-call(bf16[3,1024,1024]{2,1,0:T(8,128)(2,1)} %get-tuple-element.86.refs_4_.refs_0_, bf16[3,1024,1024]{2,1,0:T(8,128)(2,1)} %get-tuple-element.90.refs_3_.refs_1_.refs_0_, bf16[8,3,128,2048]{3,2,1,0:T(8,128)(2,1)} %bitcast.137, bf16[8,3,128,2048]{3,2,1,0:T(8,128)(2,1)} %bitcast.140, ...), custom_call_target="tpu_custom_call" | custom-call | flops 17179869184 | bytes 12582912 | tf_op jit(solution)/shard_map/ffn_down/pallas_call | solution.py:567
  467.3 36.6 %ffn_both.7 = (bf16[3,1024,1024]{2,1,0:T(8,128)(2,1)}, bf16[1024,2048]{1,0:T(8,128)(2,1)}, f32[256,2048]{1,0:T(8,128)}) custom-call(bf16[1024,2048]{1,0:T(8,128)(2,1)} %bitcast.164, bf16[1024,2048]{1,0:T(8,128)(2,1)} %bitcast.160, bf16[8,3,128,2048]{3,2,1,0:T(8,128)(2,1)} %bitcast.141, f32[1024,2048]{1,0:T(8,128)} %get-tuple-element.92.refs_3_, ...), custom_call_target="tpu_custom_call" | custom-call | flops 34359738368 | bytes 20971520 | tf_op jit(solution)/shard_map/ffn_both/pallas_call | solution.py:567
  503.9 38.4 %ffn_grads.3 = (bf16[8,3,128,2048]{3,2,1,0:T(8,128)(2,1)}, f32[256,2048]{1,0:T(8,128)}) custom-call(bf16[3,1024,1024]{2,1,0:T(8,128)(2,1)} %get-tuple-element.90.refs_3_.refs_1_.refs_0_, bf16[3,1024,1024]{2,1,0:T(8,128)(2,1)} %get-tuple-element.97.refs_1_.refs_6_, bf16[1024,2048]{1,0:T(8,128)(2,1)} %bitcast.147, bf16[1024,2048]{1,0:T(8,128)(2,1)} %bitcast.165, ...), custom_call_target="tpu_custom_call" | custom-call | flops 38654705664 | bytes 16777216 | tf_op jit(solution)/shard_map/ffn_grads/pallas_call | solution.py:567
  542.6 1.4 copy-done.5
  543.9 2.3 multiply_reduce_fusion.2
  546.7 4.0 fusion.15
  550.7 47.9 %attend_back.2 = (bf16[4,256,768]{2,1,0:T(8,128)(2,1)}, f32[2,128]{1,0:T(2,128)}, bf16[4,256,2048]{2,1,0:T(8,128)(2,1)}, bf16[4,256,2048]{2,1,0:T(8,128)(2,1)}) custom-call(s32[1]{0:T(128)} %get-tuple-element.169.refs_0_, bf16[4,256,768]{2,1,0:T(8,128)(2,1)} %get-tuple-element.98.refs_1_, bf16[4,256,2048]{2,1,0:T(8,128)(2,1)} %get-tuple-element.99.refs_2_.refs_13_, ...), custom_call_target="tpu_custom_call" | custom-call | flops 47244640256 | bytes 8388608 | tf_op jit(solution)/shard_map/attend_back/pallas_call | solution.py:567
  598.6 6.8 fusion.21
  605.5 88.3 %attend_back.3 = (bf16[4,256,768]{2,1,0:T(8,128)(2,1)}, f32[2,128]{1,0:T(2,128)}, bf16[4,256,2048]{2,1,0:T(8,128)(2,1)}, bf16[2048,512]{1,0:T(8,128)(2,1)}, f32[...) custom-call(s32[1]{0:T(128)} %get-tuple-element.170.refs_0_, bf16[4,256,768]{2,1,0:T(8,128)(2,1)} %get-tuple-element.105.refs_1_, ...), custom_call_target="tpu_custom_call" | custom-call | flops 47244640256 | bytes 8388608 | tf_op jit(solution)/shard_map/attend_back/pallas_call | solution.py:567
  693.8 0.7 add.142
  695.0 8.3 fusion.2
  703.3 2.9 fusion.4.refs_4_
  706.3 17.5 %reduce-scatter.9.cloned.1.call-done = bf16[1,384,2048]{2,1,0:T(8,128)(2,1)} async-done(((bf16[8,384,2048]{2,1,0:T(8,128)(2,1)}), bf16[1,384,2048]{2,1,0:T(8,128)(2,1)}) %reduce-scatter.9.cloned.1.call-update) | async-done | bytes 1572880 | tf_op jit(solution)/shard_map/reduce_scatter | solution.py:1353
  723.9 89.7 %ffn_down.3 = (bf16[1024,2048]{1,0:T(8,128)(2,1)}, f32[256,2048]{1,0:T(8,128)}, bf16[4,384,2048]{2,1,0:T(8,128)(2,1)}) custom-call(bf16[3,1024,1024]{2,1,0:T(8,128)(2,1)} %get-tuple-element.93.refs_1_.refs_6_.refs_0_, bf16[3,1024,1024]{2,1,0:T(8,128)(2,1)} %get-tuple-element.97.refs_1_.refs_6_, bf16[8,3,128,2048]{3,2,1,0:T(8,128)(2,1)} %bitcast.138, ...), custom_call_target="tpu_custom_call" | custom-call | flops 17179869184 | bytes 12582912 | tf_op jit(solution)/shard_map/ffn_down/pallas_call | solution.py:567
  813.7 0.6 copy-done.25
  814.3 0.9 copy-done.9
  815.3 1.8 fusion.11
  817.1 7.8 place_parts.2
  824.9 9.1 place_parts.3
  834.1 3.1 multiply_reduce_fusion.1
  837.8 0.7 copy-done.15
  839.1 1.4 fusion.12
  840.5 1.5 pad_maximum_fusion.1
  842.0 0.7 slice.95.refs_2_
  842.7 0.8 slice.94.refs_1_
  843.5 57.5 %transfer.5 = (bf16[4,256,896]{2,1,0:T(8,128)(2,1)}, bf16[4,256,512]{2,1,0:T(8,128)(2,1)}, bf16[4,256,512]{2,1,0:T(8,128)(2,1)}) custom-call(f32[256,2048]{1,0:T(8,128)} %get-tuple-element.117.refs_0_, bf16[256,896]{1,0:T(8,128)(2,1)} %slice.94.refs_1_, bf16[256,512]{1,0:T(8,128)(2,1)} %slice.95.refs_2_), custom_call_target="tpu_custom_call" | custom-call | tf_op jit(solution)/shard_map/transfer/pallas_call | solution.py:567
  901.1 1.5 convert_bitcast_fusion
  902.6 1.4 copy.51
  903.9 2.2 copy.60
  906.1 4.7 place_heads.1
  910.9 1.5 slice_reduce_fusion.2
  912.3 1.6 slice_reduce_fusion
  913.9 1.0 slice_reduce_fusion.1
  914.9 0.7 dynamic-slice_divide_fusion
  915.6 1.5 fusion.14
  917.1 1.5 pad_maximum_fusion
  (113 shorter events, 6.0 us)
Async XLA Ops:
  7.2 245.3 %all-gather.7.cloned.1.call-start = ((), (), s32[]{:S(2)}) async-start(), calls=%async_computation.8 | async-start | bytes 14155776 | tf_op jit(solution)/shard_map/all_gather | solution.py:1275
  9.3 2.0 copy-start
  11.4 3.6 copy-start.22
  13.3 5.6 copy-start.28
  13.3 5.6 copy-start.30
  62.7 0.9 copy-start.37
  62.7 0.9 copy-start.38
  62.7 1.5 copy-start.32
  62.7 267.2 %all-gather.5.cloned.1.call-start = ((), (), s32[]{:S(2)}) async-start(), calls=%async_computation.7 | async-start | bytes 14155776 | tf_op jit(solution)/shard_map/all_gather | solution.py:1275
  63.5 542.0 %reduce-scatter.7.cloned.1.call-start = ((), (), s32[]{:S(2)}) async-start(), calls=%async_computation.4 | async-start | bytes 14155776 | tf_op jit(solution)/shard_map/reduce_scatter | solution.py:1346
  126.3 43.9 %copy-start.1 = (f32[2,256,2048]{2,1,0:T(8,128)S(1)}, f32[2,256,2048]{2,1,0:T(8,128)}, u32[]{:S(2)}) copy-start(f32[2,256,2048]{2,1,0:T(8,128)} %copy-done) | copy-start | bytes 12582916
  170.2 3.2 copy-start.21
  172.1 1.3 copy-start.7
  172.1 2.5 copy-start.17
  172.2 2.8 copy-start.24
  175.0 2.6 copy-start.10
  177.7 70.4 %copy-start.19 = (bf16[4,256,512]{2,1,0:T(8,128)(2,1)S(1)}, bf16[4,256,512]{2,1,0:T(8,128)(2,1)}, u32[]{:S(2)}) copy-start(bf16[4,256,512]{2,1,0:T(8,128)(2,1)} %get-tuple-element.80.refs_0_.refs_12_) | copy-start | bytes 3145732
  177.7 70.4 %copy-start.40 = (bf16[8,64,2048]{2,1,0:T(8,128)(2,1)S(1)}, bf16[8,64,2048]{2,1,0:T(8,128)(2,1)}, u32[]{:S(2)}) copy-start(bf16[8,64,2048]{2,1,0:T(8,128)(2,1)} %get-tuple-element.78) | copy-start | bytes 6291460
  252.5 73.0 %copy-start.2 = (f32[2,256,2048]{2,1,0:T(8,128)S(1)}, f32[2,256,2048]{2,1,0:T(8,128)}, u32[]{:S(2)}) copy-start(f32[2,256,2048]{2,1,0:T(8,128)} %copy-done) | copy-start | bytes 12582916
  327.4 1.3 copy-start.4
  328.0 0.7 copy-start.26
  368.6 38.6 %copy-start.8 = (f32[256,2048]{1,0:T(8,128)S(1)}, f32[256,2048]{1,0:T(8,128)}, u32[]{:S(2)}) copy-start(f32[256,2048]{1,0:T(8,128)} %copy-done.7) | copy-start | bytes 6291460
  407.2 2.8 copy-start.11
  452.6 271.3 %reduce-scatter.9.cloned.1.call-start = ((), (), s32[]{:S(2)}) async-start(), calls=%async_computation.5 | async-start | bytes 14155776 | tf_op jit(solution)/shard_map/reduce_scatter | solution.py:1353
  542.3 1.6 copy-start.5
  542.3 1.6 copy-start.27
  542.3 271.3 %reduce-scatter.11.cloned.1.call-start = ((), (), s32[]{:S(2)}) async-start(), calls=%async_computation.6 | async-start | bytes 6488064 | tf_op jit(solution)/shard_map/reduce_scatter | solution.py:1393
  543.9 2.8 copy-start.12
  543.9 2.8 copy-start.33
  550.7 47.9 %copy-start.39 = (bf16[4,256,2048]{2,1,0:T(8,128)(2,1)S(1)}, bf16[4,256,2048]{2,1,0:T(8,128)(2,1)}, u32[]{:S(2)}) copy-start(bf16[4,256,2048]{2,1,0:T(8,128)(2,1)} %get-tuple-element.73.refs_1_.refs_8_) | copy-start | bytes 12582916
  605.5 88.3 %copy-start.36 = (f32[2,128]{1,0:T(2,128)S(1)}, f32[2,128]{1,0:T(2,128)}, u32[]{:S(2)}) copy-start(f32[2,128]{1,0:T(2,128)} %get-tuple-element.110) | copy-start | bytes 3076
  695.0 8.3 copy-start.18
  706.3 209.3 %reduce-scatter.13.cloned.1.call-start = ((), (), s32[]{:S(2)}) async-start(), calls=%async_computation.9 | async-start | bytes 5242880
  813.6 0.7 copy-start.25
  813.7 1.6 copy-start.9
  824.9 9.1 copy-start.3
  824.9 9.1 copy-start.23
  834.0 3.2 copy-start.13
  834.0 3.8 copy-start.14
  834.0 4.5 copy-start.15
  834.0 5.1 copy-start.16
  834.0 5.1 copy-start.29
  834.0 5.1 copy-start.31
  834.1 5.0 copy-start.34
  834.1 5.0 copy-start.35
  840.5 1.5 copy-start.20
  906.1 9.5 %copy-start.6 = (f32[256,2048]{1,0:T(8,128)S(1)}, f32[256,2048]{1,0:T(8,128)}, u32[]{:S(2)}) copy-start(f32[256,2048]{1,0:T(8,128)} %copy-done.4) | copy-start | bytes 6291460
Sparse Core Ops, SparseCore 0:
  62.8 141.0 all-gather.6
  205.6 117.0 all-gather.4
  452.7 141.2 reduce-scatter.6
  596.2 127.6 reduce-scatter.8
  726.6 63.1 reduce-scatter.10
  813.8 63.7 reduce-scatter.12

commit v11 on v10

--- a/solution.py
+++ b/solution.py
@@ -641,8 +641,8 @@
 
 
 def attend_kernel(sizes, hook, ins, outs, held):
-    len_ref, normal_ref, weight_ref, qg_ref, kg_ref, cos_ref, sin_ref, ones_ref = ins
-    out_ref, lse_ref, qkv_ref = outs
+    len_ref, normal_ref, weight_ref, qg_ref, kg_ref, cos_ref, sin_ref, ones_ref, *out_w = ins
+    out_ref, lse_ref, qkv_ref, *left = outs
     q_s, k_s, v_s, o_s = held
     hook(0)
 
@@ -683,6 +683,9 @@
             out_ref[j, :, p * 128 : (p + 1) * 128] = jnp.concatenate(
                 [o_s[2 * p, rows, :], o_s[2 * p + 1, rows, :]], axis=1
             )
+    for out_w_ref, left_ref in zip(out_w, left):
+        for j in range(seqs):
+            left_ref[j] = dot(out_ref[j], out_w_ref[...]).astype(BF16)
     hook(2)
 
 
@@ -808,20 +811,21 @@
     )
 
 
-def attend(sizes, length, normal, weight, gains, tables, jobs, number, after):
+def attend(sizes, length, normal, weight, gains, tables, jobs, number, after, out_w=()):
     seqs, rows_in, _ = normal.shape
     hq, hkv, _ = sizes
     slot = seqs * rows_in
     return call(
         functools.partial(attend_kernel, sizes),
-        [length, normal, weight, *gains, *tables],
-        [SMEM] + [VMEM] * 7,
+        [length, normal, weight, *gains, *tables, *out_w],
+        [SMEM] + [VMEM] * (7 + len(out_w)),
         [
             jax.ShapeDtypeStruct((seqs, rows_in, hq * HEAD), BF16),
             jax.ShapeDtypeStruct((hq, slot, 1), F32),
             jax.ShapeDtypeStruct((seqs, rows_in, weight.shape[1]), BF16),
-        ],
-        [VMEM, VMEM, VMEM],
+        ]
+        + [jax.ShapeDtypeStruct(normal.shape, BF16)] * len(out_w),
+        [VMEM] * (3 + len(out_w)),
         jobs,
         number,
         after,
@@ -835,7 +839,7 @@
             flops=56 * hq * slot * slot * HEAD, bytes_accessed=1 << 23, transcendentals=0
         ),
         name="attend",
-        late=(1, 2),
+        late=(1, 2) + tuple(range(8, 8 + len(out_w))),
     )
 
 
@@ -1262,14 +1266,13 @@
         ],
         axis=1,
     )
+    qkv_weight = lax.all_gather(qkv_own, "fsdp", axis=0, tiled=True)
     start = [
         ("gather", normal_in[0]),
         ("deal", out_weight),
         ("own", gate_weight, up_weight, down_weight),
-        ("line", qkv_own),
     ]
-    normal_0, out_own, *ffn_own, qkv_weight = transfer(start, 1)
-    qkv_weight = qkv_weight.reshape(model, -1)
+    normal_0, out_own, *ffn_own = transfer(start, 1)
     hidden_own = gate_weight.shape[0] // seqs
     part = hidden_own // CHUNKS
     ffn_weights = [lax.all_gather(own, "fsdp", axis=0) for own in ffn_own]
@@ -1281,10 +1284,10 @@
         res = inputs[b] + total
         return res, normed(res, ffn_gain).astype(BF16)
 
-    def heads(b, jobs, number, after):
+    def heads(b, jobs, number, after, out_w=()):
         return attend(
-            sizes, lengths[b : b + 1], normal_full[b], qkv_weight, gains, tables,
-            jobs, number, after,
+            sizes, lengths[b : b + 1], normal_full[b].reshape(chunked), qkv_weight, gains, tables,
+            jobs, number, after, out_w,
         )
 
     normal_full = [None] * slots
@@ -1295,7 +1298,9 @@
         0, [("gather", normal_in[1]), ("line", out_own)], 2, normal_full[0]
     )
     out_rows = out_rows.reshape(-1, model)
-    (mixed_1, lse_1, qkv_1), (total_0,) = heads(1, [("scatter", leave(mixed_0))], 3, mixed_0)
+    (mixed_1, lse_1, qkv_1, left_1), (total_0,) = heads(
+        1, [("scatter", leave(mixed_0))], 3, mixed_0, (out_rows,)
+    )
     qkv = [qkv_0, qkv_1]
     log_sums = [lse_0, lse_1]
     res_0, mid_0 = enter_ffn(0, total_0)
@@ -1327,7 +1332,7 @@
         return out.reshape(chunked), results
 
     total_1, full = ffn_step(
-        0, 0, [("scatter", leave(mixed_1)), ("gather", out_low[1])], 5, mid_full[0]
+        0, 0, [("scatter", left_1), ("gather", out_low[1])], 5, mid_full[0]
     )
     cot_full[1] = full.reshape(flat)
     res_1, mid_1 = enter_ffn(1, total_1)
@@ -1390,18 +1395,19 @@
         ],
         axis=1,
     )
-    attn_sums = lax.psum_scatter(attn_grads, "fsdp", scatter_dimension=0, tiled=True)
-    out_1, (in_total_1, ffn_parts_1) = leave_ffn(
-        1, [("scatter", pull_1), ("gather", ffn_sums[1])], 13, attn_grads, True
-    )
+    out_1, (in_total_1,) = leave_ffn(1, [("scatter", pull_1)], 13, attn_grads, True)
+    attn_sums = lax.psum_scatter(
+        follow(attn_grads, [ffn_sums[1], in_total_1]), "fsdp", scatter_dimension=0, tiled=True
+    )
+    (ffn_parts_1,) = transfer([("gather", ffn_sums[1])], 15, in_total_1)
     out_total_1 = lax.psum_scatter(
-        follow(out_1, [attn_sums]), "seq", scatter_dimension=0
+        follow(out_1, [attn_sums, ffn_parts_1]), "seq", scatter_dimension=0
     ).astype(F32)
     out_edge = attn_sums.shape[1] - model // blocks
     heads_all, _, out_parts = transfer(
         [("gather", attn_sums[:, :out_edge]), ("spread", attn_sums[:, out_edge:])],
         14,
-        in_total_1,
+        ffn_parts_1,
     )
     grad_out = jnp.swapaxes(
         out_parts.reshape(seqs, blocks, piece, model // blocks), 1, 2

time: 936 us -> 924 us (0.987)
  Pallas kernels: 797 us -> 783 us
  waiting for transfers between devices: 18.4 us -> 32.3 us
    reduce_scatter x1, waiting for transfers between devices: 0.02 us -> 31.5 us  [on_device(): lax.psum_scatter(follow(attn_grads, [ffn_sums[1], in_total_1]), 'fsdp', s...]
    reduce_scatter x1, waiting for transfers between devices: 17.5 us -> 0.02 us  [on_device(): ffn_sums.append(lax.psum_scatter(grads_1, 'fsdp', scatter_dimension=0))]
    pallas_call x15 -> x16, Pallas kernels: 775 us -> 761 us  [call(): pl.pallas_call(kernel, grid=grid, out_shape=tuple(out_shape) + tuple(shap...]
    dot_general x4 -> x3, matrix products: 25.8 us -> 21.9 us  [dot(): return lax.dot_general(a, b, dims, preferred_element_type=F32)]
  transfers between devices with their start and end apart: 6 -> 7, of which waited for: 1 -> 1; matrix products, arithmetic and copies ran while one was open for 7% -> 7% of each run, Pallas kernels for 69% -> 72%
where the time goes in v11:
time: 924 us; the launch traced here: 920 us
  Pallas kernels  783 us (85%)
  other arithmetic  42.8 us (5%)
  waiting for transfers between devices  32.3 us (3%)
  local copies, waits for them, and re-layouts  25 us (3%)
  matrix products  21.9 us (2%)
  between operations  15 us (2%)
    pallas_call x16, Pallas kernels, call(): pl.pallas_call(kernel, grid=grid, out_shape=tuple(out_shape) + tuple(shap...  761 us
    reduce_scatter x1, waiting for transfers between devices, on_device(): lax.psum_scatter(follow(attn_grads, [ffn_sums[1], in_total_1]), 'fsdp', s...  31.5 us
    dot_general x3, matrix products, dot(): return lax.dot_general(a, b, dims, preferred_element_type=F32)  21.9 us
  transfers between devices with their start and end apart: 7, of which 1 were waited for; matrix products, arithmetic and copies ran while one was open for 7% of the time, Pallas kernels for 72%

profile of v11, /device:TPU:6, one launch (start us, length us, event | category | flops | bytes accessed | tf_op | source)
XLA Modules:
  0.0 920.4 jit_solution(7871282577521894654)
XLA Ops:
  7.2 1.0 constant_dynamic-slice_fusion.2
  8.2 0.9 constant_dynamic-slice_fusion
  9.1 0.8 pad_maximum_fusion.2
  10.0 2.1 convert_element_type.79
  12.4 0.9 multiply_multiply_fusion
  13.3 0.8 copy-done
  14.1 1.7 multiply_convert_fusion.3
  15.9 38.7 %transfer.4 = (bf16[4,256,2048]{2,1,0:T(8,128)(2,1)}, bf16[64,2048]{1,0:T(8,128)(2,1)}, bf16[3,128,2048]{2,1,0:T(8,128)(2,1)}, bf16[3,128,2048]{2,1,0:T(8,128)(2,1)}) custom-call(bf16[256,2048]{1,0:T(8,128)(2,1)} %get-tuple-element.154.refs_0_, bf16[256,2048]{1,0:T(8,128)(2,1)} %refs_1_.1, bf16[1024,2048]{1,0:T(8,128)(2,1)} %refs_2_.1, ...), custom_call_target="tpu_custom_call" | custom-call | tf_op jit(solution)/shard_map/transfer/pallas_call | solution.py:567
  54.6 0.7 all-gather.8.cloned.1.call-update
  55.4 0.7 maximum_bitcast_fusion
  57.7 2.0 copy-done.10
  59.7 1.6 fusion.8
  61.3 49.4 %attend.2 = (bf16[4,256,512]{2,1,0:T(8,128)(2,1)}, f32[8,1024,1]{2,1,0:T(8,128)}, bf16[4,256,768]{2,1,0:T(8,128)(2,1)}, bf16[4,256,2048]{2,1,0:T(8,128)(2,1)}, bf16[8,64,2048]{2,1,0:T(8,128)(2,1)}) custom-call(s32[1]{0:T(128)} %get-tuple-element.169.refs_0_, bf16[4,256,2048]{2,1,0:T(8,128)(2,1)} %get-tuple-element.73.refs_1_.refs_8_, ...), custom_call_target="tpu_custom_call" | custom-call | flops 30064771072 | bytes 8388608 | tf_op jit(solution)/shard_map/attend/pallas_call | solution.py:567
  110.8 6.3 convolution_convert_fusion
  117.0 45.3 %attend.3 = (bf16[4,256,512]{2,1,0:T(8,128)(2,1)}, f32[8,1024,1]{2,1,0:T(8,128)}, bf16[4,256,768]{2,1,0:T(8,128)(2,1)}, bf16[4,256,2048]{2,1,0:T(8,128)(2,1)}, f32[256,2048]{1,0:T(8,128)}) custom-call(s32[1]{0:T(128)} %get-tuple-element.170.refs_0_, bf16[4,256,2048]{2,1,0:T(8,128)(2,1)} %get-tuple-element.75.refs_1_, ...), custom_call_target="tpu_custom_call" | custom-call | flops 30064771072 | bytes 8388608 | tf_op jit(solution)/shard_map/attend/pallas_call | solution.py:567
  162.4 1.9 multiply_reduce_fusion.7
  164.3 1.3 copy-done.7
  165.6 1.2 multiply_convert_fusion.2.refs_1_
  166.8 70.4 %transfer.5 = (bf16[4,256,2048]{2,1,0:T(8,128)(2,1)}, bf16[4,256,2048]{2,1,0:T(8,128)(2,1)}) custom-call(bf16[4,256,512]{2,1,0:T(8,128)(2,1)} %get-tuple-element.79.refs_0_.refs_12_, bf16[256,2048]{1,0:T(8,128)(2,1)} %multiply_convert_fusion.2.refs_1_, bf16[256,2048]{1,0:T(8,128)(2,1)} %get-tuple-element.156.refs_2_), custom_call_target="tpu_custom_call" | custom-call | tf_op jit(solution)/shard_map/transfer/pallas_call | solution.py:567
  237.3 73.1 %ffn_both.4 = (bf16[3,1024,1024]{2,1,0:T(8,128)(2,1)}, f32[1024,2048]{1,0:T(8,128)}, f32[256,2048]{1,0:T(8,128)}, bf16[4,256,2048]{2,1,0:T(8,128)(2,1)}) custom-call(bf16[1024,2048]{1,0:T(8,128)(2,1)} %bitcast.138, bf16[1024,2048]{1,0:T(8,128)(2,1)} %bitcast.143, bf16[8,3,128,2048]{3,2,1,0:T(8,128)(2,1)} %bitcast.130, bf16[1024,2048]{1,0:T(8,128)(2,1)} %bitcast.139, ...), custom_call_target="tpu_custom_call" | custom-call | flops 34359738368 | bytes 20971520 | tf_op jit(solution)/shard_map/ffn_both/pallas_call | solution.py:567
  310.4 1.9 multiply_reduce_fusion.6
  312.9 0.7 copy-done.4
  313.6 1.2 multiply_convert_fusion.1.refs_5_
  314.9 39.3 %ffn_both.5 = (bf16[3,1024,1024]{2,1,0:T(8,128)(2,1)}, bf16[1024,2048]{1,0:T(8,128)(2,1)}, bf16[4,256,2048]{2,1,0:T(8,128)(2,1)}) custom-call(bf16[1024,2048]{1,0:T(8,128)(2,1)} %bitcast.140, bf16[1024,2048]{1,0:T(8,128)(2,1)} %bitcast.144, bf16[8,3,128,2048]{3,2,1,0:T(8,128)(2,1)} %bitcast.134, f32[1024,2048]{1,0:T(8,128)} %get-tuple-element.85.refs_3_, ...), custom_call_target="tpu_custom_call" | custom-call | flops 34359738368 | bytes 20971520 | tf_op jit(solution)/shard_map/ffn_both/pallas_call | solution.py:567
  354.1 39.5 %ffn_both.6 = (bf16[3,1024,1024]{2,1,0:T(8,128)(2,1)}, f32[1024,2048]{1,0:T(8,128)}, f32[256,2048]{1,0:T(8,128)}) custom-call(bf16[1024,2048]{1,0:T(8,128)(2,1)} %bitcast.152, bf16[1024,2048]{1,0:T(8,128)(2,1)} %bitcast.148, bf16[8,3,128,2048]{3,2,1,0:T(8,128)(2,1)} %bitcast.131, bf16[3,1024,1024]{2,1,0:T(8,128)(2,1)} %get-tuple-element.90.refs_3_.refs_1_.refs_0_, ...), custom_call_target="tpu_custom_call" | custom-call | flops 34359738368 | bytes 20971520 | tf_op jit(solution)/shard_map/ffn_both/pallas_call | solution.py:567
  393.7 2.3 multiply_reduce_fusion.3
  396.5 3.9 fusion.16
  400.4 38.6 %ffn_grads.2 = (bf16[8,3,128,2048]{3,2,1,0:T(8,128)(2,1)}, bf16[4,256,2048]{2,1,0:T(8,128)(2,1)}) custom-call(bf16[3,1024,1024]{2,1,0:T(8,128)(2,1)} %get-tuple-element.86.refs_4_.refs_0_, bf16[3,1024,1024]{2,1,0:T(8,128)(2,1)} %get-tuple-element.93.refs_1_.refs_6_.refs_0_, bf16[1024,2048]{1,0:T(8,128)(2,1)} %bitcast.141, bf16[1024,2048]{1,0:T(8,128)(2,1)} %bitcast.153, ...), custom_call_target="tpu_custom_call" | custom-call | flops 38654705664 | bytes 16777216 | tf_op jit(solution)/shard_map/ffn_grads/pallas_call | solution.py:567
  439.1 14.6 %ffn_down.2 = bf16[1024,2048]{1,0:T(8,128)(2,1)} custom-call(bf16[3,1024,1024]{2,1,0:T(8,128)(2,1)} %get-tuple-element.86.refs_4_.refs_0_, bf16[3,1024,1024]{2,1,0:T(8,128)(2,1)} %get-tuple-element.90.refs_3_.refs_1_.refs_0_, bf16[8,3,128,2048]{3,2,1,0:T(8,128)(2,1)} %bitcast.132, bf16[8,3,128,2048]{3,2,1,0:T(8,128)(2,1)} %bitcast.135, ...), custom_call_target="tpu_custom_call" | custom-call | flops 17179869184 | bytes 12582912 | tf_op jit(solution)/shard_map/ffn_down/pallas_call | solution.py:567
  453.7 36.6 %ffn_both.7 = (bf16[3,1024,1024]{2,1,0:T(8,128)(2,1)}, bf16[1024,2048]{1,0:T(8,128)(2,1)}, f32[256,2048]{1,0:T(8,128)}) custom-call(bf16[1024,2048]{1,0:T(8,128)(2,1)} %bitcast.154, bf16[1024,2048]{1,0:T(8,128)(2,1)} %bitcast.150, bf16[8,3,128,2048]{3,2,1,0:T(8,128)(2,1)} %bitcast.136, f32[1024,2048]{1,0:T(8,128)} %get-tuple-element.92.refs_3_, ...), custom_call_target="tpu_custom_call" | custom-call | flops 34359738368 | bytes 20971520 | tf_op jit(solution)/shard_map/ffn_both/pallas_call | solution.py:567
  490.3 38.5 %ffn_grads.3 = (bf16[8,3,128,2048]{3,2,1,0:T(8,128)(2,1)}, f32[256,2048]{1,0:T(8,128)}) custom-call(bf16[3,1024,1024]{2,1,0:T(8,128)(2,1)} %get-tuple-element.90.refs_3_.refs_1_.refs_0_, bf16[3,1024,1024]{2,1,0:T(8,128)(2,1)} %get-tuple-element.97.refs_1_.refs_6_, bf16[1024,2048]{1,0:T(8,128)(2,1)} %bitcast.142, bf16[1024,2048]{1,0:T(8,128)(2,1)} %bitcast.155, ...), custom_call_target="tpu_custom_call" | custom-call | flops 38654705664 | bytes 16777216 | tf_op jit(solution)/shard_map/ffn_grads/pallas_call | solution.py:567
  529.2 1.3 copy-done.5
  530.5 2.3 multiply_reduce_fusion.2
  533.4 3.9 fusion.15
  537.3 47.8 %attend_back.2 = (bf16[4,256,768]{2,1,0:T(8,128)(2,1)}, f32[2,128]{1,0:T(2,128)}, bf16[4,256,2048]{2,1,0:T(8,128)(2,1)}, bf16[4,256,2048]{2,1,0:T(8,128)(2,1)}) custom-call(s32[1]{0:T(128)} %get-tuple-element.169.refs_0_, bf16[4,256,768]{2,1,0:T(8,128)(2,1)} %get-tuple-element.98.refs_1_, bf16[4,256,2048]{2,1,0:T(8,128)(2,1)} %get-tuple-element.99.refs_2_.refs_13_, ...), custom_call_target="tpu_custom_call" | custom-call | flops 47244640256 | bytes 8388608 | tf_op jit(solution)/shard_map/attend_back/pallas_call | solution.py:567
  585.1 7.3 fusion.21
  592.3 88.0 %attend_back.3 = (bf16[4,256,768]{2,1,0:T(8,128)(2,1)}, f32[2,128]{1,0:T(2,128)}, bf16[4,256,2048]{2,1,0:T(8,128)(2,1)}, bf16[2048,512]{1,0:T(8,128)(2,1)}, f32[...) custom-call(s32[1]{0:T(128)} %get-tuple-element.170.refs_0_, bf16[4,256,768]{2,1,0:T(8,128)(2,1)} %get-tuple-element.105.refs_1_, ...), custom_call_target="tpu_custom_call" | custom-call | flops 47244640256 | bytes 8388608 | tf_op jit(solution)/shard_map/attend_back/pallas_call | solution.py:567
  680.3 0.7 add.142
  681.5 8.3 fusion.2
  689.9 2.9 fusion.4.refs_4_
  692.8 38.3 %ffn_down.3 = (bf16[1024,2048]{1,0:T(8,128)(2,1)}, f32[256,2048]{1,0:T(8,128)}) custom-call(bf16[3,1024,1024]{2,1,0:T(8,128)(2,1)} %get-tuple-element.93.refs_1_.refs_6_.refs_0_, bf16[3,1024,1024]{2,1,0:T(8,128)(2,1)} %get-tuple-element.97.refs_1_.refs_6_, bf16[8,3,128,2048]{3,2,1,0:T(8,128)(2,1)} %bitcast.133, bf16[8,3,128,2048]{3,2,1,0:T(8,128)(2,1)} %bitcast.137, ...), custom_call_target="tpu_custom_call" | custom-call | flops 17179869184 | bytes 12582912 | tf_op jit(solution)/shard_map/ffn_down/pallas_call | solution.py:567
  731.2 47.3 %transfer.6.refs_0_ = bf16[4,384,2048]{2,1,0:T(8,128)(2,1)} custom-call(f32[256,2048]{1,0:T(8,128)} %get-tuple-element.115.refs_0_, bf16[384,2048]{1,0:T(8,128)(2,1)} %bitcast.124), custom_call_target="tpu_custom_call" | custom-call | tf_op jit(solution)/shard_map/transfer/pallas_call | solution.py:567
  778.4 31.5 %reduce-scatter.11.cloned.1.call-done = bf16[256,1408]{1,0:T(8,128)(2,1)} async-done(((bf16[2048,1408]{1,0:T(8,128)(2,1)}), bf16[256,1408]{1,0:T(8,128)(2,1)}) %reduce-scatter.11.cloned.1.call-update) | async-done | bytes 720912 | tf_op jit(solution)/shard_map/reduce_scatter | solution.py:1399
  810.6 0.9 copy-done.9
  811.5 1.8 fusion.11
  813.4 7.8 place_parts.2
  821.2 9.0 place_parts.3
  830.3 3.1 multiply_reduce_fusion.1
  834.6 0.7 copy-done.16
  835.3 1.4 fusion.12
  836.7 1.5 pad_maximum_fusion.1
  838.2 0.7 slice.95.refs_2_
  838.9 0.8 slice.94.refs_1_
  839.7 56.0 %transfer.7 = (bf16[4,256,896]{2,1,0:T(8,128)(2,1)}, bf16[4,256,512]{2,1,0:T(8,128)(2,1)}, bf16[4,256,512]{2,1,0:T(8,128)(2,1)}) custom-call(bf16[4,384,2048]{2,1,0:T(8,128)(2,1)} %transfer.6.refs_0_, bf16[256,896]{1,0:T(8,128)(2,1)} %slice.94.refs_1_, bf16[256,512]{1,0:T(8,128)(2,1)} %slice.95.refs_2_), custom_call_target="tpu_custom_call" | custom-call | tf_op jit(solution)/shard_map/transfer/pallas_call | solution.py:567
  895.7 1.5 convert_bitcast_fusion
  897.2 1.4 copy.51
  898.6 2.2 copy.60
  900.8 4.7 place_heads.1
  905.5 1.5 slice_reduce_fusion.2
  907.0 1.6 slice_reduce_fusion
  908.6 1.0 slice_reduce_fusion.1
  909.6 0.7 dynamic-slice_divide_fusion
  910.2 1.5 fusion.14
  911.7 1.5 pad_maximum_fusion
  (112 shorter events, 6.7 us)
Async XLA Ops:
  7.2 54.1 %all-gather.6.cloned.1.call-start = ((), (), s32[]{:S(2)}) async-start(), calls=%async_computation.4 | async-start | bytes 3538944 | tf_op jit(solution)/shard_map/all_gather | solution.py:1269
  9.9 227.3 %all-gather.10.cloned.1.call-start = ((), (), s32[]{:S(2)}) async-start(), calls=%async_computation.9 | async-start | bytes 14155776 | tf_op jit(solution)/shard_map/all_gather | solution.py:1278
  12.1 2.1 copy-start
  12.1 2.0 copy-start.21
  13.3 2.6 copy-start.27
  13.3 2.6 copy-start.29
  54.5 0.9 copy-start.36
  54.5 0.9 copy-start.37
  54.5 1.5 copy-start.31
  54.5 2.8 copy-start.17
  54.6 260.3 %all-gather.8.cloned.1.call-start = ((), (), s32[]{:S(2)}) async-start(), calls=%async_computation.8 | async-start | bytes 14155776 | tf_op jit(solution)/shard_map/all_gather | solution.py:1278
  55.3 537.0 %reduce-scatter.7.cloned.1.call-start = ((), (), s32[]{:S(2)}) async-start(), calls=%async_computation.5 | async-start | bytes 14155776 | tf_op jit(solution)/shard_map/reduce_scatter | solution.py:1351
  56.7 0.6 copy-start.23
  57.7 2.0 copy-start.10
  117.0 45.3 %copy-start.1 = (f32[2,256,2048]{2,1,0:T(8,128)S(1)}, f32[2,256,2048]{2,1,0:T(8,128)}, u32[]{:S(2)}) copy-start(f32[2,256,2048]{2,1,0:T(8,128)} %copy-done) | copy-start | bytes 12582916
  162.4 3.2 copy-start.20
  164.3 1.3 copy-start.7
  237.3 73.1 %copy-start.2 = (f32[2,256,2048]{2,1,0:T(8,128)S(1)}, f32[2,256,2048]{2,1,0:T(8,128)}, u32[]{:S(2)}) copy-start(f32[2,256,2048]{2,1,0:T(8,128)} %copy-done) | copy-start | bytes 12582916
  312.3 1.3 copy-start.4
  312.9 0.7 copy-start.25
  354.1 39.5 %copy-start.8 = (f32[256,2048]{1,0:T(8,128)S(1)}, f32[256,2048]{1,0:T(8,128)}, u32[]{:S(2)}) copy-start(f32[256,2048]{1,0:T(8,128)} %copy-done.7) | copy-start | bytes 6291460
  393.7 2.8 copy-start.11
  439.0 292.1 %reduce-scatter.9.cloned.1.call-start = ((), (), s32[]{:S(2)}) async-start(), calls=%async_computation.6 | async-start | bytes 14155776 | tf_op jit(solution)/shard_map/reduce_scatter | solution.py:1358
  528.9 1.6 copy-start.5
  528.9 1.6 copy-start.26
  528.9 281.0 %reduce-scatter.11.cloned.1.call-start = ((), (), s32[]{:S(2)}) async-start(), calls=%async_computation.7 | async-start | bytes 6488064 | tf_op jit(solution)/shard_map/reduce_scatter | solution.py:1399
  530.5 2.9 copy-start.12
  530.5 2.9 copy-start.32
  537.3 47.8 %copy-start.38 = (bf16[4,256,2048]{2,1,0:T(8,128)(2,1)S(1)}, bf16[4,256,2048]{2,1,0:T(8,128)(2,1)}, u32[]{:S(2)}) copy-start(bf16[4,256,2048]{2,1,0:T(8,128)(2,1)} %get-tuple-element.73.refs_1_.refs_8_) | copy-start | bytes 12582916
  592.3 88.0 %copy-start.35 = (f32[2,128]{1,0:T(2,128)S(1)}, f32[2,128]{1,0:T(2,128)}, u32[]{:S(2)}) copy-start(f32[2,128]{1,0:T(2,128)} %get-tuple-element.110) | copy-start | bytes 3076
  681.5 8.3 copy-start.18
  731.1 179.1 %reduce-scatter.13.cloned.1.call-start = ((), (), s32[]{:S(2)}) async-start(), calls=%async_computation.10 | async-start | bytes 5242880
  809.9 0.7 copy-start.24
  809.9 1.6 copy-start.9
  821.2 9.0 copy-start.3
  821.2 9.0 copy-start.22
  830.2 3.2 copy-start.13
  830.2 3.8 copy-start.14
  830.2 4.4 copy-start.15
  830.2 5.0 copy-start.16
  830.2 5.0 copy-start.28
  830.2 5.0 copy-start.30
  830.2 5.0 copy-start.33
  830.2 5.0 copy-start.34
  836.6 1.5 copy-start.19
  900.8 9.5 %copy-start.6 = (f32[256,2048]{1,0:T(8,128)S(1)}, f32[256,2048]{1,0:T(8,128)}, u32[]{:S(2)}) copy-start(f32[256,2048]{1,0:T(8,128)} %copy-done.4) | copy-start | bytes 6291460
Sparse Core Ops, SparseCore 0:
  10.2 49.3 all-gather.5
  61.2 133.8 all-gather.9
  196.8 116.4 all-gather.7
  439.2 139.9 reduce-scatter.6
  581.3 127.5 reduce-scatter.8
  731.3 78.6 reduce-scatter.10
  812.9 63.1 reduce-scatter.12

commit v12 on v11

--- a/solution.py
+++ b/solution.py
@@ -1400,14 +1400,14 @@
         follow(attn_grads, [ffn_sums[1], in_total_1]), "fsdp", scatter_dimension=0, tiled=True
     )
     (ffn_parts_1,) = transfer([("gather", ffn_sums[1])], 15, in_total_1)
-    out_total_1 = lax.psum_scatter(
-        follow(out_1, [attn_sums, ffn_parts_1]), "seq", scatter_dimension=0
-    ).astype(F32)
+    ffn_grad = ()
+    for c, parts in enumerate((ffn_parts_0, ffn_parts_1)):
+        ffn_grad = place_parts(order, parts.reshape(seqs, 3, part, model), c, ffn_grad)
     out_edge = attn_sums.shape[1] - model // blocks
     heads_all, _, out_parts = transfer(
         [("gather", attn_sums[:, :out_edge]), ("spread", attn_sums[:, out_edge:])],
         14,
-        ffn_parts_1,
+        ffn_grad[0],
     )
     grad_out = jnp.swapaxes(
         out_parts.reshape(seqs, blocks, piece, model // blocks), 1, 2
@@ -1416,13 +1416,13 @@
     for b, (in_cot, cot) in enumerate(((in_total_0, res_cot_0), (in_total_1, res_cot_1))):
         pull, _ = normed_back(inputs[b], attn_gain, in_cot)
         grad_tokens.append((cot + pull).astype(BF16))
+    out_total_1 = lax.psum_scatter(
+        follow(out_1, [attn_sums, ffn_grad[0], *grad_tokens]), "seq", scatter_dimension=0
+    ).astype(F32)
     output = [
         (live[b] * (hidden_res[b] + total)).astype(BF16)
         for b, total in enumerate((out_total_0, out_total_1))
     ]
-    ffn_grad = ()
-    for c, parts in enumerate((ffn_parts_0, ffn_parts_1)):
-        ffn_grad = place_parts(order, parts.reshape(seqs, 3, part, model), c, ffn_grad)
     ffn_grad = [v.reshape(seqs * hidden_own, model) for v in ffn_grad]
 
     edge = hq * HEAD

time: 924 us -> 915 us (level)
  waiting for transfers between devices: 32.3 us -> 8.03 us
  Pallas kernels: 783 us -> 796 us
    reduce_scatter x1, waiting for transfers between devices: 31.5 us -> 7.2 us  [on_device(): lax.psum_scatter(follow(attn_grads, [ffn_sums[1], in_total_1]), 'fsdp', s...]
    pallas_call x16, Pallas kernels: 761 us -> 775 us  [call(): pl.pallas_call(kernel, grid=grid, out_shape=tuple(out_shape) + tuple(shap...]
  transfers between devices with their start and end apart: 7 -> 7, of which waited for: 1 -> 1; matrix products, arithmetic and copies ran while one was open for 7% -> 7% of each run, Pallas kernels for 72% -> 75%
where the time goes in v12:
time: 915 us; the launch traced here: 911 us
  Pallas kernels  796 us (87%)
  other arithmetic  43.7 us (5%)
  local copies, waits for them, and re-layouts  25.2 us (3%)
  matrix products  21.9 us (2%)
  between operations  15 us (2%)
    pallas_call x16, Pallas kernels, call(): pl.pallas_call(kernel, grid=grid, out_shape=tuple(out_shape) + tuple(shap...  775 us
    dot_general x3, matrix products, dot(): return lax.dot_general(a, b, dims, preferred_element_type=F32)  21.9 us
  transfers between devices with their start and end apart: 7, of which 1 were waited for; matrix products, arithmetic and copies ran while one was open for 7% of the time, Pallas kernels for 75%

profile of v12, /device:TPU:6, one launch (start us, length us, event | category | flops | bytes accessed | tf_op | source)
XLA Modules:
  0.0 910.5 jit_solution(3740403167877204054)
XLA Ops:
  7.2 1.0 constant_dynamic-slice_fusion.2
  8.2 0.9 constant_dynamic-slice_fusion
  9.1 0.8 pad_maximum_fusion.2
  10.0 2.1 convert_element_type.79
  12.4 0.9 multiply_multiply_fusion
  13.3 0.8 copy-done
  14.1 1.7 multiply_convert_fusion.3
  15.9 38.7 %transfer.4 = (bf16[4,256,2048]{2,1,0:T(8,128)(2,1)}, bf16[64,2048]{1,0:T(8,128)(2,1)}, bf16[3,128,2048]{2,1,0:T(8,128)(2,1)}, bf16[3,128,2048]{2,1,0:T(8,128)(2,1)}) custom-call(bf16[256,2048]{1,0:T(8,128)(2,1)} %get-tuple-element.154.refs_0_, bf16[256,2048]{1,0:T(8,128)(2,1)} %refs_1_.1, bf16[1024,2048]{1,0:T(8,128)(2,1)} %refs_2_.1, ...), custom_call_target="tpu_custom_call" | custom-call | tf_op jit(solution)/shard_map/transfer/pallas_call | solution.py:567
  54.6 0.7 all-gather.8.cloned.1.call-update
  57.7 2.0 copy-done.10
  59.7 1.6 fusion.8
  61.3 49.4 %attend.2 = (bf16[4,256,512]{2,1,0:T(8,128)(2,1)}, f32[8,1024,1]{2,1,0:T(8,128)}, bf16[4,256,768]{2,1,0:T(8,128)(2,1)}, bf16[4,256,2048]{2,1,0:T(8,128)(2,1)}, bf16[8,64,2048]{2,1,0:T(8,128)(2,1)}) custom-call(s32[1]{0:T(128)} %get-tuple-element.169.refs_0_, bf16[4,256,2048]{2,1,0:T(8,128)(2,1)} %get-tuple-element.73.refs_1_.refs_8_, ...), custom_call_target="tpu_custom_call" | custom-call | flops 30064771072 | bytes 8388608 | tf_op jit(solution)/shard_map/attend/pallas_call | solution.py:567
  110.7 6.3 convolution_convert_fusion
  117.0 45.2 %attend.3 = (bf16[4,256,512]{2,1,0:T(8,128)(2,1)}, f32[8,1024,1]{2,1,0:T(8,128)}, bf16[4,256,768]{2,1,0:T(8,128)(2,1)}, bf16[4,256,2048]{2,1,0:T(8,128)(2,1)}, f32[256,2048]{1,0:T(8,128)}) custom-call(s32[1]{0:T(128)} %get-tuple-element.170.refs_0_, bf16[4,256,2048]{2,1,0:T(8,128)(2,1)} %get-tuple-element.75.refs_1_, ...), custom_call_target="tpu_custom_call" | custom-call | flops 30064771072 | bytes 8388608 | tf_op jit(solution)/shard_map/attend/pallas_call | solution.py:567
  162.3 1.9 multiply_reduce_fusion.7
  164.2 1.3 copy-done.7
  165.5 1.2 multiply_convert_fusion.2.refs_1_
  166.7 70.4 %transfer.5 = (bf16[4,256,2048]{2,1,0:T(8,128)(2,1)}, bf16[4,256,2048]{2,1,0:T(8,128)(2,1)}) custom-call(bf16[4,256,512]{2,1,0:T(8,128)(2,1)} %get-tuple-element.79.refs_0_.refs_12_, bf16[256,2048]{1,0:T(8,128)(2,1)} %multiply_convert_fusion.2.refs_1_, bf16[256,2048]{1,0:T(8,128)(2,1)} %get-tuple-element.156.refs_2_), custom_call_target="tpu_custom_call" | custom-call | tf_op jit(solution)/shard_map/transfer/pallas_call | solution.py:567
  237.1 73.1 %ffn_both.4 = (bf16[3,1024,1024]{2,1,0:T(8,128)(2,1)}, f32[1024,2048]{1,0:T(8,128)}, f32[256,2048]{1,0:T(8,128)}, bf16[4,256,2048]{2,1,0:T(8,128)(2,1)}) custom-call(bf16[1024,2048]{1,0:T(8,128)(2,1)} %bitcast.134, bf16[1024,2048]{1,0:T(8,128)(2,1)} %bitcast.139, bf16[8,3,128,2048]{3,2,1,0:T(8,128)(2,1)} %bitcast.126, bf16[1024,2048]{1,0:T(8,128)(2,1)} %bitcast.135, ...), custom_call_target="tpu_custom_call" | custom-call | flops 34359738368 | bytes 20971520 | tf_op jit(solution)/shard_map/ffn_both/pallas_call | solution.py:567
  310.3 1.9 multiply_reduce_fusion.6
  312.8 0.7 copy-done.4
  313.5 1.2 multiply_convert_fusion.1.refs_5_
  314.7 39.4 %ffn_both.5 = (bf16[3,1024,1024]{2,1,0:T(8,128)(2,1)}, bf16[1024,2048]{1,0:T(8,128)(2,1)}, bf16[4,256,2048]{2,1,0:T(8,128)(2,1)}) custom-call(bf16[1024,2048]{1,0:T(8,128)(2,1)} %bitcast.136, bf16[1024,2048]{1,0:T(8,128)(2,1)} %bitcast.140, bf16[8,3,128,2048]{3,2,1,0:T(8,128)(2,1)} %bitcast.130, f32[1024,2048]{1,0:T(8,128)} %get-tuple-element.85.refs_3_, ...), custom_call_target="tpu_custom_call" | custom-call | flops 34359738368 | bytes 20971520 | tf_op jit(solution)/shard_map/ffn_both/pallas_call | solution.py:567
  354.1 39.5 %ffn_both.6 = (bf16[3,1024,1024]{2,1,0:T(8,128)(2,1)}, f32[1024,2048]{1,0:T(8,128)}, f32[256,2048]{1,0:T(8,128)}) custom-call(bf16[1024,2048]{1,0:T(8,128)(2,1)} %bitcast.148, bf16[1024,2048]{1,0:T(8,128)(2,1)} %bitcast.144, bf16[8,3,128,2048]{3,2,1,0:T(8,128)(2,1)} %bitcast.127, bf16[3,1024,1024]{2,1,0:T(8,128)(2,1)} %get-tuple-element.90.refs_3_.refs_1_.refs_0_, ...), custom_call_target="tpu_custom_call" | custom-call | flops 34359738368 | bytes 20971520 | tf_op jit(solution)/shard_map/ffn_both/pallas_call | solution.py:567
  393.6 2.3 multiply_reduce_fusion.3
  396.4 3.9 fusion.14
  400.3 38.7 %ffn_grads.2 = (bf16[8,3,128,2048]{3,2,1,0:T(8,128)(2,1)}, bf16[4,256,2048]{2,1,0:T(8,128)(2,1)}) custom-call(bf16[3,1024,1024]{2,1,0:T(8,128)(2,1)} %get-tuple-element.86.refs_4_.refs_0_, bf16[3,1024,1024]{2,1,0:T(8,128)(2,1)} %get-tuple-element.93.refs_1_.refs_6_.refs_0_, bf16[1024,2048]{1,0:T(8,128)(2,1)} %bitcast.137, bf16[1024,2048]{1,0:T(8,128)(2,1)} %bitcast.149, ...), custom_call_target="tpu_custom_call" | custom-call | flops 38654705664 | bytes 16777216 | tf_op jit(solution)/shard_map/ffn_grads/pallas_call | solution.py:567
  439.1 14.6 %ffn_down.2 = bf16[1024,2048]{1,0:T(8,128)(2,1)} custom-call(bf16[3,1024,1024]{2,1,0:T(8,128)(2,1)} %get-tuple-element.86.refs_4_.refs_0_, bf16[3,1024,1024]{2,1,0:T(8,128)(2,1)} %get-tuple-element.90.refs_3_.refs_1_.refs_0_, bf16[8,3,128,2048]{3,2,1,0:T(8,128)(2,1)} %bitcast.128, bf16[8,3,128,2048]{3,2,1,0:T(8,128)(2,1)} %bitcast.131, ...), custom_call_target="tpu_custom_call" | custom-call | flops 17179869184 | bytes 12582912 | tf_op jit(solution)/shard_map/ffn_down/pallas_call | solution.py:567
  453.7 36.6 %ffn_both.7 = (bf16[3,1024,1024]{2,1,0:T(8,128)(2,1)}, bf16[1024,2048]{1,0:T(8,128)(2,1)}, f32[256,2048]{1,0:T(8,128)}) custom-call(bf16[1024,2048]{1,0:T(8,128)(2,1)} %bitcast.150, bf16[1024,2048]{1,0:T(8,128)(2,1)} %bitcast.146, bf16[8,3,128,2048]{3,2,1,0:T(8,128)(2,1)} %bitcast.132, f32[1024,2048]{1,0:T(8,128)} %get-tuple-element.92.refs_3_, ...), custom_call_target="tpu_custom_call" | custom-call | flops 34359738368 | bytes 20971520 | tf_op jit(solution)/shard_map/ffn_both/pallas_call | solution.py:567
  490.3 38.4 %ffn_grads.3 = (bf16[8,3,128,2048]{3,2,1,0:T(8,128)(2,1)}, f32[256,2048]{1,0:T(8,128)}) custom-call(bf16[3,1024,1024]{2,1,0:T(8,128)(2,1)} %get-tuple-element.90.refs_3_.refs_1_.refs_0_, bf16[3,1024,1024]{2,1,0:T(8,128)(2,1)} %get-tuple-element.97.refs_1_.refs_6_, bf16[1024,2048]{1,0:T(8,128)(2,1)} %bitcast.138, bf16[1024,2048]{1,0:T(8,128)(2,1)} %bitcast.151, ...), custom_call_target="tpu_custom_call" | custom-call | flops 38654705664 | bytes 16777216 | tf_op jit(solution)/shard_map/ffn_grads/pallas_call | solution.py:567
  529.0 1.3 copy-done.5
  530.3 2.3 multiply_reduce_fusion.2
  533.2 3.9 fusion.13
  537.1 47.9 %attend_back.2 = (bf16[4,256,768]{2,1,0:T(8,128)(2,1)}, f32[2,128]{1,0:T(2,128)}, bf16[4,256,2048]{2,1,0:T(8,128)(2,1)}, bf16[4,256,2048]{2,1,0:T(8,128)(2,1)}) custom-call(s32[1]{0:T(128)} %get-tuple-element.169.refs_0_, bf16[4,256,768]{2,1,0:T(8,128)(2,1)} %get-tuple-element.98.refs_1_, bf16[4,256,2048]{2,1,0:T(8,128)(2,1)} %get-tuple-element.99.refs_2_.refs_13_, ...), custom_call_target="tpu_custom_call" | custom-call | flops 47244640256 | bytes 8388608 | tf_op jit(solution)/shard_map/attend_back/pallas_call | solution.py:567
  585.0 7.3 fusion.19
  592.3 87.6 %attend_back.3 = (bf16[4,256,768]{2,1,0:T(8,128)(2,1)}, f32[2,128]{1,0:T(2,128)}, bf16[4,256,2048]{2,1,0:T(8,128)(2,1)}, bf16[2048,512]{1,0:T(8,128)(2,1)}, f32[...) custom-call(s32[1]{0:T(128)} %get-tuple-element.170.refs_0_, bf16[4,256,768]{2,1,0:T(8,128)(2,1)} %get-tuple-element.105.refs_1_, ...), custom_call_target="tpu_custom_call" | custom-call | flops 47244640256 | bytes 8388608 | tf_op jit(solution)/shard_map/attend_back/pallas_call | solution.py:567
  679.9 0.7 add.142
  681.2 8.3 fusion.2
  689.5 2.9 fusion.4.refs_4_
  692.4 38.2 %ffn_down.3 = (bf16[1024,2048]{1,0:T(8,128)(2,1)}, f32[256,2048]{1,0:T(8,128)}) custom-call(bf16[3,1024,1024]{2,1,0:T(8,128)(2,1)} %get-tuple-element.93.refs_1_.refs_6_.refs_0_, bf16[3,1024,1024]{2,1,0:T(8,128)(2,1)} %get-tuple-element.97.refs_1_.refs_6_, bf16[8,3,128,2048]{3,2,1,0:T(8,128)(2,1)} %bitcast.129, bf16[8,3,128,2048]{3,2,1,0:T(8,128)(2,1)} %bitcast.133, ...), custom_call_target="tpu_custom_call" | custom-call | flops 17179869184 | bytes 12582912 | tf_op jit(solution)/shard_map/ffn_down/pallas_call | solution.py:567
  730.7 47.9 %transfer.6 = bf16[4,384,2048]{2,1,0:T(8,128)(2,1)} custom-call(f32[256,2048]{1,0:T(8,128)} %get-tuple-element.115.refs_0_, bf16[384,2048]{1,0:T(8,128)(2,1)} %bitcast.120), custom_call_target="tpu_custom_call" | custom-call | tf_op jit(solution)/shard_map/transfer/pallas_call | solution.py:567
  778.6 7.7 place_parts.2
  786.4 8.8 place_parts.3
  795.2 2.9 multiply_reduce_fusion
  798.7 0.7 copy-done.15
  800.0 2.3 add_convert_fusion
  802.4 7.2 reduce-scatter.11.cloned.1.call-done
  809.6 0.6 copy-done.26
  810.2 0.9 copy-done.9
  811.2 2.0 fusion.11
  813.3 1.5 pad_maximum_fusion.1
  814.8 0.7 slice.95.refs_2_
  815.6 0.8 slice.94.refs_1_
  816.4 69.5 %transfer.7 = (bf16[4,256,896]{2,1,0:T(8,128)(2,1)}, bf16[4,256,512]{2,1,0:T(8,128)(2,1)}, bf16[4,256,512]{2,1,0:T(8,128)(2,1)}) custom-call(f32[4,2,128,2048]{3,2,1,0:T(8,128)} %get-tuple-element.121.refs_0_, bf16[256,896]{1,0:T(8,128)(2,1)} %slice.94.refs_1_, bf16[256,512]{1,0:T(8,128)(2,1)} %slice.95.refs_2_), custom_call_target="tpu_custom_call" | custom-call | tf_op jit(solution)/shard_map/transfer/pallas_call | solution.py:567
  885.8 1.5 convert_bitcast_fusion
  887.3 1.4 copy.51
  888.7 2.2 copy.60
  890.9 4.7 place_heads.1
  895.6 1.5 slice_reduce_fusion.2
  897.1 1.6 slice_reduce_fusion
  898.7 1.0 slice_reduce_fusion.1
  899.7 0.7 dynamic-slice_divide_fusion
  900.4 1.5 fusion.12
  901.9 1.5 pad_maximum_fusion
  (116 shorter events, 7.0 us)
Async XLA Ops:
  7.2 54.1 %all-gather.6.cloned.1.call-start = ((), (), s32[]{:S(2)}) async-start(), calls=%async_computation.4 | async-start | bytes 3538944 | tf_op jit(solution)/shard_map/all_gather | solution.py:1269
  9.9 227.2 %all-gather.10.cloned.1.call-start = ((), (), s32[]{:S(2)}) async-start(), calls=%async_computation.9 | async-start | bytes 14155776 | tf_op jit(solution)/shard_map/all_gather | solution.py:1278
  12.1 2.1 copy-start
  12.1 2.1 copy-start.23
  13.3 2.6 copy-start.29
  13.3 2.6 copy-start.31
  54.5 0.9 copy-start.38
  54.5 0.9 copy-start.39
  54.5 1.5 copy-start.33
  54.6 2.7 copy-start.19
  54.6 260.1 %all-gather.8.cloned.1.call-start = ((), (), s32[]{:S(2)}) async-start(), calls=%async_computation.8 | async-start | bytes 14155776 | tf_op jit(solution)/shard_map/all_gather | solution.py:1278
  55.3 537.0 %reduce-scatter.7.cloned.1.call-start = ((), (), s32[]{:S(2)}) async-start(), calls=%async_computation.5 | async-start | bytes 14155776 | tf_op jit(solution)/shard_map/reduce_scatter | solution.py:1351
  56.7 0.6 copy-start.25
  57.6 2.0 copy-start.10
  117.0 45.2 %copy-start.1 = (f32[2,256,2048]{2,1,0:T(8,128)S(1)}, f32[2,256,2048]{2,1,0:T(8,128)}, u32[]{:S(2)}) copy-start(f32[2,256,2048]{2,1,0:T(8,128)} %copy-done) | copy-start | bytes 12582916
  162.2 3.2 copy-start.22
  164.2 1.3 copy-start.7
  237.1 73.1 %copy-start.2 = (f32[2,256,2048]{2,1,0:T(8,128)S(1)}, f32[2,256,2048]{2,1,0:T(8,128)}, u32[]{:S(2)}) copy-start(f32[2,256,2048]{2,1,0:T(8,128)} %copy-done) | copy-start | bytes 12582916
  312.2 1.3 copy-start.4
  312.8 0.7 copy-start.27
  354.1 39.5 %copy-start.8 = (f32[256,2048]{1,0:T(8,128)S(1)}, f32[256,2048]{1,0:T(8,128)}, u32[]{:S(2)}) copy-start(f32[256,2048]{1,0:T(8,128)} %copy-done.7) | copy-start | bytes 6291460
  393.6 2.8 copy-start.11
  439.0 291.6 %reduce-scatter.9.cloned.1.call-start = ((), (), s32[]{:S(2)}) async-start(), calls=%async_computation.6 | async-start | bytes 14155776 | tf_op jit(solution)/shard_map/reduce_scatter | solution.py:1358
  528.7 1.6 copy-start.5
  528.7 1.6 copy-start.28
  528.8 280.8 %reduce-scatter.11.cloned.1.call-start = ((), (), s32[]{:S(2)}) async-start(), calls=%async_computation.7 | async-start | bytes 6488064 | tf_op jit(solution)/shard_map/reduce_scatter | solution.py:1399
  530.3 2.9 copy-start.12
  530.3 2.9 copy-start.34
  537.1 47.9 %copy-start.40 = (bf16[4,256,2048]{2,1,0:T(8,128)(2,1)S(1)}, bf16[4,256,2048]{2,1,0:T(8,128)(2,1)}, u32[]{:S(2)}) copy-start(bf16[4,256,2048]{2,1,0:T(8,128)(2,1)} %get-tuple-element.73.refs_1_.refs_8_) | copy-start | bytes 12582916
  592.3 87.6 %copy-start.37 = (f32[2,128]{1,0:T(2,128)S(1)}, f32[2,128]{1,0:T(2,128)}, u32[]{:S(2)}) copy-start(f32[2,128]{1,0:T(2,128)} %get-tuple-element.110) | copy-start | bytes 3076
  681.2 8.3 copy-start.20
  730.7 169.7 %reduce-scatter.13.cloned.1.call-start = ((), (), s32[]{:S(2)}) async-start(), calls=%async_computation.10 | async-start | bytes 5242880
  786.4 8.8 copy-start.3
  786.4 8.8 copy-start.24
  795.1 3.0 copy-start.13
  795.1 3.6 copy-start.14
  795.1 4.3 copy-start.15
  795.2 4.8 copy-start.16
  795.2 4.8 copy-start.30
  795.2 4.8 copy-start.32
  795.2 4.8 copy-start.35
  795.2 4.8 copy-start.36
  809.5 0.7 copy-start.26
  809.6 1.6 copy-start.9
  811.2 2.0 copy-start.17
  811.2 2.2 copy-start.18
  813.3 1.5 copy-start.21
  890.9 9.5 %copy-start.6 = (f32[256,2048]{1,0:T(8,128)S(1)}, f32[256,2048]{1,0:T(8,128)}, u32[]{:S(2)}) copy-start(f32[256,2048]{1,0:T(8,128)} %copy-done.4) | copy-start | bytes 6291460
Sparse Core Ops, SparseCore 0:
  10.2 49.3 all-gather.5
  61.2 133.8 all-gather.9
  196.8 116.3 all-gather.7
  439.1 139.6 reduce-scatter.6
  581.0 127.5 reduce-scatter.8
  730.8 78.7 reduce-scatter.10
  812.5 77.9 reduce-scatter.12

commit v13 on v12

--- a/solution.py
+++ b/solution.py
@@ -1395,14 +1395,13 @@
         ],
         axis=1,
     )
-    out_1, (in_total_1,) = leave_ffn(1, [("scatter", pull_1)], 13, attn_grads, True)
+    ffn_grad = place_parts(order, ffn_parts_0.reshape(seqs, 3, part, model), 0, ())
+    out_1, (in_total_1,) = leave_ffn(1, [("scatter", pull_1)], 13, ffn_sums[1], True)
     attn_sums = lax.psum_scatter(
-        follow(attn_grads, [ffn_sums[1], in_total_1]), "fsdp", scatter_dimension=0, tiled=True
+        follow(attn_grads, [ffn_sums[1], ffn_grad[0]]), "fsdp", scatter_dimension=0, tiled=True
     )
     (ffn_parts_1,) = transfer([("gather", ffn_sums[1])], 15, in_total_1)
-    ffn_grad = ()
-    for c, parts in enumerate((ffn_parts_0, ffn_parts_1)):
-        ffn_grad = place_parts(order, parts.reshape(seqs, 3, part, model), c, ffn_grad)
+    ffn_grad = place_parts(order, ffn_parts_1.reshape(seqs, 3, part, model), 1, ffn_grad)
     out_edge = attn_sums.shape[1] - model // blocks
     heads_all, _, out_parts = transfer(
         [("gather", attn_sums[:, :out_edge]), ("spread", attn_sums[:, out_edge:])],
@@ -1417,7 +1416,7 @@
         pull, _ = normed_back(inputs[b], attn_gain, in_cot)
         grad_tokens.append((cot + pull).astype(BF16))
     out_total_1 = lax.psum_scatter(
-        follow(out_1, [attn_sums, ffn_grad[0], *grad_tokens]), "seq", scatter_dimension=0
+        follow(out_1, [attn_sums, ffn_parts_1]), "seq", scatter_dimension=0
     ).astype(F32)
     output = [
         (live[b] * (hidden_res[b] + total)).astype(BF16)

time: 915 us -> 908 us (level)
  transfers between devices with their start and end apart: 7 -> 7, of which waited for: 1 -> 1; matrix products, arithmetic and copies ran while one was open for 7% -> 7% of each run, Pallas kernels for 75% -> 74%
where the time goes in v13:
time: 908 us; the launch traced here: 904 us
  Pallas kernels  790 us (87%)
  other arithmetic  42.8 us (5%)
  local copies, waits for them, and re-layouts  25 us (3%)
  matrix products  21.2 us (2%)
  between operations  15.1 us (2%)
  waiting for transfers between devices  9.59 us (1%)
    pallas_call x16, Pallas kernels, call(): pl.pallas_call(kernel, grid=grid, out_shape=tuple(out_shape) + tuple(shap...  769 us
    dot_general x3, matrix products, dot(): return lax.dot_general(a, b, dims, preferred_element_type=F32)  21.2 us
  transfers between devices with their start and end apart: 7, of which 1 were waited for; matrix products, arithmetic and copies ran while one was open for 7% of the time, Pallas kernels for 74%

profile of v13, /device:TPU:6, one launch (start us, length us, event | category | flops | bytes accessed | tf_op | source)
XLA Modules:
  0.0 904.4 jit_solution(15534357404640448531)
XLA Ops:
  7.2 1.0 constant_dynamic-slice_fusion.2
  8.2 0.9 constant_dynamic-slice_fusion
  9.1 0.8 pad_maximum_fusion.2
  10.0 2.1 convert_element_type.79
  12.4 0.9 multiply_multiply_fusion
  13.3 0.8 copy-done
  14.1 1.7 multiply_convert_fusion.3
  15.9 38.7 %transfer.4 = (bf16[4,256,2048]{2,1,0:T(8,128)(2,1)}, bf16[64,2048]{1,0:T(8,128)(2,1)}, bf16[3,128,2048]{2,1,0:T(8,128)(2,1)}, bf16[3,128,2048]{2,1,0:T(8,128)(2,1)}) custom-call(bf16[256,2048]{1,0:T(8,128)(2,1)} %get-tuple-element.154.refs_0_, bf16[256,2048]{1,0:T(8,128)(2,1)} %refs_1_.1, bf16[1024,2048]{1,0:T(8,128)(2,1)} %refs_2_.1, ...), custom_call_target="tpu_custom_call" | custom-call | tf_op jit(solution)/shard_map/transfer/pallas_call | solution.py:567
  54.6 0.7 all-gather.8.cloned.1.call-update
  57.6 2.0 copy-done.10
  59.6 1.6 fusion.8
  61.3 49.5 %attend.2 = (bf16[4,256,512]{2,1,0:T(8,128)(2,1)}, f32[8,1024,1]{2,1,0:T(8,128)}, bf16[4,256,768]{2,1,0:T(8,128)(2,1)}, bf16[4,256,2048]{2,1,0:T(8,128)(2,1)}, bf16[8,64,2048]{2,1,0:T(8,128)(2,1)}) custom-call(s32[1]{0:T(128)} %get-tuple-element.169.refs_0_, bf16[4,256,2048]{2,1,0:T(8,128)(2,1)} %get-tuple-element.73.refs_1_.refs_8_, ...), custom_call_target="tpu_custom_call" | custom-call | flops 30064771072 | bytes 8388608 | tf_op jit(solution)/shard_map/attend/pallas_call | solution.py:567
  110.7 6.3 convolution_convert_fusion
  117.0 45.4 %attend.3 = (bf16[4,256,512]{2,1,0:T(8,128)(2,1)}, f32[8,1024,1]{2,1,0:T(8,128)}, bf16[4,256,768]{2,1,0:T(8,128)(2,1)}, bf16[4,256,2048]{2,1,0:T(8,128)(2,1)}, f32[256,2048]{1,0:T(8,128)}) custom-call(s32[1]{0:T(128)} %get-tuple-element.170.refs_0_, bf16[4,256,2048]{2,1,0:T(8,128)(2,1)} %get-tuple-element.75.refs_1_, ...), custom_call_target="tpu_custom_call" | custom-call | flops 30064771072 | bytes 8388608 | tf_op jit(solution)/shard_map/attend/pallas_call | solution.py:567
  162.4 1.9 multiply_reduce_fusion.7
  164.3 1.3 copy-done.7
  165.6 1.2 multiply_convert_fusion.2.refs_1_
  166.8 70.4 %transfer.5 = (bf16[4,256,2048]{2,1,0:T(8,128)(2,1)}, bf16[4,256,2048]{2,1,0:T(8,128)(2,1)}) custom-call(bf16[4,256,512]{2,1,0:T(8,128)(2,1)} %get-tuple-element.79.refs_0_.refs_12_, bf16[256,2048]{1,0:T(8,128)(2,1)} %multiply_convert_fusion.2.refs_1_, bf16[256,2048]{1,0:T(8,128)(2,1)} %get-tuple-element.156.refs_2_), custom_call_target="tpu_custom_call" | custom-call | tf_op jit(solution)/shard_map/transfer/pallas_call | solution.py:567
  237.3 73.1 %ffn_both.4 = (bf16[3,1024,1024]{2,1,0:T(8,128)(2,1)}, f32[1024,2048]{1,0:T(8,128)}, f32[256,2048]{1,0:T(8,128)}, bf16[4,256,2048]{2,1,0:T(8,128)(2,1)}) custom-call(bf16[1024,2048]{1,0:T(8,128)(2,1)} %bitcast.139, bf16[1024,2048]{1,0:T(8,128)(2,1)} %bitcast.144, bf16[8,3,128,2048]{3,2,1,0:T(8,128)(2,1)} %bitcast.131, bf16[1024,2048]{1,0:T(8,128)(2,1)} %bitcast.140, ...), custom_call_target="tpu_custom_call" | custom-call | flops 34359738368 | bytes 20971520 | tf_op jit(solution)/shard_map/ffn_both/pallas_call | solution.py:567
  310.4 1.9 multiply_reduce_fusion.6
  312.9 0.7 copy-done.4
  313.7 1.2 multiply_convert_fusion.1.refs_5_
  314.9 39.2 %ffn_both.5 = (bf16[3,1024,1024]{2,1,0:T(8,128)(2,1)}, bf16[1024,2048]{1,0:T(8,128)(2,1)}, bf16[4,256,2048]{2,1,0:T(8,128)(2,1)}) custom-call(bf16[1024,2048]{1,0:T(8,128)(2,1)} %bitcast.141, bf16[1024,2048]{1,0:T(8,128)(2,1)} %bitcast.145, bf16[8,3,128,2048]{3,2,1,0:T(8,128)(2,1)} %bitcast.135, f32[1024,2048]{1,0:T(8,128)} %get-tuple-element.85.refs_3_, ...), custom_call_target="tpu_custom_call" | custom-call | flops 34359738368 | bytes 20971520 | tf_op jit(solution)/shard_map/ffn_both/pallas_call | solution.py:567
  354.1 39.5 %ffn_both.6 = (bf16[3,1024,1024]{2,1,0:T(8,128)(2,1)}, f32[1024,2048]{1,0:T(8,128)}, f32[256,2048]{1,0:T(8,128)}) custom-call(bf16[1024,2048]{1,0:T(8,128)(2,1)} %bitcast.153, bf16[1024,2048]{1,0:T(8,128)(2,1)} %bitcast.149, bf16[8,3,128,2048]{3,2,1,0:T(8,128)(2,1)} %bitcast.132, bf16[3,1024,1024]{2,1,0:T(8,128)(2,1)} %get-tuple-element.90.refs_3_.refs_1_.refs_0_, ...), custom_call_target="tpu_custom_call" | custom-call | flops 34359738368 | bytes 20971520 | tf_op jit(solution)/shard_map/ffn_both/pallas_call | solution.py:567
  393.7 2.3 multiply_reduce_fusion.3
  396.5 3.9 fusion.16
  400.4 38.7 %ffn_grads.2 = (bf16[8,3,128,2048]{3,2,1,0:T(8,128)(2,1)}, bf16[4,256,2048]{2,1,0:T(8,128)(2,1)}) custom-call(bf16[3,1024,1024]{2,1,0:T(8,128)(2,1)} %get-tuple-element.86.refs_4_.refs_0_, bf16[3,1024,1024]{2,1,0:T(8,128)(2,1)} %get-tuple-element.93.refs_1_.refs_6_.refs_0_, bf16[1024,2048]{1,0:T(8,128)(2,1)} %bitcast.142, bf16[1024,2048]{1,0:T(8,128)(2,1)} %bitcast.154, ...), custom_call_target="tpu_custom_call" | custom-call | flops 38654705664 | bytes 16777216 | tf_op jit(solution)/shard_map/ffn_grads/pallas_call | solution.py:567
  439.1 14.6 %ffn_down.2 = bf16[1024,2048]{1,0:T(8,128)(2,1)} custom-call(bf16[3,1024,1024]{2,1,0:T(8,128)(2,1)} %get-tuple-element.86.refs_4_.refs_0_, bf16[3,1024,1024]{2,1,0:T(8,128)(2,1)} %get-tuple-element.90.refs_3_.refs_1_.refs_0_, bf16[8,3,128,2048]{3,2,1,0:T(8,128)(2,1)} %bitcast.133, bf16[8,3,128,2048]{3,2,1,0:T(8,128)(2,1)} %bitcast.136, ...), custom_call_target="tpu_custom_call" | custom-call | flops 17179869184 | bytes 12582912 | tf_op jit(solution)/shard_map/ffn_down/pallas_call | solution.py:567
  453.7 36.6 %ffn_both.7 = (bf16[3,1024,1024]{2,1,0:T(8,128)(2,1)}, bf16[1024,2048]{1,0:T(8,128)(2,1)}, f32[256,2048]{1,0:T(8,128)}) custom-call(bf16[1024,2048]{1,0:T(8,128)(2,1)} %bitcast.155, bf16[1024,2048]{1,0:T(8,128)(2,1)} %bitcast.151, bf16[8,3,128,2048]{3,2,1,0:T(8,128)(2,1)} %bitcast.137, f32[1024,2048]{1,0:T(8,128)} %get-tuple-element.92.refs_3_, ...), custom_call_target="tpu_custom_call" | custom-call | flops 34359738368 | bytes 20971520 | tf_op jit(solution)/shard_map/ffn_both/pallas_call | solution.py:567
  490.3 38.5 %ffn_grads.3 = (bf16[8,3,128,2048]{3,2,1,0:T(8,128)(2,1)}, f32[256,2048]{1,0:T(8,128)}) custom-call(bf16[3,1024,1024]{2,1,0:T(8,128)(2,1)} %get-tuple-element.90.refs_3_.refs_1_.refs_0_, bf16[3,1024,1024]{2,1,0:T(8,128)(2,1)} %get-tuple-element.97.refs_1_.refs_6_, bf16[1024,2048]{1,0:T(8,128)(2,1)} %bitcast.143, bf16[1024,2048]{1,0:T(8,128)(2,1)} %bitcast.156, ...), custom_call_target="tpu_custom_call" | custom-call | flops 38654705664 | bytes 16777216 | tf_op jit(solution)/shard_map/ffn_grads/pallas_call | solution.py:567
  529.1 1.4 copy-done.5
  530.5 2.3 multiply_reduce_fusion.2
  533.3 3.9 fusion.15
  537.2 47.9 %attend_back.2 = (bf16[4,256,768]{2,1,0:T(8,128)(2,1)}, f32[2,128]{1,0:T(2,128)}, bf16[4,256,2048]{2,1,0:T(8,128)(2,1)}, bf16[4,256,2048]{2,1,0:T(8,128)(2,1)}) custom-call(s32[1]{0:T(128)} %get-tuple-element.169.refs_0_, bf16[4,256,768]{2,1,0:T(8,128)(2,1)} %get-tuple-element.101.refs_1_, bf16[4,256,2048]{2,1,0:T(8,128)(2,1)} %get-tuple-element.102.refs_2_.refs_13_, ...), custom_call_target="tpu_custom_call" | custom-call | flops 47244640256 | bytes 8388608 | tf_op jit(solution)/shard_map/attend_back/pallas_call | solution.py:567
  585.1 7.2 fusion.21
  592.4 88.0 %attend_back.3 = (bf16[4,256,768]{2,1,0:T(8,128)(2,1)}, f32[2,128]{1,0:T(2,128)}, bf16[4,256,2048]{2,1,0:T(8,128)(2,1)}, bf16[2048,512]{1,0:T(8,128)(2,1)}, f32[...) custom-call(s32[1]{0:T(128)} %get-tuple-element.170.refs_0_, bf16[4,256,768]{2,1,0:T(8,128)(2,1)} %get-tuple-element.100.refs_1_, ...), custom_call_target="tpu_custom_call" | custom-call | flops 47244640256 | bytes 8388608 | tf_op jit(solution)/shard_map/attend_back/pallas_call | solution.py:567
  680.4 0.7 add.142
  681.6 8.1 place_parts.2
  689.7 7.7 fusion.2
  697.5 3.0 fusion.4
  700.5 8.8 reduce-scatter.7.cloned.1.call-done
  709.3 40.9 %ffn_down.3 = (bf16[1024,2048]{1,0:T(8,128)(2,1)}, f32[256,2048]{1,0:T(8,128)}) custom-call(bf16[3,1024,1024]{2,1,0:T(8,128)(2,1)} %get-tuple-element.93.refs_1_.refs_6_.refs_0_, bf16[3,1024,1024]{2,1,0:T(8,128)(2,1)} %get-tuple-element.97.refs_1_.refs_6_, bf16[8,3,128,2048]{3,2,1,0:T(8,128)(2,1)} %bitcast.134, bf16[8,3,128,2048]{3,2,1,0:T(8,128)(2,1)} %bitcast.138, ...), custom_call_target="tpu_custom_call" | custom-call | flops 17179869184 | bytes 12582912 | tf_op jit(solution)/shard_map/ffn_down/pallas_call | solution.py:567
  750.2 50.5 %transfer.6 = bf16[4,384,2048]{2,1,0:T(8,128)(2,1)} custom-call(f32[256,2048]{1,0:T(8,128)} %get-tuple-element.118.refs_0_, bf16[384,2048]{1,0:T(8,128)(2,1)} %bitcast.125), custom_call_target="tpu_custom_call" | custom-call | tf_op jit(solution)/shard_map/transfer/pallas_call | solution.py:567
  801.5 0.9 copy-done.9
  802.4 1.8 fusion.11
  804.2 8.7 place_parts.3
  813.1 3.1 multiply_reduce_fusion.1
  816.7 0.6 copy-done.15
  817.4 0.7 copy-done.16
  818.0 1.4 fusion.12
  819.5 1.5 pad_maximum_fusion.1
  821.0 0.7 slice.95.refs_2_
  821.7 0.8 slice.94.refs_1_
  822.5 57.2 %transfer.7 = (bf16[4,256,896]{2,1,0:T(8,128)(2,1)}, bf16[4,256,512]{2,1,0:T(8,128)(2,1)}, bf16[4,256,512]{2,1,0:T(8,128)(2,1)}) custom-call(f32[4,2,128,2048]{3,2,1,0:T(8,128)} %get-tuple-element.123.refs_0_, bf16[256,896]{1,0:T(8,128)(2,1)} %slice.94.refs_1_, bf16[256,512]{1,0:T(8,128)(2,1)} %slice.95.refs_2_), custom_call_target="tpu_custom_call" | custom-call | tf_op jit(solution)/shard_map/transfer/pallas_call | solution.py:567
  879.7 1.5 convert_bitcast_fusion
  881.2 1.4 copy.51
  882.6 2.2 copy.60
  884.8 4.7 place_heads.1
  889.5 1.5 slice_reduce_fusion.2
  891.0 1.6 slice_reduce_fusion
  892.6 1.0 slice_reduce_fusion.1
  893.6 0.7 dynamic-slice_divide_fusion
  894.2 1.5 fusion.14
  895.7 1.5 pad_maximum_fusion
  (114 shorter events, 6.7 us)
Async XLA Ops:
  7.2 54.1 %all-gather.6.cloned.1.call-start = ((), (), s32[]{:S(2)}) async-start(), calls=%async_computation.4 | async-start | bytes 3538944 | tf_op jit(solution)/shard_map/all_gather | solution.py:1269
  9.9 227.3 %all-gather.10.cloned.1.call-start = ((), (), s32[]{:S(2)}) async-start(), calls=%async_computation.9 | async-start | bytes 14155776 | tf_op jit(solution)/shard_map/all_gather | solution.py:1278
  12.1 2.1 copy-start
  12.1 2.1 copy-start.21
  13.3 2.6 copy-start.27
  13.3 2.6 copy-start.29
  54.5 0.9 copy-start.36
  54.5 0.9 copy-start.37
  54.5 1.5 copy-start.31
  54.6 2.7 copy-start.17
  54.6 260.3 %all-gather.8.cloned.1.call-start = ((), (), s32[]{:S(2)}) async-start(), calls=%async_computation.8 | async-start | bytes 14155776 | tf_op jit(solution)/shard_map/all_gather | solution.py:1278
  55.3 537.0 %reduce-scatter.9.cloned.1.call-start = ((), (), s32[]{:S(2)}) async-start(), calls=%async_computation.6 | async-start | bytes 14155776 | tf_op jit(solution)/shard_map/reduce_scatter | solution.py:1351
  56.7 0.6 copy-start.23
  57.6 2.0 copy-start.10
  117.0 45.4 %copy-start.1 = (f32[2,256,2048]{2,1,0:T(8,128)S(1)}, f32[2,256,2048]{2,1,0:T(8,128)}, u32[]{:S(2)}) copy-start(f32[2,256,2048]{2,1,0:T(8,128)} %copy-done) | copy-start | bytes 12582916
  162.4 3.2 copy-start.20
  164.3 1.3 copy-start.7
  237.2 73.2 %copy-start.2 = (f32[2,256,2048]{2,1,0:T(8,128)S(1)}, f32[2,256,2048]{2,1,0:T(8,128)}, u32[]{:S(2)}) copy-start(f32[2,256,2048]{2,1,0:T(8,128)} %copy-done) | copy-start | bytes 12582916
  312.3 1.3 copy-start.4
  312.9 0.7 copy-start.25
  354.1 39.5 %copy-start.8 = (f32[256,2048]{1,0:T(8,128)S(1)}, f32[256,2048]{1,0:T(8,128)}, u32[]{:S(2)}) copy-start(f32[256,2048]{1,0:T(8,128)} %copy-done.7) | copy-start | bytes 6291460
  393.7 2.8 copy-start.11
  439.1 270.2 %reduce-scatter.7.cloned.1.call-start = ((), (), s32[]{:S(2)}) async-start(), calls=%async_computation.5 | async-start | bytes 14155776 | tf_op jit(solution)/shard_map/reduce_scatter | solution.py:1358
  528.8 1.6 copy-start.5
  528.8 1.6 copy-start.26
  528.9 271.9 %reduce-scatter.11.cloned.1.call-start = ((), (), s32[]{:S(2)}) async-start(), calls=%async_computation.7 | async-start | bytes 6488064 | tf_op jit(solution)/shard_map/reduce_scatter | solution.py:1400
  530.4 2.8 copy-start.12
  530.5 2.8 copy-start.32
  537.2 47.9 %copy-start.38 = (bf16[4,256,2048]{2,1,0:T(8,128)(2,1)S(1)}, bf16[4,256,2048]{2,1,0:T(8,128)(2,1)}, u32[]{:S(2)}) copy-start(bf16[4,256,2048]{2,1,0:T(8,128)(2,1)} %get-tuple-element.73.refs_1_.refs_8_) | copy-start | bytes 12582916
  592.4 88.0 %copy-start.35 = (f32[2,128]{1,0:T(2,128)S(1)}, f32[2,128]{1,0:T(2,128)}, u32[]{:S(2)}) copy-start(f32[2,128]{1,0:T(2,128)} %get-tuple-element.112) | copy-start | bytes 3076
  681.6 8.1 copy-start.39
  689.7 7.7 copy-start.18
  709.3 185.0 %reduce-scatter.13.cloned.1.call-start = ((), (), s32[]{:S(2)}) async-start(), calls=%async_computation.10 | async-start | bytes 5242880
  800.8 0.7 copy-start.24
  800.8 1.6 copy-start.9
  804.2 8.8 copy-start.3
  804.2 8.8 copy-start.22
  813.0 3.2 copy-start.13
  813.0 3.8 copy-start.14
  813.0 4.4 copy-start.15
  813.0 5.0 copy-start.16
  813.0 5.0 copy-start.28
  813.0 5.0 copy-start.30
  813.0 5.0 copy-start.33
  813.1 5.0 copy-start.34
  819.4 1.5 copy-start.19
  884.8 9.5 %copy-start.6 = (f32[256,2048]{1,0:T(8,128)S(1)}, f32[256,2048]{1,0:T(8,128)}, u32[]{:S(2)}) copy-start(f32[256,2048]{1,0:T(8,128)} %copy-done.4) | copy-start | bytes 6291460
Sparse Core Ops, SparseCore 0:
  10.2 49.3 all-gather.5
  61.2 133.8 all-gather.9
  196.8 116.3 all-gather.7
  439.2 140.2 reduce-scatter.8
  581.6 127.5 reduce-scatter.6
  711.4 66.8 reduce-scatter.10
  801.0 67.8 reduce-scatter.12

commit v14 on v13

--- a/solution.py
+++ b/solution.py
@@ -1395,10 +1395,12 @@
         ],
         axis=1,
     )
+    pull, _ = normed_back(inputs[0], attn_gain, in_total_0)
+    tokens_0 = (res_cot_0 + pull).astype(BF16)
     ffn_grad = place_parts(order, ffn_parts_0.reshape(seqs, 3, part, model), 0, ())
     out_1, (in_total_1,) = leave_ffn(1, [("scatter", pull_1)], 13, ffn_sums[1], True)
     attn_sums = lax.psum_scatter(
-        follow(attn_grads, [ffn_sums[1], ffn_grad[0]]), "fsdp", scatter_dimension=0, tiled=True
+        follow(attn_grads, [ffn_sums[1], ffn_grad[0], tokens_0]), "fsdp", scatter_dimension=0, tiled=True
     )
     (ffn_parts_1,) = transfer([("gather", ffn_sums[1])], 15, in_total_1)
     ffn_grad = place_parts(order, ffn_parts_1.reshape(seqs, 3, part, model), 1, ffn_grad)
@@ -1411,10 +1413,8 @@
     grad_out = jnp.swapaxes(
         out_parts.reshape(seqs, blocks, piece, model // blocks), 1, 2
     ).reshape(held, model)
-    grad_tokens = []
-    for b, (in_cot, cot) in enumerate(((in_total_0, res_cot_0), (in_total_1, res_cot_1))):
-        pull, _ = normed_back(inputs[b], attn_gain, in_cot)
-        grad_tokens.append((cot + pull).astype(BF16))
+    pull, _ = normed_back(inputs[1], attn_gain, in_total_1)
+    grad_tokens = [tokens_0, (res_cot_1 + pull).astype(BF16)]
     out_total_1 = lax.psum_scatter(
         follow(out_1, [attn_sums, ffn_parts_1]), "seq", scatter_dimension=0
     ).astype(F32)

time: 908 us -> 950 us (1.046)
  waiting for transfers between devices: 9.59 us -> 43.6 us
    reduce_scatter x1, waiting for transfers between devices: 8.76 us -> 27.8 us  [on_device(): ffn_sums.append(lax.psum_scatter(grads_1, 'fsdp', scatter_dimension=0))]
    reduce_scatter x1, waiting for transfers between devices: 0.02 us -> 15 us  [on_device(): lax.psum_scatter(follow(attn_grads, [ffn_sums[1], ffn_grad[0], tokens_0])...]
  transfers between devices with their start and end apart: 7 -> 7, of which waited for: 1 -> 2; matrix products, arithmetic and copies ran while one was open for 7% -> 5% of each run, Pallas kernels for 74% -> 66%
where the time goes in v14:
time: 950 us; the launch traced here: 946 us
  Pallas kernels  792 us (83%)
  other arithmetic  48.9 us (5%)
  waiting for transfers between devices  43.6 us (5%)
  matrix products  23.3 us (2%)
  local copies, waits for them, and re-layouts  23.1 us (2%)
  between operations  15 us (2%)
    pallas_call x16, Pallas kernels, call(): pl.pallas_call(kernel, grid=grid, out_shape=tuple(out_shape) + tuple(shap...  771 us
    reduce_scatter x1, waiting for transfers between devices, on_device(): ffn_sums.append(lax.psum_scatter(grads_1, 'fsdp', scatter_dimension=0))  27.8 us
    dot_general x3, matrix products, dot(): return lax.dot_general(a, b, dims, preferred_element_type=F32)  23.3 us
  transfers between devices with their start and end apart: 7, of which 2 were waited for; matrix products, arithmetic and copies ran while one was open for 5% of the time, Pallas kernels for 66%

profile of v14, /device:TPU:6, one launch (start us, length us, event | category | flops | bytes accessed | tf_op | source)
XLA Modules:
  0.0 946.1 jit_solution(13083761221579237842)
XLA Ops:
  7.2 1.0 constant_dynamic-slice_fusion.2
  8.2 0.9 constant_dynamic-slice_fusion
  9.1 0.8 pad_maximum_fusion.2
  10.0 2.1 convert_element_type.79
  12.4 0.9 multiply_multiply_fusion
  13.3 0.8 copy-done
  14.1 1.7 multiply_convert_fusion.3
  15.8 38.7 %transfer.4 = (bf16[4,256,2048]{2,1,0:T(8,128)(2,1)}, bf16[64,2048]{1,0:T(8,128)(2,1)}, bf16[3,128,2048]{2,1,0:T(8,128)(2,1)}, bf16[3,128,2048]{2,1,0:T(8,128)(2,1)}) custom-call(bf16[256,2048]{1,0:T(8,128)(2,1)} %get-tuple-element.154.refs_0_, bf16[256,2048]{1,0:T(8,128)(2,1)} %refs_1_.1, bf16[1024,2048]{1,0:T(8,128)(2,1)} %refs_2_.1, ...), custom_call_target="tpu_custom_call" | custom-call | tf_op jit(solution)/shard_map/transfer/pallas_call | solution.py:567
  54.6 0.7 all-gather.8.cloned.1.call-update
  55.4 0.7 maximum_bitcast_fusion
  57.7 2.0 copy-done.10
  59.7 1.6 fusion.8
  61.3 49.5 %attend.2 = (bf16[4,256,512]{2,1,0:T(8,128)(2,1)}, f32[8,1024,1]{2,1,0:T(8,128)}, bf16[4,256,768]{2,1,0:T(8,128)(2,1)}, bf16[4,256,2048]{2,1,0:T(8,128)(2,1)}, bf16[8,64,2048]{2,1,0:T(8,128)(2,1)}) custom-call(s32[1]{0:T(128)} %get-tuple-element.169.refs_0_, bf16[4,256,2048]{2,1,0:T(8,128)(2,1)} %get-tuple-element.73.refs_1_.refs_8_, ...), custom_call_target="tpu_custom_call" | custom-call | flops 30064771072 | bytes 8388608 | tf_op jit(solution)/shard_map/attend/pallas_call | solution.py:567
  110.7 6.3 convolution_convert_fusion
  117.0 45.2 %attend.3 = (bf16[4,256,512]{2,1,0:T(8,128)(2,1)}, f32[8,1024,1]{2,1,0:T(8,128)}, bf16[4,256,768]{2,1,0:T(8,128)(2,1)}, bf16[4,256,2048]{2,1,0:T(8,128)(2,1)}, f32[256,2048]{1,0:T(8,128)}) custom-call(s32[1]{0:T(128)} %get-tuple-element.170.refs_0_, bf16[4,256,2048]{2,1,0:T(8,128)(2,1)} %get-tuple-element.75.refs_1_, ...), custom_call_target="tpu_custom_call" | custom-call | flops 30064771072 | bytes 8388608 | tf_op jit(solution)/shard_map/attend/pallas_call | solution.py:567
  162.3 1.9 multiply_reduce_fusion.7
  164.2 1.3 copy-done.7
  165.5 1.2 multiply_convert_fusion.2.refs_1_
  166.8 70.4 %transfer.5 = (bf16[4,256,2048]{2,1,0:T(8,128)(2,1)}, bf16[4,256,2048]{2,1,0:T(8,128)(2,1)}) custom-call(bf16[4,256,512]{2,1,0:T(8,128)(2,1)} %get-tuple-element.79.refs_0_.refs_12_, bf16[256,2048]{1,0:T(8,128)(2,1)} %multiply_convert_fusion.2.refs_1_, bf16[256,2048]{1,0:T(8,128)(2,1)} %get-tuple-element.156.refs_2_), custom_call_target="tpu_custom_call" | custom-call | tf_op jit(solution)/shard_map/transfer/pallas_call | solution.py:567
  237.2 73.2 %ffn_both.4 = (bf16[3,1024,1024]{2,1,0:T(8,128)(2,1)}, f32[1024,2048]{1,0:T(8,128)}, f32[256,2048]{1,0:T(8,128)}, bf16[4,256,2048]{2,1,0:T(8,128)(2,1)}) custom-call(bf16[1024,2048]{1,0:T(8,128)(2,1)} %bitcast.137, bf16[1024,2048]{1,0:T(8,128)(2,1)} %bitcast.142, bf16[8,3,128,2048]{3,2,1,0:T(8,128)(2,1)} %bitcast.129, bf16[1024,2048]{1,0:T(8,128)(2,1)} %bitcast.138, ...), custom_call_target="tpu_custom_call" | custom-call | flops 34359738368 | bytes 20971520 | tf_op jit(solution)/shard_map/ffn_both/pallas_call | solution.py:567
  310.4 1.9 multiply_reduce_fusion.6
  312.9 0.7 copy-done.4
  313.6 1.2 multiply_convert_fusion.1.refs_5_
  314.8 39.3 %ffn_both.5 = (bf16[3,1024,1024]{2,1,0:T(8,128)(2,1)}, bf16[1024,2048]{1,0:T(8,128)(2,1)}, bf16[4,256,2048]{2,1,0:T(8,128)(2,1)}) custom-call(bf16[1024,2048]{1,0:T(8,128)(2,1)} %bitcast.139, bf16[1024,2048]{1,0:T(8,128)(2,1)} %bitcast.143, bf16[8,3,128,2048]{3,2,1,0:T(8,128)(2,1)} %bitcast.133, f32[1024,2048]{1,0:T(8,128)} %get-tuple-element.85.refs_3_, ...), custom_call_target="tpu_custom_call" | custom-call | flops 34359738368 | bytes 20971520 | tf_op jit(solution)/shard_map/ffn_both/pallas_call | solution.py:567
  354.1 39.5 %ffn_both.6 = (bf16[3,1024,1024]{2,1,0:T(8,128)(2,1)}, f32[1024,2048]{1,0:T(8,128)}, f32[256,2048]{1,0:T(8,128)}) custom-call(bf16[1024,2048]{1,0:T(8,128)(2,1)} %bitcast.151, bf16[1024,2048]{1,0:T(8,128)(2,1)} %bitcast.147, bf16[8,3,128,2048]{3,2,1,0:T(8,128)(2,1)} %bitcast.130, bf16[3,1024,1024]{2,1,0:T(8,128)(2,1)} %get-tuple-element.90.refs_3_.refs_1_.refs_0_, ...), custom_call_target="tpu_custom_call" | custom-call | flops 34359738368 | bytes 20971520 | tf_op jit(solution)/shard_map/ffn_both/pallas_call | solution.py:567
  393.6 2.3 multiply_reduce_fusion.3
  396.5 3.9 fusion.15
  400.4 38.6 %ffn_grads.2 = (bf16[8,3,128,2048]{3,2,1,0:T(8,128)(2,1)}, bf16[4,256,2048]{2,1,0:T(8,128)(2,1)}) custom-call(bf16[3,1024,1024]{2,1,0:T(8,128)(2,1)} %get-tuple-element.86.refs_4_.refs_0_, bf16[3,1024,1024]{2,1,0:T(8,128)(2,1)} %get-tuple-element.93.refs_1_.refs_6_.refs_0_, bf16[1024,2048]{1,0:T(8,128)(2,1)} %bitcast.140, bf16[1024,2048]{1,0:T(8,128)(2,1)} %bitcast.152, ...), custom_call_target="tpu_custom_call" | custom-call | flops 38654705664 | bytes 16777216 | tf_op jit(solution)/shard_map/ffn_grads/pallas_call | solution.py:567
  439.1 14.6 %ffn_down.2 = bf16[1024,2048]{1,0:T(8,128)(2,1)} custom-call(bf16[3,1024,1024]{2,1,0:T(8,128)(2,1)} %get-tuple-element.86.refs_4_.refs_0_, bf16[3,1024,1024]{2,1,0:T(8,128)(2,1)} %get-tuple-element.90.refs_3_.refs_1_.refs_0_, bf16[8,3,128,2048]{3,2,1,0:T(8,128)(2,1)} %bitcast.131, bf16[8,3,128,2048]{3,2,1,0:T(8,128)(2,1)} %bitcast.134, ...), custom_call_target="tpu_custom_call" | custom-call | flops 17179869184 | bytes 12582912 | tf_op jit(solution)/shard_map/ffn_down/pallas_call | solution.py:567
  453.7 36.6 %ffn_both.7 = (bf16[3,1024,1024]{2,1,0:T(8,128)(2,1)}, bf16[1024,2048]{1,0:T(8,128)(2,1)}, f32[256,2048]{1,0:T(8,128)}) custom-call(bf16[1024,2048]{1,0:T(8,128)(2,1)} %bitcast.153, bf16[1024,2048]{1,0:T(8,128)(2,1)} %bitcast.149, bf16[8,3,128,2048]{3,2,1,0:T(8,128)(2,1)} %bitcast.135, f32[1024,2048]{1,0:T(8,128)} %get-tuple-element.92.refs_3_, ...), custom_call_target="tpu_custom_call" | custom-call | flops 34359738368 | bytes 20971520 | tf_op jit(solution)/shard_map/ffn_both/pallas_call | solution.py:567
  490.3 38.5 %ffn_grads.3 = (bf16[8,3,128,2048]{3,2,1,0:T(8,128)(2,1)}, f32[256,2048]{1,0:T(8,128)}) custom-call(bf16[3,1024,1024]{2,1,0:T(8,128)(2,1)} %get-tuple-element.90.refs_3_.refs_1_.refs_0_, bf16[3,1024,1024]{2,1,0:T(8,128)(2,1)} %get-tuple-element.97.refs_1_.refs_6_, bf16[1024,2048]{1,0:T(8,128)(2,1)} %bitcast.141, bf16[1024,2048]{1,0:T(8,128)(2,1)} %bitcast.154, ...), custom_call_target="tpu_custom_call" | custom-call | flops 38654705664 | bytes 16777216 | tf_op jit(solution)/shard_map/ffn_grads/pallas_call | solution.py:567
  529.1 1.3 copy-done.5
  530.4 2.3 multiply_reduce_fusion.2
  533.3 3.9 fusion.14
  537.2 47.8 %attend_back.2 = (bf16[4,256,768]{2,1,0:T(8,128)(2,1)}, f32[2,128]{1,0:T(2,128)}, bf16[4,256,2048]{2,1,0:T(8,128)(2,1)}, bf16[4,256,2048]{2,1,0:T(8,128)(2,1)}) custom-call(s32[1]{0:T(128)} %get-tuple-element.169.refs_0_, bf16[4,256,768]{2,1,0:T(8,128)(2,1)} %get-tuple-element.101.refs_1_, bf16[4,256,2048]{2,1,0:T(8,128)(2,1)} %get-tuple-element.102.refs_2_.refs_13_, ...), custom_call_target="tpu_custom_call" | custom-call | flops 47244640256 | bytes 8388608 | tf_op jit(solution)/shard_map/attend_back/pallas_call | solution.py:567
  585.0 7.3 fusion.20
  592.3 87.9 %attend_back.3 = (bf16[4,256,768]{2,1,0:T(8,128)(2,1)}, f32[2,128]{1,0:T(2,128)}, bf16[4,256,2048]{2,1,0:T(8,128)(2,1)}, bf16[2048,512]{1,0:T(8,128)(2,1)}, f32[...) custom-call(s32[1]{0:T(128)} %get-tuple-element.170.refs_0_, bf16[4,256,768]{2,1,0:T(8,128)(2,1)} %get-tuple-element.100.refs_1_, ...), custom_call_target="tpu_custom_call" | custom-call | flops 47244640256 | bytes 8388608 | tf_op jit(solution)/shard_map/attend_back/pallas_call | solution.py:567
  680.2 0.7 add.142
  681.0 27.8 %reduce-scatter.7.cloned.1.call-done = bf16[1,384,2048]{2,1,0:T(8,128)(2,1)} async-done(((bf16[8,384,2048]{2,1,0:T(8,128)(2,1)}), bf16[1,384,2048]{2,1,0:T(8,128)(2,1)}) %reduce-scatter.7.cloned.1.call-update) | async-done | bytes 1572880 | tf_op jit(solution)/shard_map/reduce_scatter | solution.py:1358
  708.8 41.2 %ffn_down.3 = (bf16[1024,2048]{1,0:T(8,128)(2,1)}, f32[256,2048]{1,0:T(8,128)}) custom-call(bf16[3,1024,1024]{2,1,0:T(8,128)(2,1)} %get-tuple-element.93.refs_1_.refs_6_.refs_0_, bf16[3,1024,1024]{2,1,0:T(8,128)(2,1)} %get-tuple-element.97.refs_1_.refs_6_, bf16[8,3,128,2048]{3,2,1,0:T(8,128)(2,1)} %bitcast.132, bf16[8,3,128,2048]{3,2,1,0:T(8,128)(2,1)} %bitcast.136, ...), custom_call_target="tpu_custom_call" | custom-call | flops 17179869184 | bytes 12582912 | tf_op jit(solution)/shard_map/ffn_down/pallas_call | solution.py:567
  750.0 2.7 multiply_reduce_fusion
  753.2 9.7 %fusion.2 = bf16[2048,768]{1,0:T(8,128)(2,1)} fusion(f32[2048,768,1]{1,0,2:T(8,128)} %fusion.20, bf16[4,256,2048]{2,1,0:T(8,128)(2,1)} %get-tuple-element.75.refs_1_, bf16[4,256,768]{2,1,0:T(8,128)(2,1)} %get-tuple-element.111), kind=kOutput, calls=%fused_computation.5 | convolution fusion | flops 3224371200 | bytes 15204352 | tf_op jit(solution)/shard_map/dot_general | solution.py:29
  762.9 7.8 place_parts.2
  770.8 5.0 fusion.4
  775.8 5.7 fusion.12
  781.6 50.4 %transfer.6 = bf16[4,384,2048]{2,1,0:T(8,128)(2,1)} custom-call(f32[256,2048]{1,0:T(8,128)} %get-tuple-element.119.refs_0_, bf16[384,2048]{1,0:T(8,128)(2,1)} %bitcast.123), custom_call_target="tpu_custom_call" | custom-call | tf_op jit(solution)/shard_map/transfer/pallas_call | solution.py:567
  832.0 15.0 %reduce-scatter.11.cloned.1.call-done = bf16[256,1408]{1,0:T(8,128)(2,1)} async-done(((bf16[2048,1408]{1,0:T(8,128)(2,1)}), bf16[256,1408]{1,0:T(8,128)(2,1)}) %reduce-scatter.11.cloned.1.call-update) | async-done | bytes 720912 | tf_op jit(solution)/shard_map/reduce_scatter | solution.py:1402
  847.7 0.9 copy-done.9
  848.7 1.8 fusion.11
  850.5 8.0 place_parts.3
  858.5 1.5 pad_maximum_fusion.1
  860.0 0.7 slice.95.refs_2_
  860.7 0.8 slice.94.refs_1_
  861.5 59.9 %transfer.7 = (bf16[4,256,896]{2,1,0:T(8,128)(2,1)}, bf16[4,256,512]{2,1,0:T(8,128)(2,1)}, bf16[4,256,512]{2,1,0:T(8,128)(2,1)}) custom-call(f32[4,2,128,2048]{3,2,1,0:T(8,128)} %get-tuple-element.123.refs_0_, bf16[256,896]{1,0:T(8,128)(2,1)} %slice.94.refs_1_, bf16[256,512]{1,0:T(8,128)(2,1)} %slice.95.refs_2_), custom_call_target="tpu_custom_call" | custom-call | tf_op jit(solution)/shard_map/transfer/pallas_call | solution.py:567
  921.5 1.5 convert_bitcast_fusion
  923.0 1.4 copy.51
  924.3 2.2 copy.60
  926.5 4.7 place_heads.1
  931.3 1.5 slice_reduce_fusion.2
  932.8 1.6 slice_reduce_fusion
  934.3 1.0 slice_reduce_fusion.1
  935.3 0.7 dynamic-slice_divide_fusion
  936.0 1.5 fusion.13
  937.5 1.5 pad_maximum_fusion
  (110 shorter events, 5.6 us)
Async XLA Ops:
  7.2 54.1 %all-gather.6.cloned.1.call-start = ((), (), s32[]{:S(2)}) async-start(), calls=%async_computation.4 | async-start | bytes 3538944 | tf_op jit(solution)/shard_map/all_gather | solution.py:1269
  9.9 227.3 %all-gather.10.cloned.1.call-start = ((), (), s32[]{:S(2)}) async-start(), calls=%async_computation.9 | async-start | bytes 14155776 | tf_op jit(solution)/shard_map/all_gather | solution.py:1278
  12.1 2.0 copy-start
  12.1 2.0 copy-start.20
  13.3 2.5 copy-start.26
  13.3 2.5 copy-start.28
  54.5 0.9 copy-start.35
  54.5 0.9 copy-start.36
  54.5 1.5 copy-start.30
  54.5 2.8 copy-start.16
  54.6 260.3 %all-gather.8.cloned.1.call-start = ((), (), s32[]{:S(2)}) async-start(), calls=%async_computation.8 | async-start | bytes 14155776 | tf_op jit(solution)/shard_map/all_gather | solution.py:1278
  55.3 537.0 %reduce-scatter.9.cloned.1.call-start = ((), (), s32[]{:S(2)}) async-start(), calls=%async_computation.6 | async-start | bytes 14155776 | tf_op jit(solution)/shard_map/reduce_scatter | solution.py:1351
  56.7 0.6 copy-start.22
  57.6 2.0 copy-start.10
  117.0 45.3 %copy-start.1 = (f32[2,256,2048]{2,1,0:T(8,128)S(1)}, f32[2,256,2048]{2,1,0:T(8,128)}, u32[]{:S(2)}) copy-start(f32[2,256,2048]{2,1,0:T(8,128)} %copy-done) | copy-start | bytes 12582916
  162.3 3.2 copy-start.19
  164.2 1.3 copy-start.7
  237.2 73.2 %copy-start.2 = (f32[2,256,2048]{2,1,0:T(8,128)S(1)}, f32[2,256,2048]{2,1,0:T(8,128)}, u32[]{:S(2)}) copy-start(f32[2,256,2048]{2,1,0:T(8,128)} %copy-done) | copy-start | bytes 12582916
  312.3 1.3 copy-start.4
  312.9 0.7 copy-start.24
  354.1 39.5 %copy-start.8 = (f32[256,2048]{1,0:T(8,128)S(1)}, f32[256,2048]{1,0:T(8,128)}, u32[]{:S(2)}) copy-start(f32[256,2048]{1,0:T(8,128)} %copy-done.7) | copy-start | bytes 6291460
  393.6 2.8 copy-start.11
  439.0 269.7 %reduce-scatter.7.cloned.1.call-start = ((), (), s32[]{:S(2)}) async-start(), calls=%async_computation.5 | async-start | bytes 14155776 | tf_op jit(solution)/shard_map/reduce_scatter | solution.py:1358
  528.8 1.6 copy-start.5
  528.8 1.6 copy-start.25
  528.8 318.2 %reduce-scatter.11.cloned.1.call-start = ((), (), s32[]{:S(2)}) async-start(), calls=%async_computation.7 | async-start | bytes 6488064 | tf_op jit(solution)/shard_map/reduce_scatter | solution.py:1402
  530.4 2.9 copy-start.12
  530.4 2.9 copy-start.31
  537.2 47.8 %copy-start.37 = (bf16[4,256,2048]{2,1,0:T(8,128)(2,1)S(1)}, bf16[4,256,2048]{2,1,0:T(8,128)(2,1)}, u32[]{:S(2)}) copy-start(bf16[4,256,2048]{2,1,0:T(8,128)(2,1)} %get-tuple-element.73.refs_1_.refs_8_) | copy-start | bytes 12582916
  592.3 87.9 %copy-start.34 = (f32[2,128]{1,0:T(2,128)S(1)}, f32[2,128]{1,0:T(2,128)}, u32[]{:S(2)}) copy-start(f32[2,128]{1,0:T(2,128)} %get-tuple-element.112) | copy-start | bytes 3076
  708.7 41.2 %copy-start.3 = (f32[2,256,2048]{2,1,0:T(8,128)S(1)}, f32[2,256,2048]{2,1,0:T(8,128)}, u32[]{:S(2)}) copy-start(f32[2,256,2048]{2,1,0:T(8,128)} %copy-done) | copy-start | bytes 12582916
  708.7 41.2 %copy-start.21 = (f32[2048]{0:T(1024)S(1)}, f32[2048]{0:T(1024)}, u32[]{:S(2)}) copy-start(f32[2048]{0:T(1024)} %param.20) | copy-start | bytes 24580
  762.9 7.8 copy-start.17
  770.7 5.1 copy-start.13
  770.7 5.1 copy-start.27
  770.7 5.1 copy-start.29
  770.8 5.1 copy-start.32
  770.8 5.1 copy-start.33
  781.5 154.5 %reduce-scatter.13.cloned.1.call-start = ((), (), s32[]{:S(2)}) async-start(), calls=%async_computation.10 | async-start | bytes 5242880
  847.1 0.7 copy-start.23
  847.1 1.6 copy-start.9
  850.5 8.0 copy-start.14
  850.5 8.0 copy-start.15
  858.5 1.5 copy-start.18
  926.5 9.5 %copy-start.6 = (f32[256,2048]{1,0:T(8,128)S(1)}, f32[256,2048]{1,0:T(8,128)}, u32[]{:S(2)}) copy-start(f32[256,2048]{1,0:T(8,128)} %copy-done.4) | copy-start | bytes 6291460
Sparse Core Ops, SparseCore 0:
  10.2 49.3 all-gather.5
  61.2 133.8 all-gather.9
  196.8 116.3 all-gather.7
  439.2 139.7 reduce-scatter.8
  581.1 127.5 reduce-scatter.6
  781.7 65.3 reduce-scatter.10
  850.0 66.9 reduce-scatter.12
